TPU v7x, 32 devices: a whole 2x2x4 slice. The times are simulated.
32 devices in a mesh: user: 8 (over y, x, core), item: 4 (over z).
Axes of the slice: x: 2, y: 2, z: 4, core: 2. Of those that a mesh axis runs over, the one named last changes fastest.
Arguments:
- u_factors: float32 [65536, 256], P(('user', 'item')), may hold values from -1.5 to 1.5
- v_factors: float32 [16384, 256], P(('item', 'user')), may hold values from -1.5 to 1.5
- ratings: bfloat16 [8, 4, 2, 224, 128, 128], P('user', 'item'), may hold values from -6 to 6
- tile_rows: int32 [8, 4, 2, 224], P('user', 'item'), may hold values from 0 to 15, as said below
- tile_cols: int32 [8, 4, 2, 224], P('user', 'item'), may hold values from 0 to 31
- tile_counts: int32 [8, 4, 2], P('user', 'item'), may hold values from 28 to 224, as said below
- u_noise: bfloat16 [2, 65536, 256], P(None, ('user', 'item')), may hold values from -6 to 6
- v_noise: bfloat16 [2, 16384, 256], P(None, ('item', 'user')), may hold values from -6 to 6
Outputs:
- new_users: float32 [65536, 256], P(('user', 'item'))
- new_items: float32 [16384, 256], P(('item', 'user'))
Inputs may be any that keep to these rules, and one draw needn't show every extreme that they name: Within one list of a block and sub-epoch the (tile_rows, tile_cols) pairs are distinct over all 224 slots. `tile_counts`: some list in every draw is full and some has the smallest count.
All inputs are finite; a program needn't handle non-finite values.
Results may differ from a plain program's by a relative error of at most 0.00115.
Values may be sent and summed in bfloat16 or wider, within the bound.
No kernel may reach another device: no remote copies, remote signals or barrier semaphores. Data moves between devices by JAX's collectives and lax.ppermute only.
A program may use at most 128 MiB of HBM per device.

v0:
```python
import math

import jax
import jax.numpy as jnp
from jax import lax
from jax.sharding import PartitionSpec as P

HALF_STEP = 0.002
ROOT_STEP = math.sqrt(0.004)
PRIOR = 25.0


def shifted(x, axis, by):
    peers = lax.axis_size(axis)
    return lax.ppermute(x, axis, [(i, (i + by) % peers) for i in range(peers)])


def tile_grads(user_bf, group_bf, rating_list, row_list, col_list, live_count, tile_size):
    width = user_bf.shape[1]
    user_tiles = user_bf.reshape(-1, tile_size, width)
    item_tiles = group_bf.reshape(-1, tile_size, width)
    listed = rating_list.shape[0]
    step_len = math.gcd(listed, 16)

    def advance(position, carry):
        grad_user, grad_item = carry
        first = position * step_len
        ratings_now = lax.dynamic_slice_in_dim(rating_list, first, step_len, 0)
        rows_now = lax.dynamic_slice_in_dim(row_list, first, step_len, 0)
        cols_now = lax.dynamic_slice_in_dim(col_list, first, step_len, 0)
        live = first + jnp.arange(step_len) < live_count
        user_part = user_tiles[rows_now]
        item_part = item_tiles[cols_now]
        predicted = jnp.einsum(
            "tak,tbk->tab", user_part, item_part, preferred_element_type=jnp.float32
        )
        misfit = jnp.where(
            live[:, None, None], ratings_now.astype(jnp.float32) - predicted, 0.0
        ).astype(jnp.bfloat16)
        grad_user = grad_user.at[rows_now].add(
            jnp.einsum("tab,tbk->tak", misfit, item_part, preferred_element_type=jnp.float32)
        )
        grad_item = grad_item.at[cols_now].add(
            jnp.einsum("tab,tak->tbk", misfit, user_part, preferred_element_type=jnp.float32)
        )
        return (grad_user, grad_item)

    steps_needed = (live_count + step_len - 1) // step_len
    initial = (jnp.zeros(user_tiles.shape, jnp.float32), jnp.zeros(item_tiles.shape, jnp.float32))
    grad_user, grad_item = lax.fori_loop(0, steps_needed, advance, initial)
    return (grad_user.reshape(user_bf.shape), grad_item.reshape(group_bf.shape))


def body(u_factors, v_factors, ratings, tile_rows, tile_cols, tile_counts, u_noise, v_noise):
    tile_size = ratings.shape[-1]
    sections = ratings.shape[2]
    power = float(lax.axis_size("item"))
    user_master = u_factors
    item_master = v_factors
    for section in range(sections):
        group_bf = lax.all_gather(item_master.astype(jnp.bfloat16), "user", axis=0, tiled=True)
        grad_user, grad_item = tile_grads(
            user_master.astype(jnp.bfloat16),
            group_bf,
            ratings[0, 0, section],
            tile_rows[0, 0, section],
            tile_cols[0, 0, section],
            tile_counts[0, 0, section],
            tile_size,
        )
        user_master = (
            user_master
            + HALF_STEP * (power * grad_user - PRIOR * user_master)
            + ROOT_STEP * u_noise[section].astype(jnp.float32)
        )
        owned = lax.psum_scatter(grad_item, "user", scatter_dimension=0, tiled=True)
        item_master = (
            item_master
            + HALF_STEP * (power * owned - PRIOR * item_master)
            + ROOT_STEP * v_noise[section].astype(jnp.float32)
        )
        if section + 1 < sections:
            item_master = shifted(item_master, "item", 1)
    item_master = shifted(item_master, "item", 1 - sections)
    return (user_master, item_master)


def solution(mesh):
    placed = (
        P(("user", "item"), None),
        P(("item", "user"), None),
        P("user", "item", None, None, None, None),
        P("user", "item", None, None),
        P("user", "item", None, None),
        P("user", "item", None),
        P(None, ("user", "item"), None),
        P(None, ("item", "user"), None),
    )
    return jax.shard_map(
        body,
        mesh=mesh,
        in_specs=placed,
        out_specs=(P(("user", "item"), None), P(("item", "user"), None)),
        check_vma=False,
    )
```

profile of v0, /device:TPU:0, one launch (start us, length us, event | category | flops | bytes accessed | tf_op | source)
XLA Modules:
  0.0 708.9 jit_solution(4976227661782562749)
XLA Ops:
  12.8 10.8 %slice_bitcast_fusion.1 = (bf16[224,128,128]{2,1,0:T(8,128)(2,1)}, bf16[224,128,128]{2,1,0:T(8,128)(2,1)}) fusion(bf16[1,1,2,224,128,128]{5,4,3,2,1,0:T(8,128)(2,1)} %param.14), kind=kLoop, calls=%fused_computation.25 | loop fusion | bytes 29360128 | tf_op jit(solution)/shard_map/squeeze | solution.py:65
  23.6 17.5 %all-gather.3.cloned.1.call-done = bf16[4096,256]{1,0:T(8,128)(2,1)} async-done(((bf16[512,256]{1,0:T(8,128)(2,1)}), bf16[4096,256]{1,0:T(8,128)(2,1)}) %all-gather.3.cloned.1.call-update) | async-done | bytes 2097168 | tf_op jit(solution)/shard_map/all_gather | solution.py:61
  41.1 2.5 broadcast.76.clone
  45.1 36.5 %while.24 = (s32[]{:T(128)}, f32[16,128,256]{2,1,0:T(8,128)}, f32[32,128,256]{2,1,0:T(8,128)}, s32[]{:T(128)}, s32[224]{0:T(256)S(1)}, /*index=5*/s32[]{:T(128)}...) while((s32[]{:T(128)}, f32[16,128,256]{2,1,0:T(8,128)}, ...), condition=%wide.region_3.4_spmd, body=%wide.region_0.3_spmd.sunk | while | flops 404752512 | bytes 37757876 | solution.py:50
  46.1 2.2 gather_fusion.1
  52.3 5.3 scatter_fusion.1
  59.0 4.3 scatter_fusion
  64.4 2.2 gather_fusion.1
  70.5 5.2 scatter_fusion.1
  77.2 4.4 scatter_fusion
  81.7 251.8 %reduce-scatter.3.cloned.1.call-done = f32[512,256]{1,0:T(8,128)} async-done(((f32[4096,256]{1,0:T(8,128)}), f32[512,256]{1,0:T(8,128)}) %reduce-scatter.3.cloned.1.call-update) | async-done | bytes 524304 | tf_op jit(solution)/shard_map/reduce_scatter | solution.py:76
  336.2 14.0 %collective-permute-done = f32[512,256]{1,0:T(8,128)S(1)} collective-permute-done((f32[512,256]{1,0:T(8,128)S(1)}, f32[512,256]{1,0:T(8,128)S(1)}, u32[]{:S(2)}, u32[]{:S(2)}) %collective-permute-start) | collective-permute-done | bytes 524320 | tf_op jit(solution)/shard_map/ppermute | solution.py:15
  355.9 22.1 %all-gather.5.cloned.1.call-done = bf16[4096,256]{1,0:T(8,128)(2,1)} async-done(((bf16[512,256]{1,0:T(8,128)(2,1)}), bf16[4096,256]{1,0:T(8,128)(2,1)}) %all-gather.5.cloned.1.call-update) | async-done | bytes 2097168 | tf_op jit(solution)/shard_map/all_gather | solution.py:61
  378.0 2.5 broadcast.76
  382.1 109.1 %while.25 = (s32[]{:T(128)}, f32[16,128,256]{2,1,0:T(8,128)}, f32[32,128,256]{2,1,0:T(8,128)}, s32[]{:T(128)}, s32[224]{0:T(256)S(1)}, /*index=5*/s32[]{:T(128)}...) while((s32[]{:T(128)}, f32[16,128,256]{2,1,0:T(8,128)}, ...), condition=%wide.region_8.9_spmd, body=%wide.region_5.8_spmd.sunk | while | flops 404752512 | bytes 37757876 | solution.py:50
  383.0 2.2 gather_fusion.3
  389.1 5.3 scatter_fusion.3
  395.9 4.6 scatter_fusion.2
  407.5 5.2 scatter_fusion.3
  414.2 4.5 scatter_fusion.2
  425.7 5.3 scatter_fusion.3
  432.5 4.3 scatter_fusion.2
  443.9 5.2 scatter_fusion.3
  450.5 4.3 scatter_fusion.2
  461.9 5.3 scatter_fusion.3
  468.6 4.3 scatter_fusion.2
  480.0 5.2 scatter_fusion.3
  486.7 4.4 scatter_fusion.2
  494.3 191.5 %reduce-scatter.5.cloned.1.call-done = f32[512,256]{1,0:T(8,128)} async-done(((f32[4096,256]{1,0:T(8,128)}), f32[512,256]{1,0:T(8,128)}) %reduce-scatter.5.cloned.1.call-update) | async-done | bytes 524304 | tf_op jit(solution)/shard_map/reduce_scatter | solution.py:76
  687.0 3.4 collective-permute-start.1
  690.4 5.8 bitcast_add_fusion
  696.1 5.4 collective-permute-done.1
  (164 shorter events, 82.4 us)
Async XLA Ops:
  7.2 5.6 copy-start.16
  7.2 5.6 copy-start.17
  7.2 33.9 %all-gather.3.cloned.1.call-start = ((), (), s32[]{:S(2)}) async-start(), calls=%async_computation.2 | async-start | bytes 2359296 | tf_op jit(solution)/shard_map/all_gather | solution.py:61
  9.0 324.5 %reduce-scatter.3.cloned.1.call-start = ((), (), s32[]{:S(2)}) async-start(), calls=%async_computation.3 | async-start | bytes 4718592 | tf_op jit(solution)/shard_map/reduce_scatter | solution.py:76
  50.4 1.9 copy-start
  59.0 4.4 copy-start.5
  68.7 1.9 copy-start
  77.2 4.4 copy-start.5
  81.6 251.9 %copy-start.11 = (f32[512,256]{1,0:T(8,128)S(1)}, f32[512,256]{1,0:T(8,128)}, u32[]{:S(2)}) copy-start(f32[512,256]{1,0:T(8,128)} %param.13) | copy-start | bytes 1572868
  81.6 251.9 %copy-start.14 = (bf16[2,512,256]{2,1,0:T(8,128)(2,1)S(1)}, bf16[2,512,256]{2,1,0:T(8,128)(2,1)}, u32[]{:S(2)}) copy-start(bf16[2,512,256]{2,1,0:T(8,128)(2,1)} %param.19) | copy-start | bytes 1572868
  81.6 270.8 %copy-start.3 = (f32[16,128,256]{2,1,0:T(8,128)S(1)}, f32[16,128,256]{2,1,0:T(8,128)}, u32[]{:S(2)}) copy-start(f32[16,128,256]{2,1,0:T(8,128)} %get-tuple-element.110) | copy-start | bytes 6291460
  81.6 296.4 %all-gather.5.cloned.1.call-start = ((), (), s32[]{:S(2)}) async-start(), calls=%async_computation.4 | async-start | bytes 2359296 | tf_op jit(solution)/shard_map/all_gather | solution.py:61
  334.7 15.5 %collective-permute-start = (f32[512,256]{1,0:T(8,128)S(1)}, f32[512,256]{1,0:T(8,128)S(1)}, u32[]{:S(2)}, u32[]{:S(2)}) collective-permute-start(f32[512,256]{1,0:T(8,128)S(1)} %bitcast_add_fusion.3), channel_id=1, source_target_pairs={{0,1},{1,2},{2,3},{3,0},{4,5},{5,6},{6,7},{7,4},{8,9},{9,10},{10,1... | collective-permute-start | bytes 1572872 | tf_op jit(solution)/shard_map/ppermute | solution.py:15
  351.7 334.0 %reduce-scatter.5.cloned.1.call-start = ((), (), s32[]{:S(2)}) async-start(), calls=%async_computation.5 | async-start | bytes 4718592 | tf_op jit(solution)/shard_map/reduce_scatter | solution.py:76
  352.4 2.4 copy-start.8
  352.4 3.0 copy-start.10
  387.3 1.8 copy-start.1
  395.9 4.6 copy-start.7
  405.7 1.8 copy-start.1
  414.2 4.5 copy-start.7
  423.9 1.8 copy-start.1
  432.5 4.3 copy-start.7
  442.0 1.8 copy-start.1
  450.5 4.3 copy-start.7
  460.0 1.8 copy-start.1
  468.6 4.3 copy-start.7
  478.2 1.8 copy-start.1
  486.7 4.5 copy-start.7
  491.2 1.6 copy-start.2
  492.8 193.0 %copy-start.13 = (f32[512,256]{1,0:T(8,128)S(1)}, f32[512,256]{1,0:T(8,128)}, u32[]{:S(2)}) copy-start(f32[512,256]{1,0:T(8,128)} %copy-done.12) | copy-start | bytes 1572868
  492.8 193.0 %copy-start.15 = (bf16[2,512,256]{2,1,0:T(8,128)(2,1)S(1)}, bf16[2,512,256]{2,1,0:T(8,128)(2,1)}, u32[]{:S(2)}) copy-start(bf16[2,512,256]{2,1,0:T(8,128)(2,1)} %param.19) | copy-start | bytes 1572868
  687.0 14.6 %collective-permute-start.1 = (f32[512,256]{1,0:T(8,128)S(1)}, f32[512,256]{1,0:T(8,128)S(1)}, u32[]{:S(2)}, u32[]{:S(2)}) collective-permute-start(f32[512,256]{1,0:T(8,128)S(1)} %bitcast_add_fusion.2), channel_id=1, source_target_pairs={{0,3},{1,0},{2,1},{3,2},{4,7},{5,4},{6,5},{7,6},{8,11},{9,8},{10,9... | collective-permute-start | bytes 1572872 | tf_op jit(solution)/shard_map/ppermute | solution.py:15
  (10 other events, 9.9 us)
Sparse Core Ops, SparseCore 0:
  10.5 30.5 all-gather.2
  81.7 251.7 reduce-scatter.2
  351.9 26.0 all-gather.4
  491.3 194.4 reduce-scatter.4
where the time goes:
time: 712 us; the launch traced here: 709 us
  waiting for transfers between devices  502 us (71%)
  other arithmetic  97 us (14%)
  local copies, waits for them, and re-layouts  50.7 us (7%)
  matrix products  38.1 us (5%)
  between operations  15.1 us (2%)
    reduce_scatter x2, waiting for transfers between devices, body(): owned = lax.psum_scatter(grad_item, 'user', scatter_dimension=0, tiled=True)  443 us
    scatter-add x8, other arithmetic, advance(): grad_item.at[cols_now]  42 us
    all_gather x2, waiting for transfers between devices, body(): lax.all_gather(item_master.astype(jnp.bfloat16), 'user', axis=0, tiled=True)  39.5 us
    scatter-add x8, other arithmetic, advance(): grad_user.at[rows_now]  35.1 us
    ppermute x2, waiting for transfers between devices, shifted(): return lax.ppermute(x, axis, [(i, (i + by) % peers) for i in range(peers)])  19.4 us
    gather x8, local copies, waits for them, and re-layouts, advance(): item_part = item_tiles[cols_now]  17.6 us
    dot_general x8, matrix products, advance(): jnp.einsum('tab,tak->tbk', misfit, user_part, preferred_element_type=jnp....  14.6 us
  transfers between devices with their start and end apart: 6, of which 6 were waited for; matrix products, arithmetic and copies ran while one was open for 3% of the time, Pallas kernels for 0%

commit v1 on v0

v1 whole, which is shorter than its diff:
```python
import functools
import math

import jax
import jax.numpy as jnp
from jax import lax
from jax.experimental import pallas as pl
from jax.experimental.pallas import tpu as pltpu
from jax.sharding import PartitionSpec as P

HALF_STEP = 0.002
ROOT_STEP = math.sqrt(0.004)
PRIOR = 25.0
GROUP = 4
DEPTH = 16
SCALE_ROWS = 16
VMEM_LIMIT = 40 * 2**20

ANY = pl.BlockSpec(memory_space=pl.ANY)
IN_VMEM = pl.BlockSpec(memory_space=pltpu.VMEM)
IN_SMEM = pl.BlockSpec(memory_space=pltpu.SMEM)


def shifted(x, axis, by):
    peers = lax.axis_size(axis)
    return lax.ppermute(x, axis, [(i, (i + by) % peers) for i in range(peers)])


def swapped(x, axis, mask):
    peers = lax.axis_size(axis)
    return lax.ppermute(x, axis, [(i, i ^ mask) for i in range(peers)])


def widths(slots, user_tiles, item_tiles):
    bits = tuple(max(1, (n - 1).bit_length()) for n in (slots, user_tiles, item_tiles))
    assert 2 * bits[0] + 2 * bits[1] + bits[2] + 2 <= 31
    return bits


def pair_plan(rows, cols, count, me, user_tiles, item_tiles, per, span):
    slots = rows.shape[0]
    slot_bits, row_bits, col_bits = widths(slots, user_tiles, item_tiles)
    place = ((cols // per) ^ me) * per + cols % per
    n = jnp.arange(slots, dtype=jnp.int32)
    live = n < count
    same = (place[:, None] == place[None, :]) & live[None, :]
    rank = jnp.sum(same & (rows[None, :] < rows[:, None]), axis=1, dtype=jnp.int32)
    opens = live & (rank % 2 == 0)
    run = place // span
    runs = item_tiles // span
    run_ids = jnp.arange(runs, dtype=jnp.int32)
    ahead = (place[None, :] < place[:, None]) & (run[None, :] == run[:, None]) & opens[None, :]
    within = jnp.sum(ahead, axis=1, dtype=jnp.int32)
    size = jnp.sum((run[None, :] == run_ids[:, None]) & opens[None, :], axis=1, dtype=jnp.int32)
    size = (size + GROUP - 1) // GROUP * GROUP
    edges = jnp.arange(runs + 1, dtype=jnp.int32)
    starts = jnp.sum(jnp.where(run_ids[None, :] < edges[:, None], size[None, :], 0), axis=1, dtype=jnp.int32)
    base = jnp.sum(jnp.where(run_ids[None, :] < run[:, None], size[None, :], 0), axis=1, dtype=jnp.int32)
    where = base + within + rank // 2
    col_at = 2 * slot_bits + 2 * row_bits
    one = 1 << (col_at + col_bits)
    first = n | (rows << (2 * slot_bits)) | (place << col_at)
    second = (n << slot_bits) | (rows << (2 * slot_bits + row_bits))
    word = jnp.where(live, jnp.where(rank % 2 == 0, first, second) + one, 0)
    words = jnp.arange((slots + item_tiles) // 2 + runs * GROUP, dtype=jnp.int32)[:, None]
    pairs = jnp.sum(jnp.where(where[None, :] == words, word[None, :], 0), axis=1, dtype=jnp.int32)
    unused = jnp.sum(words >= starts[None, 1:], axis=1, dtype=jnp.int32) * span
    unused = jnp.minimum(unused, item_tiles - 1) << col_at
    return jnp.where(pairs == 0, unused, pairs), starts


def grads_kernel(section, first_run, last_run, span, bits, pieces, pairs, starts, ratings, users, *refs):
    piece_in = refs[:pieces]
    grad_user_out = refs[pieces]
    grad_item_out = refs[pieces + 1 : 2 * pieces + 1]
    items, rated, misfits, grad_user, grad_item, rated_sem, piece_sem, out_sem = refs[2 * pieces + 1 :]
    slot_bits, row_bits, col_bits = bits
    per = items.shape[0] // pieces
    tile = users.shape[1]
    low, high = starts[first_run], starts[last_run]
    steps = lax.div(high - low, GROUP)

    def decode(p):
        word = pairs[p]
        fields = []
        for width in (slot_bits, slot_bits, row_bits, row_bits, col_bits):
            fields.append(word & ((1 << width) - 1))
            word = word >> width
        fields[4] -= first_run * span
        return (*fields, word)

    def loads(p):
        slot = lax.rem(p - low, DEPTH)
        return [
            pltpu.make_async_copy(
                ratings.at[section, n], rated.at[slot, pl.ds(half * tile, tile)], rated_sem.at[slot, half]
            )
            for half, n in enumerate(decode(p)[:2])
        ]

    def issue(p):
        for load in loads(p):
            load.start()

    def predict(p):
        _, _, row_a, row_b, col, live = decode(p)
        both = jnp.concatenate([users[row_a], users[row_b]], axis=0)
        predicted = lax.dot_general(both, items[col], (((1,), (1,)), ((), ())), preferred_element_type=jnp.float32)
        misfit = rated[lax.rem(p - low, DEPTH)].astype(jnp.float32) - predicted
        rows = lax.broadcasted_iota(jnp.int32, (2 * tile, 1), 0)
        return jnp.where(rows < tile * live, misfit, 0.0).astype(jnp.bfloat16)

    def add_grads(p, misfit):
        _, _, row_a, row_b, col, _ = decode(p)
        to_user = jnp.dot(misfit, items[col], preferred_element_type=jnp.float32)
        both = jnp.concatenate([users[row_a], users[row_b]], axis=0)
        grad_item[col] += lax.dot_general(misfit, both, (((0,), (0,)), ((), ())), preferred_element_type=jnp.float32)
        grad_user[row_a] += to_user[:tile]
        grad_user[row_b] += to_user[tile:]

    def await_group(p):
        for j in range(GROUP):
            for load in loads(p + j):
                load.wait()

    def issue_group(step):
        @pl.when(step < steps)
        def _():
            for j in range(GROUP):
                issue(low + step * GROUP + j)

    piece_loads = [
        pltpu.make_async_copy(piece_in[i], items.at[pl.ds(i * per, per)], piece_sem.at[i]) for i in range(pieces)
    ]
    for load in piece_loads:
        load.start()
    for step in range(DEPTH // GROUP):
        issue_group(step)
    grad_user[...] = jnp.zeros_like(grad_user)
    grad_item[...] = jnp.zeros_like(grad_item)
    for load in piece_loads:
        load.wait()

    @pl.when(steps > 0)
    def _():
        await_group(low)
        for j in range(GROUP):
            misfits[j] = predict(low + j)
        issue_group(DEPTH // GROUP)

        def advance(step, carry):
            p = low + step * GROUP
            held = [misfits[j] for j in range(GROUP)]
            await_group(p + GROUP)
            following = [predict(p + GROUP + j) for j in range(GROUP)]
            for j in range(GROUP):
                add_grads(p + j, held[j])
            for j in range(GROUP):
                misfits[j] = following[j]
            issue_group(step + 1 + DEPTH // GROUP)
            return carry

        lax.fori_loop(0, steps - 1, advance, 0)
        for j in range(GROUP):
            add_grads(high - GROUP + j, misfits[j])

    stores = [pltpu.make_async_copy(grad_user, grad_user_out, out_sem.at[pieces])]
    for i in range(pieces):
        stores.append(
            pltpu.make_async_copy(grad_item.at[pl.ds(i * per, per)], grad_item_out[i], out_sem.at[i])
        )
    for store in stores:
        store.start()
    for store in stores:
        store.wait()


def tile_grads(section, first_run, last_run, span, plan, ratings, users, pieces):
    pairs, starts = plan
    count = len(pieces)
    per, tile, width = pieces[0].shape
    user_tiles = users.shape[0]
    bits = widths(ratings.shape[1], user_tiles, span * (starts.shape[0] - 1))
    busy = ratings.shape[1] * 3 // 4
    f32 = jnp.float32
    return pl.pallas_call(
        functools.partial(grads_kernel, section, first_run, last_run, span, bits, count),
        out_shape=[jax.ShapeDtypeStruct((user_tiles, tile, width), f32)]
        + [jax.ShapeDtypeStruct((per, tile, width), f32)] * count,
        in_specs=[IN_SMEM, IN_SMEM, ANY, IN_VMEM] + [ANY] * count,
        out_specs=[ANY] * (1 + count),
        scratch_shapes=[
            pltpu.VMEM((count * per, tile, width), jnp.bfloat16),
            pltpu.VMEM((DEPTH, 2 * tile, tile), jnp.bfloat16),
            pltpu.VMEM((GROUP, 2 * tile, tile), jnp.bfloat16),
            pltpu.VMEM((user_tiles, tile, width), f32),
            pltpu.VMEM((count * per, tile, width), f32),
            pltpu.SemaphoreType.DMA((DEPTH, 2)),
            pltpu.SemaphoreType.DMA((count,)),
            pltpu.SemaphoreType.DMA((count + 1,)),
        ],
        compiler_params=pltpu.CompilerParams(vmem_limit_bytes=VMEM_LIMIT),
        cost_estimate=pl.CostEstimate(
            flops=busy * 6 * tile * tile * width,
            bytes_accessed=busy * tile * tile * 2 + user_tiles * tile * width * 8,
            transcendentals=0,
        ),
    )(pairs, starts, ratings, users, *pieces)


def coded_shape(per, tile, width):
    return jax.ShapeDtypeStruct((per * tile + SCALE_ROWS, width), jnp.int16)


def encode(blocks, out):
    per = len(blocks)
    tile, width = blocks[0].shape
    row = lax.broadcasted_iota(jnp.int32, (SCALE_ROWS, width), 0)
    powers = jnp.zeros((SCALE_ROWS, width), jnp.int32)
    for t, block in enumerate(blocks):
        largest = jnp.max(jnp.abs(block), axis=0, keepdims=True)
        power = jnp.ceil(jnp.log2(jnp.maximum(largest, 1e-20)))
        scaled = jnp.round(block * jnp.exp2(15.0 - power))
        out[pl.ds(t * tile, tile)] = jnp.clip(scaled, -32767.0, 32767.0).astype(jnp.int32).astype(jnp.int16)
        powers = jnp.where(row == t, power.astype(jnp.int32), powers)
    out[pl.ds(per * tile, SCALE_ROWS)] = powers.astype(jnp.int16)


def decoded(ref, t, tile, per):
    powers = ref[pl.ds(per * tile, SCALE_ROWS)].astype(jnp.int32).astype(jnp.float32)
    unit = jnp.exp2(powers[t : t + 1] - 15.0)
    return ref[pl.ds(t * tile, tile)].astype(jnp.int32).astype(jnp.float32) * unit


def join_kernel(mine, other, out):
    encode([mine[t] + other[t] for t in range(mine.shape[0])], out)


def join(mine, other):
    return pl.pallas_call(
        join_kernel,
        out_shape=coded_shape(*mine.shape),
        in_specs=[IN_VMEM] * 2,
        out_specs=IN_VMEM,
        compiler_params=pltpu.CompilerParams(vmem_limit_bytes=VMEM_LIMIT),
    )(mine, other)


def owner_sum(mine, other, coded, t):
    per, tile, _ = mine.shape
    total = mine[t] + other[t]
    for ref in coded:
        total = total + decoded(ref, t, tile, per)
    return total


def update_kernel(power, mine, other, *refs):
    *coded, factors, noise, new, new_bf = refs
    for t in range(mine.shape[0]):
        step = HALF_STEP * power * owner_sum(mine, other, coded, t) + ROOT_STEP * noise[t].astype(jnp.float32)
        after = factors[t] - HALF_STEP * PRIOR * factors[t] + step
        new[t] = after
        new_bf[t] = after.astype(jnp.bfloat16)


def delta_kernel(power, mine, other, *refs):
    *coded, noise, out = refs
    steps = []
    for t in range(mine.shape[0]):
        steps.append(HALF_STEP * power * owner_sum(mine, other, coded, t) + ROOT_STEP * noise[t].astype(jnp.float32))
    encode(steps, out)


def arrive_kernel(coded, factors, new, new_bf):
    per, tile, _ = factors.shape
    for t in range(per):
        after = factors[t] - HALF_STEP * PRIOR * factors[t] + decoded(coded, t, tile, per)
        new[t] = after
        new_bf[t] = after.astype(jnp.bfloat16)


def in_vmem(kernel, out_shape, *operands):
    return pl.pallas_call(
        kernel,
        out_shape=out_shape,
        in_specs=[IN_VMEM] * len(operands),
        out_specs=jax.tree.map(lambda _: IN_VMEM, out_shape),
        compiler_params=pltpu.CompilerParams(vmem_limit_bytes=VMEM_LIMIT),
    )(*operands)


def body(u_factors, v_factors, ratings, tile_rows, tile_cols, tile_counts, u_noise, v_noise):
    tile = ratings.shape[-1]
    sections = ratings.shape[2]
    width = u_factors.shape[1]
    peers = lax.axis_size("user")
    power = float(lax.axis_size("item"))
    me = lax.axis_index("user")
    users = u_factors.reshape(-1, tile, width)
    items = v_factors.reshape(-1, tile, width)
    per = items.shape[0]
    item_tiles = peers * per
    span = item_tiles
    ratings = ratings.reshape(ratings.shape[2:])
    u_noise = u_noise.reshape(sections, *users.shape)
    v_noise = v_noise.reshape(sections, *items.shape)
    pair = (
        jax.ShapeDtypeStruct(items.shape, jnp.float32),
        jax.ShapeDtypeStruct(items.shape, jnp.bfloat16),
    )
    plans = [
        pair_plan(
            tile_rows[0, 0, s], tile_cols[0, 0, s], tile_counts[0, 0, s], me, users.shape[0], item_tiles, per, span
        )
        for s in range(sections)
    ]
    items_bf = items.astype(jnp.bfloat16)
    for section in range(sections):
        sent = shifted(items_bf, "item", section) if section else items_bf
        pieces = [sent] + [swapped(sent, "user", d) for d in range(2, peers, 2)]
        pieces = [p for even in pieces for p in (even, swapped(even, "user", 1))]
        grad_user, *grads = tile_grads(
            section, 0, 1, span, plans[section], ratings, users.astype(jnp.bfloat16), pieces
        )
        mine = grads[0::2]
        other = [swapped(g, "user", 1) for g in grads[1::2]]
        coded = [swapped(join(mine[d], other[d]), "user", 2 * d) for d in range(1, peers // 2)]
        if section == 0:
            items, items_bf = in_vmem(
                functools.partial(update_kernel, power), pair, mine[0], other[0], *coded, items, v_noise[section]
            )
        else:
            delta = in_vmem(
                functools.partial(delta_kernel, power),
                coded_shape(*items.shape),
                mine[0],
                other[0],
                *coded,
                v_noise[section],
            )
            items, items_bf = in_vmem(arrive_kernel, pair, shifted(delta, "item", -section), items)
        users = (
            users
            + HALF_STEP * (power * grad_user - PRIOR * users)
            + ROOT_STEP * u_noise[section].astype(jnp.float32)
        )
    return (users.reshape(u_factors.shape), items.reshape(v_factors.shape))


def solution(mesh):
    placed = (
        P(("user", "item"), None),
        P(("item", "user"), None),
        P("user", "item", None, None, None, None),
        P("user", "item", None, None),
        P("user", "item", None, None),
        P("user", "item", None),
        P(None, ("user", "item"), None),
        P(None, ("item", "user"), None),
    )
    return jax.shard_map(
        body,
        mesh=mesh,
        in_specs=placed,
        out_specs=(P(("user", "item"), None), P(("item", "user"), None)),
        check_vma=False,
    )
```

time: 712 us -> 135 us (0.19)
  waiting for transfers between devices: 502 us -> 43.4 us
  other arithmetic: 97 us -> 17.5 us
  local copies, waits for them, and re-layouts: 50.7 us -> 8.74 us
  matrix products: 38.1 us -> 0 us
  Pallas kernels: 0 us -> 30.4 us
  starting transfers between devices: 5.07 us -> 32.1 us
  between operations: 15.1 us -> 2.4 us
    reduce_scatter x2 -> x0, waiting for transfers between devices: 443 us -> none  [body(): owned = lax.psum_scatter(grad_item, 'user', scatter_dimension=0, tiled=True)]
    scatter-add x16 -> x0, other arithmetic: 77.1 us -> none  [the longest x8 42 us: advance(): grad_item.at[cols_now]]
    all_gather x2 -> x0, waiting for transfers between devices: 39.5 us -> none  [body(): lax.all_gather(item_master.astype(jnp.bfloat16), 'user', axis=0, tiled=True)]
    dot_general x24 -> x0, matrix products: 38.1 us -> none  [the longest x8 14.6 us: advance(): jnp.einsum('tab,tak->tbk', misfit, user_part, preferred_element_type=jnp....]
    ppermute x0 -> x28, waiting for transfers between devices: none -> 34.1 us  [swapped(): return lax.ppermute(x, axis, [(i, i ^ mask) for i in range(peers)])]
    pallas_call x0 -> x11, Pallas kernels: none -> 30.4 us  [the longest x2 24.4 us: tile_grads(): pl.pallas_call(functools.partial(grads_kernel, section, first_run, last_r...]
    ppermute x0 -> x28, starting transfers between devices: none -> 27.5 us  [swapped(): return lax.ppermute(x, axis, [(i, i ^ mask) for i in range(peers)])]
    gather x16 -> x0, local copies, waits for them, and re-layouts: 22.5 us -> none  [the longest x8 17.6 us: advance(): item_part = item_tiles[cols_now]]
  transfers between devices with their start and end apart: 6 -> 30, of which waited for: 6 -> 14; matrix products, arithmetic and copies ran while one was open for 3% -> 15% of each run, Pallas kernels for 0% -> 3%
where the time goes in v1:
time: 135 us; the launch traced here: 134 us
  waiting for transfers between devices  43.4 us (32%)
  starting transfers between devices  32.1 us (24%)
  Pallas kernels  30.4 us (23%)
  other arithmetic  17.5 us (13%)
  local copies, waits for them, and re-layouts  8.74 us (6%)
  between operations  2.4 us (2%)
    ppermute x28, waiting for transfers between devices, swapped(): return lax.ppermute(x, axis, [(i, i ^ mask) for i in range(peers)])  34.1 us
    ppermute x28, starting transfers between devices, swapped(): return lax.ppermute(x, axis, [(i, i ^ mask) for i in range(peers)])  27.5 us
    pallas_call x2, Pallas kernels, tile_grads(): pl.pallas_call(functools.partial(grads_kernel, section, first_run, last_r...  24.4 us
    ppermute x2, waiting for transfers between devices, shifted(): return lax.ppermute(x, axis, [(i, (i + by) % peers) for i in range(peers)])  9.28 us
    unnamed x32, local copies, waits for them, and re-layouts  4.77 us
    ppermute x2, starting transfers between devices, shifted(): return lax.ppermute(x, axis, [(i, (i + by) % peers) for i in range(peers)])  4.6 us
    pallas_call x6, Pallas kernels, join(): pl.pallas_call(join_kernel, out_shape=coded_shape(*mine.shape), in_specs=...  4.16 us
    reduce_sum x1, other arithmetic, pair_plan(): jnp.sum((run[None, :] == run_ids[:, None]) & opens[None, :], axis=1, dtyp...  2.74 us
  transfers between devices with their start and end apart: 30, of which 14 were waited for; matrix products, arithmetic and copies ran while one was open for 15% of the time, Pallas kernels for 3%

profile of v1, /device:TPU:0, one launch (start us, length us, event | category | flops | bytes accessed | tf_op | source)
XLA Modules:
  0.0 134.5 jit_solution(3516111859764216103)
XLA Ops:
  0.6 1.1 convert_element_type.63.refs_0_
  1.7 4.0 %collective-permute-start.5 = (bf16[4,128,256]{2,1,0:T(8,128)(2,1)S(1)}, bf16[4,128,256]{2,1,0:T(8,128)(2,1)S(1)}, u32[]{:S(2)}, u32[]{:S(2)}) collective-permute-start(bf16[4,128,256]{2,1,0:T(8,128)(2,1)S(1)} %convert_element_type.63.refs_0_), channel_id=1, source_target_pairs={{0,24},{4,28},{8,16},{12,20},{16,8},{20,12},{24,0},{28,4},{1,25},{... | collective-permute-start | bytes 786440 | tf_op jit(solution)/shard_map/ppermute | solution.py:31
  6.3 1.4 %fusion.30 = (s32[1,1,1]{2,1,0:T(1,128)}, s32[1,1,1]{2,1,0:T(1,128)}) fusion(s32[1,1,2]{2,1,0:T(1,128)} %param.13), kind=kLoop, calls=%fused_computation.112 | loop fusion | bytes 16 | tf_op jit(solution)/shard_map/slice | solution.py:313
  11.0 2.7 %fusion.18 = (s32[]{:T(128)}, s32[]{:T(128)}) fusion(s32[1,224]{1,0:T(1,128)S(1)} %bitcast.67, s32[]{:T(128)} %bitcast.3, s32[]{:T(128)S(6)} %axis_index.15, s32[1,1,2,224]{3,2,1,0:T(2,128)} %param.12, s32[1,224]{1,0:T(1,128)S(1)} %bitcast.66, s32[]{:T(128)} %bitcast.14), kind=kLoop, calls=%fused_computation.100 | loop fusion | flops 24638 | bytes 3604 | tf_op jit(solution)/shard_map/reduce_sum | solution.py:54
  18.6 1.7 %convert_element_type.62.users = bf16[16,128,256]{2,1,0:T(8,128)(2,1)S(1)} convert(f32[16,128,256]{2,1,0:T(8,128)} %bitcast.61) | non-fusion elementwise | flops 524288 | bytes 3145728 | tf_op jit(solution)/shard_map/convert_element_type | solution.py:323
  22.7 0.9 copy-done.10
  23.6 9.5 %shard_map.95 = (f32[16,128,256]{2,1,0:T(8,128)S(1)}, f32[4,128,256]{2,1,0:T(8,128)S(1)}, f32[4,128,256]{2,1,0:T(8,128)}, f32[4,128,256]{2,1,0:T(8,128)S(1)}, f3...) custom-call(s32[132]{0:T(256)S(1)} %compare_select_fusion.5.pairs, ...), custom_call_target="tpu_custom_call" | custom-call | flops 4227858432 | bytes 9699328 | tf_op jit(solution)/shard_map/pallas_call | solution.py:186
  33.2 2.1 %collective-permute-start.8 = (f32[4,128,256]{2,1,0:T(8,128)}, f32[4,128,256]{2,1,0:T(8,128)}, u32[]{:S(2)}, u32[]{:S(2)}) collective-permute-start(f32[4,128,256]{2,1,0:T(8,128)} %get-tuple-element.27), channel_id=1, source_target_pairs={{0,4},{4,0},{8,12},{12,8},{16,20},{20,16},{24,28},{28,24},{1,5},{5... | collective-permute-start | bytes 1572872 | tf_op jit(solution)/shard_map/ppermute | solution.py:31
  35.8 2.4 %convert_multiply_fusion.1 = (f32[1,2048,256]{2,1,0:T(8,128)}, f32[1,2048,256]{2,1,0:T(8,128)}) fusion(bf16[2,2048,256]{2,1,0:T(8,128)(2,1)S(1)} %copy-done.14), kind=kLoop, calls=%fused_computation.2 | loop fusion | flops 2097152 | bytes 6291456 | tf_op jit(solution)/shard_map/mul | solution.py:345
  39.3 1.1 copy-done.6
  40.4 1.2 shard_map.96
  41.6 4.5 %collective-permute-start.9 = (s16[528,256]{1,0:T(8,128)(2,1)S(1)}, s16[528,256]{1,0:T(8,128)(2,1)S(1)}, u32[]{:S(2)}, u32[]{:S(2)}) collective-permute-start(s16[528,256]{1,0:T(8,128)(2,1)S(1)} %shard_map.96), channel_id=1, source_target_pairs={{0,8},{4,12},{8,0},{12,4},{16,24},{20,28},{24,16},{28,20},{1,9},{5... | collective-permute-start | bytes 811016 | tf_op jit(solution)/shard_map/ppermute | solution.py:31
  46.1 1.0 copy-done.4
  47.2 1.2 shard_map.97
  48.5 1.3 shard_map.98
  49.8 1.6 %collective-permute-start.13 = (s16[528,256]{1,0:T(8,128)(2,1)S(1)}, s16[528,256]{1,0:T(8,128)(2,1)S(1)}, u32[]{:S(2)}, u32[]{:S(2)}) collective-permute-start(s16[528,256]{1,0:T(8,128)(2,1)S(1)} %shard_map.98), channel_id=1, source_target_pairs={{0,24},{4,28},{8,16},{12,20},{16,8},{20,12},{24,0},{28,4},{1,25},{... | collective-permute-start | bytes 811016 | tf_op jit(solution)/shard_map/ppermute | solution.py:31
  51.5 1.7 %collective-permute-done.9.refs_0_ = s16[528,256]{1,0:T(8,128)(2,1)S(1)} collective-permute-done((s16[528,256]{1,0:T(8,128)(2,1)S(1)}, s16[528,256]{1,0:T(8,128)(2,1)S(1)}, u32[]{:S(2)}, u32[]{:S(2)}) %collective-permute-start.9) | collective-permute-done | bytes 270368 | tf_op jit(solution)/shard_map/ppermute | solution.py:31
  53.2 9.6 %collective-permute-done.11.refs_1_ = s16[528,256]{1,0:T(8,128)(2,1)S(1)} collective-permute-done((s16[528,256]{1,0:T(8,128)(2,1)S(1)}, s16[528,256]{1,0:T(8,128)(2,1)S(1)}, u32[]{:S(2)}, u32[]{:S(2)}) %collective-permute-start.11) | collective-permute-done | bytes 270368 | tf_op jit(solution)/shard_map/ppermute | solution.py:31
  63.2 4.5 %collective-permute-start.14 = (bf16[4,128,256]{2,1,0:T(8,128)(2,1)S(1)}, bf16[4,128,256]{2,1,0:T(8,128)(2,1)S(1)}, u32[]{:S(2)}, u32[]{:S(2)}) collective-permute-start(bf16[4,128,256]{2,1,0:T(8,128)(2,1)S(1)} %get-tuple-element.32), channel_id=1, source_target_pairs={{0,1},{1,2},{2,3},{3,0},{4,5},{5,6},{6,7},{7,4},{8,9},{9,10},{10,1... | collective-permute-start | bytes 786440 | tf_op jit(solution)/shard_map/ppermute | solution.py:26
  68.5 4.1 %collective-permute-done.14.refs_0_ = bf16[4,128,256]{2,1,0:T(8,128)(2,1)S(1)} collective-permute-done((bf16[4,128,256]{2,1,0:T(8,128)(2,1)S(1)}, bf16[4,128,256]{2,1,0:T(8,128)(2,1)S(1)}, u32[]{:S(2)}, u32[]{:S(2)}) %collective-permute-start.14) | collective-permute-done | bytes 262176 | tf_op jit(solution)/shard_map/ppermute | solution.py:26
  73.1 1.6 %collective-permute-start.18 = (bf16[4,128,256]{2,1,0:T(8,128)(2,1)S(1)}, bf16[4,128,256]{2,1,0:T(8,128)(2,1)S(1)}, u32[]{:S(2)}, u32[]{:S(2)}) collective-permute-start(bf16[4,128,256]{2,1,0:T(8,128)(2,1)S(1)} %collective-permute-done.14.refs_0_), channel_id=1, source_target_pairs={{0,16},{4,20},{8,24},{12,28},{16,0},{20,4},{24,8},{28,12},{1,17},{... | collective-permute-start | bytes 786440 | tf_op jit(solution)/shard_map/ppermute | solution.py:31
  74.7 1.4 %collective-permute-start.16 = (bf16[4,128,256]{2,1,0:T(8,128)(2,1)S(1)}, bf16[4,128,256]{2,1,0:T(8,128)(2,1)S(1)}, u32[]{:S(2)}, u32[]{:S(2)}) collective-permute-start(bf16[4,128,256]{2,1,0:T(8,128)(2,1)S(1)} %collective-permute-done.14.refs_0_), channel_id=1, source_target_pairs={{0,8},{4,12},{8,0},{12,4},{16,24},{20,28},{24,16},{28,20},{1,9},{5... | collective-permute-start | bytes 786440 | tf_op jit(solution)/shard_map/ppermute | solution.py:31
  77.3 5.4 %collective-permute-done.20.refs_6_ = bf16[4,128,256]{2,1,0:T(8,128)(2,1)S(1)} collective-permute-done((bf16[4,128,256]{2,1,0:T(8,128)(2,1)S(1)}, bf16[4,128,256]{2,1,0:T(8,128)(2,1)S(1)}, u32[]{:S(2)}, u32[]{:S(2)}) %collective-permute-start.20) | collective-permute-done | bytes 262176 | tf_op jit(solution)/shard_map/ppermute | solution.py:31
  82.7 3.0 %collective-permute-done.18.refs_4_ = bf16[4,128,256]{2,1,0:T(8,128)(2,1)S(1)} collective-permute-done((bf16[4,128,256]{2,1,0:T(8,128)(2,1)S(1)}, bf16[4,128,256]{2,1,0:T(8,128)(2,1)S(1)}, u32[]{:S(2)}, u32[]{:S(2)}) %collective-permute-start.18) | collective-permute-done | bytes 262176 | tf_op jit(solution)/shard_map/ppermute | solution.py:31
  87.6 14.9 %shard_map.100 = (f32[16,128,256]{2,1,0:T(8,128)S(1)}, f32[4,128,256]{2,1,0:T(8,128)S(1)}, f32[4,128,256]{2,1,0:T(8,128)S(1)}, f32[4,128,256]{2,1,0:T(8,128)S(1)...) custom-call(s32[132]{0:T(256)S(1)} %compare_select_fusion.4.pairs, ...), custom_call_target="tpu_custom_call" | custom-call | flops 4227858432 | bytes 9699328 | tf_op jit(solution)/shard_map/pallas_call | solution.py:186
  105.4 6.9 %collective-permute-start.26 = (s16[528,256]{1,0:T(8,128)(2,1)S(1)}, s16[528,256]{1,0:T(8,128)(2,1)S(1)}, u32[]{:S(2)}, u32[]{:S(2)}) collective-permute-start(s16[528,256]{1,0:T(8,128)(2,1)S(1)} %shard_map.102), channel_id=1, source_target_pairs={{0,16},{4,20},{8,24},{12,28},{16,0},{20,4},{24,8},{28,12},{1,17},{... | collective-permute-start | bytes 811016 | tf_op jit(solution)/shard_map/ppermute | solution.py:31
  112.5 1.0 collective-permute-start.28
  113.5 10.7 %collective-permute-done.26.refs_1_ = s16[528,256]{1,0:T(8,128)(2,1)S(1)} collective-permute-done((s16[528,256]{1,0:T(8,128)(2,1)S(1)}, s16[528,256]{1,0:T(8,128)(2,1)S(1)}, u32[]{:S(2)}, u32[]{:S(2)}) %collective-permute-start.26) | collective-permute-done | bytes 270368 | tf_op jit(solution)/shard_map/ppermute | solution.py:31
  124.2 1.2 collective-permute-done.28.refs_2_
  125.8 2.5 %add_add_fusion = f32[16,128,256]{2,1,0:T(8,128)} fusion(f32[16,128,256]{2,1,0:T(8,128)S(1)} %bitcast.64, f32[16,128,256]{2,1,0:T(8,128)S(1)} %get-tuple-element.33, f32[16,128,256]{2,1,0:T(8,128)S(1)} %bitcast.60, f32[16,128,256]{2,1,0:T(8,128)S(1)} %bitcast.63, f32[16,128,256]{2,1,0:T(8,128)S(1)} %get-tuple-element.23), kind=kLoop, calls=%fused_computation.1 | loop fusion | flops 6291456 | bytes 12582912 | tf_op jit(solution)/shard_map/add | solution.py:343
  128.3 5.2 %collective-permute-done.29.coded = s16[528,256]{1,0:T(8,128)(2,1)S(1)} collective-permute-done((s16[528,256]{1,0:T(8,128)(2,1)S(1)}, s16[528,256]{1,0:T(8,128)(2,1)S(1)}, u32[]{:S(2)}, u32[]{:S(2)}) %collective-permute-start.29) | collective-permute-done | bytes 270368 | tf_op jit(solution)/shard_map/ppermute | solution.py:26
  133.5 1.0 shard_map.105
  (104 shorter events, 19.7 us)
Async XLA Ops:
  1.7 15.1 %collective-permute-start.5 = (bf16[4,128,256]{2,1,0:T(8,128)(2,1)S(1)}, bf16[4,128,256]{2,1,0:T(8,128)(2,1)S(1)}, u32[]{:S(2)}, u32[]{:S(2)}) collective-permute-start(bf16[4,128,256]{2,1,0:T(8,128)(2,1)S(1)} %convert_element_type.63.refs_0_), channel_id=1, source_target_pairs={{0,24},{4,28},{8,16},{12,20},{16,8},{20,12},{24,0},{28,4},{1,25},{... | collective-permute-start | bytes 786440 | tf_op jit(solution)/shard_map/ppermute | solution.py:31
  5.7 11.9 %collective-permute-start.3 = (bf16[4,128,256]{2,1,0:T(8,128)(2,1)S(1)}, bf16[4,128,256]{2,1,0:T(8,128)(2,1)S(1)}, u32[]{:S(2)}, u32[]{:S(2)}) collective-permute-start(bf16[4,128,256]{2,1,0:T(8,128)(2,1)S(1)} %convert_element_type.63.refs_0_), channel_id=1, source_target_pairs={{0,16},{4,20},{8,24},{12,28},{16,0},{20,4},{24,8},{28,12},{1,17},{... | collective-permute-start | bytes 786440 | tf_op jit(solution)/shard_map/ppermute | solution.py:31
  6.2 11.7 %collective-permute-start.1 = (bf16[4,128,256]{2,1,0:T(8,128)(2,1)S(1)}, bf16[4,128,256]{2,1,0:T(8,128)(2,1)S(1)}, u32[]{:S(2)}, u32[]{:S(2)}) collective-permute-start(bf16[4,128,256]{2,1,0:T(8,128)(2,1)S(1)} %convert_element_type.63.refs_0_), channel_id=1, source_target_pairs={{0,8},{4,12},{8,0},{12,4},{16,24},{20,28},{24,16},{28,20},{1,9},{5... | collective-permute-start | bytes 786440 | tf_op jit(solution)/shard_map/ppermute | solution.py:31
  6.3 14.7 %collective-permute-start = (bf16[4,128,256]{2,1,0:T(8,128)(2,1)S(1)}, bf16[4,128,256]{2,1,0:T(8,128)(2,1)S(1)}, u32[]{:S(2)}, u32[]{:S(2)}) collective-permute-start(bf16[4,128,256]{2,1,0:T(8,128)(2,1)S(1)} %convert_element_type.63.refs_0_), channel_id=1, source_target_pairs={{0,4},{4,0},{8,12},{12,8},{16,20},{20,16},{24,28},{28,24},{1,5},{5... | collective-permute-start | bytes 786440 | tf_op jit(solution)/shard_map/ppermute | solution.py:31
  16.8 4.9 %collective-permute-start.6 = (bf16[4,128,256]{2,1,0:T(8,128)(2,1)S(1)}, bf16[4,128,256]{2,1,0:T(8,128)(2,1)S(1)}, u32[]{:S(2)}, u32[]{:S(2)}) collective-permute-start(bf16[4,128,256]{2,1,0:T(8,128)(2,1)S(1)} %collective-permute-done.5.refs_6_), channel_id=1, source_target_pairs={{0,4},{4,0},{8,12},{12,8},{16,20},{20,16},{24,28},{28,24},{1,5},{5... | collective-permute-start | bytes 786440 | tf_op jit(solution)/shard_map/ppermute | solution.py:31
  17.6 4.1 %collective-permute-start.4 = (bf16[4,128,256]{2,1,0:T(8,128)(2,1)S(1)}, bf16[4,128,256]{2,1,0:T(8,128)(2,1)S(1)}, u32[]{:S(2)}, u32[]{:S(2)}) collective-permute-start(bf16[4,128,256]{2,1,0:T(8,128)(2,1)S(1)} %collective-permute-done.3.refs_4_), channel_id=1, source_target_pairs={{0,4},{4,0},{8,12},{12,8},{16,20},{20,16},{24,28},{28,24},{1,5},{5... | collective-permute-start | bytes 786440 | tf_op jit(solution)/shard_map/ppermute | solution.py:31
  17.9 3.8 %collective-permute-start.2 = (bf16[4,128,256]{2,1,0:T(8,128)(2,1)S(1)}, bf16[4,128,256]{2,1,0:T(8,128)(2,1)S(1)}, u32[]{:S(2)}, u32[]{:S(2)}) collective-permute-start(bf16[4,128,256]{2,1,0:T(8,128)(2,1)S(1)} %collective-permute-done.1.refs_2_), channel_id=1, source_target_pairs={{0,4},{4,0},{8,12},{12,8},{16,20},{20,16},{24,28},{28,24},{1,5},{5... | collective-permute-start | bytes 786440 | tf_op jit(solution)/shard_map/ppermute | solution.py:31
  33.2 6.1 %collective-permute-start.8 = (f32[4,128,256]{2,1,0:T(8,128)}, f32[4,128,256]{2,1,0:T(8,128)}, u32[]{:S(2)}, u32[]{:S(2)}) collective-permute-start(f32[4,128,256]{2,1,0:T(8,128)} %get-tuple-element.27), channel_id=1, source_target_pairs={{0,4},{4,0},{8,12},{12,8},{16,20},{20,16},{24,28},{28,24},{1,5},{5... | collective-permute-start | bytes 1572872 | tf_op jit(solution)/shard_map/ppermute | solution.py:31
  35.3 10.8 %collective-permute-start.10 = (f32[4,128,256]{2,1,0:T(8,128)}, f32[4,128,256]{2,1,0:T(8,128)}, u32[]{:S(2)}, u32[]{:S(2)}) collective-permute-start(f32[4,128,256]{2,1,0:T(8,128)} %get-tuple-element.29), channel_id=1, source_target_pairs={{0,4},{4,0},{8,12},{12,8},{16,20},{20,16},{24,28},{28,24},{1,5},{5... | collective-permute-start | bytes 1572872 | tf_op jit(solution)/shard_map/ppermute | solution.py:31
  35.4 13.0 %collective-permute-start.12 = (f32[4,128,256]{2,1,0:T(8,128)}, f32[4,128,256]{2,1,0:T(8,128)}, u32[]{:S(2)}, u32[]{:S(2)}) collective-permute-start(f32[4,128,256]{2,1,0:T(8,128)} %get-tuple-element.31), channel_id=1, source_target_pairs={{0,4},{4,0},{8,12},{12,8},{16,20},{20,16},{24,28},{28,24},{1,5},{5... | collective-permute-start | bytes 1572872 | tf_op jit(solution)/shard_map/ppermute | solution.py:31
  38.3 13.2 %collective-permute-start.7 = (f32[4,128,256]{2,1,0:T(8,128)}, f32[4,128,256]{2,1,0:T(8,128)S(1)}, u32[]{:S(2)}, u32[]{:S(2)}) collective-permute-start(f32[4,128,256]{2,1,0:T(8,128)} %get-tuple-element.25), channel_id=1, source_target_pairs={{0,4},{4,0},{8,12},{12,8},{16,20},{20,16},{24,28},{28,24},{1,5},{5... | collective-permute-start | bytes 1572872 | tf_op jit(solution)/shard_map/ppermute | solution.py:31
  41.6 11.6 %collective-permute-start.9 = (s16[528,256]{1,0:T(8,128)(2,1)S(1)}, s16[528,256]{1,0:T(8,128)(2,1)S(1)}, u32[]{:S(2)}, u32[]{:S(2)}) collective-permute-start(s16[528,256]{1,0:T(8,128)(2,1)S(1)} %shard_map.96), channel_id=1, source_target_pairs={{0,8},{4,12},{8,0},{12,4},{16,24},{20,28},{24,16},{28,20},{1,9},{5... | collective-permute-start | bytes 811016 | tf_op jit(solution)/shard_map/ppermute | solution.py:31
  48.4 14.4 %collective-permute-start.11 = (s16[528,256]{1,0:T(8,128)(2,1)S(1)}, s16[528,256]{1,0:T(8,128)(2,1)S(1)}, u32[]{:S(2)}, u32[]{:S(2)}) collective-permute-start(s16[528,256]{1,0:T(8,128)(2,1)S(1)} %shard_map.97), channel_id=1, source_target_pairs={{0,16},{4,20},{8,24},{12,28},{16,0},{20,4},{24,8},{28,12},{1,17},{... | collective-permute-start | bytes 811016 | tf_op jit(solution)/shard_map/ppermute | solution.py:31
  48.5 37.7 %copy-start.12 = (f32[2048,256]{1,0:T(8,128)S(1)}, f32[2048,256]{1,0:T(8,128)}, u32[]{:S(2)}) copy-start(f32[2048,256]{1,0:T(8,128)} %param.8) | copy-start | bytes 6291460
  49.8 36.4 %copy-start.11 = (f32[1,2048,256]{2,1,0:T(8,128)S(1)}, f32[1,2048,256]{2,1,0:T(8,128)}, u32[]{:S(2)}) copy-start(f32[1,2048,256]{2,1,0:T(8,128)} %get-tuple-element.54) | copy-start | bytes 6291460
  49.8 12.9 %collective-permute-start.13 = (s16[528,256]{1,0:T(8,128)(2,1)S(1)}, s16[528,256]{1,0:T(8,128)(2,1)S(1)}, u32[]{:S(2)}, u32[]{:S(2)}) collective-permute-start(s16[528,256]{1,0:T(8,128)(2,1)S(1)} %shard_map.98), channel_id=1, source_target_pairs={{0,24},{4,28},{8,16},{12,20},{16,8},{20,12},{24,0},{28,4},{1,25},{... | collective-permute-start | bytes 811016 | tf_op jit(solution)/shard_map/ppermute | solution.py:31
  63.2 9.4 %collective-permute-start.14 = (bf16[4,128,256]{2,1,0:T(8,128)(2,1)S(1)}, bf16[4,128,256]{2,1,0:T(8,128)(2,1)S(1)}, u32[]{:S(2)}, u32[]{:S(2)}) collective-permute-start(bf16[4,128,256]{2,1,0:T(8,128)(2,1)S(1)} %get-tuple-element.32), channel_id=1, source_target_pairs={{0,1},{1,2},{2,3},{3,0},{4,5},{5,6},{6,7},{7,4},{8,9},{9,10},{10,1... | collective-permute-start | bytes 786440 | tf_op jit(solution)/shard_map/ppermute | solution.py:26
  72.6 10.1 %collective-permute-start.20 = (bf16[4,128,256]{2,1,0:T(8,128)(2,1)S(1)}, bf16[4,128,256]{2,1,0:T(8,128)(2,1)S(1)}, u32[]{:S(2)}, u32[]{:S(2)}) collective-permute-start(bf16[4,128,256]{2,1,0:T(8,128)(2,1)S(1)} %collective-permute-done.14.refs_0_), channel_id=1, source_target_pairs={{0,24},{4,28},{8,16},{12,20},{16,8},{20,12},{24,0},{28,4},{1,25},{... | collective-permute-start | bytes 786440 | tf_op jit(solution)/shard_map/ppermute | solution.py:31
  73.1 12.5 %collective-permute-start.18 = (bf16[4,128,256]{2,1,0:T(8,128)(2,1)S(1)}, bf16[4,128,256]{2,1,0:T(8,128)(2,1)S(1)}, u32[]{:S(2)}, u32[]{:S(2)}) collective-permute-start(bf16[4,128,256]{2,1,0:T(8,128)(2,1)S(1)} %collective-permute-done.14.refs_0_), channel_id=1, source_target_pairs={{0,16},{4,20},{8,24},{12,28},{16,0},{20,4},{24,8},{28,12},{1,17},{... | collective-permute-start | bytes 786440 | tf_op jit(solution)/shard_map/ppermute | solution.py:31
  74.7 11.0 %collective-permute-start.16 = (bf16[4,128,256]{2,1,0:T(8,128)(2,1)S(1)}, bf16[4,128,256]{2,1,0:T(8,128)(2,1)S(1)}, u32[]{:S(2)}, u32[]{:S(2)}) collective-permute-start(bf16[4,128,256]{2,1,0:T(8,128)(2,1)S(1)} %collective-permute-done.14.refs_0_), channel_id=1, source_target_pairs={{0,8},{4,12},{8,0},{12,4},{16,24},{20,28},{24,16},{28,20},{1,9},{5... | collective-permute-start | bytes 786440 | tf_op jit(solution)/shard_map/ppermute | solution.py:31
  77.2 9.7 %collective-permute-start.15 = (bf16[4,128,256]{2,1,0:T(8,128)(2,1)S(1)}, bf16[4,128,256]{2,1,0:T(8,128)(2,1)S(1)}, u32[]{:S(2)}, u32[]{:S(2)}) collective-permute-start(bf16[4,128,256]{2,1,0:T(8,128)(2,1)S(1)} %collective-permute-done.14.refs_0_), channel_id=1, source_target_pairs={{0,4},{4,0},{8,12},{12,8},{16,20},{20,16},{24,28},{28,24},{1,5},{5... | collective-permute-start | bytes 786440 | tf_op jit(solution)/shard_map/ppermute | solution.py:31
  82.7 4.2 %collective-permute-start.21 = (bf16[4,128,256]{2,1,0:T(8,128)(2,1)S(1)}, bf16[4,128,256]{2,1,0:T(8,128)(2,1)S(1)}, u32[]{:S(2)}, u32[]{:S(2)}) collective-permute-start(bf16[4,128,256]{2,1,0:T(8,128)(2,1)S(1)} %collective-permute-done.20.refs_6_), channel_id=1, source_target_pairs={{0,4},{4,0},{8,12},{12,8},{16,20},{20,16},{24,28},{28,24},{1,5},{5... | collective-permute-start | bytes 786440 | tf_op jit(solution)/shard_map/ppermute | solution.py:31
  85.7 1.5 %collective-permute-start.19 = (bf16[4,128,256]{2,1,0:T(8,128)(2,1)S(1)}, bf16[4,128,256]{2,1,0:T(8,128)(2,1)S(1)}, u32[]{:S(2)}, u32[]{:S(2)}) collective-permute-start(bf16[4,128,256]{2,1,0:T(8,128)(2,1)S(1)} %collective-permute-done.18.refs_4_), channel_id=1, source_target_pairs={{0,4},{4,0},{8,12},{12,8},{16,20},{20,16},{24,28},{28,24},{1,5},{5... | collective-permute-start | bytes 786440 | tf_op jit(solution)/shard_map/ppermute | solution.py:31
  85.7 1.9 %collective-permute-start.17 = (bf16[4,128,256]{2,1,0:T(8,128)(2,1)S(1)}, bf16[4,128,256]{2,1,0:T(8,128)(2,1)S(1)}, u32[]{:S(2)}, u32[]{:S(2)}) collective-permute-start(bf16[4,128,256]{2,1,0:T(8,128)(2,1)S(1)} %collective-permute-done.16.refs_2_), channel_id=1, source_target_pairs={{0,4},{4,0},{8,12},{12,8},{16,20},{20,16},{24,28},{28,24},{1,5},{5... | collective-permute-start | bytes 786440 | tf_op jit(solution)/shard_map/ppermute | solution.py:31
  102.5 2.0 %collective-permute-start.23 = (f32[4,128,256]{2,1,0:T(8,128)S(1)}, f32[4,128,256]{2,1,0:T(8,128)S(1)}, u32[]{:S(2)}, u32[]{:S(2)}) collective-permute-start(f32[4,128,256]{2,1,0:T(8,128)S(1)} %get-tuple-element.37), channel_id=1, source_target_pairs={{0,4},{4,0},{8,12},{12,8},{16,20},{20,16},{24,28},{28,24},{1,5},{5... | collective-permute-start | bytes 1572872 | tf_op jit(solution)/shard_map/ppermute | solution.py:31
  102.6 2.6 %collective-permute-start.25 = (f32[4,128,256]{2,1,0:T(8,128)S(1)}, f32[4,128,256]{2,1,0:T(8,128)S(1)}, u32[]{:S(2)}, u32[]{:S(2)}) collective-permute-start(f32[4,128,256]{2,1,0:T(8,128)S(1)} %get-tuple-element.39), channel_id=1, source_target_pairs={{0,4},{4,0},{8,12},{12,8},{16,20},{20,16},{24,28},{28,24},{1,5},{5... | collective-permute-start | bytes 1572872 | tf_op jit(solution)/shard_map/ppermute | solution.py:31
  103.1 9.2 %collective-permute-start.27 = (f32[4,128,256]{2,1,0:T(8,128)S(1)}, f32[4,128,256]{2,1,0:T(8,128)S(1)}, u32[]{:S(2)}, u32[]{:S(2)}) collective-permute-start(f32[4,128,256]{2,1,0:T(8,128)S(1)} %get-tuple-element.41), channel_id=1, source_target_pairs={{0,4},{4,0},{8,12},{12,8},{16,20},{20,16},{24,28},{28,24},{1,5},{5... | collective-permute-start | bytes 1572872 | tf_op jit(solution)/shard_map/ppermute | solution.py:31
  103.2 10.3 %collective-permute-start.22 = (f32[4,128,256]{2,1,0:T(8,128)S(1)}, f32[4,128,256]{2,1,0:T(8,128)S(1)}, u32[]{:S(2)}, u32[]{:S(2)}) collective-permute-start(f32[4,128,256]{2,1,0:T(8,128)S(1)} %get-tuple-element.35), channel_id=1, source_target_pairs={{0,4},{4,0},{8,12},{12,8},{16,20},{20,16},{24,28},{28,24},{1,5},{5... | collective-permute-start | bytes 1572872 | tf_op jit(solution)/shard_map/ppermute | solution.py:31
  104.6 8.9 %collective-permute-start.24 = (s16[528,256]{1,0:T(8,128)(2,1)S(1)}, s16[528,256]{1,0:T(8,128)(2,1)S(1)}, u32[]{:S(2)}, u32[]{:S(2)}) collective-permute-start(s16[528,256]{1,0:T(8,128)(2,1)S(1)} %shard_map.101), channel_id=1, source_target_pairs={{0,8},{4,12},{8,0},{12,4},{16,24},{20,28},{24,16},{28,20},{1,9},{5... | collective-permute-start | bytes 811016 | tf_op jit(solution)/shard_map/ppermute | solution.py:31
  105.4 18.8 %collective-permute-start.26 = (s16[528,256]{1,0:T(8,128)(2,1)S(1)}, s16[528,256]{1,0:T(8,128)(2,1)S(1)}, u32[]{:S(2)}, u32[]{:S(2)}) collective-permute-start(s16[528,256]{1,0:T(8,128)(2,1)S(1)} %shard_map.102), channel_id=1, source_target_pairs={{0,16},{4,20},{8,24},{12,28},{16,0},{20,4},{24,8},{28,12},{1,17},{... | collective-permute-start | bytes 811016 | tf_op jit(solution)/shard_map/ppermute | solution.py:31
  112.5 12.8 %collective-permute-start.28 = (s16[528,256]{1,0:T(8,128)(2,1)S(1)}, s16[528,256]{1,0:T(8,128)(2,1)S(1)}, u32[]{:S(2)}, u32[]{:S(2)}) collective-permute-start(s16[528,256]{1,0:T(8,128)(2,1)S(1)} %shard_map.103), channel_id=1, source_target_pairs={{0,24},{4,28},{8,16},{12,20},{16,8},{20,12},{24,0},{28,4},{1,25},{... | collective-permute-start | bytes 811016 | tf_op jit(solution)/shard_map/ppermute | solution.py:31
  125.7 7.7 %collective-permute-start.29 = (s16[528,256]{1,0:T(8,128)(2,1)S(1)}, s16[528,256]{1,0:T(8,128)(2,1)S(1)}, u32[]{:S(2)}, u32[]{:S(2)}) collective-permute-start(s16[528,256]{1,0:T(8,128)(2,1)S(1)} %shard_map.104), channel_id=1, source_target_pairs={{0,3},{1,0},{2,1},{3,2},{4,7},{5,4},{6,5},{7,6},{8,11},{9,8},{10,9... | collective-permute-start | bytes 811016 | tf_op jit(solution)/shard_map/ppermute | solution.py:26
  (14 other events, 97.8 us)

commit v2 on v1

v2 whole, which is shorter than its diff:
```python
import functools
import math

import jax
import jax.numpy as jnp
from jax import lax
from jax.experimental import pallas as pl
from jax.experimental.pallas import tpu as pltpu
from jax.sharding import PartitionSpec as P

HALF_STEP = 0.002
ROOT_STEP = math.sqrt(0.004)
PRIOR = 25.0
GROUP = 4
SCALE_ROWS = 16
SMALL_LIMIT = 12 * 2**20
SCALE_STEPS = 128.0

ANY = pl.BlockSpec(memory_space=pl.ANY)
IN_VMEM = pl.BlockSpec(memory_space=pltpu.VMEM)
IN_SMEM = pl.BlockSpec(memory_space=pltpu.SMEM)


def shifted(x, axis, by):
    peers = lax.axis_size(axis)
    return lax.ppermute(x, axis, [(i, (i + by) % peers) for i in range(peers)])


def swapped(x, axis, mask):
    peers = lax.axis_size(axis)
    return lax.ppermute(x, axis, [(i, i ^ mask) for i in range(peers)])


def widths(slots, user_tiles, item_tiles):
    bits = tuple(max(1, (n - 1).bit_length()) for n in (slots, user_tiles, item_tiles))
    assert 2 * bits[0] + 2 * bits[1] + bits[2] + 2 <= 31
    return bits


def pair_plan(rows, cols, count, me, user_tiles, item_tiles, per, span):
    slots = rows.shape[0]
    slot_bits, row_bits, col_bits = widths(slots, user_tiles, item_tiles)
    place = ((cols // per) ^ me) * per + cols % per
    n = jnp.arange(slots, dtype=jnp.int32)
    live = n < count
    same = (place[:, None] == place[None, :]) & live[None, :]
    rank = jnp.sum(same & (rows[None, :] < rows[:, None]), axis=1, dtype=jnp.int32)
    opens = live & (rank % 2 == 0)
    run = place // span
    runs = item_tiles // span
    run_ids = jnp.arange(runs, dtype=jnp.int32)
    ahead = (place[None, :] < place[:, None]) & (run[None, :] == run[:, None]) & opens[None, :]
    within = jnp.sum(ahead, axis=1, dtype=jnp.int32)
    size = jnp.sum((run[None, :] == run_ids[:, None]) & opens[None, :], axis=1, dtype=jnp.int32)
    size = (size + GROUP - 1) // GROUP * GROUP
    edges = jnp.arange(runs + 1, dtype=jnp.int32)
    starts = jnp.sum(jnp.where(run_ids[None, :] < edges[:, None], size[None, :], 0), axis=1, dtype=jnp.int32)
    base = jnp.sum(jnp.where(run_ids[None, :] < run[:, None], size[None, :], 0), axis=1, dtype=jnp.int32)
    where = base + within + rank // 2
    col_at = 2 * slot_bits + 2 * row_bits
    one = 1 << (col_at + col_bits)
    first = n | (rows << (2 * slot_bits)) | (place << col_at)
    second = (n << slot_bits) | (rows << (2 * slot_bits + row_bits))
    word = jnp.where(live, jnp.where(rank % 2 == 0, first, second) + one, 0)
    words = jnp.arange((slots + item_tiles) // 2 + runs * GROUP, dtype=jnp.int32)[:, None]
    pairs = jnp.sum(jnp.where(where[None, :] == words, word[None, :], 0), axis=1, dtype=jnp.int32)
    unused = jnp.sum(words >= starts[None, 1:], axis=1, dtype=jnp.int32) * span
    unused = jnp.minimum(unused, item_tiles - 1) << col_at
    return jnp.where(pairs == 0, unused, pairs), starts


def decode_word(word, bits, first_col):
    slot_bits, row_bits, col_bits = bits
    fields = []
    for width in (slot_bits, slot_bits, row_bits, row_bits, col_bits):
        fields.append(word & ((1 << width) - 1))
        word = word >> width
    fields[4] -= first_col
    return (*fields, word)


def fetch_kernel(section, lump, counts, ratings, out, sem):
    lumps = lax.div(counts[section] + lump - 1, lump)

    def load(i):
        part = pl.ds(i * lump, lump)
        return pltpu.make_async_copy(ratings.at[section, part], out.at[part], sem.at[i])

    lax.fori_loop(0, lumps, lambda i, c: (load(i).start(), c)[1], 0)
    lax.fori_loop(0, lumps, lambda i, c: (load(i).wait(), c)[1], 0)


def fetch(section, counts, ratings):
    slots = ratings.shape[1]
    lump = math.gcd(slots, 16)
    return pl.pallas_call(
        functools.partial(fetch_kernel, section, lump),
        out_shape=jax.ShapeDtypeStruct(ratings.shape[1:], ratings.dtype),
        in_specs=[IN_SMEM, ANY],
        out_specs=IN_VMEM,
        scratch_shapes=[pltpu.SemaphoreType.DMA((slots // lump,))],
        compiler_params=pltpu.CompilerParams(vmem_limit_bytes=SMALL_LIMIT),
        cost_estimate=pl.CostEstimate(flops=0, bytes_accessed=slots * 2**15, transcendentals=0),
    )(counts, ratings)


def items_kernel(run, span, bits, pairs, starts, rated, users, even, odd, out_even, out_odd, misfits, items, grad):
    per = even.shape[0]
    tile = users.shape[1]
    low, high = starts[run], starts[run + 1]
    steps = lax.div(high - low, GROUP)
    for t in range(per):
        items[t] = even[t]
        items[per + t] = odd[t]
    grad[...] = jnp.zeros_like(grad)

    def decode(p):
        return decode_word(pairs[p], bits, run * span)

    def users_of(row_a, row_b):
        return jnp.concatenate([users[row_a], users[row_b]], axis=0)

    def predict(p):
        slot_a, slot_b, row_a, row_b, col, live = decode(p)
        predicted = lax.dot_general(
            users_of(row_a, row_b), items[col], (((1,), (1,)), ((), ())), preferred_element_type=jnp.float32
        )
        given = jnp.concatenate([rated[slot_a], rated[slot_b]], axis=0).astype(jnp.float32)
        rows = lax.broadcasted_iota(jnp.int32, (2 * tile, 1), 0)
        return jnp.where(rows < tile * live, given - predicted, 0.0).astype(jnp.bfloat16)

    def add_grad(p, misfit):
        _, _, row_a, row_b, col, _ = decode(p)
        grad[col] += lax.dot_general(
            misfit, users_of(row_a, row_b), (((0,), (0,)), ((), ())), preferred_element_type=jnp.float32
        )

    @pl.when(steps > 0)
    def _():
        for j in range(GROUP):
            misfits[j] = predict(low + j)

        def advance(step, carry):
            at = step * GROUP
            held = [misfits[at + j] for j in range(GROUP)]
            following = [predict(low + at + GROUP + j) for j in range(GROUP)]
            for j in range(GROUP):
                add_grad(low + at + j, held[j])
            for j in range(GROUP):
                misfits[at + GROUP + j] = following[j]
            return carry

        lax.fori_loop(0, steps - 1, advance, 0)
        for j in range(GROUP):
            add_grad(high - GROUP + j, misfits[high - low - GROUP + j])

    for t in range(per):
        out_even[t] = grad[t]
        out_odd[t] = grad[per + t]


def item_grads(run, span, bits, plan, rated, users, even, odd):
    per, tile, width = even.shape
    held = span * ((users.shape[0] + 1) // 2)
    held = (min(held, (rated.shape[0] + span) // 2) + GROUP - 1) // GROUP * GROUP
    f32 = jnp.float32
    return pl.pallas_call(
        functools.partial(items_kernel, run, span, bits),
        out_shape=[jax.ShapeDtypeStruct((per, tile, width), f32)] * 2
        + [jax.ShapeDtypeStruct((held, 2 * tile, tile), jnp.bfloat16)],
        in_specs=[IN_SMEM, IN_SMEM] + [IN_VMEM] * 4,
        out_specs=[IN_VMEM] * 3,
        scratch_shapes=[pltpu.VMEM((span, tile, width), jnp.bfloat16), pltpu.VMEM((span, tile, width), f32)],
        compiler_params=pltpu.CompilerParams(vmem_limit_bytes=SMALL_LIMIT),
        cost_estimate=pl.CostEstimate(flops=3 * 10**9, bytes_accessed=2**20, transcendentals=0),
    )(*plan, rated, users, even, odd)


def users_kernel(power, span, bits, runs, pairs, starts, *refs):
    pieces = refs[: 2 * runs]
    misfits = refs[2 * runs : 3 * runs]
    factors, noise, new, new_bf, items, grad = refs[3 * runs :]
    per = pieces[0].shape[0]
    tile = factors.shape[1]
    for i, piece in enumerate(pieces):
        for t in range(per):
            items[i * per + t] = piece[t]
    grad[...] = jnp.zeros_like(grad)
    for run in range(runs):
        low = starts[run]

        def advance(step, carry, low=low, held=misfits[run]):
            for j in range(GROUP):
                i = step * GROUP + j
                _, _, row_a, row_b, col, _ = decode_word(pairs[low + i], bits, 0)
                part = jnp.dot(held[i], items[col], preferred_element_type=jnp.float32)
                grad[row_a] += part[:tile]
                grad[row_b] += part[tile:]
            return carry

        lax.fori_loop(0, lax.div(starts[run + 1] - low, GROUP), advance, 0)

    def finish(t, carry):
        before = factors[t]
        after = (
            before + HALF_STEP * (power * grad[t] - PRIOR * before) + ROOT_STEP * noise[t].astype(jnp.float32)
        )
        new[t] = after
        new_bf[t] = after.astype(jnp.bfloat16)
        return carry

    lax.fori_loop(0, factors.shape[0], finish, 0)


def user_step(power, span, bits, plan, pieces, misfits, factors, noise):
    shape = factors.shape
    per, tile, width = pieces[0].shape
    f32 = jnp.float32
    return pl.pallas_call(
        functools.partial(users_kernel, power, span, bits, len(misfits)),
        out_shape=[jax.ShapeDtypeStruct(shape, f32), jax.ShapeDtypeStruct(shape, jnp.bfloat16)],
        in_specs=[IN_SMEM, IN_SMEM] + [IN_VMEM] * (len(pieces) + len(misfits) + 2),
        out_specs=[IN_VMEM] * 2,
        scratch_shapes=[pltpu.VMEM((len(pieces) * per, tile, width), jnp.bfloat16), pltpu.VMEM(shape, f32)],
        compiler_params=pltpu.CompilerParams(vmem_limit_bytes=SMALL_LIMIT),
        cost_estimate=pl.CostEstimate(flops=8 * 10**9, bytes_accessed=2**20, transcendentals=0),
    )(*plan, *pieces, *misfits, factors, noise)


def coded_shape(per, tile, width):
    return jax.ShapeDtypeStruct((per * tile + SCALE_ROWS, width), jnp.int16)


def encode(blocks, out):
    per = len(blocks)
    tile, width = blocks[0].shape
    row = lax.broadcasted_iota(jnp.int32, (SCALE_ROWS, width), 0)
    powers = jnp.zeros((SCALE_ROWS, width), jnp.int32)
    for t, block in enumerate(blocks):
        largest = jnp.max(jnp.abs(block), axis=0, keepdims=True)
        power = jnp.ceil(SCALE_STEPS * jnp.log2(jnp.maximum(largest, 1e-20)))
        scaled = jnp.round(block * jnp.exp2(15.0 - power / SCALE_STEPS))
        out[pl.ds(t * tile, tile)] = jnp.clip(scaled, -32767.0, 32767.0).astype(jnp.int32).astype(jnp.int16)
        powers = jnp.where(row == t, power.astype(jnp.int32), powers)
    out[pl.ds(per * tile, SCALE_ROWS)] = powers.astype(jnp.int16)


def decoded(ref, t, tile, per):
    powers = ref[pl.ds(per * tile, SCALE_ROWS)].astype(jnp.int32).astype(jnp.float32)
    unit = jnp.exp2(powers[t : t + 1] / SCALE_STEPS - 15.0)
    return ref[pl.ds(t * tile, tile)].astype(jnp.int32).astype(jnp.float32) * unit


def join_kernel(mine, other, out):
    encode([mine[t] + other[t] for t in range(mine.shape[0])], out)


def join(mine, other):
    return pl.pallas_call(
        join_kernel,
        out_shape=coded_shape(*mine.shape),
        in_specs=[IN_VMEM] * 2,
        out_specs=IN_VMEM,
        compiler_params=pltpu.CompilerParams(vmem_limit_bytes=SMALL_LIMIT),
    )(mine, other)


def owner_sum(mine, other, coded, t):
    per, tile, _ = mine.shape
    total = mine[t] + other[t]
    for ref in coded:
        total = total + decoded(ref, t, tile, per)
    return total


def update_kernel(power, mine, other, *refs):
    *coded, factors, noise, new, new_bf = refs
    for t in range(mine.shape[0]):
        step = HALF_STEP * power * owner_sum(mine, other, coded, t) + ROOT_STEP * noise[t].astype(jnp.float32)
        after = factors[t] - HALF_STEP * PRIOR * factors[t] + step
        new[t] = after
        new_bf[t] = after.astype(jnp.bfloat16)


def delta_kernel(power, mine, other, *refs):
    *coded, noise, out = refs
    steps = []
    for t in range(mine.shape[0]):
        steps.append(HALF_STEP * power * owner_sum(mine, other, coded, t) + ROOT_STEP * noise[t].astype(jnp.float32))
    encode(steps, out)


def arrive_kernel(coded, factors, new, new_bf):
    per, tile, _ = factors.shape
    for t in range(per):
        after = factors[t] - HALF_STEP * PRIOR * factors[t] + decoded(coded, t, tile, per)
        new[t] = after
        new_bf[t] = after.astype(jnp.bfloat16)


def in_vmem(kernel, out_shape, *operands):
    return pl.pallas_call(
        kernel,
        out_shape=out_shape,
        in_specs=[IN_VMEM] * len(operands),
        out_specs=jax.tree.map(lambda _: IN_VMEM, out_shape),
        compiler_params=pltpu.CompilerParams(vmem_limit_bytes=SMALL_LIMIT),
    )(*operands)


def body(u_factors, v_factors, ratings, tile_rows, tile_cols, tile_counts, u_noise, v_noise):
    tile = ratings.shape[-1]
    sections = ratings.shape[2]
    width = u_factors.shape[1]
    peers = lax.axis_size("user")
    power = float(lax.axis_size("item"))
    me = lax.axis_index("user")
    users = u_factors.reshape(-1, tile, width)
    items = v_factors.reshape(-1, tile, width)
    per = items.shape[0]
    item_tiles = peers * per
    span = 2 * per
    runs = item_tiles // span
    ratings = ratings.reshape(ratings.shape[2:])
    counts = tile_counts.reshape(sections)
    u_noise = u_noise.reshape(sections, *users.shape)
    v_noise = v_noise.reshape(sections, *items.shape)
    bits = widths(ratings.shape[1], users.shape[0], item_tiles)
    pair = (
        jax.ShapeDtypeStruct(items.shape, jnp.float32),
        jax.ShapeDtypeStruct(items.shape, jnp.bfloat16),
    )
    items_bf = items.astype(jnp.bfloat16)
    users_bf = users.astype(jnp.bfloat16)
    for section in range(sections):
        sent = shifted(items_bf, "item", section) if section else items_bf
        evens = [sent] + [swapped(sent, "user", 2 * d) for d in range(1, runs)]
        odds = [swapped(even, "user", 1) for even in evens]
        plan = pair_plan(
            tile_rows[0, 0, section],
            tile_cols[0, 0, section],
            counts[section],
            me,
            users.shape[0],
            item_tiles,
            per,
            span,
        )
        rated = fetch(section, counts, ratings)
        mine, other, misfits = [], [], []
        for run in range(runs):
            even_grad, odd_grad, held = item_grads(run, span, bits, plan, rated, users_bf, evens[run], odds[run])
            mine.append(even_grad)
            other.append(swapped(odd_grad, "user", 1))
            misfits.append(held)
        coded = [swapped(join(mine[d], other[d]), "user", 2 * d) for d in range(1, runs)]
        if section == 0:
            items, items_bf = in_vmem(
                functools.partial(update_kernel, power), pair, mine[0], other[0], *coded, items, v_noise[section]
            )
        else:
            delta = in_vmem(
                functools.partial(delta_kernel, power),
                coded_shape(*items.shape),
                mine[0],
                other[0],
                *coded,
                v_noise[section],
            )
            items, items_bf = in_vmem(arrive_kernel, pair, shifted(delta, "item", -section), items)
        pieces = [piece for both in zip(evens, odds) for piece in both]
        users, users_bf = user_step(power, span, bits, plan, pieces, misfits, users, u_noise[section])
    return (users.reshape(u_factors.shape), items.reshape(v_factors.shape))


def solution(mesh):
    placed = (
        P(("user", "item"), None),
        P(("item", "user"), None),
        P("user", "item", None, None, None, None),
        P("user", "item", None, None),
        P("user", "item", None, None),
        P("user", "item", None),
        P(None, ("user", "item"), None),
        P(None, ("item", "user"), None),
    )
    return jax.shard_map(
        body,
        mesh=mesh,
        in_specs=placed,
        out_specs=(P(("user", "item"), None), P(("item", "user"), None)),
        check_vma=False,
    )
```

time: 135 us -> 129 us (0.956); the launches traced: 134 us -> 126 us
  other arithmetic: 17.5 us -> 7.21 us
  local copies, waits for them, and re-layouts: 8.74 us -> 13.4 us
  waiting for transfers between devices: 43.4 us -> 39.2 us
  Pallas kernels: 30.4 us -> 33.4 us
    pallas_call x2 -> x12, Pallas kernels: 24.4 us -> 30.7 us  [the longest x8 16.8 us: item_grads(): pl.pallas_call(functools.partial(items_kernel, run, span, bits), out_shap...]
    unnamed x32 -> x38, local copies, waits for them, and re-layouts: 4.77 us -> 8.69 us
    ppermute x28, waiting for transfers between devices: 34.1 us -> 30.3 us  [swapped(): return lax.ppermute(x, axis, [(i, i ^ mask) for i in range(peers)])]
    pallas_call x6, Pallas kernels: 4.16 us -> 0.88 us  [join(): pl.pallas_call(join_kernel, out_shape=coded_shape(*mine.shape), in_specs=...]
    reduce_sum x1 -> x2, other arithmetic: 2.74 us -> 0.24 us  [pair_plan(): jnp.sum((run[None, :] == run_ids[:, None]) & opens[None, :], axis=1, dtyp...]
    add x1 -> x0, other arithmetic: 2.47 us -> none  [body(): users + HALF_STEP * (power * grad_user - PRIOR * users)]
    mul x1 -> x2, other arithmetic: 2.41 us -> 0.02 us  [pair_plan(): size = (size + GROUP - 1) // GROUP * GROUP]
    convert_element_type x2 -> x1, other arithmetic: 2.45 us -> 0.13 us  [body(): users_bf = users.astype(jnp.bfloat16)]
  transfers between devices with their start and end apart: 30 -> 30, of which waited for: 14 -> 9; matrix products, arithmetic and copies ran while one was open for 15% -> 8% of each run, Pallas kernels for 3% -> 25%
where the time goes in v2:
time: 129 us; the launch traced here: 126 us
  waiting for transfers between devices  39.2 us (30%)
  Pallas kernels  33.4 us (26%)
  starting transfers between devices  32.1 us (25%)
  local copies, waits for them, and re-layouts  13.4 us (10%)
  other arithmetic  7.21 us (6%)
    ppermute x28, waiting for transfers between devices, swapped(): return lax.ppermute(x, axis, [(i, i ^ mask) for i in range(peers)])  30.3 us
    ppermute x28, starting transfers between devices, swapped(): return lax.ppermute(x, axis, [(i, i ^ mask) for i in range(peers)])  28.3 us
    pallas_call x8, Pallas kernels, item_grads(): pl.pallas_call(functools.partial(items_kernel, run, span, bits), out_shap...  16.8 us
    pallas_call x2, Pallas kernels, user_step(): pl.pallas_call(functools.partial(users_kernel, power, span, bits, len(mis...  12.2 us
    ppermute x2, waiting for transfers between devices, shifted(): return lax.ppermute(x, axis, [(i, (i + by) % peers) for i in range(peers)])  8.93 us
    unnamed x38, local copies, waits for them, and re-layouts  8.69 us
    ppermute x2, starting transfers between devices, shifted(): return lax.ppermute(x, axis, [(i, (i + by) % peers) for i in range(peers)])  3.77 us
  transfers between devices with their start and end apart: 30, of which 9 were waited for; matrix products, arithmetic and copies ran while one was open for 8% of the time, Pallas kernels for 25%

profile of v2, /device:TPU:0, one launch (start us, length us, event | category | flops | bytes accessed | tf_op | source)
XLA Modules:
  0.0 126.5 jit_solution(13049087275092222817)
XLA Ops:
  0.7 1.2 convert_element_type.39.even.refs_0_
  1.9 3.0 %collective-permute-start.2 = (bf16[4,128,256]{2,1,0:T(8,128)(2,1)S(1)}, bf16[4,128,256]{2,1,0:T(8,128)(2,1)S(1)}, u32[]{:S(2)}, u32[]{:S(2)}) collective-permute-start(bf16[4,128,256]{2,1,0:T(8,128)(2,1)S(1)} %convert_element_type.39.even.refs_0_), channel_id=1, source_target_pairs={{0,8},{4,12},{8,0},{12,4},{16,24},{20,28},{24,16},{28,20},{1,9},{5... | collective-permute-start | bytes 786440 | tf_op jit(solution)/shard_map/ppermute | solution.py:31
  4.9 1.5 %collective-permute-start.6 = (bf16[4,128,256]{2,1,0:T(8,128)(2,1)S(1)}, bf16[4,128,256]{2,1,0:T(8,128)(2,1)S(1)}, u32[]{:S(2)}, u32[]{:S(2)}) collective-permute-start(bf16[4,128,256]{2,1,0:T(8,128)(2,1)S(1)} %convert_element_type.39.even.refs_0_), channel_id=1, source_target_pairs={{0,16},{4,20},{8,24},{12,28},{16,0},{20,4},{24,8},{28,12},{1,17},{... | collective-permute-start | bytes 786440 | tf_op jit(solution)/shard_map/ppermute | solution.py:31
  7.2 1.3 %fusion.20 = (s32[1,1,1]{2,1,0:T(1,128)}, s32[1,1,1]{2,1,0:T(1,128)}) fusion(s32[1,1,2]{2,1,0:T(1,128)} %param.13), kind=kLoop, calls=%fused_computation.86 | loop fusion | bytes 16 | tf_op jit(solution)/shard_map/slice | solution.py:342
  12.0 1.7 %fusion.16 = (bf16[1,2048,256]{2,1,0:T(8,128)(2,1)S(1)}, bf16[1,2048,256]{2,1,0:T(8,128)(2,1)S(1)}) fusion(bf16[2,2048,256]{2,1,0:T(8,128)(2,1)} %param.14), kind=kLoop, calls=%fused_computation.82 | loop fusion | bytes 4194304 | tf_op jit(solution)/shard_map/slice | solution.py:372
  15.8 2.3 %collective-permute-done.10.even.refs_6_ = bf16[4,128,256]{2,1,0:T(8,128)(2,1)S(1)} collective-permute-done((bf16[4,128,256]{2,1,0:T(8,128)(2,1)S(1)}, bf16[4,128,256]{2,1,0:T(8,128)(2,1)S(1)}, u32[]{:S(2)}, u32[]{:S(2)}) %collective-permute-start.10) | collective-permute-done | bytes 262176 | tf_op jit(solution)/shard_map/ppermute | solution.py:31
  18.4 5.2 %copy-done = bf16[1,1,2,224,128,128]{5,4,3,2,1,0:T(8,128)(2,1)S(1)} copy-done((bf16[1,1,2,224,128,128]{5,4,3,2,1,0:T(8,128)(2,1)S(1)}, bf16[1,1,2,224,128,128]{5,4,3,2,1,0:T(8,128)(2,1)}, u32[]{:S(2)}) %copy-start) | copy-done | bytes 14680088
  25.1 2.1 %shard_map.101 = (f32[4,128,256]{2,1,0:T(8,128)S(1)}, f32[4,128,256]{2,1,0:T(8,128)S(1)}, bf16[64,256,128]{2,1,0:T(8,128)(2,1)S(1)}) custom-call(s32[144]{0:T(256)S(1)} %compare_select_fusion.pairs, s32[5]{0:T(128)S(1)} %select_reduce_fusion.4.starts, bf16[224,128,128]{2,1,0:T(8,128)(2,1)S(1)} %shard_map.95.rated, ...), custom_call_target="tpu_custom_call" | custom-call | flops 3000000000 | bytes 1048576 | tf_op jit(solution)/shard_map/pallas_call | solution.py:167
  27.7 1.7 %shard_map.99 = (f32[4,128,256]{2,1,0:T(8,128)S(1)}, f32[4,128,256]{2,1,0:T(8,128)S(1)}, bf16[64,256,128]{2,1,0:T(8,128)(2,1)S(1)}) custom-call(s32[144]{0:T(256)S(1)} %compare_select_fusion.pairs, s32[5]{0:T(128)S(1)} %select_reduce_fusion.4.starts, bf16[224,128,128]{2,1,0:T(8,128)(2,1)S(1)} %shard_map.95.rated, ...), custom_call_target="tpu_custom_call" | custom-call | flops 3000000000 | bytes 1048576 | tf_op jit(solution)/shard_map/pallas_call | solution.py:167
  30.4 2.1 %shard_map.97 = (f32[4,128,256]{2,1,0:T(8,128)S(1)}, f32[4,128,256]{2,1,0:T(8,128)S(1)}, bf16[64,256,128]{2,1,0:T(8,128)(2,1)S(1)}) custom-call(s32[144]{0:T(256)S(1)} %compare_select_fusion.pairs, s32[5]{0:T(128)S(1)} %select_reduce_fusion.4.starts, bf16[224,128,128]{2,1,0:T(8,128)(2,1)S(1)} %shard_map.95.rated, ...), custom_call_target="tpu_custom_call" | custom-call | flops 3000000000 | bytes 1048576 | tf_op jit(solution)/shard_map/pallas_call | solution.py:167
  32.5 2.1 %copy-done.8 = bf16[64,256,128]{2,1,0:T(8,128)(2,1)} copy-done((bf16[64,256,128]{2,1,0:T(8,128)(2,1)}, bf16[64,256,128]{2,1,0:T(8,128)(2,1)S(1)}, u32[]{:S(2)}) %copy-start.8) | copy-done | bytes 4194328
  34.8 1.7 %shard_map.96 = (f32[4,128,256]{2,1,0:T(8,128)S(1)}, f32[4,128,256]{2,1,0:T(8,128)S(1)}, bf16[64,256,128]{2,1,0:T(8,128)(2,1)S(1)}) custom-call(s32[144]{0:T(256)S(1)} %compare_select_fusion.pairs, s32[5]{0:T(128)S(1)} %select_reduce_fusion.4.starts, bf16[224,128,128]{2,1,0:T(8,128)(2,1)S(1)} %shard_map.95.rated, ...), custom_call_target="tpu_custom_call" | custom-call | flops 3000000000 | bytes 1048576 | tf_op jit(solution)/shard_map/pallas_call | solution.py:167
  38.4 5.9 %collective-permute-start.9 = (s16[528,256]{1,0:T(8,128)(2,1)S(1)}, s16[528,256]{1,0:T(8,128)(2,1)S(1)}, u32[]{:S(2)}, u32[]{:S(2)}) collective-permute-start(s16[528,256]{1,0:T(8,128)(2,1)S(1)} %shard_map.100), channel_id=1, source_target_pairs={{0,16},{4,20},{8,24},{12,28},{16,0},{20,4},{24,8},{28,12},{1,17},{... | collective-permute-start | bytes 811016 | tf_op jit(solution)/shard_map/ppermute | solution.py:31
  44.7 2.5 %collective-permute-done.13.refs_2_ = s16[528,256]{1,0:T(8,128)(2,1)S(1)} collective-permute-done((s16[528,256]{1,0:T(8,128)(2,1)S(1)}, s16[528,256]{1,0:T(8,128)(2,1)S(1)}, u32[]{:S(2)}, u32[]{:S(2)}) %collective-permute-start.13) | collective-permute-done | bytes 270368 | tf_op jit(solution)/shard_map/ppermute | solution.py:31
  47.2 8.2 %collective-permute-done.9.refs_1_ = s16[528,256]{1,0:T(8,128)(2,1)S(1)} collective-permute-done((s16[528,256]{1,0:T(8,128)(2,1)S(1)}, s16[528,256]{1,0:T(8,128)(2,1)S(1)}, u32[]{:S(2)}, u32[]{:S(2)}) %collective-permute-start.9) | collective-permute-done | bytes 270368 | tf_op jit(solution)/shard_map/ppermute | solution.py:31
  57.7 8.9 %collective-permute-done.14.even.refs_0_ = bf16[4,128,256]{2,1,0:T(8,128)(2,1)S(1)} collective-permute-done((bf16[4,128,256]{2,1,0:T(8,128)(2,1)S(1)}, bf16[4,128,256]{2,1,0:T(8,128)(2,1)S(1)}, u32[]{:S(2)}, u32[]{:S(2)}) %collective-permute-start.14) | collective-permute-done | bytes 262176 | tf_op jit(solution)/shard_map/ppermute | solution.py:26
  66.6 1.7 %collective-permute-start.20 = (bf16[4,128,256]{2,1,0:T(8,128)(2,1)S(1)}, bf16[4,128,256]{2,1,0:T(8,128)(2,1)S(1)}, u32[]{:S(2)}, u32[]{:S(2)}) collective-permute-start(bf16[4,128,256]{2,1,0:T(8,128)(2,1)S(1)} %collective-permute-done.14.even.refs_0_), channel_id=1, source_target_pairs={{0,24},{4,28},{8,16},{12,20},{16,8},{20,12},{24,0},{28,4},{1,25},{... | collective-permute-start | bytes 786440 | tf_op jit(solution)/shard_map/ppermute | solution.py:31
  69.4 1.7 %collective-permute-start.18 = (bf16[4,128,256]{2,1,0:T(8,128)(2,1)S(1)}, bf16[4,128,256]{2,1,0:T(8,128)(2,1)S(1)}, u32[]{:S(2)}, u32[]{:S(2)}) collective-permute-start(bf16[4,128,256]{2,1,0:T(8,128)(2,1)S(1)} %collective-permute-done.14.even.refs_0_), channel_id=1, source_target_pairs={{0,16},{4,20},{8,24},{12,28},{16,0},{20,4},{24,8},{28,12},{1,17},{... | collective-permute-start | bytes 786440 | tf_op jit(solution)/shard_map/ppermute | solution.py:31
  71.2 5.6 %collective-permute-done.20.even.refs_6_ = bf16[4,128,256]{2,1,0:T(8,128)(2,1)S(1)} collective-permute-done((bf16[4,128,256]{2,1,0:T(8,128)(2,1)S(1)}, bf16[4,128,256]{2,1,0:T(8,128)(2,1)S(1)}, u32[]{:S(2)}, u32[]{:S(2)}) %collective-permute-start.20) | collective-permute-done | bytes 262176 | tf_op jit(solution)/shard_map/ppermute | solution.py:31
  76.8 4.6 %shard_map.105 = (f32[16,128,256]{2,1,0:T(8,128)S(1)}, bf16[16,128,256]{2,1,0:T(8,128)(2,1)S(1)}) custom-call(s32[144]{0:T(256)S(1)} %compare_select_fusion.pairs, s32[5]{0:T(128)S(1)} %select_reduce_fusion.4.starts, bf16[4,128,256]{2,1,0:T(8,128)(2,1)S(1)} %convert_element_type.39.even.refs_0_, bf16[4,128,256]{2,1,0:T(8,128)(2,1)S(1)} %collective-permute-done.odd.refs_1_, ...), custom_call_target="tpu_custom_call" | custom-call | flops 8000000000 | bytes 1048576 | tf_op jit(solution)/shard_map/pallas_call | solution.py:219
  81.4 1.3 %copy-done.12 = f32[16,128,256]{2,1,0:T(8,128)} copy-done((f32[16,128,256]{2,1,0:T(8,128)}, f32[16,128,256]{2,1,0:T(8,128)S(1)}, u32[]{:S(2)}) %copy-start.12) | copy-done | bytes 2097176
  82.7 1.4 %collective-permute-start.15 = (bf16[4,128,256]{2,1,0:T(8,128)(2,1)S(1)}, bf16[4,128,256]{2,1,0:T(8,128)(2,1)S(1)}, u32[]{:S(2)}, u32[]{:S(2)}) collective-permute-start(bf16[4,128,256]{2,1,0:T(8,128)(2,1)S(1)} %collective-permute-done.14.even.refs_0_), channel_id=1, source_target_pairs={{0,4},{4,0},{8,12},{12,8},{16,20},{20,16},{24,28},{28,24},{1,5},{5... | collective-permute-start | bytes 786440 | tf_op jit(solution)/shard_map/ppermute | solution.py:31
  84.7 2.1 %shard_map.109 = (f32[4,128,256]{2,1,0:T(8,128)S(1)}, f32[4,128,256]{2,1,0:T(8,128)S(1)}, bf16[64,256,128]{2,1,0:T(8,128)(2,1)S(1)}) custom-call(s32[144]{0:T(256)S(1)} %compare_select_fusion.1.pairs, s32[5]{0:T(128)S(1)} %select_reduce_fusion.5.starts, bf16[224,128,128]{2,1,0:T(8,128)(2,1)S(1)} %shard_map.104.rated, ...), custom_call_target="tpu_custom_call" | custom-call | flops 3000000000 | bytes 1048576 | tf_op jit(solution)/shard_map/pallas_call | solution.py:167
  86.9 2.3 %shard_map.108 = (f32[4,128,256]{2,1,0:T(8,128)S(1)}, f32[4,128,256]{2,1,0:T(8,128)S(1)}, bf16[64,256,128]{2,1,0:T(8,128)(2,1)S(1)}) custom-call(s32[144]{0:T(256)S(1)} %compare_select_fusion.1.pairs, s32[5]{0:T(128)S(1)} %select_reduce_fusion.5.starts, bf16[224,128,128]{2,1,0:T(8,128)(2,1)S(1)} %shard_map.104.rated, ...), custom_call_target="tpu_custom_call" | custom-call | flops 3000000000 | bytes 1048576 | tf_op jit(solution)/shard_map/pallas_call | solution.py:167
  89.7 2.5 %shard_map.107 = (f32[4,128,256]{2,1,0:T(8,128)S(1)}, f32[4,128,256]{2,1,0:T(8,128)S(1)}, bf16[64,256,128]{2,1,0:T(8,128)(2,1)S(1)}) custom-call(s32[144]{0:T(256)S(1)} %compare_select_fusion.1.pairs, s32[5]{0:T(128)S(1)} %select_reduce_fusion.5.starts, bf16[224,128,128]{2,1,0:T(8,128)(2,1)S(1)} %shard_map.104.rated, ...), custom_call_target="tpu_custom_call" | custom-call | flops 3000000000 | bytes 1048576 | tf_op jit(solution)/shard_map/pallas_call | solution.py:167
  92.3 2.5 %shard_map.106 = (f32[4,128,256]{2,1,0:T(8,128)S(1)}, f32[4,128,256]{2,1,0:T(8,128)S(1)}, bf16[64,256,128]{2,1,0:T(8,128)(2,1)S(1)}) custom-call(s32[144]{0:T(256)S(1)} %compare_select_fusion.1.pairs, s32[5]{0:T(128)S(1)} %select_reduce_fusion.5.starts, bf16[224,128,128]{2,1,0:T(8,128)(2,1)S(1)} %shard_map.104.rated, ...), custom_call_target="tpu_custom_call" | custom-call | flops 3000000000 | bytes 1048576 | tf_op jit(solution)/shard_map/pallas_call | solution.py:167
  95.0 2.0 %collective-permute-start.28 = (s16[528,256]{1,0:T(8,128)(2,1)S(1)}, s16[528,256]{1,0:T(8,128)(2,1)S(1)}, u32[]{:S(2)}, u32[]{:S(2)}) collective-permute-start(s16[528,256]{1,0:T(8,128)(2,1)S(1)} %shard_map.113), channel_id=1, source_target_pairs={{0,24},{4,28},{8,16},{12,20},{16,8},{20,12},{24,0},{28,4},{1,25},{... | collective-permute-start | bytes 811016 | tf_op jit(solution)/shard_map/ppermute | solution.py:31
  97.2 5.8 %collective-permute-start.26 = (s16[528,256]{1,0:T(8,128)(2,1)S(1)}, s16[528,256]{1,0:T(8,128)(2,1)S(1)}, u32[]{:S(2)}, u32[]{:S(2)}) collective-permute-start(s16[528,256]{1,0:T(8,128)(2,1)S(1)} %shard_map.112), channel_id=1, source_target_pairs={{0,16},{4,20},{8,24},{12,28},{16,0},{20,4},{24,8},{28,12},{1,17},{... | collective-permute-start | bytes 811016 | tf_op jit(solution)/shard_map/ppermute | solution.py:31
  103.2 1.7 %collective-permute-done.28.refs_2_ = s16[528,256]{1,0:T(8,128)(2,1)S(1)} collective-permute-done((s16[528,256]{1,0:T(8,128)(2,1)S(1)}, s16[528,256]{1,0:T(8,128)(2,1)S(1)}, u32[]{:S(2)}, u32[]{:S(2)}) %collective-permute-start.28) | collective-permute-done | bytes 270368 | tf_op jit(solution)/shard_map/ppermute | solution.py:31
  105.0 7.8 %collective-permute-done.26.refs_1_ = s16[528,256]{1,0:T(8,128)(2,1)S(1)} collective-permute-done((s16[528,256]{1,0:T(8,128)(2,1)S(1)}, s16[528,256]{1,0:T(8,128)(2,1)S(1)}, u32[]{:S(2)}, u32[]{:S(2)}) %collective-permute-start.26) | collective-permute-done | bytes 270368 | tf_op jit(solution)/shard_map/ppermute | solution.py:31
  114.2 3.7 %collective-permute-start.29 = (s16[528,256]{1,0:T(8,128)(2,1)S(1)}, s16[528,256]{1,0:T(8,128)(2,1)S(1)}, u32[]{:S(2)}, u32[]{:S(2)}) collective-permute-start(s16[528,256]{1,0:T(8,128)(2,1)S(1)} %shard_map.114), channel_id=1, source_target_pairs={{0,3},{1,0},{2,1},{3,2},{4,7},{5,4},{6,5},{7,6},{8,11},{9,8},{10,9... | collective-permute-start | bytes 811016 | tf_op jit(solution)/shard_map/ppermute | solution.py:26
  117.9 7.6 %shard_map.110 = (f32[16,128,256]{2,1,0:T(8,128)}, bf16[16,128,256]{2,1,0:T(8,128)(2,1)}) custom-call(s32[144]{0:T(256)S(1)} %compare_select_fusion.1.pairs, s32[5]{0:T(128)S(1)} %select_reduce_fusion.5.starts, bf16[4,128,256]{2,1,0:T(8,128)(2,1)S(1)} %collective-permute-done.14.even.refs_0_, bf16[4,128,256]{2,1,0:T(8,128)(2,1)S(1)} %collective-permute-done.15.odd.refs_1_, ...), custom_call_target="tpu_custom_call" | custom-call | flops 8000000000 | bytes 1048576 | tf_op jit(solution)/shard_map/pallas_call | solution.py:219
  (124 shorter events, 19.7 us)
Async XLA Ops:
  1.9 22.5 %collective-permute-start.2 = (bf16[4,128,256]{2,1,0:T(8,128)(2,1)S(1)}, bf16[4,128,256]{2,1,0:T(8,128)(2,1)S(1)}, u32[]{:S(2)}, u32[]{:S(2)}) collective-permute-start(bf16[4,128,256]{2,1,0:T(8,128)(2,1)S(1)} %convert_element_type.39.even.refs_0_), channel_id=1, source_target_pairs={{0,8},{4,12},{8,0},{12,4},{16,24},{20,28},{24,16},{28,20},{1,9},{5... | collective-permute-start | bytes 786440 | tf_op jit(solution)/shard_map/ppermute | solution.py:31
  4.9 20.2 %collective-permute-start.6 = (bf16[4,128,256]{2,1,0:T(8,128)(2,1)S(1)}, bf16[4,128,256]{2,1,0:T(8,128)(2,1)S(1)}, u32[]{:S(2)}, u32[]{:S(2)}) collective-permute-start(bf16[4,128,256]{2,1,0:T(8,128)(2,1)S(1)} %convert_element_type.39.even.refs_0_), channel_id=1, source_target_pairs={{0,16},{4,20},{8,24},{12,28},{16,0},{20,4},{24,8},{28,12},{1,17},{... | collective-permute-start | bytes 786440 | tf_op jit(solution)/shard_map/ppermute | solution.py:31
  6.4 11.7 %collective-permute-start.10 = (bf16[4,128,256]{2,1,0:T(8,128)(2,1)S(1)}, bf16[4,128,256]{2,1,0:T(8,128)(2,1)S(1)}, u32[]{:S(2)}, u32[]{:S(2)}) collective-permute-start(bf16[4,128,256]{2,1,0:T(8,128)(2,1)S(1)} %convert_element_type.39.even.refs_0_), channel_id=1, source_target_pairs={{0,24},{4,28},{8,16},{12,20},{16,8},{20,12},{24,0},{28,4},{1,25},{... | collective-permute-start | bytes 786440 | tf_op jit(solution)/shard_map/ppermute | solution.py:31
  6.4 28.3 %collective-permute-start = (bf16[4,128,256]{2,1,0:T(8,128)(2,1)S(1)}, bf16[4,128,256]{2,1,0:T(8,128)(2,1)S(1)}, u32[]{:S(2)}, u32[]{:S(2)}) collective-permute-start(bf16[4,128,256]{2,1,0:T(8,128)(2,1)S(1)} %convert_element_type.39.even.refs_0_), channel_id=1, source_target_pairs={{0,4},{4,0},{8,12},{12,8},{16,20},{20,16},{24,28},{28,24},{1,5},{5... | collective-permute-start | bytes 786440 | tf_op jit(solution)/shard_map/ppermute | solution.py:31
  18.1 7.0 %collective-permute-start.11 = (bf16[4,128,256]{2,1,0:T(8,128)(2,1)S(1)}, bf16[4,128,256]{2,1,0:T(8,128)(2,1)S(1)}, u32[]{:S(2)}, u32[]{:S(2)}) collective-permute-start(bf16[4,128,256]{2,1,0:T(8,128)(2,1)S(1)} %collective-permute-done.10.even.refs_6_), channel_id=1, source_target_pairs={{0,4},{4,0},{8,12},{12,8},{16,20},{20,16},{24,28},{28,24},{1,5},{5... | collective-permute-start | bytes 786440 | tf_op jit(solution)/shard_map/ppermute | solution.py:31
  24.4 6.0 %collective-permute-start.3 = (bf16[4,128,256]{2,1,0:T(8,128)(2,1)S(1)}, bf16[4,128,256]{2,1,0:T(8,128)(2,1)S(1)}, u32[]{:S(2)}, u32[]{:S(2)}) collective-permute-start(bf16[4,128,256]{2,1,0:T(8,128)(2,1)S(1)} %collective-permute-done.2.even.refs_2_), channel_id=1, source_target_pairs={{0,4},{4,0},{8,12},{12,8},{16,20},{20,16},{24,28},{28,24},{1,5},{5... | collective-permute-start | bytes 786440 | tf_op jit(solution)/shard_map/ppermute | solution.py:31
  25.1 2.7 %collective-permute-start.7 = (bf16[4,128,256]{2,1,0:T(8,128)(2,1)S(1)}, bf16[4,128,256]{2,1,0:T(8,128)(2,1)S(1)}, u32[]{:S(2)}, u32[]{:S(2)}) collective-permute-start(bf16[4,128,256]{2,1,0:T(8,128)(2,1)S(1)} %collective-permute-done.6.even.refs_4_), channel_id=1, source_target_pairs={{0,4},{4,0},{8,12},{12,8},{16,20},{20,16},{24,28},{28,24},{1,5},{5... | collective-permute-start | bytes 786440 | tf_op jit(solution)/shard_map/ppermute | solution.py:31
  27.2 10.2 %collective-permute-start.12 = (f32[4,128,256]{2,1,0:T(8,128)S(1)}, f32[4,128,256]{2,1,0:T(8,128)S(1)}, u32[]{:S(2)}, u32[]{:S(2)}) collective-permute-start(f32[4,128,256]{2,1,0:T(8,128)S(1)} %get-tuple-element.39), channel_id=1, source_target_pairs={{0,4},{4,0},{8,12},{12,8},{16,20},{20,16},{24,28},{28,24},{1,5},{5... | collective-permute-start | bytes 1572872 | tf_op jit(solution)/shard_map/ppermute | solution.py:31
  29.5 8.8 %collective-permute-start.8 = (f32[4,128,256]{2,1,0:T(8,128)S(1)}, f32[4,128,256]{2,1,0:T(8,128)S(1)}, u32[]{:S(2)}, u32[]{:S(2)}) collective-permute-start(f32[4,128,256]{2,1,0:T(8,128)S(1)} %get-tuple-element.37), channel_id=1, source_target_pairs={{0,4},{4,0},{8,12},{12,8},{16,20},{20,16},{24,28},{28,24},{1,5},{5... | collective-permute-start | bytes 1572872 | tf_op jit(solution)/shard_map/ppermute | solution.py:31
  30.4 38.0 %slice-start = ((s8[14680064]{0:T(1024)(128)(4,1)}), s8[4194304]{0:T(1024)(128)(4,1)S(1)}, s32[]{:S(2)}) async-start(s8[14680064]{0:T(1024)(128)(4,1)} %bitcast.17), calls=%async_computation | async-start | bytes 8388608
  30.4 38.0 %slice-start.1 = ((s8[14680064]{0:T(1024)(128)(4,1)}), s8[4194304]{0:T(1024)(128)(4,1)S(1)}, s32[]{:S(2)}) async-start(s8[14680064]{0:T(1024)(128)(4,1)} %bitcast.17), calls=%async_computation.1 | async-start | bytes 8388608
  34.6 9.6 %collective-permute-start.4 = (f32[4,128,256]{2,1,0:T(8,128)S(1)}, f32[4,128,256]{2,1,0:T(8,128)S(1)}, u32[]{:S(2)}, u32[]{:S(2)}) collective-permute-start(f32[4,128,256]{2,1,0:T(8,128)S(1)} %get-tuple-element.35), channel_id=1, source_target_pairs={{0,4},{4,0},{8,12},{12,8},{16,20},{20,16},{24,28},{28,24},{1,5},{5... | collective-permute-start | bytes 1572872 | tf_op jit(solution)/shard_map/ppermute | solution.py:31
  36.5 8.2 %collective-permute-start.1 = (f32[4,128,256]{2,1,0:T(8,128)S(1)}, f32[4,128,256]{2,1,0:T(8,128)S(1)}, u32[]{:S(2)}, u32[]{:S(2)}) collective-permute-start(f32[4,128,256]{2,1,0:T(8,128)S(1)} %get-tuple-element.33), channel_id=1, source_target_pairs={{0,4},{4,0},{8,12},{12,8},{16,20},{20,16},{24,28},{28,24},{1,5},{5... | collective-permute-start | bytes 1572872 | tf_op jit(solution)/shard_map/ppermute | solution.py:31
  37.6 9.6 %collective-permute-start.13 = (s16[528,256]{1,0:T(8,128)(2,1)S(1)}, s16[528,256]{1,0:T(8,128)(2,1)S(1)}, u32[]{:S(2)}, u32[]{:S(2)}) collective-permute-start(s16[528,256]{1,0:T(8,128)(2,1)S(1)} %shard_map.102), channel_id=1, source_target_pairs={{0,24},{4,28},{8,16},{12,20},{16,8},{20,12},{24,0},{28,4},{1,25},{... | collective-permute-start | bytes 811016 | tf_op jit(solution)/shard_map/ppermute | solution.py:31
  38.4 17.0 %collective-permute-start.9 = (s16[528,256]{1,0:T(8,128)(2,1)S(1)}, s16[528,256]{1,0:T(8,128)(2,1)S(1)}, u32[]{:S(2)}, u32[]{:S(2)}) collective-permute-start(s16[528,256]{1,0:T(8,128)(2,1)S(1)} %shard_map.100), channel_id=1, source_target_pairs={{0,16},{4,20},{8,24},{12,28},{16,0},{20,4},{24,8},{28,12},{1,17},{... | collective-permute-start | bytes 811016 | tf_op jit(solution)/shard_map/ppermute | solution.py:31
  44.4 12.1 %collective-permute-start.5 = (s16[528,256]{1,0:T(8,128)(2,1)S(1)}, s16[528,256]{1,0:T(8,128)(2,1)S(1)}, u32[]{:S(2)}, u32[]{:S(2)}) collective-permute-start(s16[528,256]{1,0:T(8,128)(2,1)S(1)} %shard_map.98), channel_id=1, source_target_pairs={{0,8},{4,12},{8,0},{12,4},{16,24},{20,28},{24,16},{28,20},{1,9},{5... | collective-permute-start | bytes 811016 | tf_op jit(solution)/shard_map/ppermute | solution.py:31
  56.8 9.8 %collective-permute-start.14 = (bf16[4,128,256]{2,1,0:T(8,128)(2,1)S(1)}, bf16[4,128,256]{2,1,0:T(8,128)(2,1)S(1)}, u32[]{:S(2)}, u32[]{:S(2)}) collective-permute-start(bf16[4,128,256]{2,1,0:T(8,128)(2,1)S(1)} %get-tuple-element.40), channel_id=1, source_target_pairs={{0,1},{1,2},{2,3},{3,0},{4,5},{5,6},{6,7},{7,4},{8,9},{9,10},{10,1... | collective-permute-start | bytes 786440 | tf_op jit(solution)/shard_map/ppermute | solution.py:26
  66.6 10.1 %collective-permute-start.20 = (bf16[4,128,256]{2,1,0:T(8,128)(2,1)S(1)}, bf16[4,128,256]{2,1,0:T(8,128)(2,1)S(1)}, u32[]{:S(2)}, u32[]{:S(2)}) collective-permute-start(bf16[4,128,256]{2,1,0:T(8,128)(2,1)S(1)} %collective-permute-done.14.even.refs_0_), channel_id=1, source_target_pairs={{0,24},{4,28},{8,16},{12,20},{16,8},{20,12},{24,0},{28,4},{1,25},{... | collective-permute-start | bytes 786440 | tf_op jit(solution)/shard_map/ppermute | solution.py:31
  69.4 14.7 %collective-permute-start.18 = (bf16[4,128,256]{2,1,0:T(8,128)(2,1)S(1)}, bf16[4,128,256]{2,1,0:T(8,128)(2,1)S(1)}, u32[]{:S(2)}, u32[]{:S(2)}) collective-permute-start(bf16[4,128,256]{2,1,0:T(8,128)(2,1)S(1)} %collective-permute-done.14.even.refs_0_), channel_id=1, source_target_pairs={{0,16},{4,20},{8,24},{12,28},{16,0},{20,4},{24,8},{28,12},{1,17},{... | collective-permute-start | bytes 786440 | tf_op jit(solution)/shard_map/ppermute | solution.py:31
  71.1 13.1 %collective-permute-start.16 = (bf16[4,128,256]{2,1,0:T(8,128)(2,1)S(1)}, bf16[4,128,256]{2,1,0:T(8,128)(2,1)S(1)}, u32[]{:S(2)}, u32[]{:S(2)}) collective-permute-start(bf16[4,128,256]{2,1,0:T(8,128)(2,1)S(1)} %collective-permute-done.14.even.refs_0_), channel_id=1, source_target_pairs={{0,8},{4,12},{8,0},{12,4},{16,24},{20,28},{24,16},{28,20},{1,9},{5... | collective-permute-start | bytes 786440 | tf_op jit(solution)/shard_map/ppermute | solution.py:31
  76.8 7.9 %collective-permute-start.21 = (bf16[4,128,256]{2,1,0:T(8,128)(2,1)S(1)}, bf16[4,128,256]{2,1,0:T(8,128)(2,1)S(1)}, u32[]{:S(2)}, u32[]{:S(2)}) collective-permute-start(bf16[4,128,256]{2,1,0:T(8,128)(2,1)S(1)} %collective-permute-done.20.even.refs_6_), channel_id=1, source_target_pairs={{0,4},{4,0},{8,12},{12,8},{16,20},{20,16},{24,28},{28,24},{1,5},{5... | collective-permute-start | bytes 786440 | tf_op jit(solution)/shard_map/ppermute | solution.py:31
  82.7 9.5 %collective-permute-start.15 = (bf16[4,128,256]{2,1,0:T(8,128)(2,1)S(1)}, bf16[4,128,256]{2,1,0:T(8,128)(2,1)S(1)}, u32[]{:S(2)}, u32[]{:S(2)}) collective-permute-start(bf16[4,128,256]{2,1,0:T(8,128)(2,1)S(1)} %collective-permute-done.14.even.refs_0_), channel_id=1, source_target_pairs={{0,4},{4,0},{8,12},{12,8},{16,20},{20,16},{24,28},{28,24},{1,5},{5... | collective-permute-start | bytes 786440 | tf_op jit(solution)/shard_map/ppermute | solution.py:31
  84.2 2.7 %collective-permute-start.19 = (bf16[4,128,256]{2,1,0:T(8,128)(2,1)S(1)}, bf16[4,128,256]{2,1,0:T(8,128)(2,1)S(1)}, u32[]{:S(2)}, u32[]{:S(2)}) collective-permute-start(bf16[4,128,256]{2,1,0:T(8,128)(2,1)S(1)} %collective-permute-done.18.even.refs_4_), channel_id=1, source_target_pairs={{0,4},{4,0},{8,12},{12,8},{16,20},{20,16},{24,28},{28,24},{1,5},{5... | collective-permute-start | bytes 786440 | tf_op jit(solution)/shard_map/ppermute | solution.py:31
  84.2 5.5 %collective-permute-start.17 = (bf16[4,128,256]{2,1,0:T(8,128)(2,1)S(1)}, bf16[4,128,256]{2,1,0:T(8,128)(2,1)S(1)}, u32[]{:S(2)}, u32[]{:S(2)}) collective-permute-start(bf16[4,128,256]{2,1,0:T(8,128)(2,1)S(1)} %collective-permute-done.16.even.refs_2_), channel_id=1, source_target_pairs={{0,4},{4,0},{8,12},{12,8},{16,20},{20,16},{24,28},{28,24},{1,5},{5... | collective-permute-start | bytes 786440 | tf_op jit(solution)/shard_map/ppermute | solution.py:31
  86.8 8.1 %collective-permute-start.27 = (f32[4,128,256]{2,1,0:T(8,128)S(1)}, f32[4,128,256]{2,1,0:T(8,128)S(1)}, u32[]{:S(2)}, u32[]{:S(2)}) collective-permute-start(f32[4,128,256]{2,1,0:T(8,128)S(1)} %get-tuple-element.59), channel_id=1, source_target_pairs={{0,4},{4,0},{8,12},{12,8},{16,20},{20,16},{24,28},{28,24},{1,5},{5... | collective-permute-start | bytes 1572872 | tf_op jit(solution)/shard_map/ppermute | solution.py:31
  89.1 7.9 %collective-permute-start.25 = (f32[4,128,256]{2,1,0:T(8,128)S(1)}, f32[4,128,256]{2,1,0:T(8,128)S(1)}, u32[]{:S(2)}, u32[]{:S(2)}) collective-permute-start(f32[4,128,256]{2,1,0:T(8,128)S(1)} %get-tuple-element.57), channel_id=1, source_target_pairs={{0,4},{4,0},{8,12},{12,8},{16,20},{20,16},{24,28},{28,24},{1,5},{5... | collective-permute-start | bytes 1572872 | tf_op jit(solution)/shard_map/ppermute | solution.py:31
  92.2 10.8 %collective-permute-start.23 = (f32[4,128,256]{2,1,0:T(8,128)S(1)}, f32[4,128,256]{2,1,0:T(8,128)S(1)}, u32[]{:S(2)}, u32[]{:S(2)}) collective-permute-start(f32[4,128,256]{2,1,0:T(8,128)S(1)} %get-tuple-element.55), channel_id=1, source_target_pairs={{0,4},{4,0},{8,12},{12,8},{16,20},{20,16},{24,28},{28,24},{1,5},{5... | collective-permute-start | bytes 1572872 | tf_op jit(solution)/shard_map/ppermute | solution.py:31
  94.8 8.4 %collective-permute-start.22 = (f32[4,128,256]{2,1,0:T(8,128)S(1)}, f32[4,128,256]{2,1,0:T(8,128)S(1)}, u32[]{:S(2)}, u32[]{:S(2)}) collective-permute-start(f32[4,128,256]{2,1,0:T(8,128)S(1)} %get-tuple-element.53), channel_id=1, source_target_pairs={{0,4},{4,0},{8,12},{12,8},{16,20},{20,16},{24,28},{28,24},{1,5},{5... | collective-permute-start | bytes 1572872 | tf_op jit(solution)/shard_map/ppermute | solution.py:31
  95.0 9.9 %collective-permute-start.28 = (s16[528,256]{1,0:T(8,128)(2,1)S(1)}, s16[528,256]{1,0:T(8,128)(2,1)S(1)}, u32[]{:S(2)}, u32[]{:S(2)}) collective-permute-start(s16[528,256]{1,0:T(8,128)(2,1)S(1)} %shard_map.113), channel_id=1, source_target_pairs={{0,24},{4,28},{8,16},{12,20},{16,8},{20,12},{24,0},{28,4},{1,25},{... | collective-permute-start | bytes 811016 | tf_op jit(solution)/shard_map/ppermute | solution.py:31
  97.2 15.6 %collective-permute-start.26 = (s16[528,256]{1,0:T(8,128)(2,1)S(1)}, s16[528,256]{1,0:T(8,128)(2,1)S(1)}, u32[]{:S(2)}, u32[]{:S(2)}) collective-permute-start(s16[528,256]{1,0:T(8,128)(2,1)S(1)} %shard_map.112), channel_id=1, source_target_pairs={{0,16},{4,20},{8,24},{12,28},{16,0},{20,4},{24,8},{28,12},{1,17},{... | collective-permute-start | bytes 811016 | tf_op jit(solution)/shard_map/ppermute | solution.py:31
  103.1 10.7 %collective-permute-start.24 = (s16[528,256]{1,0:T(8,128)(2,1)S(1)}, s16[528,256]{1,0:T(8,128)(2,1)S(1)}, u32[]{:S(2)}, u32[]{:S(2)}) collective-permute-start(s16[528,256]{1,0:T(8,128)(2,1)S(1)} %shard_map.111), channel_id=1, source_target_pairs={{0,8},{4,12},{8,0},{12,4},{16,24},{20,28},{24,16},{28,20},{1,9},{5... | collective-permute-start | bytes 811016 | tf_op jit(solution)/shard_map/ppermute | solution.py:31
  114.2 11.3 %collective-permute-start.29 = (s16[528,256]{1,0:T(8,128)(2,1)S(1)}, s16[528,256]{1,0:T(8,128)(2,1)S(1)}, u32[]{:S(2)}, u32[]{:S(2)}) collective-permute-start(s16[528,256]{1,0:T(8,128)(2,1)S(1)} %shard_map.114), channel_id=1, source_target_pairs={{0,3},{1,0},{2,1},{3,2},{4,7},{5,4},{6,5},{7,6},{8,11},{9,8},{10,9... | collective-permute-start | bytes 811016 | tf_op jit(solution)/shard_map/ppermute | solution.py:26
  (17 other events, 230.3 us)

commit v3 on v2

--- a/solution.py
+++ b/solution.py
@@ -17,6 +17,7 @@
 SCALE_STEPS = 128.0
 
 ANY = pl.BlockSpec(memory_space=pl.ANY)
+IN_HBM = pl.BlockSpec(memory_space=pltpu.HBM)
 IN_VMEM = pl.BlockSpec(memory_space=pltpu.VMEM)
 IN_SMEM = pl.BlockSpec(memory_space=pltpu.SMEM)
 
@@ -37,36 +38,68 @@
     return bits
 
 
-def pair_plan(rows, cols, count, me, user_tiles, item_tiles, per, span):
-    slots = rows.shape[0]
-    slot_bits, row_bits, col_bits = widths(slots, user_tiles, item_tiles)
-    place = ((cols // per) ^ me) * per + cols % per
-    n = jnp.arange(slots, dtype=jnp.int32)
-    live = n < count
-    same = (place[:, None] == place[None, :]) & live[None, :]
-    rank = jnp.sum(same & (rows[None, :] < rows[:, None]), axis=1, dtype=jnp.int32)
-    opens = live & (rank % 2 == 0)
-    run = place // span
-    runs = item_tiles // span
-    run_ids = jnp.arange(runs, dtype=jnp.int32)
-    ahead = (place[None, :] < place[:, None]) & (run[None, :] == run[:, None]) & opens[None, :]
-    within = jnp.sum(ahead, axis=1, dtype=jnp.int32)
-    size = jnp.sum((run[None, :] == run_ids[:, None]) & opens[None, :], axis=1, dtype=jnp.int32)
-    size = (size + GROUP - 1) // GROUP * GROUP
-    edges = jnp.arange(runs + 1, dtype=jnp.int32)
-    starts = jnp.sum(jnp.where(run_ids[None, :] < edges[:, None], size[None, :], 0), axis=1, dtype=jnp.int32)
-    base = jnp.sum(jnp.where(run_ids[None, :] < run[:, None], size[None, :], 0), axis=1, dtype=jnp.int32)
-    where = base + within + rank // 2
+def total(x, axis):
+    return jnp.sum(x.astype(jnp.float32), axis=axis, keepdims=True).astype(jnp.int32)
+
+
+def plan_kernel(section, bits, per, span, runs, me, counts, lists, pairs, starts):
+    slot_bits, row_bits, col_bits = bits
+    side = lists.shape[-1]
+    shape = (side, side)
+    count = counts[section]
+    along = lax.broadcasted_iota(jnp.int32, shape, 1)
+    down = lax.broadcasted_iota(jnp.int32, shape, 0)
+    row_along = jnp.broadcast_to(lists[section, 0:1], shape)
+    place_along = jnp.broadcast_to(lists[section, 1:2] ^ (me[0] * per), shape)
+    key = (place_along << row_bits | row_along).astype(jnp.float32).T.astype(jnp.int32)
+    row_down = key & ((1 << row_bits) - 1)
+    place_down = key >> row_bits
+    span_bits = span.bit_length() - 1
+    run_along, run_down = place_along >> span_bits, place_down >> span_bits
+    live_along, live_down = along < count, down < count
+    same = place_along == place_down
+    rank_down = total(same & live_along & (row_along < row_down), 1)
+    rank_along = total(same & live_down & (row_down < row_along), 0)
+    opens = live_along & ((rank_along & 1) == 0)
+    within = total(opens & (run_along == run_down) & (place_along < place_down), 1)
+    base = jnp.zeros((side, 1), jnp.int32)
+    begins = jnp.zeros((1, side), jnp.int32)
+    unused = jnp.zeros((1, side), jnp.int32)
+    ahead = jnp.zeros((1, 1), jnp.int32)
+    for run in range(runs):
+        size = total(opens[0:1] & (run_along[0:1] == run), 1)
+        size = (size + GROUP - 1) & ~(GROUP - 1)
+        base += jnp.where(run_down[:, 0:1] > run, size, 0)
+        begins += jnp.where(along[0:1] > run, size, 0)
+        ahead += size
+        unused += jnp.where(along[0:1] >= ahead, span, 0)
+    where = base + within + (rank_down >> 1)
     col_at = 2 * slot_bits + 2 * row_bits
-    one = 1 << (col_at + col_bits)
-    first = n | (rows << (2 * slot_bits)) | (place << col_at)
-    second = (n << slot_bits) | (rows << (2 * slot_bits + row_bits))
-    word = jnp.where(live, jnp.where(rank % 2 == 0, first, second) + one, 0)
-    words = jnp.arange((slots + item_tiles) // 2 + runs * GROUP, dtype=jnp.int32)[:, None]
-    pairs = jnp.sum(jnp.where(where[None, :] == words, word[None, :], 0), axis=1, dtype=jnp.int32)
-    unused = jnp.sum(words >= starts[None, 1:], axis=1, dtype=jnp.int32) * span
-    unused = jnp.minimum(unused, item_tiles - 1) << col_at
-    return jnp.where(pairs == 0, unused, pairs), starts
+    odd = rank_down & 1
+    n, row, place = down[:, 0:1], row_down[:, 0:1], place_down[:, 0:1]
+    word = jnp.where(odd == 0, n, n << slot_bits)
+    word += jnp.where(odd == 0, row, row << row_bits) << (2 * slot_bits)
+    word += (jnp.where(odd == 0, place, 0) << col_at) + (1 << (col_at + col_bits))
+    word = jnp.broadcast_to(word, shape)
+    hit = (where == along) & live_down
+    low = total(jnp.where(hit, word & 0xFFFF, 0), 0)
+    high = total(jnp.where(hit, word >> 16, 0), 0)
+    listed = (high << 16) | low
+    unused = jnp.minimum(unused, span * runs - 1) << col_at
+    pairs[...] = jnp.where(listed == 0, unused, listed)
+    starts[...] = begins
+
+
+def pair_plan(section, bits, per, span, runs, me, counts, lists):
+    side = lists.shape[-1]
+    return pl.pallas_call(
+        functools.partial(plan_kernel, section, bits, per, span, runs),
+        out_shape=[jax.ShapeDtypeStruct((1, side), jnp.int32)] * 2,
+        in_specs=[IN_SMEM, IN_SMEM, IN_VMEM],
+        out_specs=[IN_VMEM] * 2,
+        compiler_params=pltpu.CompilerParams(vmem_limit_bytes=SMALL_LIMIT),
+        cost_estimate=pl.CostEstimate(flops=10**9, bytes_accessed=2**12, transcendentals=0),
+    )(me, counts, lists)
 
 
 def decode_word(word, bits, first_col):
@@ -96,7 +129,7 @@
     return pl.pallas_call(
         functools.partial(fetch_kernel, section, lump),
         out_shape=jax.ShapeDtypeStruct(ratings.shape[1:], ratings.dtype),
-        in_specs=[IN_SMEM, ANY],
+        in_specs=[IN_SMEM, IN_HBM],
         out_specs=IN_VMEM,
         scratch_shapes=[pltpu.SemaphoreType.DMA((slots // lump,))],
         compiler_params=pltpu.CompilerParams(vmem_limit_bytes=SMALL_LIMIT),
@@ -104,10 +137,11 @@
     )(counts, ratings)
 
 
-def items_kernel(run, span, bits, pairs, starts, rated, users, even, odd, out_even, out_odd, misfits, items, grad):
+def items_kernel(run, span, bits, pairs, starts, rated, users, even, odd, *refs):
+    out_even, out_odd, misfits, items, grad = refs[-5:]
     per = even.shape[0]
     tile = users.shape[1]
-    low, high = starts[run], starts[run + 1]
+    low, high = starts[0, run], starts[0, run + 1]
     steps = lax.div(high - low, GROUP)
     for t in range(per):
         items[t] = even[t]
@@ -115,7 +149,7 @@
     grad[...] = jnp.zeros_like(grad)
 
     def decode(p):
-        return decode_word(pairs[p], bits, run * span)
+        return decode_word(pairs[0, p], bits, run * span)
 
     def users_of(row_a, row_b):
         return jnp.concatenate([users[row_a], users[row_b]], axis=0)
@@ -159,7 +193,7 @@
         out_odd[t] = grad[per + t]
 
 
-def item_grads(run, span, bits, plan, rated, users, even, odd):
+def item_grads(run, span, bits, plan, rated, users, even, odd, after):
     per, tile, width = even.shape
     held = span * ((users.shape[0] + 1) // 2)
     held = (min(held, (rated.shape[0] + span) // 2) + GROUP - 1) // GROUP * GROUP
@@ -168,37 +202,45 @@
         functools.partial(items_kernel, run, span, bits),
         out_shape=[jax.ShapeDtypeStruct((per, tile, width), f32)] * 2
         + [jax.ShapeDtypeStruct((held, 2 * tile, tile), jnp.bfloat16)],
-        in_specs=[IN_SMEM, IN_SMEM] + [IN_VMEM] * 4,
+        in_specs=[IN_SMEM, IN_SMEM] + [IN_VMEM] * 4 + [ANY] * len(after),
         out_specs=[IN_VMEM] * 3,
         scratch_shapes=[pltpu.VMEM((span, tile, width), jnp.bfloat16), pltpu.VMEM((span, tile, width), f32)],
         compiler_params=pltpu.CompilerParams(vmem_limit_bytes=SMALL_LIMIT),
         cost_estimate=pl.CostEstimate(flops=3 * 10**9, bytes_accessed=2**20, transcendentals=0),
-    )(*plan, rated, users, even, odd)
-
-
-def users_kernel(power, span, bits, runs, pairs, starts, *refs):
-    pieces = refs[: 2 * runs]
-    misfits = refs[2 * runs : 3 * runs]
-    factors, noise, new, new_bf, items, grad = refs[3 * runs :]
-    per = pieces[0].shape[0]
-    tile = factors.shape[1]
+    )(*plan, rated, users, even, odd, *after)
+
+
+def add_user_grads(bits, first_run, pairs, starts, pieces, misfits, items, grad):
+    per, tile = pieces[0].shape[:2]
+    first_col = 2 * per * first_run
     for i, piece in enumerate(pieces):
         for t in range(per):
             items[i * per + t] = piece[t]
-    grad[...] = jnp.zeros_like(grad)
-    for run in range(runs):
-        low = starts[run]
-
-        def advance(step, carry, low=low, held=misfits[run]):
+    for k, held in enumerate(misfits):
+        low = starts[0, first_run + k]
+
+        def advance(step, carry, low=low, held=held):
             for j in range(GROUP):
                 i = step * GROUP + j
-                _, _, row_a, row_b, col, _ = decode_word(pairs[low + i], bits, 0)
+                _, _, row_a, row_b, col, _ = decode_word(pairs[0, low + i], bits, first_col)
                 part = jnp.dot(held[i], items[col], preferred_element_type=jnp.float32)
                 grad[row_a] += part[:tile]
                 grad[row_b] += part[tile:]
             return carry
 
-        lax.fori_loop(0, lax.div(starts[run + 1] - low, GROUP), advance, 0)
+        lax.fori_loop(0, lax.div(starts[0, first_run + k + 1] - low, GROUP), advance, 0)
+
+
+def users_head_kernel(bits, runs, pairs, starts, *refs):
+    grad, items = refs[-2:]
+    grad[...] = jnp.zeros_like(grad)
+    add_user_grads(bits, 0, pairs, starts, refs[: 2 * runs], refs[2 * runs : 3 * runs], items, grad)
+
+
+def users_tail_kernel(power, bits, first_run, runs, pairs, starts, *refs):
+    factors, noise, partial, new, new_bf, items, grad = refs[3 * runs :]
+    grad[...] = partial[...]
+    add_user_grads(bits, first_run, pairs, starts, refs[: 2 * runs], refs[2 * runs : 3 * runs], items, grad)
 
     def finish(t, carry):
         before = factors[t]
@@ -212,19 +254,34 @@
     lax.fori_loop(0, factors.shape[0], finish, 0)
 
 
-def user_step(power, span, bits, plan, pieces, misfits, factors, noise):
+def users_head(bits, plan, pieces, misfits, shape):
+    per, tile, width = pieces[0].shape
+    return pl.pallas_call(
+        functools.partial(users_head_kernel, bits, len(misfits)),
+        out_shape=jax.ShapeDtypeStruct(shape, jnp.float32),
+        in_specs=[IN_SMEM, IN_SMEM] + [IN_VMEM] * (len(pieces) + len(misfits)),
+        out_specs=IN_VMEM,
+        scratch_shapes=[pltpu.VMEM((len(pieces) * per, tile, width), jnp.bfloat16)],
+        compiler_params=pltpu.CompilerParams(vmem_limit_bytes=SMALL_LIMIT),
+        cost_estimate=pl.CostEstimate(flops=6 * 10**9, bytes_accessed=2**20, transcendentals=0),
+    )(*plan, *pieces, *misfits)
+
+
+def users_tail(power, bits, first_run, plan, pieces, misfits, factors, noise, partial):
     shape = factors.shape
     per, tile, width = pieces[0].shape
-    f32 = jnp.float32
-    return pl.pallas_call(
-        functools.partial(users_kernel, power, span, bits, len(misfits)),
-        out_shape=[jax.ShapeDtypeStruct(shape, f32), jax.ShapeDtypeStruct(shape, jnp.bfloat16)],
-        in_specs=[IN_SMEM, IN_SMEM] + [IN_VMEM] * (len(pieces) + len(misfits) + 2),
+    return pl.pallas_call(
+        functools.partial(users_tail_kernel, power, bits, first_run, len(misfits)),
+        out_shape=[jax.ShapeDtypeStruct(shape, jnp.float32), jax.ShapeDtypeStruct(shape, jnp.bfloat16)],
+        in_specs=[IN_SMEM, IN_SMEM] + [IN_VMEM] * (len(pieces) + len(misfits) + 3),
         out_specs=[IN_VMEM] * 2,
-        scratch_shapes=[pltpu.VMEM((len(pieces) * per, tile, width), jnp.bfloat16), pltpu.VMEM(shape, f32)],
-        compiler_params=pltpu.CompilerParams(vmem_limit_bytes=SMALL_LIMIT),
-        cost_estimate=pl.CostEstimate(flops=8 * 10**9, bytes_accessed=2**20, transcendentals=0),
-    )(*plan, *pieces, *misfits, factors, noise)
+        scratch_shapes=[
+            pltpu.VMEM((len(pieces) * per, tile, width), jnp.bfloat16),
+            pltpu.VMEM(shape, jnp.float32),
+        ],
+        compiler_params=pltpu.CompilerParams(vmem_limit_bytes=SMALL_LIMIT),
+        cost_estimate=pl.CostEstimate(flops=5 * 10**9, bytes_accessed=2**20, transcendentals=0),
+    )(*plan, *pieces, *misfits, factors, noise, partial)
 
 
 def coded_shape(per, tile, width):
@@ -251,18 +308,19 @@
     return ref[pl.ds(t * tile, tile)].astype(jnp.int32).astype(jnp.float32) * unit
 
 
-def join_kernel(mine, other, out):
+def join_kernel(mine, other, *refs):
+    out = refs[-1]
     encode([mine[t] + other[t] for t in range(mine.shape[0])], out)
 
 
-def join(mine, other):
+def join(mine, other, after):
     return pl.pallas_call(
         join_kernel,
         out_shape=coded_shape(*mine.shape),
-        in_specs=[IN_VMEM] * 2,
+        in_specs=[IN_VMEM] * 2 + [ANY] * len(after),
         out_specs=IN_VMEM,
         compiler_params=pltpu.CompilerParams(vmem_limit_bytes=SMALL_LIMIT),
-    )(mine, other)
+    )(mine, other, *after)
 
 
 def owner_sum(mine, other, coded, t):
@@ -274,7 +332,7 @@
 
 
 def update_kernel(power, mine, other, *refs):
-    *coded, factors, noise, new, new_bf = refs
+    *coded, factors, noise, _, new, new_bf = refs
     for t in range(mine.shape[0]):
         step = HALF_STEP * power * owner_sum(mine, other, coded, t) + ROOT_STEP * noise[t].astype(jnp.float32)
         after = factors[t] - HALF_STEP * PRIOR * factors[t] + step
@@ -283,7 +341,7 @@
 
 
 def delta_kernel(power, mine, other, *refs):
-    *coded, noise, out = refs
+    *coded, noise, _, out = refs
     steps = []
     for t in range(mine.shape[0]):
         steps.append(HALF_STEP * power * owner_sum(mine, other, coded, t) + ROOT_STEP * noise[t].astype(jnp.float32))
@@ -298,14 +356,14 @@
         new_bf[t] = after.astype(jnp.bfloat16)
 
 
-def in_vmem(kernel, out_shape, *operands):
+def in_vmem(kernel, out_shape, *operands, after=()):
     return pl.pallas_call(
         kernel,
         out_shape=out_shape,
-        in_specs=[IN_VMEM] * len(operands),
+        in_specs=[IN_VMEM] * len(operands) + [ANY] * len(after),
         out_specs=jax.tree.map(lambda _: IN_VMEM, out_shape),
         compiler_params=pltpu.CompilerParams(vmem_limit_bytes=SMALL_LIMIT),
-    )(*operands)
+    )(*operands, *after)
 
 
 def body(u_factors, v_factors, ratings, tile_rows, tile_cols, tile_counts, u_noise, v_noise):
@@ -314,7 +372,7 @@
     width = u_factors.shape[1]
     peers = lax.axis_size("user")
     power = float(lax.axis_size("item"))
-    me = lax.axis_index("user")
+    me = lax.axis_index("user").astype(jnp.int32).reshape(1)
     users = u_factors.reshape(-1, tile, width)
     items = v_factors.reshape(-1, tile, width)
     per = items.shape[0]
@@ -325,6 +383,10 @@
     counts = tile_counts.reshape(sections)
     u_noise = u_noise.reshape(sections, *users.shape)
     v_noise = v_noise.reshape(sections, *items.shape)
+    side = -(-ratings.shape[1] // 128) * 128
+    lists = jnp.stack([tile_rows[0, 0], tile_cols[0, 0]], axis=1)
+    lists = jnp.pad(lists, ((0, 0), (0, 0), (0, side - ratings.shape[1])))
+    assert (ratings.shape[1] + item_tiles) // 2 + runs * GROUP <= side and span & (span - 1) == 0
     bits = widths(ratings.shape[1], users.shape[0], item_tiles)
     pair = (
         jax.ShapeDtypeStruct(items.shape, jnp.float32),
@@ -336,27 +398,35 @@
         sent = shifted(items_bf, "item", section) if section else items_bf
         evens = [sent] + [swapped(sent, "user", 2 * d) for d in range(1, runs)]
         odds = [swapped(even, "user", 1) for even in evens]
-        plan = pair_plan(
-            tile_rows[0, 0, section],
-            tile_cols[0, 0, section],
-            counts[section],
-            me,
-            users.shape[0],
-            item_tiles,
-            per,
-            span,
-        )
+        plan = pair_plan(section, bits, per, span, runs, me, counts, lists)
         rated = fetch(section, counts, ratings)
-        mine, other, misfits = [], [], []
+        mine, other, misfits, coded = [], [], [], []
+        after = ()
         for run in range(runs):
-            even_grad, odd_grad, held = item_grads(run, span, bits, plan, rated, users_bf, evens[run], odds[run])
+            even_grad, odd_grad, held = item_grads(
+                run, span, bits, plan, rated, users_bf, evens[run], odds[run], after
+            )
             mine.append(even_grad)
             other.append(swapped(odd_grad, "user", 1))
             misfits.append(held)
-        coded = [swapped(join(mine[d], other[d]), "user", 2 * d) for d in range(1, runs)]
+            after = (even_grad,)
+            if run >= 2:
+                coded.append(join(mine[run - 1], other[run - 1], after))
+                after = (coded[-1],)
+        coded.append(join(mine[-1], other[-1], after))
+        coded = [swapped(c, "user", 2 * d) for d, c in enumerate(coded, 1)]
+        pieces = [piece for both in zip(evens, odds) for piece in both]
+        partial = users_head(bits, plan, pieces[:-2], misfits[:-1], users.shape)
         if section == 0:
             items, items_bf = in_vmem(
-                functools.partial(update_kernel, power), pair, mine[0], other[0], *coded, items, v_noise[section]
+                functools.partial(update_kernel, power),
+                pair,
+                mine[0],
+                other[0],
+                *coded,
+                items,
+                v_noise[section],
+                after=(partial,),
             )
         else:
             delta = in_vmem(
@@ -366,10 +436,12 @@
                 other[0],
                 *coded,
                 v_noise[section],
+                after=(partial,),
             )
             items, items_bf = in_vmem(arrive_kernel, pair, shifted(delta, "item", -section), items)
-        pieces = [piece for both in zip(evens, odds) for piece in both]
-        users, users_bf = user_step(power, span, bits, plan, pieces, misfits, users, u_noise[section])
+        users, users_bf = users_tail(
+            power, bits, runs - 1, plan, pieces[-2:], misfits[-1:], users, u_noise[section], partial
+        )
     return (users.reshape(u_factors.shape), items.reshape(v_factors.shape))
 
 

time: 129 us -> 113 us (0.88); the launches traced: 126 us -> 113 us
  other arithmetic: 7.21 us -> 2.79 us
  waiting for transfers between devices: 39.2 us -> 34.8 us
  local copies, waits for them, and re-layouts: 13.4 us -> 9.61 us
  starting transfers between devices: 32.1 us -> 30.2 us
  Pallas kernels: 33.4 us -> 34.7 us
    ppermute x28, waiting for transfers between devices: 30.3 us -> 24.2 us  [swapped(): return lax.ppermute(x, axis, [(i, i ^ mask) for i in range(peers)])]
    ppermute x28, starting transfers between devices: 28.3 us -> 24.5 us  [swapped(): return lax.ppermute(x, axis, [(i, i ^ mask) for i in range(peers)])]
    slice x5 -> x0, local copies, waits for them, and re-layouts: 2.98 us -> none  [the longest x1 1.31 us: body(): counts[section]]
    pallas_call x2 -> x6, Pallas kernels: 12.2 us -> 14.7 us  [the longest x2 6.58 us: users_head(): pl.pallas_call(functools.partial(users_head_kernel, bits, len(misfits)),...]
    ppermute x2, starting transfers between devices: 3.77 us -> 5.7 us  [shifted(): return lax.ppermute(x, axis, [(i, (i + by) % peers) for i in range(peers)])]
    reduce_sum x14 -> x0, other arithmetic: 1.84 us -> none  [the longest x2 0.43 us: pair_plan(): within = jnp.sum(ahead, axis=1, dtype=jnp.int32)]
    ppermute x2, waiting for transfers between devices: 8.93 us -> 10.6 us  [shifted(): return lax.ppermute(x, axis, [(i, (i + by) % peers) for i in range(peers)])]
    convert_element_type x1, other arithmetic: 0.13 us -> 1.71 us  [body(): users_bf = users.astype(jnp.bfloat16)]
  transfers between devices with their start and end apart: 30 -> 30, of which waited for: 9 -> 7; matrix products, arithmetic and copies ran while one was open for 8% -> 3% of each run, Pallas kernels for 25% -> 29%
where the time goes in v3:
time: 113 us
  waiting for transfers between devices  34.8 us (31%)
  Pallas kernels  34.7 us (31%)
  starting transfers between devices  30.2 us (27%)
  local copies, waits for them, and re-layouts  9.61 us (9%)
  other arithmetic  2.79 us (2%)
    ppermute x28, starting transfers between devices, swapped(): return lax.ppermute(x, axis, [(i, i ^ mask) for i in range(peers)])  24.5 us
    ppermute x28, waiting for transfers between devices, swapped(): return lax.ppermute(x, axis, [(i, i ^ mask) for i in range(peers)])  24.2 us
    pallas_call x8, Pallas kernels, item_grads(): pl.pallas_call(functools.partial(items_kernel, run, span, bits), out_shap...  15.7 us
    ppermute x2, waiting for transfers between devices, shifted(): return lax.ppermute(x, axis, [(i, (i + by) % peers) for i in range(peers)])  10.6 us
    unnamed x30, local copies, waits for them, and re-layouts  8.06 us
    pallas_call x2, Pallas kernels, users_head(): pl.pallas_call(functools.partial(users_head_kernel, bits, len(misfits)),...  6.58 us
    pallas_call x2, Pallas kernels, users_tail(): pl.pallas_call(functools.partial(users_tail_kernel, power, bits, first_ru...  6.06 us
    ppermute x2, starting transfers between devices, shifted(): return lax.ppermute(x, axis, [(i, (i + by) % peers) for i in range(peers)])  5.7 us
  transfers between devices with their start and end apart: 30, of which 7 were waited for; matrix products, arithmetic and copies ran while one was open for 3% of the time, Pallas kernels for 29%

profile of v3, /device:TPU:0, one launch (start us, length us, event | category | flops | bytes accessed | tf_op | source)
XLA Modules:
  0.0 113.2 jit_solution(7916664260731411595)
XLA Ops:
  1.7 3.0 %collective-permute-start.2 = (bf16[4,128,256]{2,1,0:T(8,128)(2,1)S(1)}, bf16[4,128,256]{2,1,0:T(8,128)(2,1)S(1)}, u32[]{:S(2)}, u32[]{:S(2)}) collective-permute-start(bf16[4,128,256]{2,1,0:T(8,128)(2,1)S(1)} %convert_element_type.7.even.refs_0_), channel_id=1, source_target_pairs={{0,8},{4,12},{8,0},{12,4},{16,24},{20,28},{24,16},{28,20},{1,9},{5... | collective-permute-start | bytes 786440 | tf_op jit(solution)/shard_map/ppermute | solution.py:32
  4.7 1.5 %collective-permute-start.5 = (bf16[4,128,256]{2,1,0:T(8,128)(2,1)S(1)}, bf16[4,128,256]{2,1,0:T(8,128)(2,1)S(1)}, u32[]{:S(2)}, u32[]{:S(2)}) collective-permute-start(bf16[4,128,256]{2,1,0:T(8,128)(2,1)S(1)} %convert_element_type.7.even.refs_0_), channel_id=1, source_target_pairs={{0,16},{4,20},{8,24},{12,28},{16,0},{20,4},{24,8},{28,12},{1,17},{... | collective-permute-start | bytes 786440 | tf_op jit(solution)/shard_map/ppermute | solution.py:32
  7.6 1.7 %convert_element_type.6.users = bf16[16,128,256]{2,1,0:T(8,128)(2,1)S(1)} convert(f32[16,128,256]{2,1,0:T(8,128)} %bitcast.17) | non-fusion elementwise | flops 524288 | bytes 3145728 | tf_op jit(solution)/shard_map/convert_element_type | solution.py:396
  9.4 5.2 %copy-done = bf16[1,1,2,224,128,128]{5,4,3,2,1,0:T(8,128)(2,1)S(1)} copy-done((bf16[1,1,2,224,128,128]{5,4,3,2,1,0:T(8,128)(2,1)S(1)}, bf16[1,1,2,224,128,128]{5,4,3,2,1,0:T(8,128)(2,1)}, u32[]{:S(2)}) %copy-start) | copy-done | bytes 14680088
  18.1 2.1 %shard_map.98 = (f32[4,128,256]{2,1,0:T(8,128)S(1)}, f32[4,128,256]{2,1,0:T(8,128)S(1)}, bf16[64,256,128]{2,1,0:T(8,128)(2,1)S(1)}) custom-call(s32[1,256]{1,0:T(1,128)S(1)} %get-tuple-element.38.pairs, s32[1,256]{1,0:T(1,128)S(1)} %get-tuple-element.39.starts, bf16[224,128,128]{2,1,0:T(8,128)(2,1)S(1)} %shard_map.97.rated, ...), custom_call_target="tpu_custom_call" | custom-call | flops 3000000000 | bytes 1048576 | tf_op jit(solution)/shard_map/pallas_call | solution.py:201
  20.2 2.1 %shard_map.99 = (f32[4,128,256]{2,1,0:T(8,128)S(1)}, f32[4,128,256]{2,1,0:T(8,128)S(1)}, bf16[64,256,128]{2,1,0:T(8,128)(2,1)S(1)}) custom-call(s32[1,256]{1,0:T(1,128)S(1)} %get-tuple-element.38.pairs, s32[1,256]{1,0:T(1,128)S(1)} %get-tuple-element.39.starts, bf16[224,128,128]{2,1,0:T(8,128)(2,1)S(1)} %shard_map.97.rated, ...), custom_call_target="tpu_custom_call" | custom-call | flops 3000000000 | bytes 1048576 | tf_op jit(solution)/shard_map/pallas_call | solution.py:201
  22.3 2.1 %collective-permute-start.4 = (f32[4,128,256]{2,1,0:T(8,128)S(1)}, f32[4,128,256]{2,1,0:T(8,128)S(1)}, u32[]{:S(2)}, u32[]{:S(2)}) collective-permute-start(f32[4,128,256]{2,1,0:T(8,128)S(1)} %get-tuple-element.43), channel_id=1, source_target_pairs={{0,4},{4,0},{8,12},{12,8},{16,20},{20,16},{24,28},{28,24},{1,5},{5... | collective-permute-start | bytes 1572872 | tf_op jit(solution)/shard_map/ppermute | solution.py:32
  24.5 2.5 %shard_map.100 = (f32[4,128,256]{2,1,0:T(8,128)S(1)}, f32[4,128,256]{2,1,0:T(8,128)S(1)}, bf16[64,256,128]{2,1,0:T(8,128)(2,1)S(1)}) custom-call(s32[1,256]{1,0:T(1,128)S(1)} %get-tuple-element.38.pairs, s32[1,256]{1,0:T(1,128)S(1)} %get-tuple-element.39.starts, bf16[224,128,128]{2,1,0:T(8,128)(2,1)S(1)} %shard_map.97.rated, ...), custom_call_target="tpu_custom_call" | custom-call | flops 3000000000 | bytes 1048576 | tf_op jit(solution)/shard_map/pallas_call | solution.py:201
  28.1 2.1 %shard_map.102 = (f32[4,128,256]{2,1,0:T(8,128)S(1)}, f32[4,128,256]{2,1,0:T(8,128)S(1)}, bf16[64,256,128]{2,1,0:T(8,128)(2,1)S(1)}) custom-call(s32[1,256]{1,0:T(1,128)S(1)} %get-tuple-element.38.pairs, s32[1,256]{1,0:T(1,128)S(1)} %get-tuple-element.39.starts, bf16[224,128,128]{2,1,0:T(8,128)(2,1)S(1)} %shard_map.97.rated, ...), custom_call_target="tpu_custom_call" | custom-call | flops 3000000000 | bytes 1048576 | tf_op jit(solution)/shard_map/pallas_call | solution.py:201
  31.4 1.8 %collective-permute-start.11 = (s16[528,256]{1,0:T(8,128)(2,1)S(1)}, s16[528,256]{1,0:T(8,128)(2,1)S(1)}, u32[]{:S(2)}, u32[]{:S(2)}) collective-permute-start(s16[528,256]{1,0:T(8,128)(2,1)S(1)} %shard_map.103.refs_0_), channel_id=1, source_target_pairs={{0,16},{4,20},{8,24},{12,28},{16,0},{20,4},{24,8},{28,12},{1,17},{... | collective-permute-start | bytes 811016 | tf_op jit(solution)/shard_map/ppermute | solution.py:32
  33.4 1.8 %collective-permute-start.13 = (s16[528,256]{1,0:T(8,128)(2,1)S(1)}, s16[528,256]{1,0:T(8,128)(2,1)S(1)}, u32[]{:S(2)}, u32[]{:S(2)}) collective-permute-start(s16[528,256]{1,0:T(8,128)(2,1)S(1)} %shard_map.104), channel_id=1, source_target_pairs={{0,24},{4,28},{8,16},{12,20},{16,8},{20,12},{24,0},{28,4},{1,25},{... | collective-permute-start | bytes 811016 | tf_op jit(solution)/shard_map/ppermute | solution.py:32
  35.2 2.2 %copy-done.8 = bf16[64,256,128]{2,1,0:T(8,128)(2,1)S(1)} copy-done((bf16[64,256,128]{2,1,0:T(8,128)(2,1)S(1)}, bf16[64,256,128]{2,1,0:T(8,128)(2,1)}, u32[]{:S(2)}) %copy-start.8) | copy-done | bytes 4194328
  37.4 3.9 %shard_map.105.refs_5_ = f32[16,128,256]{2,1,0:T(8,128)S(1)} custom-call(s32[1,256]{1,0:T(1,128)S(1)} %get-tuple-element.38.pairs, s32[1,256]{1,0:T(1,128)S(1)} %get-tuple-element.39.starts, bf16[4,128,256]{2,1,0:T(8,128)(2,1)S(1)} %convert_element_type.7.even.refs_0_, bf16[4,128,256]{2,1,0:T(8,128)(2,1)S(1)} %collective-permute-done.odd.refs_1_, ...), custom_call_target="tpu_custom_call" | custom-call | flops 6000000000 | bytes 1048576 | tf_op jit(solution)/shard_map/pallas_call | solution.py:259
  41.4 5.3 %collective-permute-done.13.refs_2_ = s16[528,256]{1,0:T(8,128)(2,1)S(1)} collective-permute-done((s16[528,256]{1,0:T(8,128)(2,1)S(1)}, s16[528,256]{1,0:T(8,128)(2,1)S(1)}, u32[]{:S(2)}, u32[]{:S(2)}) %collective-permute-start.13) | collective-permute-done | bytes 270368 | tf_op jit(solution)/shard_map/ppermute | solution.py:32
  47.1 4.3 %collective-permute-start.14 = (bf16[4,128,256]{2,1,0:T(8,128)(2,1)S(1)}, bf16[4,128,256]{2,1,0:T(8,128)(2,1)S(1)}, u32[]{:S(2)}, u32[]{:S(2)}) collective-permute-start(bf16[4,128,256]{2,1,0:T(8,128)(2,1)S(1)} %get-tuple-element.51), channel_id=1, source_target_pairs={{0,1},{1,2},{2,3},{3,0},{4,5},{5,6},{6,7},{7,4},{8,9},{9,10},{10,1... | collective-permute-start | bytes 786440 | tf_op jit(solution)/shard_map/ppermute | solution.py:27
  53.4 8.4 %collective-permute-done.14.even.refs_0_ = bf16[4,128,256]{2,1,0:T(8,128)(2,1)S(1)} collective-permute-done((bf16[4,128,256]{2,1,0:T(8,128)(2,1)S(1)}, bf16[4,128,256]{2,1,0:T(8,128)(2,1)S(1)}, u32[]{:S(2)}, u32[]{:S(2)}) %collective-permute-start.14) | collective-permute-done | bytes 262176 | tf_op jit(solution)/shard_map/ppermute | solution.py:27
  62.4 1.2 %collective-permute-start.21 = (bf16[4,128,256]{2,1,0:T(8,128)(2,1)S(1)}, bf16[4,128,256]{2,1,0:T(8,128)(2,1)S(1)}, u32[]{:S(2)}, u32[]{:S(2)}) collective-permute-start(bf16[4,128,256]{2,1,0:T(8,128)(2,1)S(1)} %collective-permute-done.14.even.refs_0_), channel_id=1, source_target_pairs={{0,16},{4,20},{8,24},{12,28},{16,0},{20,4},{24,8},{28,12},{1,17},{... | collective-permute-start | bytes 786440 | tf_op jit(solution)/shard_map/ppermute | solution.py:32
  63.6 2.3 %shard_map.108 = (f32[16,128,256]{2,1,0:T(8,128)S(1)}, bf16[16,128,256]{2,1,0:T(8,128)(2,1)S(1)}) custom-call(s32[1,256]{1,0:T(1,128)S(1)} %get-tuple-element.38.pairs, s32[1,256]{1,0:T(1,128)S(1)} %get-tuple-element.39.starts, bf16[4,128,256]{2,1,0:T(8,128)(2,1)S(1)} %collective-permute-done.9.even.refs_0_, ...), custom_call_target="tpu_custom_call" | custom-call | flops 5000000000 | bytes 1048576 | tf_op jit(solution)/shard_map/pallas_call | solution.py:273
  65.9 1.4 %collective-permute-start.15 = (bf16[4,128,256]{2,1,0:T(8,128)(2,1)S(1)}, bf16[4,128,256]{2,1,0:T(8,128)(2,1)S(1)}, u32[]{:S(2)}, u32[]{:S(2)}) collective-permute-start(bf16[4,128,256]{2,1,0:T(8,128)(2,1)S(1)} %collective-permute-done.14.even.refs_0_), channel_id=1, source_target_pairs={{0,24},{4,28},{8,16},{12,20},{16,8},{20,12},{24,0},{28,4},{1,25},{... | collective-permute-start | bytes 786440 | tf_op jit(solution)/shard_map/ppermute | solution.py:32
  67.4 3.5 %collective-permute-done.17.even.refs_2_ = bf16[4,128,256]{2,1,0:T(8,128)(2,1)S(1)} collective-permute-done((bf16[4,128,256]{2,1,0:T(8,128)(2,1)S(1)}, bf16[4,128,256]{2,1,0:T(8,128)(2,1)S(1)}, u32[]{:S(2)}, u32[]{:S(2)}) %collective-permute-start.17) | collective-permute-done | bytes 262176 | tf_op jit(solution)/shard_map/ppermute | solution.py:32
  70.9 5.5 %collective-permute-done.21.even.refs_4_ = bf16[4,128,256]{2,1,0:T(8,128)(2,1)S(1)} collective-permute-done((bf16[4,128,256]{2,1,0:T(8,128)(2,1)S(1)}, bf16[4,128,256]{2,1,0:T(8,128)(2,1)S(1)}, u32[]{:S(2)}, u32[]{:S(2)}) %collective-permute-start.21) | collective-permute-done | bytes 262176 | tf_op jit(solution)/shard_map/ppermute | solution.py:32
  76.4 1.3 %shard_map.109 = (f32[4,128,256]{2,1,0:T(8,128)S(1)}, f32[4,128,256]{2,1,0:T(8,128)S(1)}, bf16[64,256,128]{2,1,0:T(8,128)(2,1)S(1)}) custom-call(s32[1,256]{1,0:T(1,128)S(1)} %get-tuple-element.36.pairs, s32[1,256]{1,0:T(1,128)S(1)} %get-tuple-element.37.starts, bf16[224,128,128]{2,1,0:T(8,128)(2,1)S(1)} %shard_map.107.rated, ...), custom_call_target="tpu_custom_call" | custom-call | flops 3000000000 | bytes 1048576 | tf_op jit(solution)/shard_map/pallas_call | solution.py:201
  77.7 2.1 %shard_map.110 = (f32[4,128,256]{2,1,0:T(8,128)S(1)}, f32[4,128,256]{2,1,0:T(8,128)S(1)}, bf16[64,256,128]{2,1,0:T(8,128)(2,1)S(1)}) custom-call(s32[1,256]{1,0:T(1,128)S(1)} %get-tuple-element.36.pairs, s32[1,256]{1,0:T(1,128)S(1)} %get-tuple-element.37.starts, bf16[224,128,128]{2,1,0:T(8,128)(2,1)S(1)} %shard_map.107.rated, ...), custom_call_target="tpu_custom_call" | custom-call | flops 3000000000 | bytes 1048576 | tf_op jit(solution)/shard_map/pallas_call | solution.py:201
  80.4 1.9 %shard_map.111 = (f32[4,128,256]{2,1,0:T(8,128)S(1)}, f32[4,128,256]{2,1,0:T(8,128)S(1)}, bf16[64,256,128]{2,1,0:T(8,128)(2,1)S(1)}) custom-call(s32[1,256]{1,0:T(1,128)S(1)} %get-tuple-element.36.pairs, s32[1,256]{1,0:T(1,128)S(1)} %get-tuple-element.37.starts, bf16[224,128,128]{2,1,0:T(8,128)(2,1)S(1)} %shard_map.107.rated, ...), custom_call_target="tpu_custom_call" | custom-call | flops 3000000000 | bytes 1048576 | tf_op jit(solution)/shard_map/pallas_call | solution.py:201
  82.6 1.7 %shard_map.113 = (f32[4,128,256]{2,1,0:T(8,128)S(1)}, f32[4,128,256]{2,1,0:T(8,128)S(1)}, bf16[64,256,128]{2,1,0:T(8,128)(2,1)S(1)}) custom-call(s32[1,256]{1,0:T(1,128)S(1)} %get-tuple-element.36.pairs, s32[1,256]{1,0:T(1,128)S(1)} %get-tuple-element.37.starts, bf16[224,128,128]{2,1,0:T(8,128)(2,1)S(1)} %shard_map.107.rated, ...), custom_call_target="tpu_custom_call" | custom-call | flops 3000000000 | bytes 1048576 | tf_op jit(solution)/shard_map/pallas_call | solution.py:201
  84.9 5.3 %collective-permute-start.24 = (s16[528,256]{1,0:T(8,128)(2,1)S(1)}, s16[528,256]{1,0:T(8,128)(2,1)S(1)}, u32[]{:S(2)}, u32[]{:S(2)}) collective-permute-start(s16[528,256]{1,0:T(8,128)(2,1)S(1)} %shard_map.112.refs_0_), channel_id=1, source_target_pairs={{0,8},{4,12},{8,0},{12,4},{16,24},{20,28},{24,16},{28,20},{1,9},{5... | collective-permute-start | bytes 811016 | tf_op jit(solution)/shard_map/ppermute | solution.py:32
  90.6 1.5 %collective-permute-start.28 = (s16[528,256]{1,0:T(8,128)(2,1)S(1)}, s16[528,256]{1,0:T(8,128)(2,1)S(1)}, u32[]{:S(2)}, u32[]{:S(2)}) collective-permute-start(s16[528,256]{1,0:T(8,128)(2,1)S(1)} %shard_map.117), channel_id=1, source_target_pairs={{0,24},{4,28},{8,16},{12,20},{16,8},{20,12},{24,0},{28,4},{1,25},{... | collective-permute-start | bytes 811016 | tf_op jit(solution)/shard_map/ppermute | solution.py:32
  92.1 2.7 %shard_map.114.refs_5_.refs_4_ = f32[16,128,256]{2,1,0:T(8,128)S(1)} custom-call(s32[1,256]{1,0:T(1,128)S(1)} %get-tuple-element.36.pairs, s32[1,256]{1,0:T(1,128)S(1)} %get-tuple-element.37.starts, bf16[4,128,256]{2,1,0:T(8,128)(2,1)S(1)} %collective-permute-done.14.even.refs_0_, bf16[4,128,256]{2,1,0:T(8,128)(2,1)S(1)} %collective-permute-done.19.odd.refs_1_, ...), custom_call_target="tpu_custom_call" | custom-call | flops 6000000000 | bytes 1048576 | tf_op jit(solution)/shard_map/pallas_call | solution.py:259
  94.8 9.6 %collective-permute-done.26.refs_1_ = s16[528,256]{1,0:T(8,128)(2,1)S(1)} collective-permute-done((s16[528,256]{1,0:T(8,128)(2,1)S(1)}, s16[528,256]{1,0:T(8,128)(2,1)S(1)}, u32[]{:S(2)}, u32[]{:S(2)}) %collective-permute-start.26) | collective-permute-done | bytes 270368 | tf_op jit(solution)/shard_map/ppermute | solution.py:32
  104.8 1.4 %collective-permute-start.29 = (s16[528,256]{1,0:T(8,128)(2,1)S(1)}, s16[528,256]{1,0:T(8,128)(2,1)S(1)}, u32[]{:S(2)}, u32[]{:S(2)}) collective-permute-start(s16[528,256]{1,0:T(8,128)(2,1)S(1)} %shard_map.118), channel_id=1, source_target_pairs={{0,3},{1,0},{2,1},{3,2},{4,7},{5,4},{6,5},{7,6},{8,11},{9,8},{10,9... | collective-permute-start | bytes 811016 | tf_op jit(solution)/shard_map/ppermute | solution.py:27
  106.2 3.7 %shard_map.115 = (f32[16,128,256]{2,1,0:T(8,128)}, bf16[16,128,256]{2,1,0:T(8,128)(2,1)}) custom-call(s32[1,256]{1,0:T(1,128)S(1)} %get-tuple-element.36.pairs, s32[1,256]{1,0:T(1,128)S(1)} %get-tuple-element.37.starts, bf16[4,128,256]{2,1,0:T(8,128)(2,1)S(1)} %collective-permute-done.15.even.refs_0_, ...), custom_call_target="tpu_custom_call" | custom-call | flops 5000000000 | bytes 1048576 | tf_op jit(solution)/shard_map/pallas_call | solution.py:273
  110.0 2.2 %collective-permute-done.29.coded = s16[528,256]{1,0:T(8,128)(2,1)S(1)} collective-permute-done((s16[528,256]{1,0:T(8,128)(2,1)S(1)}, s16[528,256]{1,0:T(8,128)(2,1)S(1)}, u32[]{:S(2)}, u32[]{:S(2)}) %collective-permute-start.29) | collective-permute-done | bytes 270368 | tf_op jit(solution)/shard_map/ppermute | solution.py:27
  (92 shorter events, 14.8 us)
Async XLA Ops:
  1.7 15.4 %collective-permute-start.2 = (bf16[4,128,256]{2,1,0:T(8,128)(2,1)S(1)}, bf16[4,128,256]{2,1,0:T(8,128)(2,1)S(1)}, u32[]{:S(2)}, u32[]{:S(2)}) collective-permute-start(bf16[4,128,256]{2,1,0:T(8,128)(2,1)S(1)} %convert_element_type.7.even.refs_0_), channel_id=1, source_target_pairs={{0,8},{4,12},{8,0},{12,4},{16,24},{20,28},{24,16},{28,20},{1,9},{5... | collective-permute-start | bytes 786440 | tf_op jit(solution)/shard_map/ppermute | solution.py:32
  4.7 13.4 %collective-permute-start.5 = (bf16[4,128,256]{2,1,0:T(8,128)(2,1)S(1)}, bf16[4,128,256]{2,1,0:T(8,128)(2,1)S(1)}, u32[]{:S(2)}, u32[]{:S(2)}) collective-permute-start(bf16[4,128,256]{2,1,0:T(8,128)(2,1)S(1)} %convert_element_type.7.even.refs_0_), channel_id=1, source_target_pairs={{0,16},{4,20},{8,24},{12,28},{16,0},{20,4},{24,8},{28,12},{1,17},{... | collective-permute-start | bytes 786440 | tf_op jit(solution)/shard_map/ppermute | solution.py:32
  6.2 11.9 %collective-permute-start = (bf16[4,128,256]{2,1,0:T(8,128)(2,1)S(1)}, bf16[4,128,256]{2,1,0:T(8,128)(2,1)S(1)}, u32[]{:S(2)}, u32[]{:S(2)}) collective-permute-start(bf16[4,128,256]{2,1,0:T(8,128)(2,1)S(1)} %convert_element_type.7.even.refs_0_), channel_id=1, source_target_pairs={{0,4},{4,0},{8,12},{12,8},{16,20},{20,16},{24,28},{28,24},{1,5},{5... | collective-permute-start | bytes 786440 | tf_op jit(solution)/shard_map/ppermute | solution.py:32
  6.2 18.2 %collective-permute-start.9 = (bf16[4,128,256]{2,1,0:T(8,128)(2,1)S(1)}, bf16[4,128,256]{2,1,0:T(8,128)(2,1)S(1)}, u32[]{:S(2)}, u32[]{:S(2)}) collective-permute-start(bf16[4,128,256]{2,1,0:T(8,128)(2,1)S(1)} %convert_element_type.7.even.refs_0_), channel_id=1, source_target_pairs={{0,24},{4,28},{8,16},{12,20},{16,8},{20,12},{24,0},{28,4},{1,25},{... | collective-permute-start | bytes 786440 | tf_op jit(solution)/shard_map/ppermute | solution.py:32
  17.2 3.0 %collective-permute-start.3 = (bf16[4,128,256]{2,1,0:T(8,128)(2,1)S(1)}, bf16[4,128,256]{2,1,0:T(8,128)(2,1)S(1)}, u32[]{:S(2)}, u32[]{:S(2)}) collective-permute-start(bf16[4,128,256]{2,1,0:T(8,128)(2,1)S(1)} %collective-permute-done.2.even.refs_2_), channel_id=1, source_target_pairs={{0,4},{4,0},{8,12},{12,8},{16,20},{20,16},{24,28},{28,24},{1,5},{5... | collective-permute-start | bytes 786440 | tf_op jit(solution)/shard_map/ppermute | solution.py:32
  18.1 6.4 %collective-permute-start.6 = (bf16[4,128,256]{2,1,0:T(8,128)(2,1)S(1)}, bf16[4,128,256]{2,1,0:T(8,128)(2,1)S(1)}, u32[]{:S(2)}, u32[]{:S(2)}) collective-permute-start(bf16[4,128,256]{2,1,0:T(8,128)(2,1)S(1)} %collective-permute-done.5.even.refs_4_), channel_id=1, source_target_pairs={{0,4},{4,0},{8,12},{12,8},{16,20},{20,16},{24,28},{28,24},{1,5},{5... | collective-permute-start | bytes 786440 | tf_op jit(solution)/shard_map/ppermute | solution.py:32
  22.3 5.6 %collective-permute-start.4 = (f32[4,128,256]{2,1,0:T(8,128)S(1)}, f32[4,128,256]{2,1,0:T(8,128)S(1)}, u32[]{:S(2)}, u32[]{:S(2)}) collective-permute-start(f32[4,128,256]{2,1,0:T(8,128)S(1)} %get-tuple-element.43), channel_id=1, source_target_pairs={{0,4},{4,0},{8,12},{12,8},{16,20},{20,16},{24,28},{28,24},{1,5},{5... | collective-permute-start | bytes 1572872 | tf_op jit(solution)/shard_map/ppermute | solution.py:32
  24.4 3.6 %collective-permute-start.10 = (bf16[4,128,256]{2,1,0:T(8,128)(2,1)S(1)}, bf16[4,128,256]{2,1,0:T(8,128)(2,1)S(1)}, u32[]{:S(2)}, u32[]{:S(2)}) collective-permute-start(bf16[4,128,256]{2,1,0:T(8,128)(2,1)S(1)} %collective-permute-done.9.even.refs_0_), channel_id=1, source_target_pairs={{0,4},{4,0},{8,12},{12,8},{16,20},{20,16},{24,28},{28,24},{1,5},{5... | collective-permute-start | bytes 786440 | tf_op jit(solution)/shard_map/ppermute | solution.py:32
  27.0 4.3 %collective-permute-start.8 = (f32[4,128,256]{2,1,0:T(8,128)S(1)}, f32[4,128,256]{2,1,0:T(8,128)S(1)}, u32[]{:S(2)}, u32[]{:S(2)}) collective-permute-start(f32[4,128,256]{2,1,0:T(8,128)S(1)} %get-tuple-element.45), channel_id=1, source_target_pairs={{0,4},{4,0},{8,12},{12,8},{16,20},{20,16},{24,28},{28,24},{1,5},{5... | collective-permute-start | bytes 1572872 | tf_op jit(solution)/shard_map/ppermute | solution.py:32
  30.2 3.1 %collective-permute-start.12 = (f32[4,128,256]{2,1,0:T(8,128)S(1)}, f32[4,128,256]{2,1,0:T(8,128)S(1)}, u32[]{:S(2)}, u32[]{:S(2)}) collective-permute-start(f32[4,128,256]{2,1,0:T(8,128)S(1)} %get-tuple-element.47), channel_id=1, source_target_pairs={{0,4},{4,0},{8,12},{12,8},{16,20},{20,16},{24,28},{28,24},{1,5},{5... | collective-permute-start | bytes 1572872 | tf_op jit(solution)/shard_map/ppermute | solution.py:32
  31.1 10.2 %collective-permute-start.1 = (f32[4,128,256]{2,1,0:T(8,128)S(1)}, f32[4,128,256]{2,1,0:T(8,128)S(1)}, u32[]{:S(2)}, u32[]{:S(2)}) collective-permute-start(f32[4,128,256]{2,1,0:T(8,128)S(1)} %get-tuple-element.41), channel_id=1, source_target_pairs={{0,4},{4,0},{8,12},{12,8},{16,20},{20,16},{24,28},{28,24},{1,5},{5... | collective-permute-start | bytes 1572872 | tf_op jit(solution)/shard_map/ppermute | solution.py:32
  31.2 10.2 %collective-permute-start.7 = (s16[528,256]{1,0:T(8,128)(2,1)S(1)}, s16[528,256]{1,0:T(8,128)(2,1)S(1)}, u32[]{:S(2)}, u32[]{:S(2)}) collective-permute-start(s16[528,256]{1,0:T(8,128)(2,1)S(1)} %shard_map.101.refs_0_), channel_id=1, source_target_pairs={{0,8},{4,12},{8,0},{12,4},{16,24},{20,28},{24,16},{28,20},{1,9},{5... | collective-permute-start | bytes 811016 | tf_op jit(solution)/shard_map/ppermute | solution.py:32
  31.4 9.9 %collective-permute-start.11 = (s16[528,256]{1,0:T(8,128)(2,1)S(1)}, s16[528,256]{1,0:T(8,128)(2,1)S(1)}, u32[]{:S(2)}, u32[]{:S(2)}) collective-permute-start(s16[528,256]{1,0:T(8,128)(2,1)S(1)} %shard_map.103.refs_0_), channel_id=1, source_target_pairs={{0,16},{4,20},{8,24},{12,28},{16,0},{20,4},{24,8},{28,12},{1,17},{... | collective-permute-start | bytes 811016 | tf_op jit(solution)/shard_map/ppermute | solution.py:32
  33.4 13.3 %collective-permute-start.13 = (s16[528,256]{1,0:T(8,128)(2,1)S(1)}, s16[528,256]{1,0:T(8,128)(2,1)S(1)}, u32[]{:S(2)}, u32[]{:S(2)}) collective-permute-start(s16[528,256]{1,0:T(8,128)(2,1)S(1)} %shard_map.104), channel_id=1, source_target_pairs={{0,24},{4,28},{8,16},{12,20},{16,8},{20,12},{24,0},{28,4},{1,25},{... | collective-permute-start | bytes 811016 | tf_op jit(solution)/shard_map/ppermute | solution.py:32
  37.4 14.1 %slice-start.1 = ((s8[14680064]{0:T(1024)(128)(4,1)}), s8[4194304]{0:T(1024)(128)(4,1)S(1)}, s32[]{:S(2)}) async-start(s8[14680064]{0:T(1024)(128)(4,1)} %bitcast.12), calls=%async_computation.1 | async-start | bytes 8388608
  37.4 14.1 %slice-start.2 = ((s8[14680064]{0:T(1024)(128)(4,1)}), s8[4194304]{0:T(1024)(128)(4,1)S(1)}, s32[]{:S(2)}) async-start(s8[14680064]{0:T(1024)(128)(4,1)} %bitcast.12), calls=%async_computation.2 | async-start | bytes 8388608
  47.1 14.7 %collective-permute-start.14 = (bf16[4,128,256]{2,1,0:T(8,128)(2,1)S(1)}, bf16[4,128,256]{2,1,0:T(8,128)(2,1)S(1)}, u32[]{:S(2)}, u32[]{:S(2)}) collective-permute-start(bf16[4,128,256]{2,1,0:T(8,128)(2,1)S(1)} %get-tuple-element.51), channel_id=1, source_target_pairs={{0,1},{1,2},{2,3},{3,0},{4,5},{5,6},{6,7},{7,4},{8,9},{9,10},{10,1... | collective-permute-start | bytes 786440 | tf_op jit(solution)/shard_map/ppermute | solution.py:27
  61.8 14.7 %collective-permute-start.19 = (bf16[4,128,256]{2,1,0:T(8,128)(2,1)S(1)}, bf16[4,128,256]{2,1,0:T(8,128)(2,1)S(1)}, u32[]{:S(2)}, u32[]{:S(2)}) collective-permute-start(bf16[4,128,256]{2,1,0:T(8,128)(2,1)S(1)} %collective-permute-done.14.even.refs_0_), channel_id=1, source_target_pairs={{0,4},{4,0},{8,12},{12,8},{16,20},{20,16},{24,28},{28,24},{1,5},{5... | collective-permute-start | bytes 786440 | tf_op jit(solution)/shard_map/ppermute | solution.py:32
  61.8 9.1 %collective-permute-start.17 = (bf16[4,128,256]{2,1,0:T(8,128)(2,1)S(1)}, bf16[4,128,256]{2,1,0:T(8,128)(2,1)S(1)}, u32[]{:S(2)}, u32[]{:S(2)}) collective-permute-start(bf16[4,128,256]{2,1,0:T(8,128)(2,1)S(1)} %collective-permute-done.14.even.refs_0_), channel_id=1, source_target_pairs={{0,8},{4,12},{8,0},{12,4},{16,24},{20,28},{24,16},{28,20},{1,9},{5... | collective-permute-start | bytes 786440 | tf_op jit(solution)/shard_map/ppermute | solution.py:32
  62.4 14.1 %collective-permute-start.21 = (bf16[4,128,256]{2,1,0:T(8,128)(2,1)S(1)}, bf16[4,128,256]{2,1,0:T(8,128)(2,1)S(1)}, u32[]{:S(2)}, u32[]{:S(2)}) collective-permute-start(bf16[4,128,256]{2,1,0:T(8,128)(2,1)S(1)} %collective-permute-done.14.even.refs_0_), channel_id=1, source_target_pairs={{0,16},{4,20},{8,24},{12,28},{16,0},{20,4},{24,8},{28,12},{1,17},{... | collective-permute-start | bytes 786440 | tf_op jit(solution)/shard_map/ppermute | solution.py:32
  65.9 14.1 %collective-permute-start.15 = (bf16[4,128,256]{2,1,0:T(8,128)(2,1)S(1)}, bf16[4,128,256]{2,1,0:T(8,128)(2,1)S(1)}, u32[]{:S(2)}, u32[]{:S(2)}) collective-permute-start(bf16[4,128,256]{2,1,0:T(8,128)(2,1)S(1)} %collective-permute-done.14.even.refs_0_), channel_id=1, source_target_pairs={{0,24},{4,28},{8,16},{12,20},{16,8},{20,12},{24,0},{28,4},{1,25},{... | collective-permute-start | bytes 786440 | tf_op jit(solution)/shard_map/ppermute | solution.py:32
  70.9 6.9 %collective-permute-start.18 = (bf16[4,128,256]{2,1,0:T(8,128)(2,1)S(1)}, bf16[4,128,256]{2,1,0:T(8,128)(2,1)S(1)}, u32[]{:S(2)}, u32[]{:S(2)}) collective-permute-start(bf16[4,128,256]{2,1,0:T(8,128)(2,1)S(1)} %collective-permute-done.17.even.refs_2_), channel_id=1, source_target_pairs={{0,4},{4,0},{8,12},{12,8},{16,20},{20,16},{24,28},{28,24},{1,5},{5... | collective-permute-start | bytes 786440 | tf_op jit(solution)/shard_map/ppermute | solution.py:32
  76.4 4.0 %collective-permute-start.22 = (bf16[4,128,256]{2,1,0:T(8,128)(2,1)S(1)}, bf16[4,128,256]{2,1,0:T(8,128)(2,1)S(1)}, u32[]{:S(2)}, u32[]{:S(2)}) collective-permute-start(bf16[4,128,256]{2,1,0:T(8,128)(2,1)S(1)} %collective-permute-done.21.even.refs_4_), channel_id=1, source_target_pairs={{0,4},{4,0},{8,12},{12,8},{16,20},{20,16},{24,28},{28,24},{1,5},{5... | collective-permute-start | bytes 786440 | tf_op jit(solution)/shard_map/ppermute | solution.py:32
  79.8 2.7 %collective-permute-start.20 = (f32[4,128,256]{2,1,0:T(8,128)S(1)}, f32[4,128,256]{2,1,0:T(8,128)S(1)}, u32[]{:S(2)}, u32[]{:S(2)}) collective-permute-start(f32[4,128,256]{2,1,0:T(8,128)S(1)} %get-tuple-element.56), channel_id=1, source_target_pairs={{0,4},{4,0},{8,12},{12,8},{16,20},{20,16},{24,28},{28,24},{1,5},{5... | collective-permute-start | bytes 1572872 | tf_op jit(solution)/shard_map/ppermute | solution.py:32
  80.0 2.6 %collective-permute-start.16 = (bf16[4,128,256]{2,1,0:T(8,128)(2,1)S(1)}, bf16[4,128,256]{2,1,0:T(8,128)(2,1)S(1)}, u32[]{:S(2)}, u32[]{:S(2)}) collective-permute-start(bf16[4,128,256]{2,1,0:T(8,128)(2,1)S(1)} %collective-permute-done.15.even.refs_0_), channel_id=1, source_target_pairs={{0,4},{4,0},{8,12},{12,8},{16,20},{20,16},{24,28},{28,24},{1,5},{5... | collective-permute-start | bytes 786440 | tf_op jit(solution)/shard_map/ppermute | solution.py:32
  82.3 7.9 %collective-permute-start.25 = (f32[4,128,256]{2,1,0:T(8,128)S(1)}, f32[4,128,256]{2,1,0:T(8,128)S(1)}, u32[]{:S(2)}, u32[]{:S(2)}) collective-permute-start(f32[4,128,256]{2,1,0:T(8,128)S(1)} %get-tuple-element.65), channel_id=1, source_target_pairs={{0,4},{4,0},{8,12},{12,8},{16,20},{20,16},{24,28},{28,24},{1,5},{5... | collective-permute-start | bytes 1572872 | tf_op jit(solution)/shard_map/ppermute | solution.py:32
  84.3 6.1 %collective-permute-start.27 = (f32[4,128,256]{2,1,0:T(8,128)S(1)}, f32[4,128,256]{2,1,0:T(8,128)S(1)}, u32[]{:S(2)}, u32[]{:S(2)}) collective-permute-start(f32[4,128,256]{2,1,0:T(8,128)S(1)} %get-tuple-element.67), channel_id=1, source_target_pairs={{0,4},{4,0},{8,12},{12,8},{16,20},{20,16},{24,28},{28,24},{1,5},{5... | collective-permute-start | bytes 1572872 | tf_op jit(solution)/shard_map/ppermute | solution.py:32
  84.8 10.0 %collective-permute-start.23 = (f32[4,128,256]{2,1,0:T(8,128)S(1)}, f32[4,128,256]{2,1,0:T(8,128)S(1)}, u32[]{:S(2)}, u32[]{:S(2)}) collective-permute-start(f32[4,128,256]{2,1,0:T(8,128)S(1)} %get-tuple-element.64), channel_id=1, source_target_pairs={{0,4},{4,0},{8,12},{12,8},{16,20},{20,16},{24,28},{28,24},{1,5},{5... | collective-permute-start | bytes 1572872 | tf_op jit(solution)/shard_map/ppermute | solution.py:32
  84.9 19.5 %collective-permute-start.24 = (s16[528,256]{1,0:T(8,128)(2,1)S(1)}, s16[528,256]{1,0:T(8,128)(2,1)S(1)}, u32[]{:S(2)}, u32[]{:S(2)}) collective-permute-start(s16[528,256]{1,0:T(8,128)(2,1)S(1)} %shard_map.112.refs_0_), channel_id=1, source_target_pairs={{0,8},{4,12},{8,0},{12,4},{16,24},{20,28},{24,16},{28,20},{1,9},{5... | collective-permute-start | bytes 811016 | tf_op jit(solution)/shard_map/ppermute | solution.py:32
  90.3 14.1 %collective-permute-start.26 = (s16[528,256]{1,0:T(8,128)(2,1)S(1)}, s16[528,256]{1,0:T(8,128)(2,1)S(1)}, u32[]{:S(2)}, u32[]{:S(2)}) collective-permute-start(s16[528,256]{1,0:T(8,128)(2,1)S(1)} %shard_map.116.refs_0_), channel_id=1, source_target_pairs={{0,16},{4,20},{8,24},{12,28},{16,0},{20,4},{24,8},{28,12},{1,17},{... | collective-permute-start | bytes 811016 | tf_op jit(solution)/shard_map/ppermute | solution.py:32
  90.6 13.8 %collective-permute-start.28 = (s16[528,256]{1,0:T(8,128)(2,1)S(1)}, s16[528,256]{1,0:T(8,128)(2,1)S(1)}, u32[]{:S(2)}, u32[]{:S(2)}) collective-permute-start(s16[528,256]{1,0:T(8,128)(2,1)S(1)} %shard_map.117), channel_id=1, source_target_pairs={{0,24},{4,28},{8,16},{12,20},{16,8},{20,12},{24,0},{28,4},{1,25},{... | collective-permute-start | bytes 811016 | tf_op jit(solution)/shard_map/ppermute | solution.py:32
  104.8 7.4 %collective-permute-start.29 = (s16[528,256]{1,0:T(8,128)(2,1)S(1)}, s16[528,256]{1,0:T(8,128)(2,1)S(1)}, u32[]{:S(2)}, u32[]{:S(2)}) collective-permute-start(s16[528,256]{1,0:T(8,128)(2,1)S(1)} %shard_map.118), channel_id=1, source_target_pairs={{0,3},{1,0},{2,1},{3,2},{4,7},{5,4},{6,5},{7,6},{8,11},{9,8},{10,9... | collective-permute-start | bytes 811016 | tf_op jit(solution)/shard_map/ppermute | solution.py:27
  (13 other events, 81.5 us)

commit v4 on v3

v4 whole, which is shorter than its diff:
```python
import functools
import math

import jax
import jax.numpy as jnp
from jax import lax
from jax.experimental import pallas as pl
from jax.experimental.pallas import tpu as pltpu
from jax.sharding import PartitionSpec as P

HALF_STEP = 0.002
ROOT_STEP = math.sqrt(0.004)
PRIOR = 25.0
GROUP = 4
SCALE_ROWS = 16
SMALL_LIMIT = 12 * 2**20
FETCH_LIMIT = 38 * 2**20
SCALE_STEPS = 128.0
SCALARS = 16
LONG = pl.CostEstimate(flops=4 * 10**9, bytes_accessed=2**12, transcendentals=0)
BRIEF = pl.CostEstimate(flops=10**8, bytes_accessed=2**12, transcendentals=0)

ANY = pl.BlockSpec(memory_space=pl.ANY)
IN_HBM = pl.BlockSpec(memory_space=pltpu.HBM)
IN_VMEM = pl.BlockSpec(memory_space=pltpu.VMEM)
IN_SMEM = pl.BlockSpec(memory_space=pltpu.SMEM)


def shifted(x, axis, by):
    peers = lax.axis_size(axis)
    return lax.ppermute(x, axis, [(i, (i + by) % peers) for i in range(peers)])


def swapped(x, axis, mask):
    peers = lax.axis_size(axis)
    return lax.ppermute(x, axis, [(i, i ^ mask) for i in range(peers)])


def widths(slots, user_tiles, item_tiles):
    bits = tuple(max(1, (n - 1).bit_length()) for n in (slots, user_tiles, item_tiles))
    assert 2 * bits[0] + 2 * bits[1] + bits[2] + 2 <= 31
    return bits


def total(x, axis):
    return jnp.sum(x.astype(jnp.float32), axis=axis, keepdims=True).astype(jnp.int32)


def plan_kernel(section, bits, per, span, runs, me, counts, rows, cols, words, lists):
    slot_bits, row_bits, col_bits = bits
    side = lists.shape[-1]
    slots = rows.shape[-1]
    shape = (side, side)
    count = counts[section]
    lists[...] = jnp.zeros_like(lists)
    lists[0:1, 0:slots] = rows[0, 0, section : section + 1]
    lists[1:2, 0:slots] = cols[0, 0, section : section + 1]
    along = lax.broadcasted_iota(jnp.int32, shape, 1)
    down = lax.broadcasted_iota(jnp.int32, shape, 0)
    row_along = jnp.broadcast_to(lists[0:1], shape)
    place_along = jnp.broadcast_to(lists[1:2] ^ (me[0] * per), shape)
    key = (place_along << row_bits | row_along).astype(jnp.float32).T.astype(jnp.int32)
    row_down = key & ((1 << row_bits) - 1)
    place_down = key >> row_bits
    span_bits = span.bit_length() - 1
    run_along, run_down = place_along >> span_bits, place_down >> span_bits
    live_along, live_down = along < count, down < count
    same = place_along == place_down
    rank_down = total(same & live_along & (row_along < row_down), 1)
    rank_along = total(same & live_down & (row_down < row_along), 0)
    opens = live_along & ((rank_along & 1) == 0)
    within = total(opens & (run_along == run_down) & (place_along < place_down), 1)
    base = jnp.zeros((side, 1), jnp.int32)
    begins = jnp.zeros((1, side), jnp.int32)
    unused = jnp.zeros((1, side), jnp.int32)
    ahead = jnp.zeros((1, 1), jnp.int32)
    for run in range(runs):
        size = total(opens[0:1] & (run_along[0:1] == run), 1)
        size = (size + GROUP - 1) & ~(GROUP - 1)
        base += jnp.where(run_down[:, 0:1] > run, size, 0)
        begins += jnp.where(along[0:1] > side - SCALARS + run, size, 0)
        ahead += size
        unused += jnp.where(along[0:1] >= ahead, span, 0)
    where = base + within + (rank_down >> 1)
    col_at = 2 * slot_bits + 2 * row_bits
    odd = rank_down & 1
    n, row, place = down[:, 0:1], row_down[:, 0:1], place_down[:, 0:1]
    word = jnp.where(odd == 0, n, n << slot_bits)
    word += jnp.where(odd == 0, row, row << row_bits) << (2 * slot_bits)
    word += (jnp.where(odd == 0, place, 0) << col_at) + (1 << (col_at + col_bits))
    word = jnp.broadcast_to(word, shape)
    hit = (where == along) & live_down
    low = total(jnp.where(hit, word & 0xFFFF, 0), 0)
    high = total(jnp.where(hit, word >> 16, 0), 0)
    listed = (high << 16) | low
    unused = jnp.minimum(unused, span * runs - 1) << col_at
    listed = jnp.where(listed == 0, unused, listed)
    words[...] = jnp.where(along[0:1] >= side - SCALARS, begins, listed)


def pair_plan(section, bits, per, span, runs, side, me, counts, rows, cols):
    return pl.pallas_call(
        functools.partial(plan_kernel, section, bits, per, span, runs),
        out_shape=jax.ShapeDtypeStruct((1, side), jnp.int32),
        in_specs=[IN_SMEM, IN_SMEM, IN_VMEM, IN_VMEM],
        out_specs=IN_VMEM,
        scratch_shapes=[pltpu.VMEM((8, side), jnp.int32)],
        compiler_params=pltpu.CompilerParams(vmem_limit_bytes=SMALL_LIMIT),
        cost_estimate=LONG,
    )(me, counts, rows, cols)


def bounds(words, run):
    at = words.shape[-1] - SCALARS + run
    return words[0, at], words[0, at + 1]


def decode_word(word, bits, first_col):
    slot_bits, row_bits, col_bits = bits
    fields = []
    for width in (slot_bits, slot_bits, row_bits, row_bits, col_bits):
        fields.append(word & ((1 << width) - 1))
        word = word >> width
    fields[4] -= first_col
    return (*fields, word)


def fetch_kernel(lump, counts, ratings, out, sem):
    def loads(section):
        def load(i):
            part = pl.ds(i * lump, lump)
            return pltpu.make_async_copy(ratings.at[section, part], out.at[section, part], sem.at[section, i])

        return lax.div(counts[section] + lump - 1, lump), load

    for section in range(ratings.shape[0]):
        lumps, load = loads(section)
        lax.fori_loop(0, lumps, lambda i, c, load=load: (load(i).start(), c)[1], 0)
    for section in range(ratings.shape[0]):
        lumps, load = loads(section)
        lax.fori_loop(0, lumps, lambda i, c, load=load: (load(i).wait(), c)[1], 0)


def fetch(counts, ratings):
    sections, slots = ratings.shape[:2]
    lump = math.gcd(slots, 16)
    return pl.pallas_call(
        functools.partial(fetch_kernel, lump),
        out_shape=jax.ShapeDtypeStruct(ratings.shape, ratings.dtype),
        in_specs=[IN_SMEM, IN_HBM],
        out_specs=IN_VMEM,
        scratch_shapes=[pltpu.SemaphoreType.DMA((sections, slots // lump))],
        compiler_params=pltpu.CompilerParams(vmem_limit_bytes=FETCH_LIMIT),
        cost_estimate=LONG,
    )(counts, ratings)


def gather_tiles(pieces, items):
    at = 0
    for piece in pieces:
        for t in range(piece.shape[0]):
            items[at + t] = piece[t]
        at += piece.shape[0]


def items_kernel(section, run, count, skipped, bits, words, ratings, users, *refs):
    outs, items, grad = refs[count + skipped : -2], refs[-2], refs[-1]
    out_even, *out_odd, misfits = outs
    span = items.shape[0]
    per = span // 2
    tile = users.shape[1]
    low, high = bounds(words, run)
    steps = lax.div(high - low, GROUP)
    gather_tiles(refs[:count], items)
    grad[...] = jnp.zeros_like(grad)

    def decode(p):
        return decode_word(words[0, p], bits, run * span)

    def users_of(row_a, row_b):
        return jnp.concatenate([users[row_a], users[row_b]], axis=0)

    def predict(p):
        slot_a, slot_b, row_a, row_b, col, live = decode(p)
        predicted = lax.dot_general(
            users_of(row_a, row_b), items[col], (((1,), (1,)), ((), ())), preferred_element_type=jnp.float32
        )
        given = jnp.concatenate([ratings[section, slot_a], ratings[section, slot_b]], axis=0).astype(jnp.float32)
        rows = lax.broadcasted_iota(jnp.int32, (2 * tile, 1), 0)
        return jnp.where(rows < tile * live, given - predicted, 0.0).astype(jnp.bfloat16)

    def add_grad(p, misfit):
        _, _, row_a, row_b, col, _ = decode(p)
        grad[col] += lax.dot_general(
            misfit, users_of(row_a, row_b), (((0,), (0,)), ((), ())), preferred_element_type=jnp.float32
        )

    @pl.when(steps > 0)
    def _():
        for j in range(GROUP):
            misfits[j] = predict(low + j)

        def advance(step, carry):
            at = step * GROUP
            held = [misfits[at + j] for j in range(GROUP)]
            following = [predict(low + at + GROUP + j) for j in range(GROUP)]
            for j in range(GROUP):
                add_grad(low + at + j, held[j])
            for j in range(GROUP):
                misfits[at + GROUP + j] = following[j]
            return carry

        lax.fori_loop(0, steps - 1, advance, 0)
        for j in range(GROUP):
            add_grad(high - GROUP + j, misfits[high - low - GROUP + j])

    at = 0
    for out in (out_even, *out_odd):
        for t in range(out.shape[0]):
            out[t] = grad[at + t]
        at += out.shape[0]


def item_grads(section, run, per, bits, words, ratings, users, pieces, after, parts):
    tile, width = users.shape[1:]
    f32 = jnp.float32
    held = per * (users.shape[0] + users.shape[0] % 2)
    held = -(-min(held, ratings.shape[1] // 2 + per) // GROUP) * GROUP
    even_grad, *odd_grads, misfits = pl.pallas_call(
        functools.partial(items_kernel, section, run, len(pieces), len(after), bits),
        out_shape=[jax.ShapeDtypeStruct((per, tile, width), f32)]
        + [jax.ShapeDtypeStruct((per // parts, tile, width), f32)] * parts
        + [jax.ShapeDtypeStruct((held, 2 * tile, tile), jnp.bfloat16)],
        in_specs=[IN_SMEM] + [IN_VMEM] * (2 + len(pieces)) + [ANY] * len(after),
        out_specs=[IN_VMEM] * (2 + parts),
        scratch_shapes=[pltpu.VMEM((2 * per, tile, width), jnp.bfloat16), pltpu.VMEM((2 * per, tile, width), f32)],
        compiler_params=pltpu.CompilerParams(vmem_limit_bytes=SMALL_LIMIT),
        cost_estimate=LONG,
    )(words, ratings, users, *pieces, *after)
    return even_grad, odd_grads, misfits


def add_user_grads(bits, first_run, words, pieces, misfits, items, grad):
    tile = grad.shape[1]
    first_col = first_run * items.shape[0] // len(misfits)
    gather_tiles(pieces, items)
    for run, held in enumerate(misfits, first_run):
        low, high = bounds(words, run)

        def advance(step, carry, low=low, held=held):
            for j in range(GROUP):
                at = step * GROUP + j
                _, _, row_a, row_b, col, _ = decode_word(words[0, low + at], bits, first_col)
                part = jnp.dot(held[at], items[col], preferred_element_type=jnp.float32)
                grad[row_a] += part[:tile]
                grad[row_b] += part[tile:]
            return carry

        lax.fori_loop(0, lax.div(high - low, GROUP), advance, 0)


def users_head_kernel(bits, runs, words, *refs):
    *pieces, grad, items = refs[runs:]
    grad[...] = jnp.zeros_like(grad)
    add_user_grads(bits, 0, words, pieces, refs[:runs], items, grad)


def users_tail_kernel(power, bits, first_run, words, held, *refs):
    *pieces, factors, noise, partial, new, new_bf, items, grad = refs
    grad[...] = partial[...]
    add_user_grads(bits, first_run, words, pieces, [held], items, grad)

    def finish(t, carry):
        before = factors[t]
        after = (
            before + HALF_STEP * (power * grad[t] - PRIOR * before) + ROOT_STEP * noise[t].astype(jnp.float32)
        )
        new[t] = after
        new_bf[t] = after.astype(jnp.bfloat16)
        return carry

    lax.fori_loop(0, factors.shape[0], finish, 0)


def tiles_of(pieces):
    return sum(piece.shape[0] for piece in pieces), *pieces[0].shape[1:]


def users_head(bits, words, misfits, pieces, shape):
    return pl.pallas_call(
        functools.partial(users_head_kernel, bits, len(misfits)),
        out_shape=jax.ShapeDtypeStruct(shape, jnp.float32),
        in_specs=[IN_SMEM] + [IN_VMEM] * (len(misfits) + len(pieces)),
        out_specs=IN_VMEM,
        scratch_shapes=[pltpu.VMEM(tiles_of(pieces), jnp.bfloat16)],
        compiler_params=pltpu.CompilerParams(vmem_limit_bytes=SMALL_LIMIT),
        cost_estimate=BRIEF,
    )(words, *misfits, *pieces)


def users_tail(power, bits, first_run, words, misfits, pieces, factors, noise, partial):
    shape = factors.shape
    return pl.pallas_call(
        functools.partial(users_tail_kernel, power, bits, first_run),
        out_shape=[jax.ShapeDtypeStruct(shape, jnp.float32), jax.ShapeDtypeStruct(shape, jnp.bfloat16)],
        in_specs=[IN_SMEM, IN_VMEM] + [IN_VMEM] * (len(pieces) + 3),
        out_specs=[IN_VMEM] * 2,
        scratch_shapes=[pltpu.VMEM(tiles_of(pieces), jnp.bfloat16), pltpu.VMEM(shape, jnp.float32)],
        compiler_params=pltpu.CompilerParams(vmem_limit_bytes=SMALL_LIMIT),
        cost_estimate=BRIEF,
    )(words, misfits, *pieces, factors, noise, partial)


def coded_shape(per, tile, width):
    return jax.ShapeDtypeStruct((per * tile + SCALE_ROWS, width), jnp.int16)


def encode(blocks, out):
    per = len(blocks)
    tile, width = blocks[0].shape
    row = lax.broadcasted_iota(jnp.int32, (SCALE_ROWS, width), 0)
    powers = jnp.zeros((SCALE_ROWS, width), jnp.int32)
    for t, block in enumerate(blocks):
        largest = jnp.max(jnp.abs(block), axis=0, keepdims=True)
        power = jnp.ceil(SCALE_STEPS * jnp.log2(jnp.maximum(largest, 1e-20)))
        scaled = jnp.round(block * jnp.exp2(15.0 - power / SCALE_STEPS))
        out[pl.ds(t * tile, tile)] = jnp.clip(scaled, -32767.0, 32767.0).astype(jnp.int32).astype(jnp.int16)
        powers = jnp.where(row == t, power.astype(jnp.int32), powers)
    out[pl.ds(per * tile, SCALE_ROWS)] = powers.astype(jnp.int16)


def decoded(ref, t, tile, per):
    powers = ref[pl.ds(per * tile, SCALE_ROWS)].astype(jnp.int32).astype(jnp.float32)
    unit = jnp.exp2(powers[t : t + 1] / SCALE_STEPS - 15.0)
    return ref[pl.ds(t * tile, tile)].astype(jnp.int32).astype(jnp.float32) * unit


def join_kernel(count, mine, *refs):
    others = [ref[t] for ref in refs[:count] for t in range(ref.shape[0])]
    encode([mine[t] + other for t, other in enumerate(others)], refs[-1])


def join(mine, others, after):
    return pl.pallas_call(
        functools.partial(join_kernel, len(others)),
        out_shape=coded_shape(*mine.shape),
        in_specs=[IN_VMEM] * (1 + len(others)) + [ANY] * len(after),
        out_specs=IN_VMEM,
        compiler_params=pltpu.CompilerParams(vmem_limit_bytes=SMALL_LIMIT),
        cost_estimate=BRIEF,
    )(mine, *others, *after)


def owner_sum(mine, other, coded, t):
    per, tile, _ = mine.shape
    total = mine[t] + other[t]
    for ref in coded:
        total = total + decoded(ref, t, tile, per)
    return total


def update_kernel(power, mine, other, *refs):
    *coded, factors, noise, _, new, new_bf = refs
    for t in range(mine.shape[0]):
        step = HALF_STEP * power * owner_sum(mine, other, coded, t) + ROOT_STEP * noise[t].astype(jnp.float32)
        after = factors[t] - HALF_STEP * PRIOR * factors[t] + step
        new[t] = after
        new_bf[t] = after.astype(jnp.bfloat16)


def delta_kernel(power, mine, other, *refs):
    *coded, noise, _, out = refs
    steps = []
    for t in range(mine.shape[0]):
        steps.append(HALF_STEP * power * owner_sum(mine, other, coded, t) + ROOT_STEP * noise[t].astype(jnp.float32))
    encode(steps, out)


def arrive_kernel(coded, factors, new, new_bf):
    per, tile, _ = factors.shape
    for t in range(per):
        after = factors[t] - HALF_STEP * PRIOR * factors[t] + decoded(coded, t, tile, per)
        new[t] = after
        new_bf[t] = after.astype(jnp.bfloat16)


def in_vmem(kernel, out_shape, *operands, after=()):
    return pl.pallas_call(
        kernel,
        out_shape=out_shape,
        in_specs=[IN_VMEM] * len(operands) + [ANY] * len(after),
        out_specs=jax.tree.map(lambda _: IN_VMEM, out_shape),
        compiler_params=pltpu.CompilerParams(vmem_limit_bytes=SMALL_LIMIT),
        cost_estimate=BRIEF,
    )(*operands, *after)


def gathered(own, runs):
    evens = [[own]] + [[swapped(own, "user", 2 * d)] for d in range(1, 3 if runs == 4 else runs)]
    if runs == 4:
        half = own.shape[0] // 2
        evens.append([swapped(evens[1][0][:half], "user", 4), swapped(evens[2][0][half:], "user", 2)])
    return evens


def body(u_factors, v_factors, ratings, tile_rows, tile_cols, tile_counts, u_noise, v_noise):
    tile = ratings.shape[-1]
    sections = ratings.shape[2]
    width = u_factors.shape[1]
    peers = lax.axis_size("user")
    power = float(lax.axis_size("item"))
    me = lax.axis_index("user").astype(jnp.int32).reshape(1)
    users = u_factors.reshape(-1, tile, width)
    items = v_factors.reshape(-1, tile, width)
    per = items.shape[0]
    item_tiles = peers * per
    span = 2 * per
    runs = item_tiles // span
    ratings = ratings.reshape(ratings.shape[2:])
    counts = tile_counts.reshape(sections)
    u_noise = u_noise.reshape(sections, *users.shape)
    v_noise = v_noise.reshape(sections, *items.shape)
    side = -(-ratings.shape[1] // 128) * 128
    assert (ratings.shape[1] + item_tiles) // 2 + runs * GROUP <= side - SCALARS and runs < SCALARS
    assert per & (per - 1) == 0
    bits = widths(ratings.shape[1], users.shape[0], item_tiles)
    pair = (
        jax.ShapeDtypeStruct(items.shape, jnp.float32),
        jax.ShapeDtypeStruct(items.shape, jnp.bfloat16),
    )
    rated = fetch(counts, ratings)
    items_bf = items.astype(jnp.bfloat16)
    users_bf = users.astype(jnp.bfloat16)
    for section in range(sections):
        sent = shifted(items_bf, "item", section) if section else items_bf
        evens = gathered(sent, runs)
        chunks = [even + [swapped(piece, "user", 1) for piece in even] for even in evens]
        words = pair_plan(section, bits, per, span, runs, side, me, counts, tile_rows, tile_cols)
        mine, other, sums, misfits = [], [], [], []
        after = []
        for run in range(runs):
            if run in (1, 2):
                after += evens[run + 1]
            even_grad, odd_grads, held = item_grads(
                section, run, per, bits, words, rated, users_bf, chunks[run], after, 2 if run else 1
            )
            misfits.append(held)
            mine.append(even_grad)
            other.append([swapped(grad, "user", 1) for grad in odd_grads])
            after = [even_grad]
            if run >= 2:
                coded = join(mine[run - 1], other[run - 1], after)
                sums.append(swapped(coded, "user", 2 * (run - 1)))
                after = [coded]
        coded = join(mine[-1], other[-1], after + sums[:1])
        sums.append(swapped(coded, "user", 2 * (runs - 1)))
        head = [piece for chunk in chunks[:-1] for piece in chunk]
        partial = users_head(bits, words, misfits[:-1], head, users.shape)
        if section == 0:
            items, items_bf = in_vmem(
                functools.partial(update_kernel, power),
                pair,
                mine[0],
                other[0][0],
                *sums,
                items,
                v_noise[section],
                after=(partial,),
            )
        else:
            delta = in_vmem(
                functools.partial(delta_kernel, power),
                coded_shape(*items.shape),
                mine[0],
                other[0][0],
                *sums,
                v_noise[section],
                after=(partial,),
            )
            items, items_bf = in_vmem(arrive_kernel, pair, shifted(delta, "item", -section), items)
        users, users_bf = users_tail(
            power, bits, runs - 1, words, misfits[-1], chunks[-1], users, u_noise[section], partial
        )
    return (users.reshape(u_factors.shape), items.reshape(v_factors.shape))


def solution(mesh):
    placed = (
        P(("user", "item"), None),
        P(("item", "user"), None),
        P("user", "item", None, None, None, None),
        P("user", "item", None, None),
        P("user", "item", None, None),
        P("user", "item", None),
        P(None, ("user", "item"), None),
        P(None, ("item", "user"), None),
    )
    return jax.shard_map(
        body,
        mesh=mesh,
        in_specs=placed,
        out_specs=(P(("user", "item"), None), P(("item", "user"), None)),
        check_vma=False,
    )
```

time: 113 us -> 109 us (0.965)
  Pallas kernels: 34.7 us -> 49.1 us
  local copies, waits for them, and re-layouts: 9.61 us -> 0.9 us
  waiting for transfers between devices: 34.8 us -> 29.1 us
  starting transfers between devices: 30.2 us -> 25.8 us
    pallas_call x16 -> x15, Pallas kernels: 18.3 us -> 27.4 us  [the longest x8 22.2 us: item_grads(): pl.pallas_call(functools.partial(items_kernel, section, run, len(pieces),...]
    unnamed x30 -> x16, local copies, waits for them, and re-layouts: 8.06 us -> 0.69 us
    ppermute x28 -> x38, waiting for transfers between devices: 24.2 us -> 18.2 us  [swapped(): return lax.ppermute(x, axis, [(i, i ^ mask) for i in range(peers)])]
    pallas_call x2, Pallas kernels: 6.58 us -> 10.3 us  [users_head(): pl.pallas_call(functools.partial(users_head_kernel, bits, len(misfits)),...]
    ppermute x2, starting transfers between devices: 5.7 us -> 2.57 us  [shifted(): return lax.ppermute(x, axis, [(i, (i + by) % peers) for i in range(peers)])]
    pallas_call x2, Pallas kernels: 6.06 us -> 7.57 us  [users_tail(): pl.pallas_call(functools.partial(users_tail_kernel, power, bits, first_ru...]
    another operation x2 -> x0, local copies, waits for them, and re-layouts: 1.37 us -> none  [body(): lists = jnp.stack([tile_rows[0, 0], tile_cols[0, 0]], axis=1)]
    ppermute x28 -> x38, starting transfers between devices: 24.5 us -> 23.2 us  [swapped(): return lax.ppermute(x, axis, [(i, i ^ mask) for i in range(peers)])]
  transfers between devices with their start and end apart: 30 -> 40, of which waited for: 7 -> 11; matrix products, arithmetic and copies ran while one was open for 3% -> 2% of each run, Pallas kernels for 29% -> 43%
where the time goes in v4:
time: 109 us
  Pallas kernels  49.1 us (45%)
  waiting for transfers between devices  29.1 us (27%)
  starting transfers between devices  25.8 us (24%)
  other arithmetic  2.78 us (3%)
    ppermute x38, starting transfers between devices, swapped(): return lax.ppermute(x, axis, [(i, i ^ mask) for i in range(peers)])  23.2 us
    pallas_call x8, Pallas kernels, item_grads(): pl.pallas_call(functools.partial(items_kernel, section, run, len(pieces),...  22.2 us
    ppermute x38, waiting for transfers between devices, swapped(): return lax.ppermute(x, axis, [(i, i ^ mask) for i in range(peers)])  18.2 us
    ppermute x2, waiting for transfers between devices, shifted(): return lax.ppermute(x, axis, [(i, (i + by) % peers) for i in range(peers)])  11 us
    pallas_call x2, Pallas kernels, users_head(): pl.pallas_call(functools.partial(users_head_kernel, bits, len(misfits)),...  10.3 us
    pallas_call x2, Pallas kernels, users_tail(): pl.pallas_call(functools.partial(users_tail_kernel, power, bits, first_ru...  7.57 us
    pallas_call x1, Pallas kernels, fetch(): pl.pallas_call(functools.partial(fetch_kernel, lump), out_shape=jax.Shape...  4.35 us
    ppermute x2, starting transfers between devices, shifted(): return lax.ppermute(x, axis, [(i, (i + by) % peers) for i in range(peers)])  2.57 us
  transfers between devices with their start and end apart: 40, of which 11 were waited for; matrix products, arithmetic and copies ran while one was open for 2% of the time, Pallas kernels for 43%

profile of v4, /device:TPU:0, one launch (start us, length us, event | category | flops | bytes accessed | tf_op | source)
XLA Modules:
  0.0 108.9 jit_solution(1381443371708099832)
XLA Ops:
  0.6 1.1 convert_element_type.7.refs_0_.refs_3_
  2.2 2.6 %collective-permute-start.2 = (bf16[4,128,256]{2,1,0:T(8,128)(2,1)S(1)}, bf16[4,128,256]{2,1,0:T(8,128)(2,1)S(1)}, u32[]{:S(2)}, u32[]{:S(2)}) collective-permute-start(bf16[4,128,256]{2,1,0:T(8,128)(2,1)S(1)} %convert_element_type.7.refs_0_.refs_3_), channel_id=1, source_target_pairs={{0,16},{4,20},{8,24},{12,28},{16,0},{20,4},{24,8},{28,12},{1,17},{... | collective-permute-start | bytes 786440 | tf_op jit(solution)/shard_map/ppermute | solution.py:36
  4.8 1.5 %collective-permute-start = (bf16[4,128,256]{2,1,0:T(8,128)(2,1)S(1)}, bf16[4,128,256]{2,1,0:T(8,128)(2,1)S(1)}, u32[]{:S(2)}, u32[]{:S(2)}) collective-permute-start(bf16[4,128,256]{2,1,0:T(8,128)(2,1)S(1)} %convert_element_type.7.refs_0_.refs_3_), channel_id=1, source_target_pairs={{0,8},{4,12},{8,0},{12,4},{16,24},{20,28},{24,16},{28,20},{1,9},{5... | collective-permute-start | bytes 786440 | tf_op jit(solution)/shard_map/ppermute | solution.py:36
  6.3 1.7 %convert_element_type.6.users = bf16[16,128,256]{2,1,0:T(8,128)(2,1)S(1)} convert(f32[16,128,256]{2,1,0:T(8,128)} %bitcast.11) | non-fusion elementwise | flops 524288 | bytes 3145728 | tf_op jit(solution)/shard_map/convert_element_type | solution.py:433
  8.7 4.3 %shard_map.96.ratings = bf16[2,224,128,128]{3,2,1,0:T(8,128)(2,1)S(1)} custom-call(s32[2]{0:T(128)S(1)} %bitcast.19, bf16[2,224,128,128]{3,2,1,0:T(8,128)(2,1)} %bitcast.22), custom_call_target="tpu_custom_call" | custom-call | flops 4000000000 | bytes 4096 | tf_op jit(solution)/shard_map/pallas_call | solution.py:147
  13.1 1.0 shard_map.97.words
  15.6 3.6 %shard_map.98 = (f32[4,128,256]{2,1,0:T(8,128)S(1)}, f32[4,128,256]{2,1,0:T(8,128)S(1)}, bf16[64,256,128]{2,1,0:T(8,128)(2,1)S(1)}) custom-call(s32[1,256]{1,0:T(1,128)S(1)} %shard_map.97.words, bf16[2,224,128,128]{3,2,1,0:T(8,128)(2,1)S(1)} %shard_map.96.ratings, bf16[16,128,256]{2,1,0:T(8,128)(2,1)S(1)} %convert_element_type.6.users, ...), custom_call_target="tpu_custom_call" | custom-call | flops 4000000000 | bytes 4096 | tf_op jit(solution)/shard_map/pallas_call | solution.py:229
  19.9 3.3 %shard_map.99 = (f32[4,128,256]{2,1,0:T(8,128)S(1)}, f32[2,128,256]{2,1,0:T(8,128)S(1)}, f32[2,128,256]{2,1,0:T(8,128)S(1)}, bf16[64,256,128]{2,1,0:T(8,128)(2,1)S(1)}) custom-call(s32[1,256]{1,0:T(1,128)S(1)} %shard_map.97.words, bf16[2,224,128,128]{3,2,1,0:T(8,128)(2,1)S(1)} %shard_map.96.ratings, bf16[16,128,256]{2,1,0:T(8,128)(2,1)S(1)} %convert_element_type.6.users, ...), custom_call_target="tpu_custom_call" | custom-call | flops 4000000000 | bytes 4096 | tf_op jit(solution)/shard_map/pallas_call | solution.py:229
  23.7 3.6 %shard_map.100 = (f32[4,128,256]{2,1,0:T(8,128)S(1)}, f32[2,128,256]{2,1,0:T(8,128)S(1)}, f32[2,128,256]{2,1,0:T(8,128)S(1)}, bf16[64,256,128]{2,1,0:T(8,128)(2,1)S(1)}) custom-call(s32[1,256]{1,0:T(1,128)S(1)} %shard_map.97.words, bf16[2,224,128,128]{3,2,1,0:T(8,128)(2,1)S(1)} %shard_map.96.ratings, bf16[16,128,256]{2,1,0:T(8,128)(2,1)S(1)} %convert_element_type.6.users, ...), custom_call_target="tpu_custom_call" | custom-call | flops 4000000000 | bytes 4096 | tf_op jit(solution)/shard_map/pallas_call | solution.py:229
  28.2 3.6 %shard_map.102 = (f32[4,128,256]{2,1,0:T(8,128)S(1)}, f32[2,128,256]{2,1,0:T(8,128)S(1)}, f32[2,128,256]{2,1,0:T(8,128)S(1)}, bf16[64,256,128]{2,1,0:T(8,128)(2,1)S(1)}) custom-call(s32[1,256]{1,0:T(1,128)S(1)} %shard_map.97.words, bf16[2,224,128,128]{3,2,1,0:T(8,128)(2,1)S(1)} %shard_map.96.ratings, bf16[16,128,256]{2,1,0:T(8,128)(2,1)S(1)} %convert_element_type.6.users, ...), custom_call_target="tpu_custom_call" | custom-call | flops 4000000000 | bytes 4096 | tf_op jit(solution)/shard_map/pallas_call | solution.py:229
  33.8 2.8 %collective-permute-done.12.refs_3_.refs_0_ = s16[528,256]{1,0:T(8,128)(2,1)S(1)} collective-permute-done((s16[528,256]{1,0:T(8,128)(2,1)S(1)}, s16[528,256]{1,0:T(8,128)(2,1)S(1)}, u32[]{:S(2)}, u32[]{:S(2)}) %collective-permute-start.12) | collective-permute-done | bytes 270368 | tf_op jit(solution)/shard_map/ppermute | solution.py:36
  36.9 7.0 %shard_map.103.refs_6_.refs_5_ = f32[16,128,256]{2,1,0:T(8,128)S(1)} custom-call(s32[1,256]{1,0:T(1,128)S(1)} %shard_map.97.words, bf16[64,256,128]{2,1,0:T(8,128)(2,1)S(1)} %get-tuple-element.44.refs_0_, bf16[64,256,128]{2,1,0:T(8,128)(2,1)S(1)} %get-tuple-element.45.refs_1_, bf16[64,256,128]{2,1,0:T(8,128)(2,1)S(1)} %get-tuple-element.46.refs_2_, ...), custom_call_target="tpu_custom_call" | custom-call | flops 100000000 | bytes 4096 | tf_op jit(solution)/shard_map/pallas_call | solution.py:290
  44.0 3.4 %collective-permute-done.15.refs_1_ = s16[528,256]{1,0:T(8,128)(2,1)S(1)} collective-permute-done((s16[528,256]{1,0:T(8,128)(2,1)S(1)}, s16[528,256]{1,0:T(8,128)(2,1)S(1)}, u32[]{:S(2)}, u32[]{:S(2)}) %collective-permute-start.15) | collective-permute-done | bytes 270368 | tf_op jit(solution)/shard_map/ppermute | solution.py:36
  47.8 2.5 %collective-permute-start.19 = (bf16[4,128,256]{2,1,0:T(8,128)(2,1)S(1)}, bf16[4,128,256]{2,1,0:T(8,128)(2,1)S(1)}, u32[]{:S(2)}, u32[]{:S(2)}) collective-permute-start(bf16[4,128,256]{2,1,0:T(8,128)(2,1)S(1)} %get-tuple-element.54), channel_id=1, source_target_pairs={{0,1},{1,2},{2,3},{3,0},{4,5},{5,6},{6,7},{7,4},{8,9},{9,10},{10,1... | collective-permute-start | bytes 786440 | tf_op jit(solution)/shard_map/ppermute | solution.py:31
  50.4 7.1 %collective-permute-done.19.refs_0_.refs_3_ = bf16[4,128,256]{2,1,0:T(8,128)(2,1)S(1)} collective-permute-done((bf16[4,128,256]{2,1,0:T(8,128)(2,1)S(1)}, bf16[4,128,256]{2,1,0:T(8,128)(2,1)S(1)}, u32[]{:S(2)}, u32[]{:S(2)}) %collective-permute-start.19) | collective-permute-done | bytes 262176 | tf_op jit(solution)/shard_map/ppermute | solution.py:31
  58.8 1.0 shard_map.95.words
  59.8 3.5 %shard_map.104 = (f32[16,128,256]{2,1,0:T(8,128)S(1)}, bf16[16,128,256]{2,1,0:T(8,128)(2,1)S(1)}) custom-call(s32[1,256]{1,0:T(1,128)S(1)} %shard_map.97.words, bf16[64,256,128]{2,1,0:T(8,128)(2,1)S(1)} %get-tuple-element.43.held, bf16[2,128,256]{2,1,0:T(8,128)(2,1)S(1)} %collective-permute-done.1.refs_3_.refs_0_, ...), custom_call_target="tpu_custom_call" | custom-call | flops 100000000 | bytes 4096 | tf_op jit(solution)/shard_map/pallas_call | solution.py:303
  63.4 2.8 %collective-permute-done.22.refs_3_.refs_0_.refs_7_ = bf16[4,128,256]{2,1,0:T(8,128)(2,1)S(1)} collective-permute-done((bf16[4,128,256]{2,1,0:T(8,128)(2,1)S(1)}, bf16[4,128,256]{2,1,0:T(8,128)(2,1)S(1)}, u32[]{:S(2)}, u32[]{:S(2)}) %collective-permute-start.22) | collective-permute-done | bytes 262176 | tf_op jit(solution)/shard_map/ppermute | solution.py:36
  68.5 1.7 %shard_map.108 = (f32[4,128,256]{2,1,0:T(8,128)S(1)}, f32[4,128,256]{2,1,0:T(8,128)S(1)}, bf16[64,256,128]{2,1,0:T(8,128)(2,1)S(1)}) custom-call(s32[1,256]{1,0:T(1,128)S(1)} %shard_map.95.words, bf16[2,224,128,128]{3,2,1,0:T(8,128)(2,1)S(1)} %shard_map.96.ratings, bf16[16,128,256]{2,1,0:T(8,128)(2,1)S(1)} %get-tuple-element.47.users, ...), custom_call_target="tpu_custom_call" | custom-call | flops 4000000000 | bytes 4096 | tf_op jit(solution)/shard_map/pallas_call | solution.py:229
  70.2 1.2 %collective-permute-done.23.refs_4_.refs_1_ = bf16[2,128,256]{2,1,0:T(8,128)(2,1)S(1)} collective-permute-done((bf16[2,128,256]{2,1,0:T(8,128)(2,1)S(1)}, bf16[2,128,256]{2,1,0:T(8,128)(2,1)S(1)}, u32[]{:S(2)}, u32[]{:S(2)}) %collective-permute-start.23) | collective-permute-done | bytes 131104 | tf_op jit(solution)/shard_map/ppermute | solution.py:36
  72.2 1.9 %shard_map.109 = (f32[4,128,256]{2,1,0:T(8,128)S(1)}, f32[2,128,256]{2,1,0:T(8,128)S(1)}, f32[2,128,256]{2,1,0:T(8,128)S(1)}, bf16[64,256,128]{2,1,0:T(8,128)(2,1)S(1)}) custom-call(s32[1,256]{1,0:T(1,128)S(1)} %shard_map.95.words, bf16[2,224,128,128]{3,2,1,0:T(8,128)(2,1)S(1)} %shard_map.96.ratings, bf16[16,128,256]{2,1,0:T(8,128)(2,1)S(1)} %get-tuple-element.47.users, ...), custom_call_target="tpu_custom_call" | custom-call | flops 4000000000 | bytes 4096 | tf_op jit(solution)/shard_map/pallas_call | solution.py:229
  74.0 1.4 %collective-permute-start.28 = (f32[2,128,256]{2,1,0:T(8,128)S(1)}, f32[2,128,256]{2,1,0:T(8,128)S(1)}, u32[]{:S(2)}, u32[]{:S(2)}) collective-permute-start(f32[2,128,256]{2,1,0:T(8,128)S(1)} %get-tuple-element.57), channel_id=1, source_target_pairs={{0,4},{4,0},{8,12},{12,8},{16,20},{20,16},{24,28},{28,24},{1,5},{5... | collective-permute-start | bytes 786440 | tf_op jit(solution)/shard_map/ppermute | solution.py:36
  75.5 2.5 %shard_map.110 = (f32[4,128,256]{2,1,0:T(8,128)S(1)}, f32[2,128,256]{2,1,0:T(8,128)S(1)}, f32[2,128,256]{2,1,0:T(8,128)S(1)}, bf16[64,256,128]{2,1,0:T(8,128)(2,1)S(1)}) custom-call(s32[1,256]{1,0:T(1,128)S(1)} %shard_map.95.words, bf16[2,224,128,128]{3,2,1,0:T(8,128)(2,1)S(1)} %shard_map.96.ratings, bf16[16,128,256]{2,1,0:T(8,128)(2,1)S(1)} %get-tuple-element.47.users, ...), custom_call_target="tpu_custom_call" | custom-call | flops 4000000000 | bytes 4096 | tf_op jit(solution)/shard_map/pallas_call | solution.py:229
  78.7 1.3 %collective-permute-start.32 = (s16[528,256]{1,0:T(8,128)(2,1)S(1)}, s16[528,256]{1,0:T(8,128)(2,1)S(1)}, u32[]{:S(2)}, u32[]{:S(2)}) collective-permute-start(s16[528,256]{1,0:T(8,128)(2,1)S(1)} %shard_map.111.refs_4_), channel_id=1, source_target_pairs={{0,8},{4,12},{8,0},{12,4},{16,24},{20,28},{24,16},{28,20},{1,9},{5... | collective-permute-start | bytes 811016 | tf_op jit(solution)/shard_map/ppermute | solution.py:36
  80.0 2.1 %shard_map.112 = (f32[4,128,256]{2,1,0:T(8,128)S(1)}, f32[2,128,256]{2,1,0:T(8,128)S(1)}, f32[2,128,256]{2,1,0:T(8,128)S(1)}, bf16[64,256,128]{2,1,0:T(8,128)(2,1)S(1)}) custom-call(s32[1,256]{1,0:T(1,128)S(1)} %shard_map.95.words, bf16[2,224,128,128]{3,2,1,0:T(8,128)(2,1)S(1)} %shard_map.96.ratings, bf16[16,128,256]{2,1,0:T(8,128)(2,1)S(1)} %get-tuple-element.47.users, ...), custom_call_target="tpu_custom_call" | custom-call | flops 4000000000 | bytes 4096 | tf_op jit(solution)/shard_map/pallas_call | solution.py:229
  83.3 3.6 %collective-permute-start.35 = (s16[528,256]{1,0:T(8,128)(2,1)S(1)}, s16[528,256]{1,0:T(8,128)(2,1)S(1)}, u32[]{:S(2)}, u32[]{:S(2)}) collective-permute-start(s16[528,256]{1,0:T(8,128)(2,1)S(1)} %shard_map.115.refs_2_), channel_id=1, source_target_pairs={{0,16},{4,20},{8,24},{12,28},{16,0},{20,4},{24,8},{28,12},{1,17},{... | collective-permute-start | bytes 811016 | tf_op jit(solution)/shard_map/ppermute | solution.py:36
  87.7 3.0 %collective-permute-start.38 = (s16[528,256]{1,0:T(8,128)(2,1)S(1)}, s16[528,256]{1,0:T(8,128)(2,1)S(1)}, u32[]{:S(2)}, u32[]{:S(2)}) collective-permute-start(s16[528,256]{1,0:T(8,128)(2,1)S(1)} %shard_map.116), channel_id=1, source_target_pairs={{0,24},{4,28},{8,16},{12,20},{16,8},{20,12},{24,0},{28,4},{1,25},{... | collective-permute-start | bytes 811016 | tf_op jit(solution)/shard_map/ppermute | solution.py:36
  90.7 3.3 %shard_map.113.refs_6_.refs_4_ = f32[16,128,256]{2,1,0:T(8,128)S(1)} custom-call(s32[1,256]{1,0:T(1,128)S(1)} %shard_map.95.words, bf16[64,256,128]{2,1,0:T(8,128)(2,1)S(1)} %get-tuple-element.62.refs_0_, bf16[64,256,128]{2,1,0:T(8,128)(2,1)S(1)} %get-tuple-element.63.refs_1_, bf16[64,256,128]{2,1,0:T(8,128)(2,1)S(1)} %get-tuple-element.64.refs_2_, ...), custom_call_target="tpu_custom_call" | custom-call | flops 100000000 | bytes 4096 | tf_op jit(solution)/shard_map/pallas_call | solution.py:290
  94.0 5.4 %collective-permute-done.35.refs_1_ = s16[528,256]{1,0:T(8,128)(2,1)S(1)} collective-permute-done((s16[528,256]{1,0:T(8,128)(2,1)S(1)}, s16[528,256]{1,0:T(8,128)(2,1)S(1)}, u32[]{:S(2)}, u32[]{:S(2)}) %collective-permute-start.35) | collective-permute-done | bytes 270368 | tf_op jit(solution)/shard_map/ppermute | solution.py:36
  99.9 4.0 %shard_map.114 = (f32[16,128,256]{2,1,0:T(8,128)}, bf16[16,128,256]{2,1,0:T(8,128)(2,1)}) custom-call(s32[1,256]{1,0:T(1,128)S(1)} %shard_map.95.words, bf16[64,256,128]{2,1,0:T(8,128)(2,1)S(1)} %get-tuple-element.60.held, bf16[2,128,256]{2,1,0:T(8,128)(2,1)S(1)} %collective-permute-done.21.refs_3_.refs_0_, ...), custom_call_target="tpu_custom_call" | custom-call | flops 100000000 | bytes 4096 | tf_op jit(solution)/shard_map/pallas_call | solution.py:303
  103.9 3.9 %collective-permute-done.39.coded = s16[528,256]{1,0:T(8,128)(2,1)S(1)} collective-permute-done((s16[528,256]{1,0:T(8,128)(2,1)S(1)}, s16[528,256]{1,0:T(8,128)(2,1)S(1)}, u32[]{:S(2)}, u32[]{:S(2)}) %collective-permute-start.39) | collective-permute-done | bytes 270368 | tf_op jit(solution)/shard_map/ppermute | solution.py:31
  107.8 1.0 shard_map.118
  (96 shorter events, 15.1 us)
Async XLA Ops:
  1.7 13.9 %collective-permute-start.7 = (bf16[4,128,256]{2,1,0:T(8,128)(2,1)S(1)}, bf16[4,128,256]{2,1,0:T(8,128)(2,1)S(1)}, u32[]{:S(2)}, u32[]{:S(2)}) collective-permute-start(bf16[4,128,256]{2,1,0:T(8,128)(2,1)S(1)} %convert_element_type.7.refs_0_.refs_3_), channel_id=1, source_target_pairs={{0,4},{4,0},{8,12},{12,8},{16,20},{20,16},{24,28},{28,24},{1,5},{5... | collective-permute-start | bytes 786440 | tf_op jit(solution)/shard_map/ppermute | solution.py:36
  2.2 11.9 %collective-permute-start.2 = (bf16[4,128,256]{2,1,0:T(8,128)(2,1)S(1)}, bf16[4,128,256]{2,1,0:T(8,128)(2,1)S(1)}, u32[]{:S(2)}, u32[]{:S(2)}) collective-permute-start(bf16[4,128,256]{2,1,0:T(8,128)(2,1)S(1)} %convert_element_type.7.refs_0_.refs_3_), channel_id=1, source_target_pairs={{0,16},{4,20},{8,24},{12,28},{16,0},{20,4},{24,8},{28,12},{1,17},{... | collective-permute-start | bytes 786440 | tf_op jit(solution)/shard_map/ppermute | solution.py:36
  4.8 9.4 %collective-permute-start = (bf16[4,128,256]{2,1,0:T(8,128)(2,1)S(1)}, bf16[4,128,256]{2,1,0:T(8,128)(2,1)S(1)}, u32[]{:S(2)}, u32[]{:S(2)}) collective-permute-start(bf16[4,128,256]{2,1,0:T(8,128)(2,1)S(1)} %convert_element_type.7.refs_0_.refs_3_), channel_id=1, source_target_pairs={{0,8},{4,12},{8,0},{12,4},{16,24},{20,28},{24,16},{28,20},{1,9},{5... | collective-permute-start | bytes 786440 | tf_op jit(solution)/shard_map/ppermute | solution.py:36
  14.1 5.1 %collective-permute-start.3 = (bf16[2,128,256]{2,1,0:T(8,128)(2,1)S(1)}, bf16[2,128,256]{2,1,0:T(8,128)(2,1)S(1)}, u32[]{:S(2)}, u32[]{:S(2)}) collective-permute-start(bf16[2,128,256]{2,1,0:T(8,128)(2,1)S(1)} %slice.37), channel_id=1, source_target_pairs={{0,8},{4,12},{8,0},{12,4},{16,24},{20,28},{24,16},{28,20},{1,9},{5... | collective-permute-start | bytes 393224 | tf_op jit(solution)/shard_map/ppermute | solution.py:36
  14.2 5.1 %collective-permute-start.1 = (bf16[2,128,256]{2,1,0:T(8,128)(2,1)S(1)}, bf16[2,128,256]{2,1,0:T(8,128)(2,1)S(1)}, u32[]{:S(2)}, u32[]{:S(2)}) collective-permute-start(bf16[2,128,256]{2,1,0:T(8,128)(2,1)S(1)} %slice.36), channel_id=1, source_target_pairs={{0,16},{4,20},{8,24},{12,28},{16,0},{20,4},{24,8},{28,12},{1,17},{... | collective-permute-start | bytes 393224 | tf_op jit(solution)/shard_map/ppermute | solution.py:36
  15.1 8.6 %collective-permute-start.10 = (bf16[4,128,256]{2,1,0:T(8,128)(2,1)S(1)}, bf16[4,128,256]{2,1,0:T(8,128)(2,1)S(1)}, u32[]{:S(2)}, u32[]{:S(2)}) collective-permute-start(bf16[4,128,256]{2,1,0:T(8,128)(2,1)S(1)} %collective-permute-done.2.refs_3_.refs_0_.refs_7_), channel_id=1, source_target_pairs={{0,4},{4,0},{8,12},{12,8},{16,20},{20,16},{24,28},{28,24},{1,5},{5... | collective-permute-start | bytes 786440 | tf_op jit(solution)/shard_map/ppermute | solution.py:36
  19.3 8.9 %collective-permute-start.5 = (bf16[2,128,256]{2,1,0:T(8,128)(2,1)S(1)}, bf16[2,128,256]{2,1,0:T(8,128)(2,1)S(1)}, u32[]{:S(2)}, u32[]{:S(2)}) collective-permute-start(bf16[2,128,256]{2,1,0:T(8,128)(2,1)S(1)} %collective-permute-done.3.refs_4_.refs_1_), channel_id=1, source_target_pairs={{0,4},{4,0},{8,12},{12,8},{16,20},{20,16},{24,28},{28,24},{1,5},{5... | collective-permute-start | bytes 393224 | tf_op jit(solution)/shard_map/ppermute | solution.py:36
  19.4 8.8 %collective-permute-start.4 = (bf16[2,128,256]{2,1,0:T(8,128)(2,1)S(1)}, bf16[2,128,256]{2,1,0:T(8,128)(2,1)S(1)}, u32[]{:S(2)}, u32[]{:S(2)}) collective-permute-start(bf16[2,128,256]{2,1,0:T(8,128)(2,1)S(1)} %collective-permute-done.1.refs_3_.refs_0_), channel_id=1, source_target_pairs={{0,4},{4,0},{8,12},{12,8},{16,20},{20,16},{24,28},{28,24},{1,5},{5... | collective-permute-start | bytes 393224 | tf_op jit(solution)/shard_map/ppermute | solution.py:36
  23.2 4.7 %collective-permute-start.9 = (f32[2,128,256]{2,1,0:T(8,128)S(1)}, f32[2,128,256]{2,1,0:T(8,128)S(1)}, u32[]{:S(2)}, u32[]{:S(2)}) collective-permute-start(f32[2,128,256]{2,1,0:T(8,128)S(1)} %get-tuple-element.41), channel_id=1, source_target_pairs={{0,4},{4,0},{8,12},{12,8},{16,20},{20,16},{24,28},{28,24},{1,5},{5... | collective-permute-start | bytes 786440 | tf_op jit(solution)/shard_map/ppermute | solution.py:36
  27.4 5.1 %collective-permute-start.13 = (f32[2,128,256]{2,1,0:T(8,128)S(1)}, f32[2,128,256]{2,1,0:T(8,128)S(1)}, u32[]{:S(2)}, u32[]{:S(2)}) collective-permute-start(f32[2,128,256]{2,1,0:T(8,128)S(1)} %get-tuple-element.49), channel_id=1, source_target_pairs={{0,4},{4,0},{8,12},{12,8},{16,20},{20,16},{24,28},{28,24},{1,5},{5... | collective-permute-start | bytes 786440 | tf_op jit(solution)/shard_map/ppermute | solution.py:36
  27.4 5.1 %collective-permute-start.14 = (f32[2,128,256]{2,1,0:T(8,128)S(1)}, f32[2,128,256]{2,1,0:T(8,128)S(1)}, u32[]{:S(2)}, u32[]{:S(2)}) collective-permute-start(f32[2,128,256]{2,1,0:T(8,128)S(1)} %get-tuple-element.50), channel_id=1, source_target_pairs={{0,4},{4,0},{8,12},{12,8},{16,20},{20,16},{24,28},{28,24},{1,5},{5... | collective-permute-start | bytes 786440 | tf_op jit(solution)/shard_map/ppermute | solution.py:36
  28.1 8.5 %collective-permute-start.12 = (s16[528,256]{1,0:T(8,128)(2,1)S(1)}, s16[528,256]{1,0:T(8,128)(2,1)S(1)}, u32[]{:S(2)}, u32[]{:S(2)}) collective-permute-start(s16[528,256]{1,0:T(8,128)(2,1)S(1)} %shard_map.101.refs_4_), channel_id=1, source_target_pairs={{0,8},{4,12},{8,0},{12,4},{16,24},{20,28},{24,16},{28,20},{1,9},{5... | collective-permute-start | bytes 811016 | tf_op jit(solution)/shard_map/ppermute | solution.py:36
  32.4 11.5 %collective-permute-start.11 = (f32[4,128,256]{2,1,0:T(8,128)S(1)}, f32[4,128,256]{2,1,0:T(8,128)S(1)}, u32[]{:S(2)}, u32[]{:S(2)}) collective-permute-start(f32[4,128,256]{2,1,0:T(8,128)S(1)} %get-tuple-element.48), channel_id=1, source_target_pairs={{0,4},{4,0},{8,12},{12,8},{16,20},{20,16},{24,28},{28,24},{1,5},{5... | collective-permute-start | bytes 1572872 | tf_op jit(solution)/shard_map/ppermute | solution.py:36
  32.7 14.7 %collective-permute-start.15 = (s16[528,256]{1,0:T(8,128)(2,1)S(1)}, s16[528,256]{1,0:T(8,128)(2,1)S(1)}, u32[]{:S(2)}, u32[]{:S(2)}) collective-permute-start(s16[528,256]{1,0:T(8,128)(2,1)S(1)} %shard_map.105.refs_2_), channel_id=1, source_target_pairs={{0,16},{4,20},{8,24},{12,28},{16,0},{20,4},{24,8},{28,12},{1,17},{... | collective-permute-start | bytes 811016 | tf_op jit(solution)/shard_map/ppermute | solution.py:36
  36.8 10.6 %collective-permute-start.18 = (s16[528,256]{1,0:T(8,128)(2,1)S(1)}, s16[528,256]{1,0:T(8,128)(2,1)S(1)}, u32[]{:S(2)}, u32[]{:S(2)}) collective-permute-start(s16[528,256]{1,0:T(8,128)(2,1)S(1)} %shard_map.106), channel_id=1, source_target_pairs={{0,24},{4,28},{8,16},{12,20},{16,8},{20,12},{24,0},{28,4},{1,25},{... | collective-permute-start | bytes 811016 | tf_op jit(solution)/shard_map/ppermute | solution.py:36
  47.8 9.7 %collective-permute-start.19 = (bf16[4,128,256]{2,1,0:T(8,128)(2,1)S(1)}, bf16[4,128,256]{2,1,0:T(8,128)(2,1)S(1)}, u32[]{:S(2)}, u32[]{:S(2)}) collective-permute-start(bf16[4,128,256]{2,1,0:T(8,128)(2,1)S(1)} %get-tuple-element.54), channel_id=1, source_target_pairs={{0,1},{1,2},{2,3},{3,0},{4,5},{5,6},{6,7},{7,4},{8,9},{9,10},{10,1... | collective-permute-start | bytes 786440 | tf_op jit(solution)/shard_map/ppermute | solution.py:31
  57.5 11.1 %collective-permute-start.27 = (bf16[4,128,256]{2,1,0:T(8,128)(2,1)S(1)}, bf16[4,128,256]{2,1,0:T(8,128)(2,1)S(1)}, u32[]{:S(2)}, u32[]{:S(2)}) collective-permute-start(bf16[4,128,256]{2,1,0:T(8,128)(2,1)S(1)} %collective-permute-done.19.refs_0_.refs_3_), channel_id=1, source_target_pairs={{0,4},{4,0},{8,12},{12,8},{16,20},{20,16},{24,28},{28,24},{1,5},{5... | collective-permute-start | bytes 786440 | tf_op jit(solution)/shard_map/ppermute | solution.py:36
  57.5 8.7 %collective-permute-start.22 = (bf16[4,128,256]{2,1,0:T(8,128)(2,1)S(1)}, bf16[4,128,256]{2,1,0:T(8,128)(2,1)S(1)}, u32[]{:S(2)}, u32[]{:S(2)}) collective-permute-start(bf16[4,128,256]{2,1,0:T(8,128)(2,1)S(1)} %collective-permute-done.19.refs_0_.refs_3_), channel_id=1, source_target_pairs={{0,16},{4,20},{8,24},{12,28},{16,0},{20,4},{24,8},{28,12},{1,17},{... | collective-permute-start | bytes 786440 | tf_op jit(solution)/shard_map/ppermute | solution.py:36
  57.9 9.2 %collective-permute-start.20 = (bf16[4,128,256]{2,1,0:T(8,128)(2,1)S(1)}, bf16[4,128,256]{2,1,0:T(8,128)(2,1)S(1)}, u32[]{:S(2)}, u32[]{:S(2)}) collective-permute-start(bf16[4,128,256]{2,1,0:T(8,128)(2,1)S(1)} %collective-permute-done.19.refs_0_.refs_3_), channel_id=1, source_target_pairs={{0,8},{4,12},{8,0},{12,4},{16,24},{20,28},{24,16},{28,20},{1,9},{5... | collective-permute-start | bytes 786440 | tf_op jit(solution)/shard_map/ppermute | solution.py:36
  66.2 5.2 %collective-permute-start.23 = (bf16[2,128,256]{2,1,0:T(8,128)(2,1)S(1)}, bf16[2,128,256]{2,1,0:T(8,128)(2,1)S(1)}, u32[]{:S(2)}, u32[]{:S(2)}) collective-permute-start(bf16[2,128,256]{2,1,0:T(8,128)(2,1)S(1)} %slice.39), channel_id=1, source_target_pairs={{0,8},{4,12},{8,0},{12,4},{16,24},{20,28},{24,16},{28,20},{1,9},{5... | collective-permute-start | bytes 393224 | tf_op jit(solution)/shard_map/ppermute | solution.py:36
  67.1 5.0 %collective-permute-start.21 = (bf16[2,128,256]{2,1,0:T(8,128)(2,1)S(1)}, bf16[2,128,256]{2,1,0:T(8,128)(2,1)S(1)}, u32[]{:S(2)}, u32[]{:S(2)}) collective-permute-start(bf16[2,128,256]{2,1,0:T(8,128)(2,1)S(1)} %slice.38), channel_id=1, source_target_pairs={{0,16},{4,20},{8,24},{12,28},{16,0},{20,4},{24,8},{28,12},{1,17},{... | collective-permute-start | bytes 393224 | tf_op jit(solution)/shard_map/ppermute | solution.py:36
  68.0 7.4 %collective-permute-start.30 = (bf16[4,128,256]{2,1,0:T(8,128)(2,1)S(1)}, bf16[4,128,256]{2,1,0:T(8,128)(2,1)S(1)}, u32[]{:S(2)}, u32[]{:S(2)}) collective-permute-start(bf16[4,128,256]{2,1,0:T(8,128)(2,1)S(1)} %collective-permute-done.22.refs_3_.refs_0_.refs_7_), channel_id=1, source_target_pairs={{0,4},{4,0},{8,12},{12,8},{16,20},{20,16},{24,28},{28,24},{1,5},{5... | collective-permute-start | bytes 786440 | tf_op jit(solution)/shard_map/ppermute | solution.py:36
  71.4 8.5 %collective-permute-start.25 = (bf16[2,128,256]{2,1,0:T(8,128)(2,1)S(1)}, bf16[2,128,256]{2,1,0:T(8,128)(2,1)S(1)}, u32[]{:S(2)}, u32[]{:S(2)}) collective-permute-start(bf16[2,128,256]{2,1,0:T(8,128)(2,1)S(1)} %collective-permute-done.23.refs_4_.refs_1_), channel_id=1, source_target_pairs={{0,4},{4,0},{8,12},{12,8},{16,20},{20,16},{24,28},{28,24},{1,5},{5... | collective-permute-start | bytes 393224 | tf_op jit(solution)/shard_map/ppermute | solution.py:36
  72.2 7.8 %collective-permute-start.24 = (bf16[2,128,256]{2,1,0:T(8,128)(2,1)S(1)}, bf16[2,128,256]{2,1,0:T(8,128)(2,1)S(1)}, u32[]{:S(2)}, u32[]{:S(2)}) collective-permute-start(bf16[2,128,256]{2,1,0:T(8,128)(2,1)S(1)} %collective-permute-done.21.refs_3_.refs_0_), channel_id=1, source_target_pairs={{0,4},{4,0},{8,12},{12,8},{16,20},{20,16},{24,28},{28,24},{1,5},{5... | collective-permute-start | bytes 393224 | tf_op jit(solution)/shard_map/ppermute | solution.py:36
  77.9 4.8 %collective-permute-start.33 = (f32[2,128,256]{2,1,0:T(8,128)S(1)}, f32[2,128,256]{2,1,0:T(8,128)S(1)}, u32[]{:S(2)}, u32[]{:S(2)}) collective-permute-start(f32[2,128,256]{2,1,0:T(8,128)S(1)} %get-tuple-element.67), channel_id=1, source_target_pairs={{0,4},{4,0},{8,12},{12,8},{16,20},{20,16},{24,28},{28,24},{1,5},{5... | collective-permute-start | bytes 786440 | tf_op jit(solution)/shard_map/ppermute | solution.py:36
  78.4 4.7 %collective-permute-start.34 = (f32[2,128,256]{2,1,0:T(8,128)S(1)}, f32[2,128,256]{2,1,0:T(8,128)S(1)}, u32[]{:S(2)}, u32[]{:S(2)}) collective-permute-start(f32[2,128,256]{2,1,0:T(8,128)S(1)} %get-tuple-element.68), channel_id=1, source_target_pairs={{0,4},{4,0},{8,12},{12,8},{16,20},{20,16},{24,28},{28,24},{1,5},{5... | collective-permute-start | bytes 786440 | tf_op jit(solution)/shard_map/ppermute | solution.py:36
  78.7 8.9 %collective-permute-start.32 = (s16[528,256]{1,0:T(8,128)(2,1)S(1)}, s16[528,256]{1,0:T(8,128)(2,1)S(1)}, u32[]{:S(2)}, u32[]{:S(2)}) collective-permute-start(s16[528,256]{1,0:T(8,128)(2,1)S(1)} %shard_map.111.refs_4_), channel_id=1, source_target_pairs={{0,8},{4,12},{8,0},{12,4},{16,24},{20,28},{24,16},{28,20},{1,9},{5... | collective-permute-start | bytes 811016 | tf_op jit(solution)/shard_map/ppermute | solution.py:36
  82.0 4.9 %collective-permute-start.36 = (f32[2,128,256]{2,1,0:T(8,128)S(1)}, f32[2,128,256]{2,1,0:T(8,128)S(1)}, u32[]{:S(2)}, u32[]{:S(2)}) collective-permute-start(f32[2,128,256]{2,1,0:T(8,128)S(1)} %get-tuple-element.70), channel_id=1, source_target_pairs={{0,4},{4,0},{8,12},{12,8},{16,20},{20,16},{24,28},{28,24},{1,5},{5... | collective-permute-start | bytes 786440 | tf_op jit(solution)/shard_map/ppermute | solution.py:36
  82.7 11.3 %collective-permute-start.31 = (f32[4,128,256]{2,1,0:T(8,128)S(1)}, f32[4,128,256]{2,1,0:T(8,128)S(1)}, u32[]{:S(2)}, u32[]{:S(2)}) collective-permute-start(f32[4,128,256]{2,1,0:T(8,128)S(1)} %get-tuple-element.66), channel_id=1, source_target_pairs={{0,4},{4,0},{8,12},{12,8},{16,20},{20,16},{24,28},{28,24},{1,5},{5... | collective-permute-start | bytes 1572872 | tf_op jit(solution)/shard_map/ppermute | solution.py:36
  83.3 16.1 %collective-permute-start.35 = (s16[528,256]{1,0:T(8,128)(2,1)S(1)}, s16[528,256]{1,0:T(8,128)(2,1)S(1)}, u32[]{:S(2)}, u32[]{:S(2)}) collective-permute-start(s16[528,256]{1,0:T(8,128)(2,1)S(1)} %shard_map.115.refs_2_), channel_id=1, source_target_pairs={{0,16},{4,20},{8,24},{12,28},{16,0},{20,4},{24,8},{28,12},{1,17},{... | collective-permute-start | bytes 811016 | tf_op jit(solution)/shard_map/ppermute | solution.py:36
  87.7 11.7 %collective-permute-start.38 = (s16[528,256]{1,0:T(8,128)(2,1)S(1)}, s16[528,256]{1,0:T(8,128)(2,1)S(1)}, u32[]{:S(2)}, u32[]{:S(2)}) collective-permute-start(s16[528,256]{1,0:T(8,128)(2,1)S(1)} %shard_map.116), channel_id=1, source_target_pairs={{0,24},{4,28},{8,16},{12,20},{16,8},{20,12},{24,0},{28,4},{1,25},{... | collective-permute-start | bytes 811016 | tf_op jit(solution)/shard_map/ppermute | solution.py:36
  99.8 8.0 %collective-permute-start.39 = (s16[528,256]{1,0:T(8,128)(2,1)S(1)}, s16[528,256]{1,0:T(8,128)(2,1)S(1)}, u32[]{:S(2)}, u32[]{:S(2)}) collective-permute-start(s16[528,256]{1,0:T(8,128)(2,1)S(1)} %shard_map.117), channel_id=1, source_target_pairs={{0,3},{1,0},{2,1},{3,2},{4,7},{5,4},{6,5},{7,6},{8,11},{9,8},{10,9... | collective-permute-start | bytes 811016 | tf_op jit(solution)/shard_map/ppermute | solution.py:31
  (16 other events, 84.2 us)

commit v5 on v4

--- a/solution.py
+++ b/solution.py
@@ -384,6 +384,10 @@
         new_bf[t] = after.astype(jnp.bfloat16)
 
 
+def pass_kernel(given, *refs):
+    refs[-1][...] = given[...]
+
+
 def in_vmem(kernel, out_shape, *operands, after=()):
     return pl.pallas_call(
         kernel,
@@ -396,10 +400,10 @@
 
 
 def gathered(own, runs):
-    evens = [[own]] + [[swapped(own, "user", 2 * d)] for d in range(1, 3 if runs == 4 else runs)]
-    if runs == 4:
-        half = own.shape[0] // 2
-        evens.append([swapped(evens[1][0][:half], "user", 4), swapped(evens[2][0][half:], "user", 2)])
+    evens = [own]
+    for d in range(1, runs):
+        relayed = runs == 4 and d == 3
+        evens.append(swapped(evens[1] if relayed else own, "user", 4 if relayed else 2 * d))
     return evens
 
 
@@ -432,28 +436,32 @@
     items_bf = items.astype(jnp.bfloat16)
     users_bf = users.astype(jnp.bfloat16)
     for section in range(sections):
-        sent = shifted(items_bf, "item", section) if section else items_bf
+        words = pair_plan(section, bits, per, span, runs, side, me, counts, tile_rows, tile_cols)
+        sent = items_bf
+        if section:
+            sent = shifted(items_bf, "item", section)
+            sent = in_vmem(pass_kernel, jax.ShapeDtypeStruct(sent.shape, sent.dtype), sent, after=(users_bf, words))
         evens = gathered(sent, runs)
-        chunks = [even + [swapped(piece, "user", 1) for piece in even] for even in evens]
-        words = pair_plan(section, bits, per, span, runs, side, me, counts, tile_rows, tile_cols)
-        mine, other, sums, misfits = [], [], [], []
-        after = []
-        for run in range(runs):
-            if run in (1, 2):
-                after += evens[run + 1]
-            even_grad, odd_grads, held = item_grads(
-                section, run, per, bits, words, rated, users_bf, chunks[run], after, 2 if run else 1
-            )
-            misfits.append(held)
-            mine.append(even_grad)
-            other.append([swapped(grad, "user", 1) for grad in odd_grads])
-            after = [even_grad]
-            if run >= 2:
-                coded = join(mine[run - 1], other[run - 1], after)
-                sums.append(swapped(coded, "user", 2 * (run - 1)))
-                after = [coded]
-        coded = join(mine[-1], other[-1], after + sums[:1])
-        sums.append(swapped(coded, "user", 2 * (runs - 1)))
+        chunks = [[even, swapped(even, "user", 1)] for even in evens]
+        mine, other, sums, misfits = {}, {}, {}, {}
+        after = [evens[2]]
+        order = [(item_grads, run) for run in range(1, runs - 1)]
+        order += [(join, run) for run in range(1, runs - 1)]
+        order += [(item_grads, 0), (item_grads, runs - 1), (join, runs - 1)]
+        for call, run in order:
+            if call is item_grads:
+                mine[run], odd_grads, misfits[run] = item_grads(
+                    section, run, per, bits, words, rated, users_bf, chunks[run], after, 2 if run else 1
+                )
+                other[run] = [swapped(grad, "user", 1) for grad in odd_grads]
+                after = [mine[run]]
+            else:
+                if run == runs - 1:
+                    after += list(sums.values())
+                after = [join(mine[run], other[run], after)]
+                sums[run] = swapped(after[0], "user", 2 * run)
+        sums = [sums[run] for run in range(1, runs)]
+        misfits = [misfits[run] for run in range(runs)]
         head = [piece for chunk in chunks[:-1] for piece in chunk]
         partial = users_head(bits, words, misfits[:-1], head, users.shape)
         if section == 0:

time: 109 us -> 100 us (0.917)
  Pallas kernels: 49.1 us -> 34.8 us
  starting transfers between devices: 25.8 us -> 29.9 us
  waiting for transfers between devices: 29.1 us -> 30.8 us
    pallas_call x8, Pallas kernels: 22.2 us -> 15.2 us  [item_grads(): pl.pallas_call(functools.partial(items_kernel, section, run, len(pieces),...]
    ppermute x38 -> x34, waiting for transfers between devices: 18.2 us -> 22.8 us  [swapped(): return lax.ppermute(x, axis, [(i, i ^ mask) for i in range(peers)])]
    pallas_call x2, Pallas kernels: 10.3 us -> 5.93 us  [users_head(): pl.pallas_call(functools.partial(users_head_kernel, bits, len(misfits)),...]
    ppermute x2, waiting for transfers between devices: 11 us -> 8.06 us  [shifted(): return lax.ppermute(x, axis, [(i, (i + by) % peers) for i in range(peers)])]
    ppermute x38 -> x34, starting transfers between devices: 23.2 us -> 25.4 us  [swapped(): return lax.ppermute(x, axis, [(i, i ^ mask) for i in range(peers)])]
    ppermute x2, starting transfers between devices: 2.57 us -> 4.47 us  [shifted(): return lax.ppermute(x, axis, [(i, (i + by) % peers) for i in range(peers)])]
    pallas_call x1, Pallas kernels: 4.35 us -> 2.64 us  [fetch(): pl.pallas_call(functools.partial(fetch_kernel, lump), out_shape=jax.Shape...]
    pallas_call x2, Pallas kernels: 7.57 us -> 6.31 us  [users_tail(): pl.pallas_call(functools.partial(users_tail_kernel, power, bits, first_ru...]
  transfers between devices with their start and end apart: 40 -> 36, of which waited for: 11 -> 15; matrix products, arithmetic and copies ran while one was open for 2% -> 2% of each run, Pallas kernels for 43% -> 33%
where the time goes in v5:
time: 100 us
  Pallas kernels  34.8 us (35%)
  waiting for transfers between devices  30.8 us (31%)
  starting transfers between devices  29.9 us (30%)
  other arithmetic  2.78 us (3%)
    ppermute x34, starting transfers between devices, swapped(): return lax.ppermute(x, axis, [(i, i ^ mask) for i in range(peers)])  25.4 us
    ppermute x34, waiting for transfers between devices, swapped(): return lax.ppermute(x, axis, [(i, i ^ mask) for i in range(peers)])  22.8 us
    pallas_call x8, Pallas kernels, item_grads(): pl.pallas_call(functools.partial(items_kernel, section, run, len(pieces),...  15.2 us
    ppermute x2, waiting for transfers between devices, shifted(): return lax.ppermute(x, axis, [(i, (i + by) % peers) for i in range(peers)])  8.06 us
    pallas_call x2, Pallas kernels, users_tail(): pl.pallas_call(functools.partial(users_tail_kernel, power, bits, first_ru...  6.31 us
    pallas_call x2, Pallas kernels, users_head(): pl.pallas_call(functools.partial(users_head_kernel, bits, len(misfits)),...  5.93 us
    ppermute x2, starting transfers between devices, shifted(): return lax.ppermute(x, axis, [(i, (i + by) % peers) for i in range(peers)])  4.47 us
    pallas_call x1, Pallas kernels, fetch(): pl.pallas_call(functools.partial(fetch_kernel, lump), out_shape=jax.Shape...  2.64 us
  transfers between devices with their start and end apart: 36, of which 15 were waited for; matrix products, arithmetic and copies ran while one was open for 2% of the time, Pallas kernels for 33%

profile of v5, /device:TPU:0, one launch (start us, length us, event | category | flops | bytes accessed | tf_op | source)
XLA Modules:
  0.0 100.1 jit_solution(15322940476746473069)
XLA Ops:
  1.7 3.0 %collective-permute-start.4 = (bf16[4,128,256]{2,1,0:T(8,128)(2,1)S(1)}, bf16[4,128,256]{2,1,0:T(8,128)(2,1)S(1)}, u32[]{:S(2)}, u32[]{:S(2)}) collective-permute-start(bf16[4,128,256]{2,1,0:T(8,128)(2,1)S(1)} %convert_element_type.7.refs_0_.refs_3_), channel_id=1, source_target_pairs={{0,16},{4,20},{8,24},{12,28},{16,0},{20,4},{24,8},{28,12},{1,17},{... | collective-permute-start | bytes 786440 | tf_op jit(solution)/shard_map/ppermute | solution.py:36
  4.7 1.5 %collective-permute-start = (bf16[4,128,256]{2,1,0:T(8,128)(2,1)S(1)}, bf16[4,128,256]{2,1,0:T(8,128)(2,1)S(1)}, u32[]{:S(2)}, u32[]{:S(2)}) collective-permute-start(bf16[4,128,256]{2,1,0:T(8,128)(2,1)S(1)} %convert_element_type.7.refs_0_.refs_3_), channel_id=1, source_target_pairs={{0,8},{4,12},{8,0},{12,4},{16,24},{20,28},{24,16},{28,20},{1,9},{5... | collective-permute-start | bytes 786440 | tf_op jit(solution)/shard_map/ppermute | solution.py:36
  6.2 1.7 %convert_element_type.6.users = bf16[16,128,256]{2,1,0:T(8,128)(2,1)S(1)} convert(f32[16,128,256]{2,1,0:T(8,128)} %bitcast.11) | non-fusion elementwise | flops 524288 | bytes 3145728 | tf_op jit(solution)/shard_map/convert_element_type | solution.py:437
  8.6 2.6 %shard_map.96.ratings = bf16[2,224,128,128]{3,2,1,0:T(8,128)(2,1)S(1)} custom-call(s32[2]{0:T(128)S(1)} %bitcast.19, bf16[2,224,128,128]{3,2,1,0:T(8,128)(2,1)} %bitcast.22), custom_call_target="tpu_custom_call" | custom-call | flops 4000000000 | bytes 4096 | tf_op jit(solution)/shard_map/pallas_call | solution.py:147
  11.3 1.2 %collective-permute-done.refs_0_.refs_5_ = bf16[4,128,256]{2,1,0:T(8,128)(2,1)S(1)} collective-permute-done((bf16[4,128,256]{2,1,0:T(8,128)(2,1)S(1)}, bf16[4,128,256]{2,1,0:T(8,128)(2,1)S(1)}, u32[]{:S(2)}, u32[]{:S(2)}) %collective-permute-start) | collective-permute-done | bytes 262176 | tf_op jit(solution)/shard_map/ppermute | solution.py:36
  14.2 2.1 %shard_map.98 = (f32[4,128,256]{2,1,0:T(8,128)S(1)}, f32[2,128,256]{2,1,0:T(8,128)S(1)}, f32[2,128,256]{2,1,0:T(8,128)S(1)}, bf16[64,256,128]{2,1,0:T(8,128)(2,1)S(1)}) custom-call(s32[1,256]{1,0:T(1,128)S(1)} %shard_map.97.words, bf16[2,224,128,128]{3,2,1,0:T(8,128)(2,1)S(1)} %shard_map.96.ratings, bf16[16,128,256]{2,1,0:T(8,128)(2,1)S(1)} %convert_element_type.6.users, ...), custom_call_target="tpu_custom_call" | custom-call | flops 4000000000 | bytes 4096 | tf_op jit(solution)/shard_map/pallas_call | solution.py:229
  16.9 1.7 %shard_map.99 = (f32[4,128,256]{2,1,0:T(8,128)S(1)}, f32[2,128,256]{2,1,0:T(8,128)S(1)}, f32[2,128,256]{2,1,0:T(8,128)S(1)}, bf16[64,256,128]{2,1,0:T(8,128)(2,1)S(1)}) custom-call(s32[1,256]{1,0:T(1,128)S(1)} %shard_map.97.words, bf16[2,224,128,128]{3,2,1,0:T(8,128)(2,1)S(1)} %shard_map.96.ratings, bf16[16,128,256]{2,1,0:T(8,128)(2,1)S(1)} %convert_element_type.6.users, ...), custom_call_target="tpu_custom_call" | custom-call | flops 4000000000 | bytes 4096 | tf_op jit(solution)/shard_map/pallas_call | solution.py:229
  19.2 3.2 %collective-permute-done.1.refs_0_ = bf16[4,128,256]{2,1,0:T(8,128)(2,1)S(1)} collective-permute-done((bf16[4,128,256]{2,1,0:T(8,128)(2,1)S(1)}, bf16[4,128,256]{2,1,0:T(8,128)(2,1)S(1)}, u32[]{:S(2)}, u32[]{:S(2)}) %collective-permute-start.1) | collective-permute-done | bytes 262176 | tf_op jit(solution)/shard_map/ppermute | solution.py:36
  23.0 1.6 %collective-permute-start.12 = (s16[528,256]{1,0:T(8,128)(2,1)S(1)}, s16[528,256]{1,0:T(8,128)(2,1)S(1)}, u32[]{:S(2)}, u32[]{:S(2)}) collective-permute-start(s16[528,256]{1,0:T(8,128)(2,1)S(1)} %shard_map.100.refs_2_), channel_id=1, source_target_pairs={{0,8},{4,12},{8,0},{12,4},{16,24},{20,28},{24,16},{28,20},{1,9},{5... | collective-permute-start | bytes 811016 | tf_op jit(solution)/shard_map/ppermute | solution.py:36
  25.3 2.1 %shard_map.102 = (f32[4,128,256]{2,1,0:T(8,128)S(1)}, f32[4,128,256]{2,1,0:T(8,128)S(1)}, bf16[64,256,128]{2,1,0:T(8,128)(2,1)S(1)}) custom-call(s32[1,256]{1,0:T(1,128)S(1)} %shard_map.97.words, bf16[2,224,128,128]{3,2,1,0:T(8,128)(2,1)S(1)} %shard_map.96.ratings, bf16[16,128,256]{2,1,0:T(8,128)(2,1)S(1)} %convert_element_type.6.users, ...), custom_call_target="tpu_custom_call" | custom-call | flops 4000000000 | bytes 4096 | tf_op jit(solution)/shard_map/pallas_call | solution.py:229
  27.4 2.5 %shard_map.103 = (f32[4,128,256]{2,1,0:T(8,128)S(1)}, f32[2,128,256]{2,1,0:T(8,128)S(1)}, f32[2,128,256]{2,1,0:T(8,128)S(1)}, bf16[64,256,128]{2,1,0:T(8,128)(2,1)S(1)}) custom-call(s32[1,256]{1,0:T(1,128)S(1)} %shard_map.97.words, bf16[2,224,128,128]{3,2,1,0:T(8,128)(2,1)S(1)} %shard_map.96.ratings, bf16[16,128,256]{2,1,0:T(8,128)(2,1)S(1)} %convert_element_type.6.users, ...), custom_call_target="tpu_custom_call" | custom-call | flops 4000000000 | bytes 4096 | tf_op jit(solution)/shard_map/pallas_call | solution.py:229
  33.7 3.3 %shard_map.104.refs_4_.refs_5_ = f32[16,128,256]{2,1,0:T(8,128)S(1)} custom-call(s32[1,256]{1,0:T(1,128)S(1)} %shard_map.97.words, bf16[64,256,128]{2,1,0:T(8,128)(2,1)S(1)} %get-tuple-element.46.refs_0_, bf16[64,256,128]{2,1,0:T(8,128)(2,1)S(1)} %get-tuple-element.47.refs_1_, bf16[64,256,128]{2,1,0:T(8,128)(2,1)S(1)} %get-tuple-element.48.refs_2_, ...), custom_call_target="tpu_custom_call" | custom-call | flops 100000000 | bytes 4096 | tf_op jit(solution)/shard_map/pallas_call | solution.py:290
  37.0 4.5 %collective-permute-done.16.refs_2_ = s16[528,256]{1,0:T(8,128)(2,1)S(1)} collective-permute-done((s16[528,256]{1,0:T(8,128)(2,1)S(1)}, s16[528,256]{1,0:T(8,128)(2,1)S(1)}, u32[]{:S(2)}, u32[]{:S(2)}) %collective-permute-start.16) | collective-permute-done | bytes 270368 | tf_op jit(solution)/shard_map/ppermute | solution.py:36
  41.9 1.4 %collective-permute-start.17 = (bf16[4,128,256]{2,1,0:T(8,128)(2,1)S(1)}, bf16[4,128,256]{2,1,0:T(8,128)(2,1)S(1)}, u32[]{:S(2)}, u32[]{:S(2)}) collective-permute-start(bf16[4,128,256]{2,1,0:T(8,128)(2,1)S(1)} %get-tuple-element.54), channel_id=1, source_target_pairs={{0,1},{1,2},{2,3},{3,0},{4,5},{5,6},{6,7},{7,4},{8,9},{9,10},{10,1... | collective-permute-start | bytes 786440 | tf_op jit(solution)/shard_map/ppermute | solution.py:31
  44.3 2.6 %shard_map.105 = (f32[16,128,256]{2,1,0:T(8,128)S(1)}, bf16[16,128,256]{2,1,0:T(8,128)(2,1)S(1)}) custom-call(s32[1,256]{1,0:T(1,128)S(1)} %shard_map.97.words, bf16[64,256,128]{2,1,0:T(8,128)(2,1)S(1)} %get-tuple-element.45.held, bf16[4,128,256]{2,1,0:T(8,128)(2,1)S(1)} %collective-permute-done.1.refs_0_, ...), custom_call_target="tpu_custom_call" | custom-call | flops 100000000 | bytes 4096 | tf_op jit(solution)/shard_map/pallas_call | solution.py:303
  46.9 6.3 %collective-permute-done.17.given = bf16[4,128,256]{2,1,0:T(8,128)(2,1)S(1)} collective-permute-done((bf16[4,128,256]{2,1,0:T(8,128)(2,1)S(1)}, bf16[4,128,256]{2,1,0:T(8,128)(2,1)S(1)}, u32[]{:S(2)}, u32[]{:S(2)}) %collective-permute-start.17) | collective-permute-done | bytes 262176 | tf_op jit(solution)/shard_map/ppermute | solution.py:31
  54.4 1.8 %collective-permute-start.22 = (bf16[4,128,256]{2,1,0:T(8,128)(2,1)S(1)}, bf16[4,128,256]{2,1,0:T(8,128)(2,1)S(1)}, u32[]{:S(2)}, u32[]{:S(2)}) collective-permute-start(bf16[4,128,256]{2,1,0:T(8,128)(2,1)S(1)} %shard_map.108.refs_0_.refs_3_), channel_id=1, source_target_pairs={{0,16},{4,20},{8,24},{12,28},{16,0},{20,4},{24,8},{28,12},{1,17},{... | collective-permute-start | bytes 786440 | tf_op jit(solution)/shard_map/ppermute | solution.py:36
  56.2 4.4 %collective-permute-done.18.refs_0_.refs_5_ = bf16[4,128,256]{2,1,0:T(8,128)(2,1)S(1)} collective-permute-done((bf16[4,128,256]{2,1,0:T(8,128)(2,1)S(1)}, bf16[4,128,256]{2,1,0:T(8,128)(2,1)S(1)}, u32[]{:S(2)}, u32[]{:S(2)}) %collective-permute-start.18) | collective-permute-done | bytes 262176 | tf_op jit(solution)/shard_map/ppermute | solution.py:36
  62.1 1.7 %shard_map.109 = (f32[4,128,256]{2,1,0:T(8,128)S(1)}, f32[2,128,256]{2,1,0:T(8,128)S(1)}, f32[2,128,256]{2,1,0:T(8,128)S(1)}, bf16[64,256,128]{2,1,0:T(8,128)(2,1)S(1)}) custom-call(s32[1,256]{1,0:T(1,128)S(1)} %shard_map.95.refs_1_.words, bf16[2,224,128,128]{3,2,1,0:T(8,128)(2,1)S(1)} %shard_map.96.ratings, ...), custom_call_target="tpu_custom_call" | custom-call | flops 4000000000 | bytes 4096 | tf_op jit(solution)/shard_map/pallas_call | solution.py:229
  63.8 1.4 %collective-permute-start.27 = (f32[2,128,256]{2,1,0:T(8,128)S(1)}, f32[2,128,256]{2,1,0:T(8,128)S(1)}, u32[]{:S(2)}, u32[]{:S(2)}) collective-permute-start(f32[2,128,256]{2,1,0:T(8,128)S(1)} %get-tuple-element.59), channel_id=1, source_target_pairs={{0,4},{4,0},{8,12},{12,8},{16,20},{20,16},{24,28},{28,24},{1,5},{5... | collective-permute-start | bytes 786440 | tf_op jit(solution)/shard_map/ppermute | solution.py:36
  65.3 1.9 %shard_map.110 = (f32[4,128,256]{2,1,0:T(8,128)S(1)}, f32[2,128,256]{2,1,0:T(8,128)S(1)}, f32[2,128,256]{2,1,0:T(8,128)S(1)}, bf16[64,256,128]{2,1,0:T(8,128)(2,1)S(1)}) custom-call(s32[1,256]{1,0:T(1,128)S(1)} %shard_map.95.refs_1_.words, bf16[2,224,128,128]{3,2,1,0:T(8,128)(2,1)S(1)} %shard_map.96.ratings, ...), custom_call_target="tpu_custom_call" | custom-call | flops 4000000000 | bytes 4096 | tf_op jit(solution)/shard_map/pallas_call | solution.py:229
  67.1 1.3 %collective-permute-start.25 = (f32[2,128,256]{2,1,0:T(8,128)S(1)}, f32[2,128,256]{2,1,0:T(8,128)S(1)}, u32[]{:S(2)}, u32[]{:S(2)}) collective-permute-start(f32[2,128,256]{2,1,0:T(8,128)S(1)} %get-tuple-element.57), channel_id=1, source_target_pairs={{0,4},{4,0},{8,12},{12,8},{16,20},{20,16},{24,28},{28,24},{1,5},{5... | collective-permute-start | bytes 786440 | tf_op jit(solution)/shard_map/ppermute | solution.py:36
  71.0 2.7 %collective-permute-start.31 = (s16[528,256]{1,0:T(8,128)(2,1)S(1)}, s16[528,256]{1,0:T(8,128)(2,1)S(1)}, u32[]{:S(2)}, u32[]{:S(2)}) collective-permute-start(s16[528,256]{1,0:T(8,128)(2,1)S(1)} %shard_map.112.refs_2_), channel_id=1, source_target_pairs={{0,16},{4,20},{8,24},{12,28},{16,0},{20,4},{24,8},{28,12},{1,17},{... | collective-permute-start | bytes 811016 | tf_op jit(solution)/shard_map/ppermute | solution.py:36
  73.6 1.7 %shard_map.113 = (f32[4,128,256]{2,1,0:T(8,128)S(1)}, f32[4,128,256]{2,1,0:T(8,128)S(1)}, bf16[64,256,128]{2,1,0:T(8,128)(2,1)S(1)}) custom-call(s32[1,256]{1,0:T(1,128)S(1)} %shard_map.95.refs_1_.words, bf16[2,224,128,128]{3,2,1,0:T(8,128)(2,1)S(1)} %shard_map.96.ratings, bf16[16,128,256]{2,1,0:T(8,128)(2,1)S(1)} %get-tuple-element.49.refs_0_.users, ...), custom_call_target="tpu_custom_call" | custom-call | flops 4000000000 | bytes 4096 | tf_op jit(solution)/shard_map/pallas_call | solution.py:229
  75.3 1.7 %shard_map.114 = (f32[4,128,256]{2,1,0:T(8,128)S(1)}, f32[2,128,256]{2,1,0:T(8,128)S(1)}, f32[2,128,256]{2,1,0:T(8,128)S(1)}, bf16[64,256,128]{2,1,0:T(8,128)(2,1)S(1)}) custom-call(s32[1,256]{1,0:T(1,128)S(1)} %shard_map.95.refs_1_.words, bf16[2,224,128,128]{3,2,1,0:T(8,128)(2,1)S(1)} %shard_map.96.ratings, ...), custom_call_target="tpu_custom_call" | custom-call | flops 4000000000 | bytes 4096 | tf_op jit(solution)/shard_map/pallas_call | solution.py:229
  77.0 1.7 %collective-permute-start.32 = (f32[2,128,256]{2,1,0:T(8,128)S(1)}, f32[2,128,256]{2,1,0:T(8,128)S(1)}, u32[]{:S(2)}, u32[]{:S(2)}) collective-permute-start(f32[2,128,256]{2,1,0:T(8,128)S(1)} %get-tuple-element.70), channel_id=1, source_target_pairs={{0,4},{4,0},{8,12},{12,8},{16,20},{20,16},{24,28},{28,24},{1,5},{5... | collective-permute-start | bytes 786440 | tf_op jit(solution)/shard_map/ppermute | solution.py:36
  80.8 2.3 %collective-permute-start.34 = (s16[528,256]{1,0:T(8,128)(2,1)S(1)}, s16[528,256]{1,0:T(8,128)(2,1)S(1)}, u32[]{:S(2)}, u32[]{:S(2)}) collective-permute-start(s16[528,256]{1,0:T(8,128)(2,1)S(1)} %shard_map.117), channel_id=1, source_target_pairs={{0,24},{4,28},{8,16},{12,20},{16,8},{20,12},{24,0},{28,4},{1,25},{... | collective-permute-start | bytes 811016 | tf_op jit(solution)/shard_map/ppermute | solution.py:36
  83.1 2.7 %shard_map.115.refs_4_ = f32[16,128,256]{2,1,0:T(8,128)S(1)} custom-call(s32[1,256]{1,0:T(1,128)S(1)} %shard_map.95.refs_1_.words, bf16[64,256,128]{2,1,0:T(8,128)(2,1)S(1)} %get-tuple-element.64.refs_0_, bf16[64,256,128]{2,1,0:T(8,128)(2,1)S(1)} %get-tuple-element.65.refs_1_, bf16[64,256,128]{2,1,0:T(8,128)(2,1)S(1)} %get-tuple-element.66.refs_2_, ...), custom_call_target="tpu_custom_call" | custom-call | flops 100000000 | bytes 4096 | tf_op jit(solution)/shard_map/pallas_call | solution.py:290
  85.8 4.3 %collective-permute-done.34.refs_2_ = s16[528,256]{1,0:T(8,128)(2,1)S(1)} collective-permute-done((s16[528,256]{1,0:T(8,128)(2,1)S(1)}, s16[528,256]{1,0:T(8,128)(2,1)S(1)}, u32[]{:S(2)}, u32[]{:S(2)}) %collective-permute-start.34) | collective-permute-done | bytes 270368 | tf_op jit(solution)/shard_map/ppermute | solution.py:36
  90.5 3.1 %collective-permute-start.35 = (s16[528,256]{1,0:T(8,128)(2,1)S(1)}, s16[528,256]{1,0:T(8,128)(2,1)S(1)}, u32[]{:S(2)}, u32[]{:S(2)}) collective-permute-start(s16[528,256]{1,0:T(8,128)(2,1)S(1)} %shard_map.118), channel_id=1, source_target_pairs={{0,3},{1,0},{2,1},{3,2},{4,7},{5,4},{6,5},{7,6},{8,11},{9,8},{10,9... | collective-permute-start | bytes 811016 | tf_op jit(solution)/shard_map/ppermute | solution.py:31
  93.6 3.7 %shard_map.116 = (f32[16,128,256]{2,1,0:T(8,128)}, bf16[16,128,256]{2,1,0:T(8,128)(2,1)}) custom-call(s32[1,256]{1,0:T(1,128)S(1)} %shard_map.95.refs_1_.words, bf16[64,256,128]{2,1,0:T(8,128)(2,1)S(1)} %get-tuple-element.62.held, bf16[4,128,256]{2,1,0:T(8,128)(2,1)S(1)} %collective-permute-done.19.refs_0_, ...), custom_call_target="tpu_custom_call" | custom-call | flops 100000000 | bytes 4096 | tf_op jit(solution)/shard_map/pallas_call | solution.py:303
  97.3 1.8 %collective-permute-done.35.coded = s16[528,256]{1,0:T(8,128)(2,1)S(1)} collective-permute-done((s16[528,256]{1,0:T(8,128)(2,1)S(1)}, s16[528,256]{1,0:T(8,128)(2,1)S(1)}, u32[]{:S(2)}, u32[]{:S(2)}) %collective-permute-start.35) | collective-permute-done | bytes 270368 | tf_op jit(solution)/shard_map/ppermute | solution.py:31
  (85 shorter events, 19.9 us)
Async XLA Ops:
  1.7 12.3 %collective-permute-start.4 = (bf16[4,128,256]{2,1,0:T(8,128)(2,1)S(1)}, bf16[4,128,256]{2,1,0:T(8,128)(2,1)S(1)}, u32[]{:S(2)}, u32[]{:S(2)}) collective-permute-start(bf16[4,128,256]{2,1,0:T(8,128)(2,1)S(1)} %convert_element_type.7.refs_0_.refs_3_), channel_id=1, source_target_pairs={{0,16},{4,20},{8,24},{12,28},{16,0},{20,4},{24,8},{28,12},{1,17},{... | collective-permute-start | bytes 786440 | tf_op jit(solution)/shard_map/ppermute | solution.py:36
  4.7 7.8 %collective-permute-start = (bf16[4,128,256]{2,1,0:T(8,128)(2,1)S(1)}, bf16[4,128,256]{2,1,0:T(8,128)(2,1)S(1)}, u32[]{:S(2)}, u32[]{:S(2)}) collective-permute-start(bf16[4,128,256]{2,1,0:T(8,128)(2,1)S(1)} %convert_element_type.7.refs_0_.refs_3_), channel_id=1, source_target_pairs={{0,8},{4,12},{8,0},{12,4},{16,24},{20,28},{24,16},{28,20},{1,9},{5... | collective-permute-start | bytes 786440 | tf_op jit(solution)/shard_map/ppermute | solution.py:36
  13.5 8.8 %collective-permute-start.1 = (bf16[4,128,256]{2,1,0:T(8,128)(2,1)S(1)}, bf16[4,128,256]{2,1,0:T(8,128)(2,1)S(1)}, u32[]{:S(2)}, u32[]{:S(2)}) collective-permute-start(bf16[4,128,256]{2,1,0:T(8,128)(2,1)S(1)} %collective-permute-done.refs_0_.refs_5_), channel_id=1, source_target_pairs={{0,16},{4,20},{8,24},{12,28},{16,0},{20,4},{24,8},{28,12},{1,17},{... | collective-permute-start | bytes 786440 | tf_op jit(solution)/shard_map/ppermute | solution.py:36
  14.0 2.9 %collective-permute-start.5 = (bf16[4,128,256]{2,1,0:T(8,128)(2,1)S(1)}, bf16[4,128,256]{2,1,0:T(8,128)(2,1)S(1)}, u32[]{:S(2)}, u32[]{:S(2)}) collective-permute-start(bf16[4,128,256]{2,1,0:T(8,128)(2,1)S(1)} %collective-permute-done.4.refs_2_.refs_0_.refs_7_), channel_id=1, source_target_pairs={{0,4},{4,0},{8,12},{12,8},{16,20},{20,16},{24,28},{28,24},{1,5},{5... | collective-permute-start | bytes 786440 | tf_op jit(solution)/shard_map/ppermute | solution.py:36
  16.3 6.0 %collective-permute-start.9 = (f32[2,128,256]{2,1,0:T(8,128)S(1)}, f32[2,128,256]{2,1,0:T(8,128)S(1)}, u32[]{:S(2)}, u32[]{:S(2)}) collective-permute-start(f32[2,128,256]{2,1,0:T(8,128)S(1)} %get-tuple-element.42), channel_id=1, source_target_pairs={{0,4},{4,0},{8,12},{12,8},{16,20},{20,16},{24,28},{28,24},{1,5},{5... | collective-permute-start | bytes 786440 | tf_op jit(solution)/shard_map/ppermute | solution.py:36
  16.4 6.5 %collective-permute-start.10 = (f32[2,128,256]{2,1,0:T(8,128)S(1)}, f32[2,128,256]{2,1,0:T(8,128)S(1)}, u32[]{:S(2)}, u32[]{:S(2)}) collective-permute-start(f32[2,128,256]{2,1,0:T(8,128)S(1)} %get-tuple-element.43), channel_id=1, source_target_pairs={{0,4},{4,0},{8,12},{12,8},{16,20},{20,16},{24,28},{28,24},{1,5},{5... | collective-permute-start | bytes 786440 | tf_op jit(solution)/shard_map/ppermute | solution.py:36
  18.6 6.0 %collective-permute-start.7 = (f32[2,128,256]{2,1,0:T(8,128)S(1)}, f32[2,128,256]{2,1,0:T(8,128)S(1)}, u32[]{:S(2)}, u32[]{:S(2)}) collective-permute-start(f32[2,128,256]{2,1,0:T(8,128)S(1)} %get-tuple-element.40), channel_id=1, source_target_pairs={{0,4},{4,0},{8,12},{12,8},{16,20},{20,16},{24,28},{28,24},{1,5},{5... | collective-permute-start | bytes 786440 | tf_op jit(solution)/shard_map/ppermute | solution.py:36
  19.1 5.5 %collective-permute-start.8 = (f32[2,128,256]{2,1,0:T(8,128)S(1)}, f32[2,128,256]{2,1,0:T(8,128)S(1)}, u32[]{:S(2)}, u32[]{:S(2)}) collective-permute-start(f32[2,128,256]{2,1,0:T(8,128)S(1)} %get-tuple-element.41), channel_id=1, source_target_pairs={{0,4},{4,0},{8,12},{12,8},{16,20},{20,16},{24,28},{28,24},{1,5},{5... | collective-permute-start | bytes 786440 | tf_op jit(solution)/shard_map/ppermute | solution.py:36
  22.3 3.0 %collective-permute-start.3 = (bf16[4,128,256]{2,1,0:T(8,128)(2,1)S(1)}, bf16[4,128,256]{2,1,0:T(8,128)(2,1)S(1)}, u32[]{:S(2)}, u32[]{:S(2)}) collective-permute-start(bf16[4,128,256]{2,1,0:T(8,128)(2,1)S(1)} %convert_element_type.7.refs_0_.refs_3_), channel_id=1, source_target_pairs={{0,4},{4,0},{8,12},{12,8},{16,20},{20,16},{24,28},{28,24},{1,5},{5... | collective-permute-start | bytes 786440 | tf_op jit(solution)/shard_map/ppermute | solution.py:36
  22.3 5.0 %collective-permute-start.2 = (bf16[4,128,256]{2,1,0:T(8,128)(2,1)S(1)}, bf16[4,128,256]{2,1,0:T(8,128)(2,1)S(1)}, u32[]{:S(2)}, u32[]{:S(2)}) collective-permute-start(bf16[4,128,256]{2,1,0:T(8,128)(2,1)S(1)} %collective-permute-done.1.refs_0_), channel_id=1, source_target_pairs={{0,4},{4,0},{8,12},{12,8},{16,20},{20,16},{24,28},{28,24},{1,5},{5... | collective-permute-start | bytes 786440 | tf_op jit(solution)/shard_map/ppermute | solution.py:36
  23.0 9.9 %collective-permute-start.12 = (s16[528,256]{1,0:T(8,128)(2,1)S(1)}, s16[528,256]{1,0:T(8,128)(2,1)S(1)}, u32[]{:S(2)}, u32[]{:S(2)}) collective-permute-start(s16[528,256]{1,0:T(8,128)(2,1)S(1)} %shard_map.100.refs_2_), channel_id=1, source_target_pairs={{0,8},{4,12},{8,0},{12,4},{16,24},{20,28},{24,16},{28,20},{1,9},{5... | collective-permute-start | bytes 811016 | tf_op jit(solution)/shard_map/ppermute | solution.py:36
  24.7 8.2 %collective-permute-start.13 = (s16[528,256]{1,0:T(8,128)(2,1)S(1)}, s16[528,256]{1,0:T(8,128)(2,1)S(1)}, u32[]{:S(2)}, u32[]{:S(2)}) collective-permute-start(s16[528,256]{1,0:T(8,128)(2,1)S(1)} %shard_map.101.refs_2_), channel_id=1, source_target_pairs={{0,16},{4,20},{8,24},{12,28},{16,0},{20,4},{24,8},{28,12},{1,17},{... | collective-permute-start | bytes 811016 | tf_op jit(solution)/shard_map/ppermute | solution.py:36
  30.0 1.9 %collective-permute-start.15 = (f32[2,128,256]{2,1,0:T(8,128)S(1)}, f32[2,128,256]{2,1,0:T(8,128)S(1)}, u32[]{:S(2)}, u32[]{:S(2)}) collective-permute-start(f32[2,128,256]{2,1,0:T(8,128)S(1)} %get-tuple-element.53), channel_id=1, source_target_pairs={{0,4},{4,0},{8,12},{12,8},{16,20},{20,16},{24,28},{28,24},{1,5},{5... | collective-permute-start | bytes 786440 | tf_op jit(solution)/shard_map/ppermute | solution.py:36
  30.4 6.5 %collective-permute-start.11 = (f32[4,128,256]{2,1,0:T(8,128)S(1)}, f32[4,128,256]{2,1,0:T(8,128)S(1)}, u32[]{:S(2)}, u32[]{:S(2)}) collective-permute-start(f32[4,128,256]{2,1,0:T(8,128)S(1)} %get-tuple-element.50), channel_id=1, source_target_pairs={{0,4},{4,0},{8,12},{12,8},{16,20},{20,16},{24,28},{28,24},{1,5},{5... | collective-permute-start | bytes 1572872 | tf_op jit(solution)/shard_map/ppermute | solution.py:36
  33.1 8.5 %collective-permute-start.16 = (s16[528,256]{1,0:T(8,128)(2,1)S(1)}, s16[528,256]{1,0:T(8,128)(2,1)S(1)}, u32[]{:S(2)}, u32[]{:S(2)}) collective-permute-start(s16[528,256]{1,0:T(8,128)(2,1)S(1)} %shard_map.106), channel_id=1, source_target_pairs={{0,24},{4,28},{8,16},{12,20},{16,8},{20,12},{24,0},{28,4},{1,25},{... | collective-permute-start | bytes 811016 | tf_op jit(solution)/shard_map/ppermute | solution.py:36
  41.9 11.3 %collective-permute-start.17 = (bf16[4,128,256]{2,1,0:T(8,128)(2,1)S(1)}, bf16[4,128,256]{2,1,0:T(8,128)(2,1)S(1)}, u32[]{:S(2)}, u32[]{:S(2)}) collective-permute-start(bf16[4,128,256]{2,1,0:T(8,128)(2,1)S(1)} %get-tuple-element.54), channel_id=1, source_target_pairs={{0,1},{1,2},{2,3},{3,0},{4,5},{5,6},{6,7},{7,4},{8,9},{9,10},{10,1... | collective-permute-start | bytes 786440 | tf_op jit(solution)/shard_map/ppermute | solution.py:31
  53.3 7.3 %collective-permute-start.18 = (bf16[4,128,256]{2,1,0:T(8,128)(2,1)S(1)}, bf16[4,128,256]{2,1,0:T(8,128)(2,1)S(1)}, u32[]{:S(2)}, u32[]{:S(2)}) collective-permute-start(bf16[4,128,256]{2,1,0:T(8,128)(2,1)S(1)} %shard_map.108.refs_0_.refs_3_), channel_id=1, source_target_pairs={{0,8},{4,12},{8,0},{12,4},{16,24},{20,28},{24,16},{28,20},{1,9},{5... | collective-permute-start | bytes 786440 | tf_op jit(solution)/shard_map/ppermute | solution.py:36
  54.4 7.0 %collective-permute-start.22 = (bf16[4,128,256]{2,1,0:T(8,128)(2,1)S(1)}, bf16[4,128,256]{2,1,0:T(8,128)(2,1)S(1)}, u32[]{:S(2)}, u32[]{:S(2)}) collective-permute-start(bf16[4,128,256]{2,1,0:T(8,128)(2,1)S(1)} %shard_map.108.refs_0_.refs_3_), channel_id=1, source_target_pairs={{0,16},{4,20},{8,24},{12,28},{16,0},{20,4},{24,8},{28,12},{1,17},{... | collective-permute-start | bytes 786440 | tf_op jit(solution)/shard_map/ppermute | solution.py:36
  60.6 8.7 %collective-permute-start.19 = (bf16[4,128,256]{2,1,0:T(8,128)(2,1)S(1)}, bf16[4,128,256]{2,1,0:T(8,128)(2,1)S(1)}, u32[]{:S(2)}, u32[]{:S(2)}) collective-permute-start(bf16[4,128,256]{2,1,0:T(8,128)(2,1)S(1)} %collective-permute-done.18.refs_0_.refs_5_), channel_id=1, source_target_pairs={{0,16},{4,20},{8,24},{12,28},{16,0},{20,4},{24,8},{28,12},{1,17},{... | collective-permute-start | bytes 786440 | tf_op jit(solution)/shard_map/ppermute | solution.py:36
  61.4 3.9 %collective-permute-start.23 = (bf16[4,128,256]{2,1,0:T(8,128)(2,1)S(1)}, bf16[4,128,256]{2,1,0:T(8,128)(2,1)S(1)}, u32[]{:S(2)}, u32[]{:S(2)}) collective-permute-start(bf16[4,128,256]{2,1,0:T(8,128)(2,1)S(1)} %collective-permute-done.22.refs_2_.refs_0_.refs_7_), channel_id=1, source_target_pairs={{0,4},{4,0},{8,12},{12,8},{16,20},{20,16},{24,28},{28,24},{1,5},{5... | collective-permute-start | bytes 786440 | tf_op jit(solution)/shard_map/ppermute | solution.py:36
  63.8 5.5 %collective-permute-start.27 = (f32[2,128,256]{2,1,0:T(8,128)S(1)}, f32[2,128,256]{2,1,0:T(8,128)S(1)}, u32[]{:S(2)}, u32[]{:S(2)}) collective-permute-start(f32[2,128,256]{2,1,0:T(8,128)S(1)} %get-tuple-element.59), channel_id=1, source_target_pairs={{0,4},{4,0},{8,12},{12,8},{16,20},{20,16},{24,28},{28,24},{1,5},{5... | collective-permute-start | bytes 786440 | tf_op jit(solution)/shard_map/ppermute | solution.py:36
  65.2 4.6 %collective-permute-start.28 = (f32[2,128,256]{2,1,0:T(8,128)S(1)}, f32[2,128,256]{2,1,0:T(8,128)S(1)}, u32[]{:S(2)}, u32[]{:S(2)}) collective-permute-start(f32[2,128,256]{2,1,0:T(8,128)S(1)} %get-tuple-element.60), channel_id=1, source_target_pairs={{0,4},{4,0},{8,12},{12,8},{16,20},{20,16},{24,28},{28,24},{1,5},{5... | collective-permute-start | bytes 786440 | tf_op jit(solution)/shard_map/ppermute | solution.py:36
  67.1 3.7 %collective-permute-start.25 = (f32[2,128,256]{2,1,0:T(8,128)S(1)}, f32[2,128,256]{2,1,0:T(8,128)S(1)}, u32[]{:S(2)}, u32[]{:S(2)}) collective-permute-start(f32[2,128,256]{2,1,0:T(8,128)S(1)} %get-tuple-element.57), channel_id=1, source_target_pairs={{0,4},{4,0},{8,12},{12,8},{16,20},{20,16},{24,28},{28,24},{1,5},{5... | collective-permute-start | bytes 786440 | tf_op jit(solution)/shard_map/ppermute | solution.py:36
  68.4 2.4 %collective-permute-start.26 = (f32[2,128,256]{2,1,0:T(8,128)S(1)}, f32[2,128,256]{2,1,0:T(8,128)S(1)}, u32[]{:S(2)}, u32[]{:S(2)}) collective-permute-start(f32[2,128,256]{2,1,0:T(8,128)S(1)} %get-tuple-element.58), channel_id=1, source_target_pairs={{0,4},{4,0},{8,12},{12,8},{16,20},{20,16},{24,28},{28,24},{1,5},{5... | collective-permute-start | bytes 786440 | tf_op jit(solution)/shard_map/ppermute | solution.py:36
  69.3 4.3 %collective-permute-start.21 = (bf16[4,128,256]{2,1,0:T(8,128)(2,1)S(1)}, bf16[4,128,256]{2,1,0:T(8,128)(2,1)S(1)}, u32[]{:S(2)}, u32[]{:S(2)}) collective-permute-start(bf16[4,128,256]{2,1,0:T(8,128)(2,1)S(1)} %shard_map.108.refs_0_.refs_3_), channel_id=1, source_target_pairs={{0,4},{4,0},{8,12},{12,8},{16,20},{20,16},{24,28},{28,24},{1,5},{5... | collective-permute-start | bytes 786440 | tf_op jit(solution)/shard_map/ppermute | solution.py:36
  69.3 6.0 %collective-permute-start.20 = (bf16[4,128,256]{2,1,0:T(8,128)(2,1)S(1)}, bf16[4,128,256]{2,1,0:T(8,128)(2,1)S(1)}, u32[]{:S(2)}, u32[]{:S(2)}) collective-permute-start(bf16[4,128,256]{2,1,0:T(8,128)(2,1)S(1)} %collective-permute-done.19.refs_0_), channel_id=1, source_target_pairs={{0,4},{4,0},{8,12},{12,8},{16,20},{20,16},{24,28},{28,24},{1,5},{5... | collective-permute-start | bytes 786440 | tf_op jit(solution)/shard_map/ppermute | solution.py:36
  70.0 10.7 %collective-permute-start.30 = (s16[528,256]{1,0:T(8,128)(2,1)S(1)}, s16[528,256]{1,0:T(8,128)(2,1)S(1)}, u32[]{:S(2)}, u32[]{:S(2)}) collective-permute-start(s16[528,256]{1,0:T(8,128)(2,1)S(1)} %shard_map.111.refs_2_), channel_id=1, source_target_pairs={{0,8},{4,12},{8,0},{12,4},{16,24},{20,28},{24,16},{28,20},{1,9},{5... | collective-permute-start | bytes 811016 | tf_op jit(solution)/shard_map/ppermute | solution.py:36
  71.0 9.7 %collective-permute-start.31 = (s16[528,256]{1,0:T(8,128)(2,1)S(1)}, s16[528,256]{1,0:T(8,128)(2,1)S(1)}, u32[]{:S(2)}, u32[]{:S(2)}) collective-permute-start(s16[528,256]{1,0:T(8,128)(2,1)S(1)} %shard_map.112.refs_2_), channel_id=1, source_target_pairs={{0,16},{4,20},{8,24},{12,28},{16,0},{20,4},{24,8},{28,12},{1,17},{... | collective-permute-start | bytes 811016 | tf_op jit(solution)/shard_map/ppermute | solution.py:36
  77.0 2.9 %collective-permute-start.32 = (f32[2,128,256]{2,1,0:T(8,128)S(1)}, f32[2,128,256]{2,1,0:T(8,128)S(1)}, u32[]{:S(2)}, u32[]{:S(2)}) collective-permute-start(f32[2,128,256]{2,1,0:T(8,128)S(1)} %get-tuple-element.70), channel_id=1, source_target_pairs={{0,4},{4,0},{8,12},{12,8},{16,20},{20,16},{24,28},{28,24},{1,5},{5... | collective-permute-start | bytes 786440 | tf_op jit(solution)/shard_map/ppermute | solution.py:36
  78.8 7.0 %collective-permute-start.29 = (f32[4,128,256]{2,1,0:T(8,128)S(1)}, f32[4,128,256]{2,1,0:T(8,128)S(1)}, u32[]{:S(2)}, u32[]{:S(2)}) collective-permute-start(f32[4,128,256]{2,1,0:T(8,128)S(1)} %get-tuple-element.68), channel_id=1, source_target_pairs={{0,4},{4,0},{8,12},{12,8},{16,20},{20,16},{24,28},{28,24},{1,5},{5... | collective-permute-start | bytes 1572872 | tf_op jit(solution)/shard_map/ppermute | solution.py:36
  80.8 9.4 %collective-permute-start.34 = (s16[528,256]{1,0:T(8,128)(2,1)S(1)}, s16[528,256]{1,0:T(8,128)(2,1)S(1)}, u32[]{:S(2)}, u32[]{:S(2)}) collective-permute-start(s16[528,256]{1,0:T(8,128)(2,1)S(1)} %shard_map.117), channel_id=1, source_target_pairs={{0,24},{4,28},{8,16},{12,20},{16,8},{20,12},{24,0},{28,4},{1,25},{... | collective-permute-start | bytes 811016 | tf_op jit(solution)/shard_map/ppermute | solution.py:36
  90.5 8.6 %collective-permute-start.35 = (s16[528,256]{1,0:T(8,128)(2,1)S(1)}, s16[528,256]{1,0:T(8,128)(2,1)S(1)}, u32[]{:S(2)}, u32[]{:S(2)}) collective-permute-start(s16[528,256]{1,0:T(8,128)(2,1)S(1)} %shard_map.118), channel_id=1, source_target_pairs={{0,3},{1,0},{2,1},{3,2},{4,7},{5,4},{6,5},{7,6},{8,11},{9,8},{10,9... | collective-permute-start | bytes 811016 | tf_op jit(solution)/shard_map/ppermute | solution.py:31
  (12 other events, 41.3 us)

commit v6 on v5

--- a/solution.py
+++ b/solution.py
@@ -240,17 +240,16 @@
     return even_grad, odd_grads, misfits
 
 
-def add_user_grads(bits, first_run, words, pieces, misfits, items, grad):
+def add_user_grads(bits, words, pieces, misfits, items, grad):
     tile = grad.shape[1]
-    first_col = first_run * items.shape[0] // len(misfits)
     gather_tiles(pieces, items)
-    for run, held in enumerate(misfits, first_run):
+    for run, held in enumerate(misfits):
         low, high = bounds(words, run)
 
         def advance(step, carry, low=low, held=held):
             for j in range(GROUP):
                 at = step * GROUP + j
-                _, _, row_a, row_b, col, _ = decode_word(words[0, low + at], bits, first_col)
+                _, _, row_a, row_b, col, _ = decode_word(words[0, low + at], bits, 0)
                 part = jnp.dot(held[at], items[col], preferred_element_type=jnp.float32)
                 grad[row_a] += part[:tile]
                 grad[row_b] += part[tile:]
@@ -259,16 +258,10 @@
         lax.fori_loop(0, lax.div(high - low, GROUP), advance, 0)
 
 
-def users_head_kernel(bits, runs, words, *refs):
-    *pieces, grad, items = refs[runs:]
+def users_kernel(power, bits, runs, words, *refs):
+    *pieces, factors, noise, new, new_bf, items, grad = refs[runs:]
     grad[...] = jnp.zeros_like(grad)
-    add_user_grads(bits, 0, words, pieces, refs[:runs], items, grad)
-
-
-def users_tail_kernel(power, bits, first_run, words, held, *refs):
-    *pieces, factors, noise, partial, new, new_bf, items, grad = refs
-    grad[...] = partial[...]
-    add_user_grads(bits, first_run, words, pieces, [held], items, grad)
+    add_user_grads(bits, words, pieces, refs[:runs], items, grad)
 
     def finish(t, carry):
         before = factors[t]
@@ -286,29 +279,17 @@
     return sum(piece.shape[0] for piece in pieces), *pieces[0].shape[1:]
 
 
-def users_head(bits, words, misfits, pieces, shape):
-    return pl.pallas_call(
-        functools.partial(users_head_kernel, bits, len(misfits)),
-        out_shape=jax.ShapeDtypeStruct(shape, jnp.float32),
-        in_specs=[IN_SMEM] + [IN_VMEM] * (len(misfits) + len(pieces)),
-        out_specs=IN_VMEM,
-        scratch_shapes=[pltpu.VMEM(tiles_of(pieces), jnp.bfloat16)],
-        compiler_params=pltpu.CompilerParams(vmem_limit_bytes=SMALL_LIMIT),
-        cost_estimate=BRIEF,
-    )(words, *misfits, *pieces)
-
-
-def users_tail(power, bits, first_run, words, misfits, pieces, factors, noise, partial):
+def user_step(power, bits, words, misfits, pieces, factors, noise):
     shape = factors.shape
     return pl.pallas_call(
-        functools.partial(users_tail_kernel, power, bits, first_run),
+        functools.partial(users_kernel, power, bits, len(misfits)),
         out_shape=[jax.ShapeDtypeStruct(shape, jnp.float32), jax.ShapeDtypeStruct(shape, jnp.bfloat16)],
-        in_specs=[IN_SMEM, IN_VMEM] + [IN_VMEM] * (len(pieces) + 3),
+        in_specs=[IN_SMEM] + [IN_VMEM] * (len(misfits) + len(pieces) + 2),
         out_specs=[IN_VMEM] * 2,
         scratch_shapes=[pltpu.VMEM(tiles_of(pieces), jnp.bfloat16), pltpu.VMEM(shape, jnp.float32)],
         compiler_params=pltpu.CompilerParams(vmem_limit_bytes=SMALL_LIMIT),
-        cost_estimate=BRIEF,
-    )(words, misfits, *pieces, factors, noise, partial)
+        cost_estimate=LONG,
+    )(words, *misfits, *pieces, factors, noise)
 
 
 def coded_shape(per, tile, width):
@@ -360,7 +341,7 @@
 
 
 def update_kernel(power, mine, other, *refs):
-    *coded, factors, noise, _, new, new_bf = refs
+    *coded, factors, noise, new, new_bf = refs
     for t in range(mine.shape[0]):
         step = HALF_STEP * power * owner_sum(mine, other, coded, t) + ROOT_STEP * noise[t].astype(jnp.float32)
         after = factors[t] - HALF_STEP * PRIOR * factors[t] + step
@@ -369,7 +350,7 @@
 
 
 def delta_kernel(power, mine, other, *refs):
-    *coded, noise, _, out = refs
+    *coded, noise, out = refs
     steps = []
     for t in range(mine.shape[0]):
         steps.append(HALF_STEP * power * owner_sum(mine, other, coded, t) + ROOT_STEP * noise[t].astype(jnp.float32))
@@ -447,7 +428,7 @@
         after = [evens[2]]
         order = [(item_grads, run) for run in range(1, runs - 1)]
         order += [(join, run) for run in range(1, runs - 1)]
-        order += [(item_grads, 0), (item_grads, runs - 1), (join, runs - 1)]
+        order += [(item_grads, runs - 1), (item_grads, 0), (join, runs - 1)]
         for call, run in order:
             if call is item_grads:
                 mine[run], odd_grads, misfits[run] = item_grads(
@@ -462,8 +443,7 @@
                 sums[run] = swapped(after[0], "user", 2 * run)
         sums = [sums[run] for run in range(1, runs)]
         misfits = [misfits[run] for run in range(runs)]
-        head = [piece for chunk in chunks[:-1] for piece in chunk]
-        partial = users_head(bits, words, misfits[:-1], head, users.shape)
+        pieces = [piece for chunk in chunks for piece in chunk]
         if section == 0:
             items, items_bf = in_vmem(
                 functools.partial(update_kernel, power),
@@ -473,7 +453,6 @@
                 *sums,
                 items,
                 v_noise[section],
-                after=(partial,),
             )
         else:
             delta = in_vmem(
@@ -483,12 +462,9 @@
                 other[0][0],
                 *sums,
                 v_noise[section],
-                after=(partial,),
             )
             items, items_bf = in_vmem(arrive_kernel, pair, shifted(delta, "item", -section), items)
-        users, users_bf = users_tail(
-            power, bits, runs - 1, words, misfits[-1], chunks[-1], users, u_noise[section], partial
-        )
+        users, users_bf = user_step(power, bits, words, misfits, pieces, users, u_noise[section])
     return (users.reshape(u_factors.shape), items.reshape(v_factors.shape))
 
 

time: 100 us -> 102 us (1.020)
  the two profiles are of different devices: /device:TPU:0 before, /device:TPU:2 now
where the time goes in v6:
time: 102 us
  Pallas kernels  48.4 us (47%)
  waiting for transfers between devices  30.3 us (30%)
  starting transfers between devices  18.7 us (18%)
  other arithmetic  2.78 us (3%)
    ppermute x34, waiting for transfers between devices, swapped(): return lax.ppermute(x, axis, [(i, i ^ mask) for i in range(peers)])  28.5 us
    pallas_call x8, Pallas kernels, item_grads(): pl.pallas_call(functools.partial(items_kernel, section, run, len(pieces),...  22.6 us
    ppermute x34, starting transfers between devices, swapped(): return lax.ppermute(x, axis, [(i, i ^ mask) for i in range(peers)])  16.9 us
    pallas_call x2, Pallas kernels, user_step(): pl.pallas_call(functools.partial(users_kernel, power, bits, len(misfits))...  16.8 us
    pallas_call x1, Pallas kernels, fetch(): pl.pallas_call(functools.partial(fetch_kernel, lump), out_shape=jax.Shape...  4.35 us
    pallas_call x2, Pallas kernels, pair_plan(): pl.pallas_call(functools.partial(plan_kernel, section, bits, per, span, r...  2.05 us
  transfers between devices with their start and end apart: 36, of which 11 were waited for; matrix products, arithmetic and copies ran while one was open for 2% of the time, Pallas kernels for 46%

profile of v6, /device:TPU:2, one launch (start us, length us, event | category | flops | bytes accessed | tf_op | source)
XLA Modules:
  0.0 102.1 jit_solution(2453264530899641031)
XLA Ops:
  0.6 1.1 %convert_element_type.7.refs_0_.refs_4_ = bf16[4,128,256]{2,1,0:T(8,128)(2,1)S(1)} convert(f32[4,128,256]{2,1,0:T(8,128)} %bitcast.15) | non-fusion elementwise | flops 131072 | bytes 786432 | tf_op jit(solution)/shard_map/convert_element_type | solution.py:417
  1.8 2.0 %collective-permute-start.4 = (bf16[4,128,256]{2,1,0:T(8,128)(2,1)S(1)}, bf16[4,128,256]{2,1,0:T(8,128)(2,1)S(1)}, u32[]{:S(2)}, u32[]{:S(2)}) collective-permute-start(bf16[4,128,256]{2,1,0:T(8,128)(2,1)S(1)} %convert_element_type.7.refs_0_.refs_4_), channel_id=1, source_target_pairs={{0,16},{4,20},{8,24},{12,28},{16,0},{20,4},{24,8},{28,12},{1,17},{... | collective-permute-start | bytes 786440 | tf_op jit(solution)/shard_map/ppermute | solution.py:36
  3.8 1.7 %convert_element_type.6.users = bf16[16,128,256]{2,1,0:T(8,128)(2,1)S(1)} convert(f32[16,128,256]{2,1,0:T(8,128)} %bitcast.11) | non-fusion elementwise | flops 524288 | bytes 3145728 | tf_op jit(solution)/shard_map/convert_element_type | solution.py:418
  5.6 0.6 copy-done.2
  6.2 4.3 %shard_map.96.ratings = bf16[2,224,128,128]{3,2,1,0:T(8,128)(2,1)S(1)} custom-call(s32[2]{0:T(128)S(1)} %bitcast.19, bf16[2,224,128,128]{3,2,1,0:T(8,128)(2,1)} %bitcast.22), custom_call_target="tpu_custom_call" | custom-call | flops 4000000000 | bytes 4096 | tf_op jit(solution)/shard_map/pallas_call | solution.py:147
  10.7 1.0 %shard_map.97.words = s32[1,256]{1,0:T(1,128)S(1)} custom-call(s32[1]{0:T(128)} %bitcast.me, s32[2]{0:T(128)S(1)} %bitcast.20, s32[1,1,2,224]{3,2,1,0:T(2,128)S(1)} %copy-done.4, s32[1,1,2,224]{3,2,1,0:T(2,128)S(1)} %copy-done.5), custom_call_target="tpu_custom_call" | custom-call | flops 4000000000 | bytes 4096 | tf_op jit(solution)/shard_map/pallas_call | solution.py:102
  11.7 0.7 collective-permute-start.2
  12.7 2.1 %shard_map.98 = (f32[4,128,256]{2,1,0:T(8,128)S(1)}, f32[2,128,256]{2,1,0:T(8,128)S(1)}, f32[2,128,256]{2,1,0:T(8,128)S(1)}, bf16[64,256,128]{2,1,0:T(8,128)(2,1)S(1)}) custom-call(s32[1,256]{1,0:T(1,128)S(1)} %shard_map.97.words, bf16[2,224,128,128]{3,2,1,0:T(8,128)(2,1)S(1)} %shard_map.96.ratings, bf16[16,128,256]{2,1,0:T(8,128)(2,1)S(1)} %convert_element_type.6.users, ...), custom_call_target="tpu_custom_call" | custom-call | flops 4000000000 | bytes 4096 | tf_op jit(solution)/shard_map/pallas_call | solution.py:229
  15.3 2.1 %shard_map.99 = (f32[4,128,256]{2,1,0:T(8,128)S(1)}, f32[2,128,256]{2,1,0:T(8,128)S(1)}, f32[2,128,256]{2,1,0:T(8,128)S(1)}, bf16[64,256,128]{2,1,0:T(8,128)(2,1)S(1)}) custom-call(s32[1,256]{1,0:T(1,128)S(1)} %shard_map.97.words, bf16[2,224,128,128]{3,2,1,0:T(8,128)(2,1)S(1)} %shard_map.96.ratings, bf16[16,128,256]{2,1,0:T(8,128)(2,1)S(1)} %convert_element_type.6.users, ...), custom_call_target="tpu_custom_call" | custom-call | flops 4000000000 | bytes 4096 | tf_op jit(solution)/shard_map/pallas_call | solution.py:229
  18.0 2.5 %collective-permute-done.2.refs_0_.refs_10_ = bf16[4,128,256]{2,1,0:T(8,128)(2,1)S(1)} collective-permute-done((bf16[4,128,256]{2,1,0:T(8,128)(2,1)S(1)}, bf16[4,128,256]{2,1,0:T(8,128)(2,1)S(1)}, u32[]{:S(2)}, u32[]{:S(2)}) %collective-permute-start.2) | collective-permute-done | bytes 262176 | tf_op jit(solution)/shard_map/ppermute | solution.py:36
  21.3 1.3 %collective-permute-start.12 = (s16[528,256]{1,0:T(8,128)(2,1)S(1)}, s16[528,256]{1,0:T(8,128)(2,1)S(1)}, u32[]{:S(2)}, u32[]{:S(2)}) collective-permute-start(s16[528,256]{1,0:T(8,128)(2,1)S(1)} %shard_map.100.refs_2_), channel_id=1, source_target_pairs={{0,8},{4,12},{8,0},{12,4},{16,24},{20,28},{24,16},{28,20},{1,9},{5... | collective-permute-start | bytes 811016 | tf_op jit(solution)/shard_map/ppermute | solution.py:36
  23.1 1.7 %shard_map.102 = (f32[4,128,256]{2,1,0:T(8,128)S(1)}, f32[2,128,256]{2,1,0:T(8,128)S(1)}, f32[2,128,256]{2,1,0:T(8,128)S(1)}, bf16[64,256,128]{2,1,0:T(8,128)(2,1)S(1)}) custom-call(s32[1,256]{1,0:T(1,128)S(1)} %shard_map.97.words, bf16[2,224,128,128]{3,2,1,0:T(8,128)(2,1)S(1)} %shard_map.96.ratings, bf16[16,128,256]{2,1,0:T(8,128)(2,1)S(1)} %convert_element_type.6.users, ...), custom_call_target="tpu_custom_call" | custom-call | flops 4000000000 | bytes 4096 | tf_op jit(solution)/shard_map/pallas_call | solution.py:229
  25.4 1.7 %shard_map.103 = (f32[4,128,256]{2,1,0:T(8,128)S(1)}, f32[4,128,256]{2,1,0:T(8,128)S(1)}, bf16[64,256,128]{2,1,0:T(8,128)(2,1)S(1)}) custom-call(s32[1,256]{1,0:T(1,128)S(1)} %shard_map.97.words, bf16[2,224,128,128]{3,2,1,0:T(8,128)(2,1)S(1)} %shard_map.96.ratings, bf16[16,128,256]{2,1,0:T(8,128)(2,1)S(1)} %convert_element_type.6.users, ...), custom_call_target="tpu_custom_call" | custom-call | flops 4000000000 | bytes 4096 | tf_op jit(solution)/shard_map/pallas_call | solution.py:229
  27.2 3.7 %collective-permute-done.13.refs_4_.refs_1_ = s16[528,256]{1,0:T(8,128)(2,1)S(1)} collective-permute-done((s16[528,256]{1,0:T(8,128)(2,1)S(1)}, s16[528,256]{1,0:T(8,128)(2,1)S(1)}, u32[]{:S(2)}, u32[]{:S(2)}) %collective-permute-start.13) | collective-permute-done | bytes 270368 | tf_op jit(solution)/shard_map/ppermute | solution.py:36
  31.1 1.0 %collective-permute-start.16 = (s16[528,256]{1,0:T(8,128)(2,1)S(1)}, s16[528,256]{1,0:T(8,128)(2,1)S(1)}, u32[]{:S(2)}, u32[]{:S(2)}) collective-permute-start(s16[528,256]{1,0:T(8,128)(2,1)S(1)} %shard_map.105), channel_id=1, source_target_pairs={{0,24},{4,28},{8,16},{12,20},{16,8},{20,12},{24,0},{28,4},{1,25},{... | collective-permute-start | bytes 811016 | tf_op jit(solution)/shard_map/ppermute | solution.py:36
  32.1 1.0 %shard_map.95.refs_1_.words = s32[1,256]{1,0:T(1,128)S(1)} custom-call(s32[1]{0:T(128)} %bitcast.me, s32[2]{0:T(128)S(1)} %bitcast.21, s32[1,1,2,224]{3,2,1,0:T(2,128)S(1)} %copy-done.4, s32[1,1,2,224]{3,2,1,0:T(2,128)S(1)} %copy-done.5), custom_call_target="tpu_custom_call" | custom-call | flops 4000000000 | bytes 4096 | tf_op jit(solution)/shard_map/pallas_call | solution.py:102
  33.3 6.1 %collective-permute-done.16.refs_2_ = s16[528,256]{1,0:T(8,128)(2,1)S(1)} collective-permute-done((s16[528,256]{1,0:T(8,128)(2,1)S(1)}, s16[528,256]{1,0:T(8,128)(2,1)S(1)}, u32[]{:S(2)}, u32[]{:S(2)}) %collective-permute-start.16) | collective-permute-done | bytes 270368 | tf_op jit(solution)/shard_map/ppermute | solution.py:36
  39.7 1.8 %collective-permute-start.17 = (bf16[4,128,256]{2,1,0:T(8,128)(2,1)S(1)}, bf16[4,128,256]{2,1,0:T(8,128)(2,1)S(1)}, u32[]{:S(2)}, u32[]{:S(2)}) collective-permute-start(bf16[4,128,256]{2,1,0:T(8,128)(2,1)S(1)} %get-tuple-element.54), channel_id=1, source_target_pairs={{0,1},{1,2},{2,3},{3,0},{4,5},{5,6},{6,7},{7,4},{8,9},{9,10},{10,1... | collective-permute-start | bytes 786440 | tf_op jit(solution)/shard_map/ppermute | solution.py:31
  41.5 4.6 %shard_map.104 = (f32[16,128,256]{2,1,0:T(8,128)S(1)}, bf16[16,128,256]{2,1,0:T(8,128)(2,1)S(1)}) custom-call(s32[1,256]{1,0:T(1,128)S(1)} %shard_map.97.words, bf16[64,256,128]{2,1,0:T(8,128)(2,1)S(1)} %get-tuple-element.45.refs_0_, bf16[64,256,128]{2,1,0:T(8,128)(2,1)S(1)} %get-tuple-element.46.refs_1_, ...), custom_call_target="tpu_custom_call" | custom-call | flops 4000000000 | bytes 4096 | tf_op jit(solution)/shard_map/pallas_call | solution.py:284
  46.1 1.8 %collective-permute-done.17.given = bf16[4,128,256]{2,1,0:T(8,128)(2,1)S(1)} collective-permute-done((bf16[4,128,256]{2,1,0:T(8,128)(2,1)S(1)}, bf16[4,128,256]{2,1,0:T(8,128)(2,1)S(1)}, u32[]{:S(2)}, u32[]{:S(2)}) %collective-permute-start.17) | collective-permute-done | bytes 262176 | tf_op jit(solution)/shard_map/ppermute | solution.py:31
  48.0 5.3 %collective-permute-start.19 = (bf16[4,128,256]{2,1,0:T(8,128)(2,1)S(1)}, bf16[4,128,256]{2,1,0:T(8,128)(2,1)S(1)}, u32[]{:S(2)}, u32[]{:S(2)}) collective-permute-start(bf16[4,128,256]{2,1,0:T(8,128)(2,1)S(1)} %shard_map.107.refs_0_.refs_4_), channel_id=1, source_target_pairs={{0,8},{4,12},{8,0},{12,4},{16,24},{20,28},{24,16},{28,20},{1,9},{5... | collective-permute-start | bytes 786440 | tf_op jit(solution)/shard_map/ppermute | solution.py:36
  53.3 4.3 %collective-permute-done.19.refs_0_.refs_6_ = bf16[4,128,256]{2,1,0:T(8,128)(2,1)S(1)} collective-permute-done((bf16[4,128,256]{2,1,0:T(8,128)(2,1)S(1)}, bf16[4,128,256]{2,1,0:T(8,128)(2,1)S(1)}, u32[]{:S(2)}, u32[]{:S(2)}) %collective-permute-start.19) | collective-permute-done | bytes 262176 | tf_op jit(solution)/shard_map/ppermute | solution.py:36
  57.7 2.0 %collective-permute-done.22.refs_2_.refs_0_.refs_8_ = bf16[4,128,256]{2,1,0:T(8,128)(2,1)S(1)} collective-permute-done((bf16[4,128,256]{2,1,0:T(8,128)(2,1)S(1)}, bf16[4,128,256]{2,1,0:T(8,128)(2,1)S(1)}, u32[]{:S(2)}, u32[]{:S(2)}) %collective-permute-start.22) | collective-permute-done | bytes 262176 | tf_op jit(solution)/shard_map/ppermute | solution.py:36
  59.7 3.6 %shard_map.108 = (f32[4,128,256]{2,1,0:T(8,128)S(1)}, f32[2,128,256]{2,1,0:T(8,128)S(1)}, f32[2,128,256]{2,1,0:T(8,128)S(1)}, bf16[64,256,128]{2,1,0:T(8,128)(2,1)S(1)}) custom-call(s32[1,256]{1,0:T(1,128)S(1)} %shard_map.95.refs_1_.words, bf16[2,224,128,128]{3,2,1,0:T(8,128)(2,1)S(1)} %shard_map.96.ratings, ...), custom_call_target="tpu_custom_call" | custom-call | flops 4000000000 | bytes 4096 | tf_op jit(solution)/shard_map/pallas_call | solution.py:229
  63.9 3.8 %shard_map.109 = (f32[4,128,256]{2,1,0:T(8,128)S(1)}, f32[2,128,256]{2,1,0:T(8,128)S(1)}, f32[2,128,256]{2,1,0:T(8,128)S(1)}, bf16[64,256,128]{2,1,0:T(8,128)(2,1)S(1)}) custom-call(s32[1,256]{1,0:T(1,128)S(1)} %shard_map.95.refs_1_.words, bf16[2,224,128,128]{3,2,1,0:T(8,128)(2,1)S(1)} %shard_map.96.ratings, ...), custom_call_target="tpu_custom_call" | custom-call | flops 4000000000 | bytes 4096 | tf_op jit(solution)/shard_map/pallas_call | solution.py:229
  70.1 4.0 %shard_map.112 = (f32[4,128,256]{2,1,0:T(8,128)S(1)}, f32[2,128,256]{2,1,0:T(8,128)S(1)}, f32[2,128,256]{2,1,0:T(8,128)S(1)}, bf16[64,256,128]{2,1,0:T(8,128)(2,1)S(1)}) custom-call(s32[1,256]{1,0:T(1,128)S(1)} %shard_map.95.refs_1_.words, bf16[2,224,128,128]{3,2,1,0:T(8,128)(2,1)S(1)} %shard_map.96.ratings, ...), custom_call_target="tpu_custom_call" | custom-call | flops 4000000000 | bytes 4096 | tf_op jit(solution)/shard_map/pallas_call | solution.py:229
  74.7 3.6 %shard_map.113 = (f32[4,128,256]{2,1,0:T(8,128)S(1)}, f32[4,128,256]{2,1,0:T(8,128)S(1)}, bf16[64,256,128]{2,1,0:T(8,128)(2,1)S(1)}) custom-call(s32[1,256]{1,0:T(1,128)S(1)} %shard_map.95.refs_1_.words, bf16[2,224,128,128]{3,2,1,0:T(8,128)(2,1)S(1)} %shard_map.96.ratings, bf16[16,128,256]{2,1,0:T(8,128)(2,1)S(1)} %get-tuple-element.49.refs_0_.users, ...), custom_call_target="tpu_custom_call" | custom-call | flops 4000000000 | bytes 4096 | tf_op jit(solution)/shard_map/pallas_call | solution.py:229
  78.6 0.8 collective-permute-start.34
  79.4 0.9 collective-permute-done.29.other
  80.3 8.1 %collective-permute-done.34.refs_2_ = s16[528,256]{1,0:T(8,128)(2,1)S(1)} collective-permute-done((s16[528,256]{1,0:T(8,128)(2,1)S(1)}, s16[528,256]{1,0:T(8,128)(2,1)S(1)}, u32[]{:S(2)}, u32[]{:S(2)}) %collective-permute-start.34) | collective-permute-done | bytes 270368 | tf_op jit(solution)/shard_map/ppermute | solution.py:36
  88.9 12.2 %shard_map.114 = (f32[16,128,256]{2,1,0:T(8,128)}, bf16[16,128,256]{2,1,0:T(8,128)(2,1)}) custom-call(s32[1,256]{1,0:T(1,128)S(1)} %shard_map.95.refs_1_.words, bf16[64,256,128]{2,1,0:T(8,128)(2,1)S(1)} %get-tuple-element.62.refs_0_, bf16[64,256,128]{2,1,0:T(8,128)(2,1)S(1)} %get-tuple-element.63.refs_1_, ...), custom_call_target="tpu_custom_call" | custom-call | flops 4000000000 | bytes 4096 | tf_op jit(solution)/shard_map/pallas_call | solution.py:284
  101.1 1.0 shard_map.117
  (83 shorter events, 8.4 us)
Async XLA Ops:
  1.7 8.9 %collective-permute-start.1 = (bf16[4,128,256]{2,1,0:T(8,128)(2,1)S(1)}, bf16[4,128,256]{2,1,0:T(8,128)(2,1)S(1)}, u32[]{:S(2)}, u32[]{:S(2)}) collective-permute-start(bf16[4,128,256]{2,1,0:T(8,128)(2,1)S(1)} %convert_element_type.7.refs_0_.refs_4_), channel_id=1, source_target_pairs={{0,8},{4,12},{8,0},{12,4},{16,24},{20,28},{24,16},{28,20},{1,9},{5... | collective-permute-start | bytes 786440 | tf_op jit(solution)/shard_map/ppermute | solution.py:36
  1.8 10.7 %collective-permute-start.4 = (bf16[4,128,256]{2,1,0:T(8,128)(2,1)S(1)}, bf16[4,128,256]{2,1,0:T(8,128)(2,1)S(1)}, u32[]{:S(2)}, u32[]{:S(2)}) collective-permute-start(bf16[4,128,256]{2,1,0:T(8,128)(2,1)S(1)} %convert_element_type.7.refs_0_.refs_4_), channel_id=1, source_target_pairs={{0,16},{4,20},{8,24},{12,28},{16,0},{20,4},{24,8},{28,12},{1,17},{... | collective-permute-start | bytes 786440 | tf_op jit(solution)/shard_map/ppermute | solution.py:36
  10.6 2.1 %collective-permute-start.6 = (bf16[4,128,256]{2,1,0:T(8,128)(2,1)S(1)}, bf16[4,128,256]{2,1,0:T(8,128)(2,1)S(1)}, u32[]{:S(2)}, u32[]{:S(2)}) collective-permute-start(bf16[4,128,256]{2,1,0:T(8,128)(2,1)S(1)} %collective-permute-done.1.refs_0_.refs_6_), channel_id=1, source_target_pairs={{0,4},{4,0},{8,12},{12,8},{16,20},{20,16},{24,28},{28,24},{1,5},{5... | collective-permute-start | bytes 786440 | tf_op jit(solution)/shard_map/ppermute | solution.py:36
  11.7 8.8 %collective-permute-start.2 = (bf16[4,128,256]{2,1,0:T(8,128)(2,1)S(1)}, bf16[4,128,256]{2,1,0:T(8,128)(2,1)S(1)}, u32[]{:S(2)}, u32[]{:S(2)}) collective-permute-start(bf16[4,128,256]{2,1,0:T(8,128)(2,1)S(1)} %collective-permute-done.1.refs_0_.refs_6_), channel_id=1, source_target_pairs={{0,16},{4,20},{8,24},{12,28},{16,0},{20,4},{24,8},{28,12},{1,17},{... | collective-permute-start | bytes 786440 | tf_op jit(solution)/shard_map/ppermute | solution.py:36
  12.4 2.9 %collective-permute-start.5 = (bf16[4,128,256]{2,1,0:T(8,128)(2,1)S(1)}, bf16[4,128,256]{2,1,0:T(8,128)(2,1)S(1)}, u32[]{:S(2)}, u32[]{:S(2)}) collective-permute-start(bf16[4,128,256]{2,1,0:T(8,128)(2,1)S(1)} %collective-permute-done.4.refs_2_.refs_0_.refs_8_), channel_id=1, source_target_pairs={{0,4},{4,0},{8,12},{12,8},{16,20},{20,16},{24,28},{28,24},{1,5},{5... | collective-permute-start | bytes 786440 | tf_op jit(solution)/shard_map/ppermute | solution.py:36
  14.8 5.9 %collective-permute-start.10 = (f32[2,128,256]{2,1,0:T(8,128)S(1)}, f32[2,128,256]{2,1,0:T(8,128)S(1)}, u32[]{:S(2)}, u32[]{:S(2)}) collective-permute-start(f32[2,128,256]{2,1,0:T(8,128)S(1)} %get-tuple-element.43), channel_id=1, source_target_pairs={{0,4},{4,0},{8,12},{12,8},{16,20},{20,16},{24,28},{28,24},{1,5},{5... | collective-permute-start | bytes 786440 | tf_op jit(solution)/shard_map/ppermute | solution.py:36
  14.8 6.4 %collective-permute-start.9 = (f32[2,128,256]{2,1,0:T(8,128)S(1)}, f32[2,128,256]{2,1,0:T(8,128)S(1)}, u32[]{:S(2)}, u32[]{:S(2)}) collective-permute-start(f32[2,128,256]{2,1,0:T(8,128)S(1)} %get-tuple-element.42), channel_id=1, source_target_pairs={{0,4},{4,0},{8,12},{12,8},{16,20},{20,16},{24,28},{28,24},{1,5},{5... | collective-permute-start | bytes 786440 | tf_op jit(solution)/shard_map/ppermute | solution.py:36
  17.4 5.2 %collective-permute-start.7 = (f32[2,128,256]{2,1,0:T(8,128)S(1)}, f32[2,128,256]{2,1,0:T(8,128)S(1)}, u32[]{:S(2)}, u32[]{:S(2)}) collective-permute-start(f32[2,128,256]{2,1,0:T(8,128)S(1)} %get-tuple-element.40), channel_id=1, source_target_pairs={{0,4},{4,0},{8,12},{12,8},{16,20},{20,16},{24,28},{28,24},{1,5},{5... | collective-permute-start | bytes 786440 | tf_op jit(solution)/shard_map/ppermute | solution.py:36
  17.5 5.1 %collective-permute-start.8 = (f32[2,128,256]{2,1,0:T(8,128)S(1)}, f32[2,128,256]{2,1,0:T(8,128)S(1)}, u32[]{:S(2)}, u32[]{:S(2)}) collective-permute-start(f32[2,128,256]{2,1,0:T(8,128)S(1)} %get-tuple-element.41), channel_id=1, source_target_pairs={{0,4},{4,0},{8,12},{12,8},{16,20},{20,16},{24,28},{28,24},{1,5},{5... | collective-permute-start | bytes 786440 | tf_op jit(solution)/shard_map/ppermute | solution.py:36
  20.5 2.6 %collective-permute-start.3 = (bf16[4,128,256]{2,1,0:T(8,128)(2,1)S(1)}, bf16[4,128,256]{2,1,0:T(8,128)(2,1)S(1)}, u32[]{:S(2)}, u32[]{:S(2)}) collective-permute-start(bf16[4,128,256]{2,1,0:T(8,128)(2,1)S(1)} %collective-permute-done.2.refs_0_.refs_10_), channel_id=1, source_target_pairs={{0,4},{4,0},{8,12},{12,8},{16,20},{20,16},{24,28},{28,24},{1,5},{5... | collective-permute-start | bytes 786440 | tf_op jit(solution)/shard_map/ppermute | solution.py:36
  20.6 4.7 %collective-permute-start = (bf16[4,128,256]{2,1,0:T(8,128)(2,1)S(1)}, bf16[4,128,256]{2,1,0:T(8,128)(2,1)S(1)}, u32[]{:S(2)}, u32[]{:S(2)}) collective-permute-start(bf16[4,128,256]{2,1,0:T(8,128)(2,1)S(1)} %convert_element_type.7.refs_0_.refs_4_), channel_id=1, source_target_pairs={{0,4},{4,0},{8,12},{12,8},{16,20},{20,16},{24,28},{28,24},{1,5},{5... | collective-permute-start | bytes 786440 | tf_op jit(solution)/shard_map/ppermute | solution.py:36
  21.3 9.6 %collective-permute-start.12 = (s16[528,256]{1,0:T(8,128)(2,1)S(1)}, s16[528,256]{1,0:T(8,128)(2,1)S(1)}, u32[]{:S(2)}, u32[]{:S(2)}) collective-permute-start(s16[528,256]{1,0:T(8,128)(2,1)S(1)} %shard_map.100.refs_2_), channel_id=1, source_target_pairs={{0,8},{4,12},{8,0},{12,4},{16,24},{20,28},{24,16},{28,20},{1,9},{5... | collective-permute-start | bytes 811016 | tf_op jit(solution)/shard_map/ppermute | solution.py:36
  22.7 8.2 %collective-permute-start.13 = (s16[528,256]{1,0:T(8,128)(2,1)S(1)}, s16[528,256]{1,0:T(8,128)(2,1)S(1)}, u32[]{:S(2)}, u32[]{:S(2)}) collective-permute-start(s16[528,256]{1,0:T(8,128)(2,1)S(1)} %shard_map.101.refs_2_), channel_id=1, source_target_pairs={{0,16},{4,20},{8,24},{12,28},{16,0},{20,4},{24,8},{28,12},{1,17},{... | collective-permute-start | bytes 811016 | tf_op jit(solution)/shard_map/ppermute | solution.py:36
  24.8 2.4 %collective-permute-start.14 = (f32[2,128,256]{2,1,0:T(8,128)S(1)}, f32[2,128,256]{2,1,0:T(8,128)S(1)}, u32[]{:S(2)}, u32[]{:S(2)}) collective-permute-start(f32[2,128,256]{2,1,0:T(8,128)S(1)} %get-tuple-element.52), channel_id=1, source_target_pairs={{0,4},{4,0},{8,12},{12,8},{16,20},{20,16},{24,28},{28,24},{1,5},{5... | collective-permute-start | bytes 786440 | tf_op jit(solution)/shard_map/ppermute | solution.py:36
  24.9 2.3 %collective-permute-start.15 = (f32[2,128,256]{2,1,0:T(8,128)S(1)}, f32[2,128,256]{2,1,0:T(8,128)S(1)}, u32[]{:S(2)}, u32[]{:S(2)}) collective-permute-start(f32[2,128,256]{2,1,0:T(8,128)S(1)} %get-tuple-element.53), channel_id=1, source_target_pairs={{0,4},{4,0},{8,12},{12,8},{16,20},{20,16},{24,28},{28,24},{1,5},{5... | collective-permute-start | bytes 786440 | tf_op jit(solution)/shard_map/ppermute | solution.py:36
  27.0 6.2 %collective-permute-start.11 = (f32[4,128,256]{2,1,0:T(8,128)S(1)}, f32[4,128,256]{2,1,0:T(8,128)S(1)}, u32[]{:S(2)}, u32[]{:S(2)}) collective-permute-start(f32[4,128,256]{2,1,0:T(8,128)S(1)} %get-tuple-element.51), channel_id=1, source_target_pairs={{0,4},{4,0},{8,12},{12,8},{16,20},{20,16},{24,28},{28,24},{1,5},{5... | collective-permute-start | bytes 1572872 | tf_op jit(solution)/shard_map/ppermute | solution.py:36
  31.1 8.2 %collective-permute-start.16 = (s16[528,256]{1,0:T(8,128)(2,1)S(1)}, s16[528,256]{1,0:T(8,128)(2,1)S(1)}, u32[]{:S(2)}, u32[]{:S(2)}) collective-permute-start(s16[528,256]{1,0:T(8,128)(2,1)S(1)} %shard_map.105), channel_id=1, source_target_pairs={{0,24},{4,28},{8,16},{12,20},{16,8},{20,12},{24,0},{28,4},{1,25},{... | collective-permute-start | bytes 811016 | tf_op jit(solution)/shard_map/ppermute | solution.py:36
  39.7 8.2 %collective-permute-start.17 = (bf16[4,128,256]{2,1,0:T(8,128)(2,1)S(1)}, bf16[4,128,256]{2,1,0:T(8,128)(2,1)S(1)}, u32[]{:S(2)}, u32[]{:S(2)}) collective-permute-start(bf16[4,128,256]{2,1,0:T(8,128)(2,1)S(1)} %get-tuple-element.54), channel_id=1, source_target_pairs={{0,1},{1,2},{2,3},{3,0},{4,5},{5,6},{6,7},{7,4},{8,9},{9,10},{10,1... | collective-permute-start | bytes 786440 | tf_op jit(solution)/shard_map/ppermute | solution.py:31
  48.0 9.7 %collective-permute-start.19 = (bf16[4,128,256]{2,1,0:T(8,128)(2,1)S(1)}, bf16[4,128,256]{2,1,0:T(8,128)(2,1)S(1)}, u32[]{:S(2)}, u32[]{:S(2)}) collective-permute-start(bf16[4,128,256]{2,1,0:T(8,128)(2,1)S(1)} %shard_map.107.refs_0_.refs_4_), channel_id=1, source_target_pairs={{0,8},{4,12},{8,0},{12,4},{16,24},{20,28},{24,16},{28,20},{1,9},{5... | collective-permute-start | bytes 786440 | tf_op jit(solution)/shard_map/ppermute | solution.py:36
  53.3 6.4 %collective-permute-start.22 = (bf16[4,128,256]{2,1,0:T(8,128)(2,1)S(1)}, bf16[4,128,256]{2,1,0:T(8,128)(2,1)S(1)}, u32[]{:S(2)}, u32[]{:S(2)}) collective-permute-start(bf16[4,128,256]{2,1,0:T(8,128)(2,1)S(1)} %shard_map.107.refs_0_.refs_4_), channel_id=1, source_target_pairs={{0,16},{4,20},{8,24},{12,28},{16,0},{20,4},{24,8},{28,12},{1,17},{... | collective-permute-start | bytes 786440 | tf_op jit(solution)/shard_map/ppermute | solution.py:36
  57.7 2.0 %collective-permute-start.24 = (bf16[4,128,256]{2,1,0:T(8,128)(2,1)S(1)}, bf16[4,128,256]{2,1,0:T(8,128)(2,1)S(1)}, u32[]{:S(2)}, u32[]{:S(2)}) collective-permute-start(bf16[4,128,256]{2,1,0:T(8,128)(2,1)S(1)} %collective-permute-done.19.refs_0_.refs_6_), channel_id=1, source_target_pairs={{0,4},{4,0},{8,12},{12,8},{16,20},{20,16},{24,28},{28,24},{1,5},{5... | collective-permute-start | bytes 786440 | tf_op jit(solution)/shard_map/ppermute | solution.py:36
  57.7 10.7 %collective-permute-start.20 = (bf16[4,128,256]{2,1,0:T(8,128)(2,1)S(1)}, bf16[4,128,256]{2,1,0:T(8,128)(2,1)S(1)}, u32[]{:S(2)}, u32[]{:S(2)}) collective-permute-start(bf16[4,128,256]{2,1,0:T(8,128)(2,1)S(1)} %collective-permute-done.19.refs_0_.refs_6_), channel_id=1, source_target_pairs={{0,16},{4,20},{8,24},{12,28},{16,0},{20,4},{24,8},{28,12},{1,17},{... | collective-permute-start | bytes 786440 | tf_op jit(solution)/shard_map/ppermute | solution.py:36
  59.7 4.2 %collective-permute-start.23 = (bf16[4,128,256]{2,1,0:T(8,128)(2,1)S(1)}, bf16[4,128,256]{2,1,0:T(8,128)(2,1)S(1)}, u32[]{:S(2)}, u32[]{:S(2)}) collective-permute-start(bf16[4,128,256]{2,1,0:T(8,128)(2,1)S(1)} %collective-permute-done.22.refs_2_.refs_0_.refs_8_), channel_id=1, source_target_pairs={{0,4},{4,0},{8,12},{12,8},{16,20},{20,16},{24,28},{28,24},{1,5},{5... | collective-permute-start | bytes 786440 | tf_op jit(solution)/shard_map/ppermute | solution.py:36
  63.3 5.1 %collective-permute-start.27 = (f32[2,128,256]{2,1,0:T(8,128)S(1)}, f32[2,128,256]{2,1,0:T(8,128)S(1)}, u32[]{:S(2)}, u32[]{:S(2)}) collective-permute-start(f32[2,128,256]{2,1,0:T(8,128)S(1)} %get-tuple-element.59), channel_id=1, source_target_pairs={{0,4},{4,0},{8,12},{12,8},{16,20},{20,16},{24,28},{28,24},{1,5},{5... | collective-permute-start | bytes 786440 | tf_op jit(solution)/shard_map/ppermute | solution.py:36
  63.4 5.4 %collective-permute-start.28 = (f32[2,128,256]{2,1,0:T(8,128)S(1)}, f32[2,128,256]{2,1,0:T(8,128)S(1)}, u32[]{:S(2)}, u32[]{:S(2)}) collective-permute-start(f32[2,128,256]{2,1,0:T(8,128)S(1)} %get-tuple-element.60), channel_id=1, source_target_pairs={{0,4},{4,0},{8,12},{12,8},{16,20},{20,16},{24,28},{28,24},{1,5},{5... | collective-permute-start | bytes 786440 | tf_op jit(solution)/shard_map/ppermute | solution.py:36
  68.4 6.3 %collective-permute-start.18 = (bf16[4,128,256]{2,1,0:T(8,128)(2,1)S(1)}, bf16[4,128,256]{2,1,0:T(8,128)(2,1)S(1)}, u32[]{:S(2)}, u32[]{:S(2)}) collective-permute-start(bf16[4,128,256]{2,1,0:T(8,128)(2,1)S(1)} %shard_map.107.refs_0_.refs_4_), channel_id=1, source_target_pairs={{0,4},{4,0},{8,12},{12,8},{16,20},{20,16},{24,28},{28,24},{1,5},{5... | collective-permute-start | bytes 786440 | tf_op jit(solution)/shard_map/ppermute | solution.py:36
  69.0 9.5 %collective-permute-start.30 = (s16[528,256]{1,0:T(8,128)(2,1)S(1)}, s16[528,256]{1,0:T(8,128)(2,1)S(1)}, u32[]{:S(2)}, u32[]{:S(2)}) collective-permute-start(s16[528,256]{1,0:T(8,128)(2,1)S(1)} %shard_map.110.refs_2_), channel_id=1, source_target_pairs={{0,8},{4,12},{8,0},{12,4},{16,24},{20,28},{24,16},{28,20},{1,9},{5... | collective-permute-start | bytes 811016 | tf_op jit(solution)/shard_map/ppermute | solution.py:36
  69.9 8.6 %collective-permute-start.31 = (s16[528,256]{1,0:T(8,128)(2,1)S(1)}, s16[528,256]{1,0:T(8,128)(2,1)S(1)}, u32[]{:S(2)}, u32[]{:S(2)}) collective-permute-start(s16[528,256]{1,0:T(8,128)(2,1)S(1)} %shard_map.111.refs_2_), channel_id=1, source_target_pairs={{0,16},{4,20},{8,24},{12,28},{16,0},{20,4},{24,8},{28,12},{1,17},{... | collective-permute-start | bytes 811016 | tf_op jit(solution)/shard_map/ppermute | solution.py:36
  74.1 4.3 %collective-permute-start.32 = (f32[2,128,256]{2,1,0:T(8,128)S(1)}, f32[2,128,256]{2,1,0:T(8,128)S(1)}, u32[]{:S(2)}, u32[]{:S(2)}) collective-permute-start(f32[2,128,256]{2,1,0:T(8,128)S(1)} %get-tuple-element.70), channel_id=1, source_target_pairs={{0,4},{4,0},{8,12},{12,8},{16,20},{20,16},{24,28},{28,24},{1,5},{5... | collective-permute-start | bytes 786440 | tf_op jit(solution)/shard_map/ppermute | solution.py:36
  74.2 4.2 %collective-permute-start.33 = (f32[2,128,256]{2,1,0:T(8,128)S(1)}, f32[2,128,256]{2,1,0:T(8,128)S(1)}, u32[]{:S(2)}, u32[]{:S(2)}) collective-permute-start(f32[2,128,256]{2,1,0:T(8,128)S(1)} %get-tuple-element.71), channel_id=1, source_target_pairs={{0,4},{4,0},{8,12},{12,8},{16,20},{20,16},{24,28},{28,24},{1,5},{5... | collective-permute-start | bytes 786440 | tf_op jit(solution)/shard_map/ppermute | solution.py:36
  78.6 9.8 %collective-permute-start.34 = (s16[528,256]{1,0:T(8,128)(2,1)S(1)}, s16[528,256]{1,0:T(8,128)(2,1)S(1)}, u32[]{:S(2)}, u32[]{:S(2)}) collective-permute-start(s16[528,256]{1,0:T(8,128)(2,1)S(1)} %shard_map.115), channel_id=1, source_target_pairs={{0,24},{4,28},{8,16},{12,20},{16,8},{20,12},{24,0},{28,4},{1,25},{... | collective-permute-start | bytes 811016 | tf_op jit(solution)/shard_map/ppermute | solution.py:36
  88.9 12.2 %collective-permute-start.35 = (s16[528,256]{1,0:T(8,128)(2,1)S(1)}, s16[528,256]{1,0:T(8,128)(2,1)S(1)}, u32[]{:S(2)}, u32[]{:S(2)}) collective-permute-start(s16[528,256]{1,0:T(8,128)(2,1)S(1)} %shard_map.116), channel_id=1, source_target_pairs={{0,3},{1,0},{2,1},{3,2},{4,7},{5,4},{6,5},{7,6},{8,11},{9,8},{10,9... | collective-permute-start | bytes 811016 | tf_op jit(solution)/shard_map/ppermute | solution.py:31
  (12 other events, 47.4 us)

commit v7 on v5

--- a/solution.py
+++ b/solution.py
@@ -163,16 +163,20 @@
         at += piece.shape[0]
 
 
-def items_kernel(section, run, count, skipped, bits, words, ratings, users, *refs):
-    outs, items, grad = refs[count + skipped : -2], refs[-2], refs[-1]
+def items_kernel(section, run, count, skipped, bits, listed, ratings, users, *refs):
+    outs = refs[count + skipped : -4]
+    items, grad, words, sem = refs[-4:]
+    load = pltpu.make_async_copy(listed, words, sem)
+    load.start()
     out_even, *out_odd, misfits = outs
     span = items.shape[0]
     per = span // 2
     tile = users.shape[1]
+    gather_tiles(refs[:count], items)
+    grad[...] = jnp.zeros_like(grad)
+    load.wait()
     low, high = bounds(words, run)
     steps = lax.div(high - low, GROUP)
-    gather_tiles(refs[:count], items)
-    grad[...] = jnp.zeros_like(grad)
 
     def decode(p):
         return decode_word(words[0, p], bits, run * span)
@@ -183,7 +187,7 @@
     def predict(p):
         slot_a, slot_b, row_a, row_b, col, live = decode(p)
         predicted = lax.dot_general(
-            users_of(row_a, row_b), items[col], (((1,), (1,)), ((), ())), preferred_element_type=jnp.float32
+            users_of(row_a, row_b), items[col], (((1,), (0,)), ((), ())), preferred_element_type=jnp.float32
         )
         given = jnp.concatenate([ratings[section, slot_a], ratings[section, slot_b]], axis=0).astype(jnp.float32)
         rows = lax.broadcasted_iota(jnp.int32, (2 * tile, 1), 0)
@@ -231,9 +235,14 @@
         out_shape=[jax.ShapeDtypeStruct((per, tile, width), f32)]
         + [jax.ShapeDtypeStruct((per // parts, tile, width), f32)] * parts
         + [jax.ShapeDtypeStruct((held, 2 * tile, tile), jnp.bfloat16)],
-        in_specs=[IN_SMEM] + [IN_VMEM] * (2 + len(pieces)) + [ANY] * len(after),
+        in_specs=[ANY] + [IN_VMEM] * (2 + len(pieces)) + [ANY] * len(after),
         out_specs=[IN_VMEM] * (2 + parts),
-        scratch_shapes=[pltpu.VMEM((2 * per, tile, width), jnp.bfloat16), pltpu.VMEM((2 * per, tile, width), f32)],
+        scratch_shapes=[
+            pltpu.VMEM((2 * per, width, tile), jnp.bfloat16),
+            pltpu.VMEM((2 * per, tile, width), f32),
+            pltpu.SMEM(words.shape, jnp.int32),
+            pltpu.SemaphoreType.DMA,
+        ],
         compiler_params=pltpu.CompilerParams(vmem_limit_bytes=SMALL_LIMIT),
         cost_estimate=LONG,
     )(words, ratings, users, *pieces, *after)
@@ -251,7 +260,9 @@
             for j in range(GROUP):
                 at = step * GROUP + j
                 _, _, row_a, row_b, col, _ = decode_word(words[0, low + at], bits, first_col)
-                part = jnp.dot(held[at], items[col], preferred_element_type=jnp.float32)
+                part = lax.dot_general(
+                    held[at], items[col], (((1,), (1,)), ((), ())), preferred_element_type=jnp.float32
+                )
                 grad[row_a] += part[:tile]
                 grad[row_b] += part[tile:]
             return carry
@@ -365,7 +376,7 @@
         step = HALF_STEP * power * owner_sum(mine, other, coded, t) + ROOT_STEP * noise[t].astype(jnp.float32)
         after = factors[t] - HALF_STEP * PRIOR * factors[t] + step
         new[t] = after
-        new_bf[t] = after.astype(jnp.bfloat16)
+        new_bf[t] = after.astype(jnp.bfloat16).T
 
 
 def delta_kernel(power, mine, other, *refs):
@@ -376,12 +387,18 @@
     encode(steps, out)
 
 
-def arrive_kernel(coded, factors, new, new_bf):
+def arrive_kernel(coded, factors, new, *new_bf):
     per, tile, _ = factors.shape
     for t in range(per):
         after = factors[t] - HALF_STEP * PRIOR * factors[t] + decoded(coded, t, tile, per)
         new[t] = after
-        new_bf[t] = after.astype(jnp.bfloat16)
+        for out in new_bf:
+            out[t] = after.astype(jnp.bfloat16).T
+
+
+def turn_kernel(factors, out):
+    for t in range(factors.shape[0]):
+        out[t] = factors[t].astype(jnp.bfloat16).T
 
 
 def pass_kernel(given, *refs):
@@ -430,10 +447,10 @@
     bits = widths(ratings.shape[1], users.shape[0], item_tiles)
     pair = (
         jax.ShapeDtypeStruct(items.shape, jnp.float32),
-        jax.ShapeDtypeStruct(items.shape, jnp.bfloat16),
+        jax.ShapeDtypeStruct((per, width, tile), jnp.bfloat16),
     )
     rated = fetch(counts, ratings)
-    items_bf = items.astype(jnp.bfloat16)
+    items_bf = in_vmem(turn_kernel, pair[1], items)
     users_bf = users.astype(jnp.bfloat16)
     for section in range(sections):
         words = pair_plan(section, bits, per, span, runs, side, me, counts, tile_rows, tile_cols)
@@ -447,7 +464,7 @@
         after = [evens[2]]
         order = [(item_grads, run) for run in range(1, runs - 1)]
         order += [(join, run) for run in range(1, runs - 1)]
-        order += [(item_grads, 0), (item_grads, runs - 1), (join, runs - 1)]
+        order += [(item_grads, runs - 1), (item_grads, 0), (join, runs - 1)]
         for call, run in order:
             if call is item_grads:
                 mine[run], odd_grads, misfits[run] = item_grads(
@@ -485,7 +502,9 @@
                 v_noise[section],
                 after=(partial,),
             )
-            items, items_bf = in_vmem(arrive_kernel, pair, shifted(delta, "item", -section), items)
+            wanted = pair if section + 1 < sections else pair[:1]
+            items, *turned = in_vmem(arrive_kernel, wanted, shifted(delta, "item", -section), items)
+            items_bf = turned[0] if turned else None
         users, users_bf = users_tail(
             power, bits, runs - 1, words, misfits[-1], chunks[-1], users, u_noise[section], partial
         )

time: 100 us -> 96.1 us (0.961); the launches traced: 100 us -> 94.1 us
  Pallas kernels: 34.8 us -> 29.9 us
  starting transfers between devices: 29.9 us -> 28 us
  other arithmetic: 2.78 us -> 1.71 us
  local copies, waits for them, and re-layouts: 0.86 us -> 1.9 us
    pallas_call x8, Pallas kernels: 15.2 us -> 12.1 us  [item_grads(): pl.pallas_call(functools.partial(items_kernel, section, run, len(pieces),...]
    ppermute x34, waiting for transfers between devices: 22.8 us -> 24.6 us  [swapped(): return lax.ppermute(x, axis, [(i, i ^ mask) for i in range(peers)])]
    ppermute x34, starting transfers between devices: 25.4 us -> 23.9 us  [swapped(): return lax.ppermute(x, axis, [(i, i ^ mask) for i in range(peers)])]
    pallas_call x2, Pallas kernels: 5.93 us -> 4.84 us  [users_head(): pl.pallas_call(functools.partial(users_head_kernel, bits, len(misfits)),...]
    convert_element_type x1 -> x0, other arithmetic: 1.07 us -> none  [body(): items_bf = items.astype(jnp.bfloat16)]
    unnamed x16 -> x18, local copies, waits for them, and re-layouts: 0.69 us -> 1.72 us
  transfers between devices with their start and end apart: 36 -> 36, of which waited for: 15 -> 11; matrix products, arithmetic and copies ran while one was open for 2% -> 2% of each run, Pallas kernels for 33% -> 30%
where the time goes in v7:
time: 96.1 us; the launch traced here: 94.1 us
  waiting for transfers between devices  31.7 us (33%)
  Pallas kernels  29.9 us (31%)
  starting transfers between devices  28 us (29%)
  local copies, waits for them, and re-layouts  1.9 us (2%)
  other arithmetic  1.71 us (2%)
    ppermute x34, waiting for transfers between devices, swapped(): return lax.ppermute(x, axis, [(i, i ^ mask) for i in range(peers)])  24.6 us
    ppermute x34, starting transfers between devices, swapped(): return lax.ppermute(x, axis, [(i, i ^ mask) for i in range(peers)])  23.9 us
    pallas_call x8, Pallas kernels, item_grads(): pl.pallas_call(functools.partial(items_kernel, section, run, len(pieces),...  12.1 us
    ppermute x2, waiting for transfers between devices, shifted(): return lax.ppermute(x, axis, [(i, (i + by) % peers) for i in range(peers)])  7.17 us
    pallas_call x2, Pallas kernels, users_tail(): pl.pallas_call(functools.partial(users_tail_kernel, power, bits, first_ru...  5.76 us
    pallas_call x2, Pallas kernels, users_head(): pl.pallas_call(functools.partial(users_head_kernel, bits, len(misfits)),...  4.84 us
    ppermute x2, starting transfers between devices, shifted(): return lax.ppermute(x, axis, [(i, (i + by) % peers) for i in range(peers)])  4.05 us
    pallas_call x1, Pallas kernels, fetch(): pl.pallas_call(functools.partial(fetch_kernel, lump), out_shape=jax.Shape...  2.32 us
  transfers between devices with their start and end apart: 36, of which 11 were waited for; matrix products, arithmetic and copies ran while one was open for 2% of the time, Pallas kernels for 30%

profile of v7, /device:TPU:0, one launch (start us, length us, event | category | flops | bytes accessed | tf_op | source)
XLA Modules:
  0.0 94.1 jit_solution(9114180828672955281)
XLA Ops:
  1.8 3.0 %collective-permute-start.3 = (bf16[4,256,128]{2,1,0:T(8,128)(2,1)S(1)}, bf16[4,256,128]{2,1,0:T(8,128)(2,1)S(1)}, u32[]{:S(2)}, u32[]{:S(2)}) collective-permute-start(bf16[4,256,128]{2,1,0:T(8,128)(2,1)S(1)} %shard_map.98.refs_0_.refs_3_), channel_id=1, source_target_pairs={{0,16},{4,20},{8,24},{12,28},{16,0},{20,4},{24,8},{28,12},{1,17},{... | collective-permute-start | bytes 786440 | tf_op jit(solution)/shard_map/ppermute | solution.py:36
  4.8 1.5 %collective-permute-start = (bf16[4,256,128]{2,1,0:T(8,128)(2,1)S(1)}, bf16[4,256,128]{2,1,0:T(8,128)(2,1)S(1)}, u32[]{:S(2)}, u32[]{:S(2)}) collective-permute-start(bf16[4,256,128]{2,1,0:T(8,128)(2,1)S(1)} %shard_map.98.refs_0_.refs_3_), channel_id=1, source_target_pairs={{0,8},{4,12},{8,0},{12,4},{16,24},{20,28},{24,16},{28,20},{1,9},{5... | collective-permute-start | bytes 786440 | tf_op jit(solution)/shard_map/ppermute | solution.py:36
  6.3 1.7 %convert_element_type.3.users = bf16[16,128,256]{2,1,0:T(8,128)(2,1)S(1)} convert(f32[16,128,256]{2,1,0:T(8,128)} %bitcast.11) | non-fusion elementwise | flops 524288 | bytes 3145728 | tf_op jit(solution)/shard_map/convert_element_type | solution.py:454
  8.7 2.3 %shard_map.96.ratings = bf16[2,224,128,128]{3,2,1,0:T(8,128)(2,1)S(1)} custom-call(s32[2]{0:T(128)S(1)} %bitcast.19, bf16[2,224,128,128]{3,2,1,0:T(8,128)(2,1)} %bitcast.22), custom_call_target="tpu_custom_call" | custom-call | flops 4000000000 | bytes 4096 | tf_op jit(solution)/shard_map/pallas_call | solution.py:147
  11.0 1.6 %collective-permute-done.refs_0_.refs_5_ = bf16[4,256,128]{2,1,0:T(8,128)(2,1)S(1)} collective-permute-done((bf16[4,256,128]{2,1,0:T(8,128)(2,1)S(1)}, bf16[4,256,128]{2,1,0:T(8,128)(2,1)S(1)}, u32[]{:S(2)}, u32[]{:S(2)}) %collective-permute-start) | collective-permute-done | bytes 262176 | tf_op jit(solution)/shard_map/ppermute | solution.py:36
  14.3 1.6 %shard_map.99 = (f32[4,128,256]{2,1,0:T(8,128)S(1)}, f32[2,128,256]{2,1,0:T(8,128)S(1)}, f32[2,128,256]{2,1,0:T(8,128)S(1)}, bf16[64,256,128]{2,1,0:T(8,128)(2,1)S(1)}) custom-call(s32[1,256]{1,0:T(1,128)S(1)} %shard_map.97.listed.words, bf16[2,224,128,128]{3,2,1,0:T(8,128)(2,1)S(1)} %shard_map.96.ratings, ...), custom_call_target="tpu_custom_call" | custom-call | flops 4000000000 | bytes 4096 | tf_op jit(solution)/shard_map/pallas_call | solution.py:233
  17.9 1.6 %collective-permute-start.6 = (f32[2,128,256]{2,1,0:T(8,128)S(1)}, f32[2,128,256]{2,1,0:T(8,128)S(1)}, u32[]{:S(2)}, u32[]{:S(2)}) collective-permute-start(f32[2,128,256]{2,1,0:T(8,128)S(1)} %get-tuple-element.39), channel_id=1, source_target_pairs={{0,4},{4,0},{8,12},{12,8},{16,20},{20,16},{24,28},{28,24},{1,5},{5... | collective-permute-start | bytes 786440 | tf_op jit(solution)/shard_map/ppermute | solution.py:36
  19.6 2.8 %collective-permute-done.1.refs_0_ = bf16[4,256,128]{2,1,0:T(8,128)(2,1)S(1)} collective-permute-done((bf16[4,256,128]{2,1,0:T(8,128)(2,1)S(1)}, bf16[4,256,128]{2,1,0:T(8,128)(2,1)S(1)}, u32[]{:S(2)}, u32[]{:S(2)}) %collective-permute-start.1) | collective-permute-done | bytes 262176 | tf_op jit(solution)/shard_map/ppermute | solution.py:36
  23.1 1.6 %collective-permute-start.12 = (s16[528,256]{1,0:T(8,128)(2,1)S(1)}, s16[528,256]{1,0:T(8,128)(2,1)S(1)}, u32[]{:S(2)}, u32[]{:S(2)}) collective-permute-start(s16[528,256]{1,0:T(8,128)(2,1)S(1)} %shard_map.101.refs_2_), channel_id=1, source_target_pairs={{0,8},{4,12},{8,0},{12,4},{16,24},{20,28},{24,16},{28,20},{1,9},{5... | collective-permute-start | bytes 811016 | tf_op jit(solution)/shard_map/ppermute | solution.py:36
  25.4 1.6 %shard_map.103 = (f32[4,128,256]{2,1,0:T(8,128)S(1)}, f32[2,128,256]{2,1,0:T(8,128)S(1)}, f32[2,128,256]{2,1,0:T(8,128)S(1)}, bf16[64,256,128]{2,1,0:T(8,128)(2,1)S(1)}) custom-call(s32[1,256]{1,0:T(1,128)S(1)} %shard_map.97.listed.words, bf16[2,224,128,128]{3,2,1,0:T(8,128)(2,1)S(1)} %shard_map.96.ratings, ...), custom_call_target="tpu_custom_call" | custom-call | flops 4000000000 | bytes 4096 | tf_op jit(solution)/shard_map/pallas_call | solution.py:233
  27.7 1.6 %shard_map.104 = (f32[4,128,256]{2,1,0:T(8,128)S(1)}, f32[4,128,256]{2,1,0:T(8,128)S(1)}, bf16[64,256,128]{2,1,0:T(8,128)(2,1)S(1)}) custom-call(s32[1,256]{1,0:T(1,128)S(1)} %shard_map.97.listed.words, bf16[2,224,128,128]{3,2,1,0:T(8,128)(2,1)S(1)} %shard_map.96.ratings, bf16[16,128,256]{2,1,0:T(8,128)(2,1)S(1)} %convert_element_type.3.users, ...), custom_call_target="tpu_custom_call" | custom-call | flops 4000000000 | bytes 4096 | tf_op jit(solution)/shard_map/pallas_call | solution.py:233
  29.3 1.3 %collective-permute-start.11 = (f32[4,128,256]{2,1,0:T(8,128)S(1)}, f32[4,128,256]{2,1,0:T(8,128)S(1)}, u32[]{:S(2)}, u32[]{:S(2)}) collective-permute-start(f32[4,128,256]{2,1,0:T(8,128)S(1)} %get-tuple-element.50), channel_id=1, source_target_pairs={{0,4},{4,0},{8,12},{12,8},{16,20},{20,16},{24,28},{28,24},{1,5},{5... | collective-permute-start | bytes 1572872 | tf_op jit(solution)/shard_map/ppermute | solution.py:36
  30.6 2.4 %collective-permute-done.13.refs_4_.refs_1_ = s16[528,256]{1,0:T(8,128)(2,1)S(1)} collective-permute-done((s16[528,256]{1,0:T(8,128)(2,1)S(1)}, s16[528,256]{1,0:T(8,128)(2,1)S(1)}, u32[]{:S(2)}, u32[]{:S(2)}) %collective-permute-start.13) | collective-permute-done | bytes 270368 | tf_op jit(solution)/shard_map/ppermute | solution.py:36
  33.8 2.4 %shard_map.105.refs_4_.refs_5_ = f32[16,128,256]{2,1,0:T(8,128)S(1)} custom-call(s32[1,256]{1,0:T(1,128)S(1)} %shard_map.97.listed.words, bf16[64,256,128]{2,1,0:T(8,128)(2,1)S(1)} %get-tuple-element.45.refs_0_, bf16[64,256,128]{2,1,0:T(8,128)(2,1)S(1)} %get-tuple-element.46.refs_1_, bf16[64,256,128]{2,1,0:T(8,128)(2,1)S(1)} %get-tuple-element.47.refs_2_, ...), custom_call_target="tpu_custom_call" | custom-call | flops 100000000 | bytes 4096 | tf_op jit(solution)/shard_map/pallas_call | solution.py:301
  36.2 5.1 %collective-permute-done.16.refs_2_ = s16[528,256]{1,0:T(8,128)(2,1)S(1)} collective-permute-done((s16[528,256]{1,0:T(8,128)(2,1)S(1)}, s16[528,256]{1,0:T(8,128)(2,1)S(1)}, u32[]{:S(2)}, u32[]{:S(2)}) %collective-permute-start.16) | collective-permute-done | bytes 270368 | tf_op jit(solution)/shard_map/ppermute | solution.py:36
  41.8 1.6 %collective-permute-start.17 = (bf16[4,256,128]{2,1,0:T(8,128)(2,1)S(1)}, bf16[4,256,128]{2,1,0:T(8,128)(2,1)S(1)}, u32[]{:S(2)}, u32[]{:S(2)}) collective-permute-start(bf16[4,256,128]{2,1,0:T(8,128)(2,1)S(1)} %get-tuple-element.53), channel_id=1, source_target_pairs={{0,1},{1,2},{2,3},{3,0},{4,5},{5,6},{6,7},{7,4},{8,9},{9,10},{10,1... | collective-permute-start | bytes 786440 | tf_op jit(solution)/shard_map/ppermute | solution.py:31
  44.5 2.0 %shard_map.106 = (f32[16,128,256]{2,1,0:T(8,128)S(1)}, bf16[16,128,256]{2,1,0:T(8,128)(2,1)S(1)}) custom-call(s32[1,256]{1,0:T(1,128)S(1)} %shard_map.97.listed.words, bf16[64,256,128]{2,1,0:T(8,128)(2,1)S(1)} %get-tuple-element.43.held, bf16[4,256,128]{2,1,0:T(8,128)(2,1)S(1)} %collective-permute-done.1.refs_0_, ...), custom_call_target="tpu_custom_call" | custom-call | flops 100000000 | bytes 4096 | tf_op jit(solution)/shard_map/pallas_call | solution.py:314
  46.5 3.7 %collective-permute-done.17.given = bf16[4,256,128]{2,1,0:T(8,128)(2,1)S(1)} collective-permute-done((bf16[4,256,128]{2,1,0:T(8,128)(2,1)S(1)}, bf16[4,256,128]{2,1,0:T(8,128)(2,1)S(1)}, u32[]{:S(2)}, u32[]{:S(2)}) %collective-permute-start.17) | collective-permute-done | bytes 262176 | tf_op jit(solution)/shard_map/ppermute | solution.py:31
  51.4 5.3 %collective-permute-done.18.refs_0_.refs_5_ = bf16[4,256,128]{2,1,0:T(8,128)(2,1)S(1)} collective-permute-done((bf16[4,256,128]{2,1,0:T(8,128)(2,1)S(1)}, bf16[4,256,128]{2,1,0:T(8,128)(2,1)S(1)}, u32[]{:S(2)}, u32[]{:S(2)}) %collective-permute-start.18) | collective-permute-done | bytes 262176 | tf_op jit(solution)/shard_map/ppermute | solution.py:36
  59.5 1.7 %collective-permute-start.26 = (f32[2,128,256]{2,1,0:T(8,128)S(1)}, f32[2,128,256]{2,1,0:T(8,128)S(1)}, u32[]{:S(2)}, u32[]{:S(2)}) collective-permute-start(f32[2,128,256]{2,1,0:T(8,128)S(1)} %get-tuple-element.58), channel_id=1, source_target_pairs={{0,4},{4,0},{8,12},{12,8},{16,20},{20,16},{24,28},{28,24},{1,5},{5... | collective-permute-start | bytes 786440 | tf_op jit(solution)/shard_map/ppermute | solution.py:36
  61.3 1.8 %shard_map.111 = (f32[4,128,256]{2,1,0:T(8,128)S(1)}, f32[2,128,256]{2,1,0:T(8,128)S(1)}, f32[2,128,256]{2,1,0:T(8,128)S(1)}, bf16[64,256,128]{2,1,0:T(8,128)(2,1)S(1)}) custom-call(s32[1,256]{1,0:T(1,128)S(1)} %shard_map.95.refs_1_.listed.words, bf16[2,224,128,128]{3,2,1,0:T(8,128)(2,1)S(1)} %shard_map.96.ratings, ...), custom_call_target="tpu_custom_call" | custom-call | flops 4000000000 | bytes 4096 | tf_op jit(solution)/shard_map/pallas_call | solution.py:233
  63.0 1.3 %collective-permute-start.24 = (f32[2,128,256]{2,1,0:T(8,128)S(1)}, f32[2,128,256]{2,1,0:T(8,128)S(1)}, u32[]{:S(2)}, u32[]{:S(2)}) collective-permute-start(f32[2,128,256]{2,1,0:T(8,128)S(1)} %get-tuple-element.56), channel_id=1, source_target_pairs={{0,4},{4,0},{8,12},{12,8},{16,20},{20,16},{24,28},{28,24},{1,5},{5... | collective-permute-start | bytes 786440 | tf_op jit(solution)/shard_map/ppermute | solution.py:36
  67.4 1.6 %shard_map.114 = (f32[4,128,256]{2,1,0:T(8,128)S(1)}, f32[2,128,256]{2,1,0:T(8,128)S(1)}, f32[2,128,256]{2,1,0:T(8,128)S(1)}, bf16[64,256,128]{2,1,0:T(8,128)(2,1)S(1)}) custom-call(s32[1,256]{1,0:T(1,128)S(1)} %shard_map.95.refs_1_.listed.words, bf16[2,224,128,128]{3,2,1,0:T(8,128)(2,1)S(1)} %shard_map.96.ratings, ...), custom_call_target="tpu_custom_call" | custom-call | flops 4000000000 | bytes 4096 | tf_op jit(solution)/shard_map/pallas_call | solution.py:233
  69.7 1.6 %shard_map.115 = (f32[4,128,256]{2,1,0:T(8,128)S(1)}, f32[4,128,256]{2,1,0:T(8,128)S(1)}, bf16[64,256,128]{2,1,0:T(8,128)(2,1)S(1)}) custom-call(s32[1,256]{1,0:T(1,128)S(1)} %shard_map.95.refs_1_.listed.words, bf16[2,224,128,128]{3,2,1,0:T(8,128)(2,1)S(1)} %shard_map.96.ratings, bf16[16,128,256]{2,1,0:T(8,128)(2,1)S(1)} %get-tuple-element.48.refs_0_.users, ...), custom_call_target="tpu_custom_call" | custom-call | flops 4000000000 | bytes 4096 | tf_op jit(solution)/shard_map/pallas_call | solution.py:233
  71.3 1.3 %collective-permute-start.29 = (f32[4,128,256]{2,1,0:T(8,128)S(1)}, f32[4,128,256]{2,1,0:T(8,128)S(1)}, u32[]{:S(2)}, u32[]{:S(2)}) collective-permute-start(f32[4,128,256]{2,1,0:T(8,128)S(1)} %get-tuple-element.68), channel_id=1, source_target_pairs={{0,4},{4,0},{8,12},{12,8},{16,20},{20,16},{24,28},{28,24},{1,5},{5... | collective-permute-start | bytes 1572872 | tf_op jit(solution)/shard_map/ppermute | solution.py:36
  72.5 2.3 %collective-permute-done.31.refs_4_.refs_1_ = s16[528,256]{1,0:T(8,128)(2,1)S(1)} collective-permute-done((s16[528,256]{1,0:T(8,128)(2,1)S(1)}, s16[528,256]{1,0:T(8,128)(2,1)S(1)}, u32[]{:S(2)}, u32[]{:S(2)}) %collective-permute-start.31) | collective-permute-done | bytes 270368 | tf_op jit(solution)/shard_map/ppermute | solution.py:36
  75.0 2.2 %collective-permute-start.34 = (s16[528,256]{1,0:T(8,128)(2,1)S(1)}, s16[528,256]{1,0:T(8,128)(2,1)S(1)}, u32[]{:S(2)}, u32[]{:S(2)}) collective-permute-start(s16[528,256]{1,0:T(8,128)(2,1)S(1)} %shard_map.118), channel_id=1, source_target_pairs={{0,24},{4,28},{8,16},{12,20},{16,8},{20,12},{24,0},{28,4},{1,25},{... | collective-permute-start | bytes 811016 | tf_op jit(solution)/shard_map/ppermute | solution.py:36
  77.2 2.4 %shard_map.116.refs_4_ = f32[16,128,256]{2,1,0:T(8,128)S(1)} custom-call(s32[1,256]{1,0:T(1,128)S(1)} %shard_map.95.refs_1_.listed.words, bf16[64,256,128]{2,1,0:T(8,128)(2,1)S(1)} %get-tuple-element.63.refs_0_, bf16[64,256,128]{2,1,0:T(8,128)(2,1)S(1)} %get-tuple-element.64.refs_1_, bf16[64,256,128]{2,1,0:T(8,128)(2,1)S(1)} %get-tuple-element.65.refs_2_, ...), custom_call_target="tpu_custom_call" | custom-call | flops 100000000 | bytes 4096 | tf_op jit(solution)/shard_map/pallas_call | solution.py:301
  79.6 3.6 %collective-permute-done.34.refs_2_ = s16[528,256]{1,0:T(8,128)(2,1)S(1)} collective-permute-done((s16[528,256]{1,0:T(8,128)(2,1)S(1)}, s16[528,256]{1,0:T(8,128)(2,1)S(1)}, u32[]{:S(2)}, u32[]{:S(2)}) %collective-permute-start.34) | collective-permute-done | bytes 270368 | tf_op jit(solution)/shard_map/ppermute | solution.py:36
  83.6 2.4 %collective-permute-start.35 = (s16[528,256]{1,0:T(8,128)(2,1)S(1)}, s16[528,256]{1,0:T(8,128)(2,1)S(1)}, u32[]{:S(2)}, u32[]{:S(2)}) collective-permute-start(s16[528,256]{1,0:T(8,128)(2,1)S(1)} %shard_map.119), channel_id=1, source_target_pairs={{0,3},{1,0},{2,1},{3,2},{4,7},{5,4},{6,5},{7,6},{8,11},{9,8},{10,9... | collective-permute-start | bytes 811016 | tf_op jit(solution)/shard_map/ppermute | solution.py:31
  86.1 3.7 %shard_map.117 = (f32[16,128,256]{2,1,0:T(8,128)}, bf16[16,128,256]{2,1,0:T(8,128)(2,1)}) custom-call(s32[1,256]{1,0:T(1,128)S(1)} %shard_map.95.refs_1_.listed.words, bf16[64,256,128]{2,1,0:T(8,128)(2,1)S(1)} %get-tuple-element.60.held, bf16[4,256,128]{2,1,0:T(8,128)(2,1)S(1)} %collective-permute-done.19.refs_0_, ...), custom_call_target="tpu_custom_call" | custom-call | flops 100000000 | bytes 4096 | tf_op jit(solution)/shard_map/pallas_call | solution.py:314
  89.8 3.4 %collective-permute-done.35.coded = s16[528,256]{1,0:T(8,128)(2,1)S(1)} collective-permute-done((s16[528,256]{1,0:T(8,128)(2,1)S(1)}, s16[528,256]{1,0:T(8,128)(2,1)S(1)}, u32[]{:S(2)}, u32[]{:S(2)}) %collective-permute-start.35) | collective-permute-done | bytes 270368 | tf_op jit(solution)/shard_map/ppermute | solution.py:31
  (87 shorter events, 19.2 us)
Async XLA Ops:
  1.8 12.3 %collective-permute-start.3 = (bf16[4,256,128]{2,1,0:T(8,128)(2,1)S(1)}, bf16[4,256,128]{2,1,0:T(8,128)(2,1)S(1)}, u32[]{:S(2)}, u32[]{:S(2)}) collective-permute-start(bf16[4,256,128]{2,1,0:T(8,128)(2,1)S(1)} %shard_map.98.refs_0_.refs_3_), channel_id=1, source_target_pairs={{0,16},{4,20},{8,24},{12,28},{16,0},{20,4},{24,8},{28,12},{1,17},{... | collective-permute-start | bytes 786440 | tf_op jit(solution)/shard_map/ppermute | solution.py:36
  4.8 7.8 %collective-permute-start = (bf16[4,256,128]{2,1,0:T(8,128)(2,1)S(1)}, bf16[4,256,128]{2,1,0:T(8,128)(2,1)S(1)}, u32[]{:S(2)}, u32[]{:S(2)}) collective-permute-start(bf16[4,256,128]{2,1,0:T(8,128)(2,1)S(1)} %shard_map.98.refs_0_.refs_3_), channel_id=1, source_target_pairs={{0,8},{4,12},{8,0},{12,4},{16,24},{20,28},{24,16},{28,20},{1,9},{5... | collective-permute-start | bytes 786440 | tf_op jit(solution)/shard_map/ppermute | solution.py:36
  13.6 8.8 %collective-permute-start.1 = (bf16[4,256,128]{2,1,0:T(8,128)(2,1)S(1)}, bf16[4,256,128]{2,1,0:T(8,128)(2,1)S(1)}, u32[]{:S(2)}, u32[]{:S(2)}) collective-permute-start(bf16[4,256,128]{2,1,0:T(8,128)(2,1)S(1)} %collective-permute-done.refs_0_.refs_5_), channel_id=1, source_target_pairs={{0,16},{4,20},{8,24},{12,28},{16,0},{20,4},{24,8},{28,12},{1,17},{... | collective-permute-start | bytes 786440 | tf_op jit(solution)/shard_map/ppermute | solution.py:36
  14.1 2.6 %collective-permute-start.4 = (bf16[4,256,128]{2,1,0:T(8,128)(2,1)S(1)}, bf16[4,256,128]{2,1,0:T(8,128)(2,1)S(1)}, u32[]{:S(2)}, u32[]{:S(2)}) collective-permute-start(bf16[4,256,128]{2,1,0:T(8,128)(2,1)S(1)} %collective-permute-done.3.refs_2_.refs_0_.refs_7_), channel_id=1, source_target_pairs={{0,4},{4,0},{8,12},{12,8},{16,20},{20,16},{24,28},{28,24},{1,5},{5... | collective-permute-start | bytes 786440 | tf_op jit(solution)/shard_map/ppermute | solution.py:36
  15.9 6.5 %collective-permute-start.8 = (f32[2,128,256]{2,1,0:T(8,128)S(1)}, f32[2,128,256]{2,1,0:T(8,128)S(1)}, u32[]{:S(2)}, u32[]{:S(2)}) collective-permute-start(f32[2,128,256]{2,1,0:T(8,128)S(1)} %get-tuple-element.41), channel_id=1, source_target_pairs={{0,4},{4,0},{8,12},{12,8},{16,20},{20,16},{24,28},{28,24},{1,5},{5... | collective-permute-start | bytes 786440 | tf_op jit(solution)/shard_map/ppermute | solution.py:36
  16.6 6.3 %collective-permute-start.9 = (f32[2,128,256]{2,1,0:T(8,128)S(1)}, f32[2,128,256]{2,1,0:T(8,128)S(1)}, u32[]{:S(2)}, u32[]{:S(2)}) collective-permute-start(f32[2,128,256]{2,1,0:T(8,128)S(1)} %get-tuple-element.42), channel_id=1, source_target_pairs={{0,4},{4,0},{8,12},{12,8},{16,20},{20,16},{24,28},{28,24},{1,5},{5... | collective-permute-start | bytes 786440 | tf_op jit(solution)/shard_map/ppermute | solution.py:36
  17.9 6.7 %collective-permute-start.6 = (f32[2,128,256]{2,1,0:T(8,128)S(1)}, f32[2,128,256]{2,1,0:T(8,128)S(1)}, u32[]{:S(2)}, u32[]{:S(2)}) collective-permute-start(f32[2,128,256]{2,1,0:T(8,128)S(1)} %get-tuple-element.39), channel_id=1, source_target_pairs={{0,4},{4,0},{8,12},{12,8},{16,20},{20,16},{24,28},{28,24},{1,5},{5... | collective-permute-start | bytes 786440 | tf_op jit(solution)/shard_map/ppermute | solution.py:36
  19.5 5.1 %collective-permute-start.7 = (f32[2,128,256]{2,1,0:T(8,128)S(1)}, f32[2,128,256]{2,1,0:T(8,128)S(1)}, u32[]{:S(2)}, u32[]{:S(2)}) collective-permute-start(f32[2,128,256]{2,1,0:T(8,128)S(1)} %get-tuple-element.40), channel_id=1, source_target_pairs={{0,4},{4,0},{8,12},{12,8},{16,20},{20,16},{24,28},{28,24},{1,5},{5... | collective-permute-start | bytes 786440 | tf_op jit(solution)/shard_map/ppermute | solution.py:36
  22.4 3.0 %collective-permute-start.2 = (bf16[4,256,128]{2,1,0:T(8,128)(2,1)S(1)}, bf16[4,256,128]{2,1,0:T(8,128)(2,1)S(1)}, u32[]{:S(2)}, u32[]{:S(2)}) collective-permute-start(bf16[4,256,128]{2,1,0:T(8,128)(2,1)S(1)} %collective-permute-done.1.refs_0_), channel_id=1, source_target_pairs={{0,4},{4,0},{8,12},{12,8},{16,20},{20,16},{24,28},{28,24},{1,5},{5... | collective-permute-start | bytes 786440 | tf_op jit(solution)/shard_map/ppermute | solution.py:36
  22.4 5.3 %collective-permute-start.10 = (bf16[4,256,128]{2,1,0:T(8,128)(2,1)S(1)}, bf16[4,256,128]{2,1,0:T(8,128)(2,1)S(1)}, u32[]{:S(2)}, u32[]{:S(2)}) collective-permute-start(bf16[4,256,128]{2,1,0:T(8,128)(2,1)S(1)} %shard_map.98.refs_0_.refs_3_), channel_id=1, source_target_pairs={{0,4},{4,0},{8,12},{12,8},{16,20},{20,16},{24,28},{28,24},{1,5},{5... | collective-permute-start | bytes 786440 | tf_op jit(solution)/shard_map/ppermute | solution.py:36
  23.1 9.9 %collective-permute-start.12 = (s16[528,256]{1,0:T(8,128)(2,1)S(1)}, s16[528,256]{1,0:T(8,128)(2,1)S(1)}, u32[]{:S(2)}, u32[]{:S(2)}) collective-permute-start(s16[528,256]{1,0:T(8,128)(2,1)S(1)} %shard_map.101.refs_2_), channel_id=1, source_target_pairs={{0,8},{4,12},{8,0},{12,4},{16,24},{20,28},{24,16},{28,20},{1,9},{5... | collective-permute-start | bytes 811016 | tf_op jit(solution)/shard_map/ppermute | solution.py:36
  24.8 8.2 %collective-permute-start.13 = (s16[528,256]{1,0:T(8,128)(2,1)S(1)}, s16[528,256]{1,0:T(8,128)(2,1)S(1)}, u32[]{:S(2)}, u32[]{:S(2)}) collective-permute-start(s16[528,256]{1,0:T(8,128)(2,1)S(1)} %shard_map.102.refs_2_), channel_id=1, source_target_pairs={{0,16},{4,20},{8,24},{12,28},{16,0},{20,4},{24,8},{28,12},{1,17},{... | collective-permute-start | bytes 811016 | tf_op jit(solution)/shard_map/ppermute | solution.py:36
  27.0 3.6 %collective-permute-start.14 = (f32[2,128,256]{2,1,0:T(8,128)S(1)}, f32[2,128,256]{2,1,0:T(8,128)S(1)}, u32[]{:S(2)}, u32[]{:S(2)}) collective-permute-start(f32[2,128,256]{2,1,0:T(8,128)S(1)} %get-tuple-element.51), channel_id=1, source_target_pairs={{0,4},{4,0},{8,12},{12,8},{16,20},{20,16},{24,28},{28,24},{1,5},{5... | collective-permute-start | bytes 786440 | tf_op jit(solution)/shard_map/ppermute | solution.py:36
  27.6 2.9 %collective-permute-start.15 = (f32[2,128,256]{2,1,0:T(8,128)S(1)}, f32[2,128,256]{2,1,0:T(8,128)S(1)}, u32[]{:S(2)}, u32[]{:S(2)}) collective-permute-start(f32[2,128,256]{2,1,0:T(8,128)S(1)} %get-tuple-element.52), channel_id=1, source_target_pairs={{0,4},{4,0},{8,12},{12,8},{16,20},{20,16},{24,28},{28,24},{1,5},{5... | collective-permute-start | bytes 786440 | tf_op jit(solution)/shard_map/ppermute | solution.py:36
  29.3 6.9 %collective-permute-start.11 = (f32[4,128,256]{2,1,0:T(8,128)S(1)}, f32[4,128,256]{2,1,0:T(8,128)S(1)}, u32[]{:S(2)}, u32[]{:S(2)}) collective-permute-start(f32[4,128,256]{2,1,0:T(8,128)S(1)} %get-tuple-element.50), channel_id=1, source_target_pairs={{0,4},{4,0},{8,12},{12,8},{16,20},{20,16},{24,28},{28,24},{1,5},{5... | collective-permute-start | bytes 1572872 | tf_op jit(solution)/shard_map/ppermute | solution.py:36
  33.2 8.2 %collective-permute-start.16 = (s16[528,256]{1,0:T(8,128)(2,1)S(1)}, s16[528,256]{1,0:T(8,128)(2,1)S(1)}, u32[]{:S(2)}, u32[]{:S(2)}) collective-permute-start(s16[528,256]{1,0:T(8,128)(2,1)S(1)} %shard_map.107), channel_id=1, source_target_pairs={{0,24},{4,28},{8,16},{12,20},{16,8},{20,12},{24,0},{28,4},{1,25},{... | collective-permute-start | bytes 811016 | tf_op jit(solution)/shard_map/ppermute | solution.py:36
  41.8 8.4 %collective-permute-start.17 = (bf16[4,256,128]{2,1,0:T(8,128)(2,1)S(1)}, bf16[4,256,128]{2,1,0:T(8,128)(2,1)S(1)}, u32[]{:S(2)}, u32[]{:S(2)}) collective-permute-start(bf16[4,256,128]{2,1,0:T(8,128)(2,1)S(1)} %get-tuple-element.53), channel_id=1, source_target_pairs={{0,1},{1,2},{2,3},{3,0},{4,5},{5,6},{6,7},{7,4},{8,9},{9,10},{10,1... | collective-permute-start | bytes 786440 | tf_op jit(solution)/shard_map/ppermute | solution.py:31
  50.3 6.4 %collective-permute-start.18 = (bf16[4,256,128]{2,1,0:T(8,128)(2,1)S(1)}, bf16[4,256,128]{2,1,0:T(8,128)(2,1)S(1)}, u32[]{:S(2)}, u32[]{:S(2)}) collective-permute-start(bf16[4,256,128]{2,1,0:T(8,128)(2,1)S(1)} %shard_map.109.refs_0_.refs_3_), channel_id=1, source_target_pairs={{0,8},{4,12},{8,0},{12,4},{16,24},{20,28},{24,16},{28,20},{1,9},{5... | collective-permute-start | bytes 786440 | tf_op jit(solution)/shard_map/ppermute | solution.py:36
  50.7 7.1 %collective-permute-start.21 = (bf16[4,256,128]{2,1,0:T(8,128)(2,1)S(1)}, bf16[4,256,128]{2,1,0:T(8,128)(2,1)S(1)}, u32[]{:S(2)}, u32[]{:S(2)}) collective-permute-start(bf16[4,256,128]{2,1,0:T(8,128)(2,1)S(1)} %shard_map.109.refs_0_.refs_3_), channel_id=1, source_target_pairs={{0,16},{4,20},{8,24},{12,28},{16,0},{20,4},{24,8},{28,12},{1,17},{... | collective-permute-start | bytes 786440 | tf_op jit(solution)/shard_map/ppermute | solution.py:36
  56.7 8.7 %collective-permute-start.19 = (bf16[4,256,128]{2,1,0:T(8,128)(2,1)S(1)}, bf16[4,256,128]{2,1,0:T(8,128)(2,1)S(1)}, u32[]{:S(2)}, u32[]{:S(2)}) collective-permute-start(bf16[4,256,128]{2,1,0:T(8,128)(2,1)S(1)} %collective-permute-done.18.refs_0_.refs_5_), channel_id=1, source_target_pairs={{0,16},{4,20},{8,24},{12,28},{16,0},{20,4},{24,8},{28,12},{1,17},{... | collective-permute-start | bytes 786440 | tf_op jit(solution)/shard_map/ppermute | solution.py:36
  57.7 3.5 %collective-permute-start.22 = (bf16[4,256,128]{2,1,0:T(8,128)(2,1)S(1)}, bf16[4,256,128]{2,1,0:T(8,128)(2,1)S(1)}, u32[]{:S(2)}, u32[]{:S(2)}) collective-permute-start(bf16[4,256,128]{2,1,0:T(8,128)(2,1)S(1)} %collective-permute-done.21.refs_2_.refs_0_.refs_7_), channel_id=1, source_target_pairs={{0,4},{4,0},{8,12},{12,8},{16,20},{20,16},{24,28},{28,24},{1,5},{5... | collective-permute-start | bytes 786440 | tf_op jit(solution)/shard_map/ppermute | solution.py:36
  59.5 6.0 %collective-permute-start.26 = (f32[2,128,256]{2,1,0:T(8,128)S(1)}, f32[2,128,256]{2,1,0:T(8,128)S(1)}, u32[]{:S(2)}, u32[]{:S(2)}) collective-permute-start(f32[2,128,256]{2,1,0:T(8,128)S(1)} %get-tuple-element.58), channel_id=1, source_target_pairs={{0,4},{4,0},{8,12},{12,8},{16,20},{20,16},{24,28},{28,24},{1,5},{5... | collective-permute-start | bytes 786440 | tf_op jit(solution)/shard_map/ppermute | solution.py:36
  61.2 4.8 %collective-permute-start.27 = (f32[2,128,256]{2,1,0:T(8,128)S(1)}, f32[2,128,256]{2,1,0:T(8,128)S(1)}, u32[]{:S(2)}, u32[]{:S(2)}) collective-permute-start(f32[2,128,256]{2,1,0:T(8,128)S(1)} %get-tuple-element.59), channel_id=1, source_target_pairs={{0,4},{4,0},{8,12},{12,8},{16,20},{20,16},{24,28},{28,24},{1,5},{5... | collective-permute-start | bytes 786440 | tf_op jit(solution)/shard_map/ppermute | solution.py:36
  63.0 3.5 %collective-permute-start.24 = (f32[2,128,256]{2,1,0:T(8,128)S(1)}, f32[2,128,256]{2,1,0:T(8,128)S(1)}, u32[]{:S(2)}, u32[]{:S(2)}) collective-permute-start(f32[2,128,256]{2,1,0:T(8,128)S(1)} %get-tuple-element.56), channel_id=1, source_target_pairs={{0,4},{4,0},{8,12},{12,8},{16,20},{20,16},{24,28},{28,24},{1,5},{5... | collective-permute-start | bytes 786440 | tf_op jit(solution)/shard_map/ppermute | solution.py:36
  65.4 4.2 %collective-permute-start.28 = (bf16[4,256,128]{2,1,0:T(8,128)(2,1)S(1)}, bf16[4,256,128]{2,1,0:T(8,128)(2,1)S(1)}, u32[]{:S(2)}, u32[]{:S(2)}) collective-permute-start(bf16[4,256,128]{2,1,0:T(8,128)(2,1)S(1)} %shard_map.109.refs_0_.refs_3_), channel_id=1, source_target_pairs={{0,4},{4,0},{8,12},{12,8},{16,20},{20,16},{24,28},{28,24},{1,5},{5... | collective-permute-start | bytes 786440 | tf_op jit(solution)/shard_map/ppermute | solution.py:36
  66.1 8.7 %collective-permute-start.30 = (s16[528,256]{1,0:T(8,128)(2,1)S(1)}, s16[528,256]{1,0:T(8,128)(2,1)S(1)}, u32[]{:S(2)}, u32[]{:S(2)}) collective-permute-start(s16[528,256]{1,0:T(8,128)(2,1)S(1)} %shard_map.112.refs_2_), channel_id=1, source_target_pairs={{0,8},{4,12},{8,0},{12,4},{16,24},{20,28},{24,16},{28,20},{1,9},{5... | collective-permute-start | bytes 811016 | tf_op jit(solution)/shard_map/ppermute | solution.py:36
  66.7 8.2 %collective-permute-start.31 = (s16[528,256]{1,0:T(8,128)(2,1)S(1)}, s16[528,256]{1,0:T(8,128)(2,1)S(1)}, u32[]{:S(2)}, u32[]{:S(2)}) collective-permute-start(s16[528,256]{1,0:T(8,128)(2,1)S(1)} %shard_map.113.refs_2_), channel_id=1, source_target_pairs={{0,16},{4,20},{8,24},{12,28},{16,0},{20,4},{24,8},{28,12},{1,17},{... | collective-permute-start | bytes 811016 | tf_op jit(solution)/shard_map/ppermute | solution.py:36
  69.0 3.5 %collective-permute-start.32 = (f32[2,128,256]{2,1,0:T(8,128)S(1)}, f32[2,128,256]{2,1,0:T(8,128)S(1)}, u32[]{:S(2)}, u32[]{:S(2)}) collective-permute-start(f32[2,128,256]{2,1,0:T(8,128)S(1)} %get-tuple-element.69), channel_id=1, source_target_pairs={{0,4},{4,0},{8,12},{12,8},{16,20},{20,16},{24,28},{28,24},{1,5},{5... | collective-permute-start | bytes 786440 | tf_op jit(solution)/shard_map/ppermute | solution.py:36
  69.6 2.9 %collective-permute-start.33 = (f32[2,128,256]{2,1,0:T(8,128)S(1)}, f32[2,128,256]{2,1,0:T(8,128)S(1)}, u32[]{:S(2)}, u32[]{:S(2)}) collective-permute-start(f32[2,128,256]{2,1,0:T(8,128)S(1)} %get-tuple-element.70), channel_id=1, source_target_pairs={{0,4},{4,0},{8,12},{12,8},{16,20},{20,16},{24,28},{28,24},{1,5},{5... | collective-permute-start | bytes 786440 | tf_op jit(solution)/shard_map/ppermute | solution.py:36
  71.3 8.4 %collective-permute-start.29 = (f32[4,128,256]{2,1,0:T(8,128)S(1)}, f32[4,128,256]{2,1,0:T(8,128)S(1)}, u32[]{:S(2)}, u32[]{:S(2)}) collective-permute-start(f32[4,128,256]{2,1,0:T(8,128)S(1)} %get-tuple-element.68), channel_id=1, source_target_pairs={{0,4},{4,0},{8,12},{12,8},{16,20},{20,16},{24,28},{28,24},{1,5},{5... | collective-permute-start | bytes 1572872 | tf_op jit(solution)/shard_map/ppermute | solution.py:36
  75.0 8.2 %collective-permute-start.34 = (s16[528,256]{1,0:T(8,128)(2,1)S(1)}, s16[528,256]{1,0:T(8,128)(2,1)S(1)}, u32[]{:S(2)}, u32[]{:S(2)}) collective-permute-start(s16[528,256]{1,0:T(8,128)(2,1)S(1)} %shard_map.118), channel_id=1, source_target_pairs={{0,24},{4,28},{8,16},{12,20},{16,8},{20,12},{24,0},{28,4},{1,25},{... | collective-permute-start | bytes 811016 | tf_op jit(solution)/shard_map/ppermute | solution.py:36
  83.6 9.6 %collective-permute-start.35 = (s16[528,256]{1,0:T(8,128)(2,1)S(1)}, s16[528,256]{1,0:T(8,128)(2,1)S(1)}, u32[]{:S(2)}, u32[]{:S(2)}) collective-permute-start(s16[528,256]{1,0:T(8,128)(2,1)S(1)} %shard_map.119), channel_id=1, source_target_pairs={{0,3},{1,0},{2,1},{3,2},{4,7},{5,4},{6,5},{7,6},{8,11},{9,8},{10,9... | collective-permute-start | bytes 811016 | tf_op jit(solution)/shard_map/ppermute | solution.py:31
  (13 other events, 44.7 us)

commit v8 on v7

--- a/solution.py
+++ b/solution.py
@@ -276,8 +276,10 @@
     add_user_grads(bits, 0, words, pieces, refs[:runs], items, grad)
 
 
-def users_tail_kernel(power, bits, first_run, words, held, *refs):
-    *pieces, factors, noise, partial, new, new_bf, items, grad = refs
+def users_tail_kernel(power, bits, first_run, more, words, held, *refs):
+    *pieces, factors, noise, partial = refs[: -3 - more]
+    new, *new_bf = refs[-3 - more : -2]
+    items, grad = refs[-2:]
     grad[...] = partial[...]
     add_user_grads(bits, first_run, words, pieces, [held], items, grad)
 
@@ -287,7 +289,8 @@
             before + HALF_STEP * (power * grad[t] - PRIOR * before) + ROOT_STEP * noise[t].astype(jnp.float32)
         )
         new[t] = after
-        new_bf[t] = after.astype(jnp.bfloat16)
+        for out in new_bf:
+            out[t] = after.astype(jnp.bfloat16)
         return carry
 
     lax.fori_loop(0, factors.shape[0], finish, 0)
@@ -309,13 +312,13 @@
     )(words, *misfits, *pieces)
 
 
-def users_tail(power, bits, first_run, words, misfits, pieces, factors, noise, partial):
+def users_tail(power, bits, first_run, words, misfits, pieces, factors, noise, partial, more):
     shape = factors.shape
     return pl.pallas_call(
-        functools.partial(users_tail_kernel, power, bits, first_run),
-        out_shape=[jax.ShapeDtypeStruct(shape, jnp.float32), jax.ShapeDtypeStruct(shape, jnp.bfloat16)],
+        functools.partial(users_tail_kernel, power, bits, first_run, more),
+        out_shape=[jax.ShapeDtypeStruct(shape, jnp.float32), jax.ShapeDtypeStruct(shape, jnp.bfloat16)][: 1 + more],
         in_specs=[IN_SMEM, IN_VMEM] + [IN_VMEM] * (len(pieces) + 3),
-        out_specs=[IN_VMEM] * 2,
+        out_specs=[IN_VMEM] * (1 + more),
         scratch_shapes=[pltpu.VMEM(tiles_of(pieces), jnp.bfloat16), pltpu.VMEM(shape, jnp.float32)],
         compiler_params=pltpu.CompilerParams(vmem_limit_bytes=SMALL_LIMIT),
         cost_estimate=BRIEF,
@@ -416,11 +419,13 @@
     )(*operands, *after)
 
 
-def gathered(own, runs):
+def gathered(own, runs, after):
     evens = [own]
     for d in range(1, runs):
         relayed = runs == 4 and d == 3
         evens.append(swapped(evens[1] if relayed else own, "user", 4 if relayed else 2 * d))
+        if d == 1 and after:
+            evens[1] = in_vmem(pass_kernel, jax.ShapeDtypeStruct(own.shape, own.dtype), evens[1], after=after)
     return evens
 
 
@@ -458,7 +463,7 @@
         if section:
             sent = shifted(items_bf, "item", section)
             sent = in_vmem(pass_kernel, jax.ShapeDtypeStruct(sent.shape, sent.dtype), sent, after=(users_bf, words))
-        evens = gathered(sent, runs)
+        evens = gathered(sent, runs, () if section else (words, rated))
         chunks = [[even, swapped(even, "user", 1)] for even in evens]
         mine, other, sums, misfits = {}, {}, {}, {}
         after = [evens[2]]
@@ -505,9 +510,11 @@
             wanted = pair if section + 1 < sections else pair[:1]
             items, *turned = in_vmem(arrive_kernel, wanted, shifted(delta, "item", -section), items)
             items_bf = turned[0] if turned else None
-        users, users_bf = users_tail(
-            power, bits, runs - 1, words, misfits[-1], chunks[-1], users, u_noise[section], partial
+        more = int(section + 1 < sections)
+        users, *rounded = users_tail(
+            power, bits, runs - 1, words, misfits[-1], chunks[-1], users, u_noise[section], partial, more
         )
+        users_bf = rounded[0] if rounded else None
     return (users.reshape(u_factors.shape), items.reshape(v_factors.shape))
 
 

time: 96.1 us -> 97.6 us (1.016); the launches traced: 94.1 us -> 97.6 us
  waiting for transfers between devices: 31.7 us -> 35.9 us
  Pallas kernels: 29.9 us -> 31.9 us
  other arithmetic: 1.71 us -> 0.13 us
  starting transfers between devices: 28 us -> 26.7 us
    ppermute x34, starting transfers between devices: 23.9 us -> 16.7 us  [swapped(): return lax.ppermute(x, axis, [(i, i ^ mask) for i in range(peers)])]
    ppermute x34, waiting for transfers between devices: 24.6 us -> 31.1 us  [swapped(): return lax.ppermute(x, axis, [(i, i ^ mask) for i in range(peers)])]
    ppermute x2, starting transfers between devices: 4.05 us -> 9.99 us  [shifted(): return lax.ppermute(x, axis, [(i, (i + by) % peers) for i in range(peers)])]
    ppermute x2, waiting for transfers between devices: 7.17 us -> 4.85 us  [shifted(): return lax.ppermute(x, axis, [(i, (i + by) % peers) for i in range(peers)])]
    convert_element_type x1, other arithmetic: 1.71 us -> 0.13 us  [body(): users_bf = users.astype(jnp.bfloat16)]
    pallas_call x8, Pallas kernels: 12.1 us -> 13.2 us  [item_grads(): pl.pallas_call(functools.partial(items_kernel, section, run, len(pieces),...]
  transfers between devices with their start and end apart: 36 -> 36, of which waited for: 11 -> 12; matrix products, arithmetic and copies ran while one was open for 2% -> 0% of each run, Pallas kernels for 30% -> 31%
where the time goes in v8:
time: 97.6 us
  waiting for transfers between devices  35.9 us (37%)
  Pallas kernels  31.9 us (33%)
  starting transfers between devices  26.7 us (27%)
  local copies, waits for them, and re-layouts  1.91 us (2%)
  between operations  1.06 us (1%)
    ppermute x34, waiting for transfers between devices, swapped(): return lax.ppermute(x, axis, [(i, i ^ mask) for i in range(peers)])  31.1 us
    ppermute x34, starting transfers between devices, swapped(): return lax.ppermute(x, axis, [(i, i ^ mask) for i in range(peers)])  16.7 us
    pallas_call x8, Pallas kernels, item_grads(): pl.pallas_call(functools.partial(items_kernel, section, run, len(pieces),...  13.2 us
    ppermute x2, starting transfers between devices, shifted(): return lax.ppermute(x, axis, [(i, (i + by) % peers) for i in range(peers)])  9.99 us
    pallas_call x2, Pallas kernels, users_head(): pl.pallas_call(functools.partial(users_head_kernel, bits, len(misfits)),...  5.81 us
    pallas_call x2, Pallas kernels, users_tail(): pl.pallas_call(functools.partial(users_tail_kernel, power, bits, first_ru...  5.35 us
    ppermute x2, waiting for transfers between devices, shifted(): return lax.ppermute(x, axis, [(i, (i + by) % peers) for i in range(peers)])  4.85 us
    pallas_call x1, Pallas kernels, fetch(): pl.pallas_call(functools.partial(fetch_kernel, lump), out_shape=jax.Shape...  2.64 us
  transfers between devices with their start and end apart: 36, of which 12 were waited for; matrix products, arithmetic and copies ran while one was open for 0% of the time, Pallas kernels for 31%

profile of v8, /device:TPU:0, one launch (start us, length us, event | category | flops | bytes accessed | tf_op | source)
XLA Modules:
  0.0 97.6 jit_solution(537642803987763348)
XLA Ops:
  0.6 1.0 %copy-done.3 = f32[512,256]{1,0:T(8,128)S(1)} copy-done((f32[512,256]{1,0:T(8,128)S(1)}, f32[512,256]{1,0:T(8,128)}, u32[]{:S(2)}) %copy-start.3) | copy-done | bytes 524312
  1.8 3.0 %collective-permute-start.3 = (bf16[4,256,128]{2,1,0:T(8,128)(2,1)S(1)}, bf16[4,256,128]{2,1,0:T(8,128)(2,1)S(1)}, u32[]{:S(2)}, u32[]{:S(2)}) collective-permute-start(bf16[4,256,128]{2,1,0:T(8,128)(2,1)S(1)} %shard_map.98.refs_0_.refs_3_), channel_id=1, source_target_pairs={{0,16},{4,20},{8,24},{12,28},{16,0},{20,4},{24,8},{28,12},{1,17},{... | collective-permute-start | bytes 786440 | tf_op jit(solution)/shard_map/ppermute | solution.py:36
  4.8 1.5 %collective-permute-start = (bf16[4,256,128]{2,1,0:T(8,128)(2,1)S(1)}, bf16[4,256,128]{2,1,0:T(8,128)(2,1)S(1)}, u32[]{:S(2)}, u32[]{:S(2)}) collective-permute-start(bf16[4,256,128]{2,1,0:T(8,128)(2,1)S(1)} %shard_map.98.refs_0_.refs_3_), channel_id=1, source_target_pairs={{0,8},{4,12},{8,0},{12,4},{16,24},{20,28},{24,16},{28,20},{1,9},{5... | collective-permute-start | bytes 786440 | tf_op jit(solution)/shard_map/ppermute | solution.py:36
  7.0 2.6 %shard_map.96.refs_1_.ratings = bf16[2,224,128,128]{3,2,1,0:T(8,128)(2,1)S(1)} custom-call(s32[2]{0:T(128)S(1)} %bitcast.19, bf16[2,224,128,128]{3,2,1,0:T(8,128)(2,1)} %bitcast.22), custom_call_target="tpu_custom_call" | custom-call | flops 4000000000 | bytes 4096 | tf_op jit(solution)/shard_map/pallas_call | solution.py:147
  9.7 1.0 %shard_map.97.refs_0_.listed.words = s32[1,256]{1,0:T(1,128)S(1)} custom-call(s32[1]{0:T(128)} %bitcast.me, s32[2]{0:T(128)S(1)} %bitcast.20, s32[1,1,2,224]{3,2,1,0:T(2,128)S(1)} %copy-done.7, s32[1,1,2,224]{3,2,1,0:T(2,128)S(1)} %copy-done.8), custom_call_target="tpu_custom_call" | custom-call | flops 4000000000 | bytes 4096 | tf_op jit(solution)/shard_map/pallas_call | solution.py:102
  10.7 1.9 %collective-permute-done.given = bf16[4,256,128]{2,1,0:T(8,128)(2,1)S(1)} collective-permute-done((bf16[4,256,128]{2,1,0:T(8,128)(2,1)S(1)}, bf16[4,256,128]{2,1,0:T(8,128)(2,1)S(1)}, u32[]{:S(2)}, u32[]{:S(2)}) %collective-permute-start) | collective-permute-done | bytes 262176 | tf_op jit(solution)/shard_map/ppermute | solution.py:36
  14.2 1.6 %shard_map.100 = (f32[4,128,256]{2,1,0:T(8,128)S(1)}, f32[2,128,256]{2,1,0:T(8,128)S(1)}, f32[2,128,256]{2,1,0:T(8,128)S(1)}, bf16[64,256,128]{2,1,0:T(8,128)(2,1)S(1)}) custom-call(s32[1,256]{1,0:T(1,128)S(1)} %shard_map.97.refs_0_.listed.words, bf16[2,224,128,128]{3,2,1,0:T(8,128)(2,1)S(1)} %shard_map.96.refs_1_.ratings, ...), custom_call_target="tpu_custom_call" | custom-call | flops 4000000000 | bytes 4096 | tf_op jit(solution)/shard_map/pallas_call | solution.py:233
  16.4 1.6 %shard_map.101 = (f32[4,128,256]{2,1,0:T(8,128)S(1)}, f32[2,128,256]{2,1,0:T(8,128)S(1)}, f32[2,128,256]{2,1,0:T(8,128)S(1)}, bf16[64,256,128]{2,1,0:T(8,128)(2,1)S(1)}) custom-call(s32[1,256]{1,0:T(1,128)S(1)} %shard_map.97.refs_0_.listed.words, bf16[2,224,128,128]{3,2,1,0:T(8,128)(2,1)S(1)} %shard_map.96.refs_1_.ratings, ...), custom_call_target="tpu_custom_call" | custom-call | flops 4000000000 | bytes 4096 | tf_op jit(solution)/shard_map/pallas_call | solution.py:233
  18.7 3.0 %collective-permute-done.1.refs_0_ = bf16[4,256,128]{2,1,0:T(8,128)(2,1)S(1)} collective-permute-done((bf16[4,256,128]{2,1,0:T(8,128)(2,1)S(1)}, bf16[4,256,128]{2,1,0:T(8,128)(2,1)S(1)}, u32[]{:S(2)}, u32[]{:S(2)}) %collective-permute-start.1) | collective-permute-done | bytes 262176 | tf_op jit(solution)/shard_map/ppermute | solution.py:36
  22.3 1.6 %collective-permute-start.12 = (s16[528,256]{1,0:T(8,128)(2,1)S(1)}, s16[528,256]{1,0:T(8,128)(2,1)S(1)}, u32[]{:S(2)}, u32[]{:S(2)}) collective-permute-start(s16[528,256]{1,0:T(8,128)(2,1)S(1)} %shard_map.102.refs_2_), channel_id=1, source_target_pairs={{0,8},{4,12},{8,0},{12,4},{16,24},{20,28},{24,16},{28,20},{1,9},{5... | collective-permute-start | bytes 811016 | tf_op jit(solution)/shard_map/ppermute | solution.py:36
  24.6 1.6 %shard_map.104 = (f32[4,128,256]{2,1,0:T(8,128)S(1)}, f32[2,128,256]{2,1,0:T(8,128)S(1)}, f32[2,128,256]{2,1,0:T(8,128)S(1)}, bf16[64,256,128]{2,1,0:T(8,128)(2,1)S(1)}) custom-call(s32[1,256]{1,0:T(1,128)S(1)} %shard_map.97.refs_0_.listed.words, bf16[2,224,128,128]{3,2,1,0:T(8,128)(2,1)S(1)} %shard_map.96.refs_1_.ratings, ...), custom_call_target="tpu_custom_call" | custom-call | flops 4000000000 | bytes 4096 | tf_op jit(solution)/shard_map/pallas_call | solution.py:233
  26.8 2.0 %shard_map.105 = (f32[4,128,256]{2,1,0:T(8,128)S(1)}, f32[4,128,256]{2,1,0:T(8,128)S(1)}, bf16[64,256,128]{2,1,0:T(8,128)(2,1)S(1)}) custom-call(s32[1,256]{1,0:T(1,128)S(1)} %shard_map.97.refs_0_.listed.words, bf16[2,224,128,128]{3,2,1,0:T(8,128)(2,1)S(1)} %shard_map.96.refs_1_.ratings, bf16[16,128,256]{2,1,0:T(8,128)(2,1)S(1)} %convert_element_type.3.users, ...), custom_call_target="tpu_custom_call" | custom-call | flops 4000000000 | bytes 4096 | tf_op jit(solution)/shard_map/pallas_call | solution.py:233
  28.9 3.3 %collective-permute-done.13.refs_4_.refs_1_ = s16[528,256]{1,0:T(8,128)(2,1)S(1)} collective-permute-done((s16[528,256]{1,0:T(8,128)(2,1)S(1)}, s16[528,256]{1,0:T(8,128)(2,1)S(1)}, u32[]{:S(2)}, u32[]{:S(2)}) %collective-permute-start.13) | collective-permute-done | bytes 270368 | tf_op jit(solution)/shard_map/ppermute | solution.py:36
  32.9 3.1 %shard_map.106.refs_4_.refs_5_ = f32[16,128,256]{2,1,0:T(8,128)S(1)} custom-call(s32[1,256]{1,0:T(1,128)S(1)} %shard_map.97.refs_0_.listed.words, bf16[64,256,128]{2,1,0:T(8,128)(2,1)S(1)} %get-tuple-element.44.refs_0_, bf16[64,256,128]{2,1,0:T(8,128)(2,1)S(1)} %get-tuple-element.45.refs_1_, bf16[64,256,128]{2,1,0:T(8,128)(2,1)S(1)} %copy-done.2, ...), custom_call_target="tpu_custom_call" | custom-call | flops 100000000 | bytes 4096 | tf_op jit(solution)/shard_map/pallas_call | solution.py:304
  36.0 4.5 %collective-permute-done.16.refs_2_ = s16[528,256]{1,0:T(8,128)(2,1)S(1)} collective-permute-done((s16[528,256]{1,0:T(8,128)(2,1)S(1)}, s16[528,256]{1,0:T(8,128)(2,1)S(1)}, u32[]{:S(2)}, u32[]{:S(2)}) %collective-permute-start.16) | collective-permute-done | bytes 270368 | tf_op jit(solution)/shard_map/ppermute | solution.py:36
  41.0 1.6 %collective-permute-start.17 = (bf16[4,256,128]{2,1,0:T(8,128)(2,1)S(1)}, bf16[4,256,128]{2,1,0:T(8,128)(2,1)S(1)}, u32[]{:S(2)}, u32[]{:S(2)}) collective-permute-start(bf16[4,256,128]{2,1,0:T(8,128)(2,1)S(1)} %get-tuple-element.52), channel_id=1, source_target_pairs={{0,1},{1,2},{2,3},{3,0},{4,5},{5,6},{6,7},{7,4},{8,9},{9,10},{10,1... | collective-permute-start | bytes 786440 | tf_op jit(solution)/shard_map/ppermute | solution.py:31
  42.6 1.0 %shard_map.95.refs_1_.listed.words = s32[1,256]{1,0:T(1,128)S(1)} custom-call(s32[1]{0:T(128)} %bitcast.me, s32[2]{0:T(128)S(1)} %bitcast.21, s32[1,1,2,224]{3,2,1,0:T(2,128)S(1)} %copy-done.7, s32[1,1,2,224]{3,2,1,0:T(2,128)S(1)} %copy-done.8), custom_call_target="tpu_custom_call" | custom-call | flops 4000000000 | bytes 4096 | tf_op jit(solution)/shard_map/pallas_call | solution.py:102
  43.6 2.0 %shard_map.107 = (f32[16,128,256]{2,1,0:T(8,128)S(1)}, bf16[16,128,256]{2,1,0:T(8,128)(2,1)S(1)}) custom-call(s32[1,256]{1,0:T(1,128)S(1)} %shard_map.97.refs_0_.listed.words, bf16[64,256,128]{2,1,0:T(8,128)(2,1)S(1)} %get-tuple-element.42.held, bf16[4,256,128]{2,1,0:T(8,128)(2,1)S(1)} %collective-permute-done.1.refs_0_, ...), custom_call_target="tpu_custom_call" | custom-call | flops 100000000 | bytes 4096 | tf_op jit(solution)/shard_map/pallas_call | solution.py:317
  45.7 3.5 %collective-permute-done.17.given = bf16[4,256,128]{2,1,0:T(8,128)(2,1)S(1)} collective-permute-done((bf16[4,256,128]{2,1,0:T(8,128)(2,1)S(1)}, bf16[4,256,128]{2,1,0:T(8,128)(2,1)S(1)}, u32[]{:S(2)}, u32[]{:S(2)}) %collective-permute-start.17) | collective-permute-done | bytes 262176 | tf_op jit(solution)/shard_map/ppermute | solution.py:31
  50.4 5.2 %collective-permute-done.18.refs_0_.refs_5_ = bf16[4,256,128]{2,1,0:T(8,128)(2,1)S(1)} collective-permute-done((bf16[4,256,128]{2,1,0:T(8,128)(2,1)S(1)}, bf16[4,256,128]{2,1,0:T(8,128)(2,1)S(1)}, u32[]{:S(2)}, u32[]{:S(2)}) %collective-permute-start.18) | collective-permute-done | bytes 262176 | tf_op jit(solution)/shard_map/ppermute | solution.py:36
  57.2 1.6 %shard_map.111 = (f32[4,128,256]{2,1,0:T(8,128)S(1)}, f32[2,128,256]{2,1,0:T(8,128)S(1)}, f32[2,128,256]{2,1,0:T(8,128)S(1)}, bf16[64,256,128]{2,1,0:T(8,128)(2,1)S(1)}) custom-call(s32[1,256]{1,0:T(1,128)S(1)} %shard_map.95.refs_1_.listed.words, bf16[2,224,128,128]{3,2,1,0:T(8,128)(2,1)S(1)} %shard_map.96.refs_1_.ratings, ...), custom_call_target="tpu_custom_call" | custom-call | flops 4000000000 | bytes 4096 | tf_op jit(solution)/shard_map/pallas_call | solution.py:233
  59.4 1.8 %shard_map.112 = (f32[4,128,256]{2,1,0:T(8,128)S(1)}, f32[2,128,256]{2,1,0:T(8,128)S(1)}, f32[2,128,256]{2,1,0:T(8,128)S(1)}, bf16[64,256,128]{2,1,0:T(8,128)(2,1)S(1)}) custom-call(s32[1,256]{1,0:T(1,128)S(1)} %shard_map.95.refs_1_.listed.words, bf16[2,224,128,128]{3,2,1,0:T(8,128)(2,1)S(1)} %shard_map.96.refs_1_.ratings, ...), custom_call_target="tpu_custom_call" | custom-call | flops 4000000000 | bytes 4096 | tf_op jit(solution)/shard_map/pallas_call | solution.py:233
  61.7 2.7 %collective-permute-done.19.refs_0_ = bf16[4,256,128]{2,1,0:T(8,128)(2,1)S(1)} collective-permute-done((bf16[4,256,128]{2,1,0:T(8,128)(2,1)S(1)}, bf16[4,256,128]{2,1,0:T(8,128)(2,1)S(1)}, u32[]{:S(2)}, u32[]{:S(2)}) %collective-permute-start.19) | collective-permute-done | bytes 262176 | tf_op jit(solution)/shard_map/ppermute | solution.py:36
  65.1 1.3 %collective-permute-start.30 = (s16[528,256]{1,0:T(8,128)(2,1)S(1)}, s16[528,256]{1,0:T(8,128)(2,1)S(1)}, u32[]{:S(2)}, u32[]{:S(2)}) collective-permute-start(s16[528,256]{1,0:T(8,128)(2,1)S(1)} %shard_map.113.refs_2_), channel_id=1, source_target_pairs={{0,8},{4,12},{8,0},{12,4},{16,24},{20,28},{24,16},{28,20},{1,9},{5... | collective-permute-start | bytes 811016 | tf_op jit(solution)/shard_map/ppermute | solution.py:36
  66.7 1.6 %shard_map.115 = (f32[4,128,256]{2,1,0:T(8,128)S(1)}, f32[2,128,256]{2,1,0:T(8,128)S(1)}, f32[2,128,256]{2,1,0:T(8,128)S(1)}, bf16[64,256,128]{2,1,0:T(8,128)(2,1)S(1)}) custom-call(s32[1,256]{1,0:T(1,128)S(1)} %shard_map.95.refs_1_.listed.words, bf16[2,224,128,128]{3,2,1,0:T(8,128)(2,1)S(1)} %shard_map.96.refs_1_.ratings, ...), custom_call_target="tpu_custom_call" | custom-call | flops 4000000000 | bytes 4096 | tf_op jit(solution)/shard_map/pallas_call | solution.py:233
  68.8 1.6 %shard_map.116 = (f32[4,128,256]{2,1,0:T(8,128)S(1)}, f32[4,128,256]{2,1,0:T(8,128)S(1)}, bf16[64,256,128]{2,1,0:T(8,128)(2,1)S(1)}) custom-call(s32[1,256]{1,0:T(1,128)S(1)} %shard_map.95.refs_1_.listed.words, bf16[2,224,128,128]{3,2,1,0:T(8,128)(2,1)S(1)} %shard_map.96.refs_1_.ratings, bf16[16,128,256]{2,1,0:T(8,128)(2,1)S(1)} %get-tuple-element.47.refs_0_.users, ...), custom_call_target="tpu_custom_call" | custom-call | flops 4000000000 | bytes 4096 | tf_op jit(solution)/shard_map/pallas_call | solution.py:233
  70.5 4.3 %collective-permute-done.31.refs_4_.refs_1_ = s16[528,256]{1,0:T(8,128)(2,1)S(1)} collective-permute-done((s16[528,256]{1,0:T(8,128)(2,1)S(1)}, s16[528,256]{1,0:T(8,128)(2,1)S(1)}, u32[]{:S(2)}, u32[]{:S(2)}) %collective-permute-start.31) | collective-permute-done | bytes 270368 | tf_op jit(solution)/shard_map/ppermute | solution.py:36
  75.7 2.7 %shard_map.117.refs_4_ = f32[16,128,256]{2,1,0:T(8,128)S(1)} custom-call(s32[1,256]{1,0:T(1,128)S(1)} %shard_map.95.refs_1_.listed.words, bf16[64,256,128]{2,1,0:T(8,128)(2,1)S(1)} %get-tuple-element.62.refs_0_, bf16[64,256,128]{2,1,0:T(8,128)(2,1)S(1)} %get-tuple-element.63.refs_1_, bf16[64,256,128]{2,1,0:T(8,128)(2,1)S(1)} %get-tuple-element.64.refs_2_, ...), custom_call_target="tpu_custom_call" | custom-call | flops 100000000 | bytes 4096 | tf_op jit(solution)/shard_map/pallas_call | solution.py:304
  78.5 4.7 %collective-permute-done.34.refs_2_ = s16[528,256]{1,0:T(8,128)(2,1)S(1)} collective-permute-done((s16[528,256]{1,0:T(8,128)(2,1)S(1)}, s16[528,256]{1,0:T(8,128)(2,1)S(1)}, u32[]{:S(2)}, u32[]{:S(2)}) %collective-permute-start.34) | collective-permute-done | bytes 270368 | tf_op jit(solution)/shard_map/ppermute | solution.py:36
  83.7 8.4 %collective-permute-start.35 = (s16[528,256]{1,0:T(8,128)(2,1)S(1)}, s16[528,256]{1,0:T(8,128)(2,1)S(1)}, u32[]{:S(2)}, u32[]{:S(2)}) collective-permute-start(s16[528,256]{1,0:T(8,128)(2,1)S(1)} %shard_map.120), channel_id=1, source_target_pairs={{0,3},{1,0},{2,1},{3,2},{4,7},{5,4},{6,5},{7,6},{8,11},{9,8},{10,9... | collective-permute-start | bytes 811016 | tf_op jit(solution)/shard_map/ppermute | solution.py:31
  92.0 3.3 %shard_map.118 = f32[16,128,256]{2,1,0:T(8,128)} custom-call(s32[1,256]{1,0:T(1,128)S(1)} %shard_map.95.refs_1_.listed.words, bf16[64,256,128]{2,1,0:T(8,128)(2,1)S(1)} %get-tuple-element.59.held, bf16[4,256,128]{2,1,0:T(8,128)(2,1)S(1)} %collective-permute-done.19.refs_0_, bf16[4,256,128]{2,1,0:T(8,128)(2,1)S(1)} %collective-permute-done.20.refs_1_, ...), custom_call_target="tpu_custom_call" | custom-call | flops 100000000 | bytes 4096 | tf_op jit(solution)/shard_map/pallas_call | solution.py:317
  95.4 1.3 %collective-permute-done.35.coded = s16[528,256]{1,0:T(8,128)(2,1)S(1)} collective-permute-done((s16[528,256]{1,0:T(8,128)(2,1)S(1)}, s16[528,256]{1,0:T(8,128)(2,1)S(1)}, u32[]{:S(2)}, u32[]{:S(2)}) %collective-permute-start.35) | collective-permute-done | bytes 270368 | tf_op jit(solution)/shard_map/ppermute | solution.py:31
  (92 shorter events, 14.6 us)
Async XLA Ops:
  1.8 11.8 %collective-permute-start.3 = (bf16[4,256,128]{2,1,0:T(8,128)(2,1)S(1)}, bf16[4,256,128]{2,1,0:T(8,128)(2,1)S(1)}, u32[]{:S(2)}, u32[]{:S(2)}) collective-permute-start(bf16[4,256,128]{2,1,0:T(8,128)(2,1)S(1)} %shard_map.98.refs_0_.refs_3_), channel_id=1, source_target_pairs={{0,16},{4,20},{8,24},{12,28},{16,0},{20,4},{24,8},{28,12},{1,17},{... | collective-permute-start | bytes 786440 | tf_op jit(solution)/shard_map/ppermute | solution.py:36
  4.8 7.8 %collective-permute-start = (bf16[4,256,128]{2,1,0:T(8,128)(2,1)S(1)}, bf16[4,256,128]{2,1,0:T(8,128)(2,1)S(1)}, u32[]{:S(2)}, u32[]{:S(2)}) collective-permute-start(bf16[4,256,128]{2,1,0:T(8,128)(2,1)S(1)} %shard_map.98.refs_0_.refs_3_), channel_id=1, source_target_pairs={{0,8},{4,12},{8,0},{12,4},{16,24},{20,28},{24,16},{28,20},{1,9},{5... | collective-permute-start | bytes 786440 | tf_op jit(solution)/shard_map/ppermute | solution.py:36
  12.8 8.8 %collective-permute-start.1 = (bf16[4,256,128]{2,1,0:T(8,128)(2,1)S(1)}, bf16[4,256,128]{2,1,0:T(8,128)(2,1)S(1)}, u32[]{:S(2)}, u32[]{:S(2)}) collective-permute-start(bf16[4,256,128]{2,1,0:T(8,128)(2,1)S(1)} %shard_map.99.refs_0_.refs_5_), channel_id=1, source_target_pairs={{0,16},{4,20},{8,24},{12,28},{16,0},{20,4},{24,8},{28,12},{1,17},{... | collective-permute-start | bytes 786440 | tf_op jit(solution)/shard_map/ppermute | solution.py:36
  13.6 2.8 %collective-permute-start.4 = (bf16[4,256,128]{2,1,0:T(8,128)(2,1)S(1)}, bf16[4,256,128]{2,1,0:T(8,128)(2,1)S(1)}, u32[]{:S(2)}, u32[]{:S(2)}) collective-permute-start(bf16[4,256,128]{2,1,0:T(8,128)(2,1)S(1)} %collective-permute-done.3.refs_2_.refs_0_.refs_7_), channel_id=1, source_target_pairs={{0,4},{4,0},{8,12},{12,8},{16,20},{20,16},{24,28},{28,24},{1,5},{5... | collective-permute-start | bytes 786440 | tf_op jit(solution)/shard_map/ppermute | solution.py:36
  15.8 5.8 %collective-permute-start.8 = (f32[2,128,256]{2,1,0:T(8,128)S(1)}, f32[2,128,256]{2,1,0:T(8,128)S(1)}, u32[]{:S(2)}, u32[]{:S(2)}) collective-permute-start(f32[2,128,256]{2,1,0:T(8,128)S(1)} %get-tuple-element.40), channel_id=1, source_target_pairs={{0,4},{4,0},{8,12},{12,8},{16,20},{20,16},{24,28},{28,24},{1,5},{5... | collective-permute-start | bytes 786440 | tf_op jit(solution)/shard_map/ppermute | solution.py:36
  16.0 6.1 %collective-permute-start.9 = (f32[2,128,256]{2,1,0:T(8,128)S(1)}, f32[2,128,256]{2,1,0:T(8,128)S(1)}, u32[]{:S(2)}, u32[]{:S(2)}) collective-permute-start(f32[2,128,256]{2,1,0:T(8,128)S(1)} %get-tuple-element.41), channel_id=1, source_target_pairs={{0,4},{4,0},{8,12},{12,8},{16,20},{20,16},{24,28},{28,24},{1,5},{5... | collective-permute-start | bytes 786440 | tf_op jit(solution)/shard_map/ppermute | solution.py:36
  18.0 5.8 %collective-permute-start.6 = (f32[2,128,256]{2,1,0:T(8,128)S(1)}, f32[2,128,256]{2,1,0:T(8,128)S(1)}, u32[]{:S(2)}, u32[]{:S(2)}) collective-permute-start(f32[2,128,256]{2,1,0:T(8,128)S(1)} %get-tuple-element.38), channel_id=1, source_target_pairs={{0,4},{4,0},{8,12},{12,8},{16,20},{20,16},{24,28},{28,24},{1,5},{5... | collective-permute-start | bytes 786440 | tf_op jit(solution)/shard_map/ppermute | solution.py:36
  18.6 5.3 %collective-permute-start.7 = (f32[2,128,256]{2,1,0:T(8,128)S(1)}, f32[2,128,256]{2,1,0:T(8,128)S(1)}, u32[]{:S(2)}, u32[]{:S(2)}) collective-permute-start(f32[2,128,256]{2,1,0:T(8,128)S(1)} %get-tuple-element.39), channel_id=1, source_target_pairs={{0,4},{4,0},{8,12},{12,8},{16,20},{20,16},{24,28},{28,24},{1,5},{5... | collective-permute-start | bytes 786440 | tf_op jit(solution)/shard_map/ppermute | solution.py:36
  21.6 3.0 %collective-permute-start.2 = (bf16[4,256,128]{2,1,0:T(8,128)(2,1)S(1)}, bf16[4,256,128]{2,1,0:T(8,128)(2,1)S(1)}, u32[]{:S(2)}, u32[]{:S(2)}) collective-permute-start(bf16[4,256,128]{2,1,0:T(8,128)(2,1)S(1)} %collective-permute-done.1.refs_0_), channel_id=1, source_target_pairs={{0,4},{4,0},{8,12},{12,8},{16,20},{20,16},{24,28},{28,24},{1,5},{5... | collective-permute-start | bytes 786440 | tf_op jit(solution)/shard_map/ppermute | solution.py:36
  21.6 5.1 %collective-permute-start.10 = (bf16[4,256,128]{2,1,0:T(8,128)(2,1)S(1)}, bf16[4,256,128]{2,1,0:T(8,128)(2,1)S(1)}, u32[]{:S(2)}, u32[]{:S(2)}) collective-permute-start(bf16[4,256,128]{2,1,0:T(8,128)(2,1)S(1)} %shard_map.98.refs_0_.refs_3_), channel_id=1, source_target_pairs={{0,4},{4,0},{8,12},{12,8},{16,20},{20,16},{24,28},{28,24},{1,5},{5... | collective-permute-start | bytes 786440 | tf_op jit(solution)/shard_map/ppermute | solution.py:36
  22.3 9.9 %collective-permute-start.12 = (s16[528,256]{1,0:T(8,128)(2,1)S(1)}, s16[528,256]{1,0:T(8,128)(2,1)S(1)}, u32[]{:S(2)}, u32[]{:S(2)}) collective-permute-start(s16[528,256]{1,0:T(8,128)(2,1)S(1)} %shard_map.102.refs_2_), channel_id=1, source_target_pairs={{0,8},{4,12},{8,0},{12,4},{16,24},{20,28},{24,16},{28,20},{1,9},{5... | collective-permute-start | bytes 811016 | tf_op jit(solution)/shard_map/ppermute | solution.py:36
  24.0 8.2 %collective-permute-start.13 = (s16[528,256]{1,0:T(8,128)(2,1)S(1)}, s16[528,256]{1,0:T(8,128)(2,1)S(1)}, u32[]{:S(2)}, u32[]{:S(2)}) collective-permute-start(s16[528,256]{1,0:T(8,128)(2,1)S(1)} %shard_map.103.refs_2_), channel_id=1, source_target_pairs={{0,16},{4,20},{8,24},{12,28},{16,0},{20,4},{24,8},{28,12},{1,17},{... | collective-permute-start | bytes 811016 | tf_op jit(solution)/shard_map/ppermute | solution.py:36
  26.2 2.7 %collective-permute-start.14 = (f32[2,128,256]{2,1,0:T(8,128)S(1)}, f32[2,128,256]{2,1,0:T(8,128)S(1)}, u32[]{:S(2)}, u32[]{:S(2)}) collective-permute-start(f32[2,128,256]{2,1,0:T(8,128)S(1)} %get-tuple-element.50), channel_id=1, source_target_pairs={{0,4},{4,0},{8,12},{12,8},{16,20},{20,16},{24,28},{28,24},{1,5},{5... | collective-permute-start | bytes 786440 | tf_op jit(solution)/shard_map/ppermute | solution.py:36
  26.3 2.6 %collective-permute-start.15 = (f32[2,128,256]{2,1,0:T(8,128)S(1)}, f32[2,128,256]{2,1,0:T(8,128)S(1)}, u32[]{:S(2)}, u32[]{:S(2)}) collective-permute-start(f32[2,128,256]{2,1,0:T(8,128)S(1)} %get-tuple-element.51), channel_id=1, source_target_pairs={{0,4},{4,0},{8,12},{12,8},{16,20},{20,16},{24,28},{28,24},{1,5},{5... | collective-permute-start | bytes 786440 | tf_op jit(solution)/shard_map/ppermute | solution.py:36
  28.8 7.3 %collective-permute-start.11 = (f32[4,128,256]{2,1,0:T(8,128)S(1)}, f32[4,128,256]{2,1,0:T(8,128)S(1)}, u32[]{:S(2)}, u32[]{:S(2)}) collective-permute-start(f32[4,128,256]{2,1,0:T(8,128)S(1)} %get-tuple-element.49), channel_id=1, source_target_pairs={{0,4},{4,0},{8,12},{12,8},{16,20},{20,16},{24,28},{28,24},{1,5},{5... | collective-permute-start | bytes 1572872 | tf_op jit(solution)/shard_map/ppermute | solution.py:36
  32.3 8.2 %collective-permute-start.16 = (s16[528,256]{1,0:T(8,128)(2,1)S(1)}, s16[528,256]{1,0:T(8,128)(2,1)S(1)}, u32[]{:S(2)}, u32[]{:S(2)}) collective-permute-start(s16[528,256]{1,0:T(8,128)(2,1)S(1)} %shard_map.108), channel_id=1, source_target_pairs={{0,24},{4,28},{8,16},{12,20},{16,8},{20,12},{24,0},{28,4},{1,25},{... | collective-permute-start | bytes 811016 | tf_op jit(solution)/shard_map/ppermute | solution.py:36
  41.0 8.2 %collective-permute-start.17 = (bf16[4,256,128]{2,1,0:T(8,128)(2,1)S(1)}, bf16[4,256,128]{2,1,0:T(8,128)(2,1)S(1)}, u32[]{:S(2)}, u32[]{:S(2)}) collective-permute-start(bf16[4,256,128]{2,1,0:T(8,128)(2,1)S(1)} %get-tuple-element.52), channel_id=1, source_target_pairs={{0,1},{1,2},{2,3},{3,0},{4,5},{5,6},{6,7},{7,4},{8,9},{9,10},{10,1... | collective-permute-start | bytes 786440 | tf_op jit(solution)/shard_map/ppermute | solution.py:31
  49.2 6.4 %collective-permute-start.18 = (bf16[4,256,128]{2,1,0:T(8,128)(2,1)S(1)}, bf16[4,256,128]{2,1,0:T(8,128)(2,1)S(1)}, u32[]{:S(2)}, u32[]{:S(2)}) collective-permute-start(bf16[4,256,128]{2,1,0:T(8,128)(2,1)S(1)} %shard_map.110.refs_0_.refs_3_), channel_id=1, source_target_pairs={{0,8},{4,12},{8,0},{12,4},{16,24},{20,28},{24,16},{28,20},{1,9},{5... | collective-permute-start | bytes 786440 | tf_op jit(solution)/shard_map/ppermute | solution.py:36
  49.8 6.4 %collective-permute-start.21 = (bf16[4,256,128]{2,1,0:T(8,128)(2,1)S(1)}, bf16[4,256,128]{2,1,0:T(8,128)(2,1)S(1)}, u32[]{:S(2)}, u32[]{:S(2)}) collective-permute-start(bf16[4,256,128]{2,1,0:T(8,128)(2,1)S(1)} %shard_map.110.refs_0_.refs_3_), channel_id=1, source_target_pairs={{0,16},{4,20},{8,24},{12,28},{16,0},{20,4},{24,8},{28,12},{1,17},{... | collective-permute-start | bytes 786440 | tf_op jit(solution)/shard_map/ppermute | solution.py:36
  55.7 8.7 %collective-permute-start.19 = (bf16[4,256,128]{2,1,0:T(8,128)(2,1)S(1)}, bf16[4,256,128]{2,1,0:T(8,128)(2,1)S(1)}, u32[]{:S(2)}, u32[]{:S(2)}) collective-permute-start(bf16[4,256,128]{2,1,0:T(8,128)(2,1)S(1)} %collective-permute-done.18.refs_0_.refs_5_), channel_id=1, source_target_pairs={{0,16},{4,20},{8,24},{12,28},{16,0},{20,4},{24,8},{28,12},{1,17},{... | collective-permute-start | bytes 786440 | tf_op jit(solution)/shard_map/ppermute | solution.py:36
  56.2 3.2 %collective-permute-start.22 = (bf16[4,256,128]{2,1,0:T(8,128)(2,1)S(1)}, bf16[4,256,128]{2,1,0:T(8,128)(2,1)S(1)}, u32[]{:S(2)}, u32[]{:S(2)}) collective-permute-start(bf16[4,256,128]{2,1,0:T(8,128)(2,1)S(1)} %collective-permute-done.21.refs_2_.refs_0_.refs_7_), channel_id=1, source_target_pairs={{0,4},{4,0},{8,12},{12,8},{16,20},{20,16},{24,28},{28,24},{1,5},{5... | collective-permute-start | bytes 786440 | tf_op jit(solution)/shard_map/ppermute | solution.py:36
  58.8 5.6 %collective-permute-start.26 = (f32[2,128,256]{2,1,0:T(8,128)S(1)}, f32[2,128,256]{2,1,0:T(8,128)S(1)}, u32[]{:S(2)}, u32[]{:S(2)}) collective-permute-start(f32[2,128,256]{2,1,0:T(8,128)S(1)} %get-tuple-element.57), channel_id=1, source_target_pairs={{0,4},{4,0},{8,12},{12,8},{16,20},{20,16},{24,28},{28,24},{1,5},{5... | collective-permute-start | bytes 786440 | tf_op jit(solution)/shard_map/ppermute | solution.py:36
  59.0 5.9 %collective-permute-start.27 = (f32[2,128,256]{2,1,0:T(8,128)S(1)}, f32[2,128,256]{2,1,0:T(8,128)S(1)}, u32[]{:S(2)}, u32[]{:S(2)}) collective-permute-start(f32[2,128,256]{2,1,0:T(8,128)S(1)} %get-tuple-element.58), channel_id=1, source_target_pairs={{0,4},{4,0},{8,12},{12,8},{16,20},{20,16},{24,28},{28,24},{1,5},{5... | collective-permute-start | bytes 786440 | tf_op jit(solution)/shard_map/ppermute | solution.py:36
  61.1 5.3 %collective-permute-start.24 = (f32[2,128,256]{2,1,0:T(8,128)S(1)}, f32[2,128,256]{2,1,0:T(8,128)S(1)}, u32[]{:S(2)}, u32[]{:S(2)}) collective-permute-start(f32[2,128,256]{2,1,0:T(8,128)S(1)} %get-tuple-element.55), channel_id=1, source_target_pairs={{0,4},{4,0},{8,12},{12,8},{16,20},{20,16},{24,28},{28,24},{1,5},{5... | collective-permute-start | bytes 786440 | tf_op jit(solution)/shard_map/ppermute | solution.py:36
  61.3 5.1 %collective-permute-start.25 = (f32[2,128,256]{2,1,0:T(8,128)S(1)}, f32[2,128,256]{2,1,0:T(8,128)S(1)}, u32[]{:S(2)}, u32[]{:S(2)}) collective-permute-start(f32[2,128,256]{2,1,0:T(8,128)S(1)} %get-tuple-element.56), channel_id=1, source_target_pairs={{0,4},{4,0},{8,12},{12,8},{16,20},{20,16},{24,28},{28,24},{1,5},{5... | collective-permute-start | bytes 786440 | tf_op jit(solution)/shard_map/ppermute | solution.py:36
  64.4 2.3 %collective-permute-start.20 = (bf16[4,256,128]{2,1,0:T(8,128)(2,1)S(1)}, bf16[4,256,128]{2,1,0:T(8,128)(2,1)S(1)}, u32[]{:S(2)}, u32[]{:S(2)}) collective-permute-start(bf16[4,256,128]{2,1,0:T(8,128)(2,1)S(1)} %collective-permute-done.19.refs_0_), channel_id=1, source_target_pairs={{0,4},{4,0},{8,12},{12,8},{16,20},{20,16},{24,28},{28,24},{1,5},{5... | collective-permute-start | bytes 786440 | tf_op jit(solution)/shard_map/ppermute | solution.py:36
  64.4 4.4 %collective-permute-start.28 = (bf16[4,256,128]{2,1,0:T(8,128)(2,1)S(1)}, bf16[4,256,128]{2,1,0:T(8,128)(2,1)S(1)}, u32[]{:S(2)}, u32[]{:S(2)}) collective-permute-start(bf16[4,256,128]{2,1,0:T(8,128)(2,1)S(1)} %shard_map.110.refs_0_.refs_3_), channel_id=1, source_target_pairs={{0,4},{4,0},{8,12},{12,8},{16,20},{20,16},{24,28},{28,24},{1,5},{5... | collective-permute-start | bytes 786440 | tf_op jit(solution)/shard_map/ppermute | solution.py:36
  65.1 9.8 %collective-permute-start.30 = (s16[528,256]{1,0:T(8,128)(2,1)S(1)}, s16[528,256]{1,0:T(8,128)(2,1)S(1)}, u32[]{:S(2)}, u32[]{:S(2)}) collective-permute-start(s16[528,256]{1,0:T(8,128)(2,1)S(1)} %shard_map.113.refs_2_), channel_id=1, source_target_pairs={{0,8},{4,12},{8,0},{12,4},{16,24},{20,28},{24,16},{28,20},{1,9},{5... | collective-permute-start | bytes 811016 | tf_op jit(solution)/shard_map/ppermute | solution.py:36
  66.6 8.3 %collective-permute-start.31 = (s16[528,256]{1,0:T(8,128)(2,1)S(1)}, s16[528,256]{1,0:T(8,128)(2,1)S(1)}, u32[]{:S(2)}, u32[]{:S(2)}) collective-permute-start(s16[528,256]{1,0:T(8,128)(2,1)S(1)} %shard_map.114.refs_2_), channel_id=1, source_target_pairs={{0,16},{4,20},{8,24},{12,28},{16,0},{20,4},{24,8},{28,12},{1,17},{... | collective-permute-start | bytes 811016 | tf_op jit(solution)/shard_map/ppermute | solution.py:36
  70.4 8.1 %collective-permute-start.29 = (f32[4,128,256]{2,1,0:T(8,128)S(1)}, f32[4,128,256]{2,1,0:T(8,128)S(1)}, u32[]{:S(2)}, u32[]{:S(2)}) collective-permute-start(f32[4,128,256]{2,1,0:T(8,128)S(1)} %get-tuple-element.66), channel_id=1, source_target_pairs={{0,4},{4,0},{8,12},{12,8},{16,20},{20,16},{24,28},{28,24},{1,5},{5... | collective-permute-start | bytes 1572872 | tf_op jit(solution)/shard_map/ppermute | solution.py:36
  75.0 8.3 %collective-permute-start.34 = (s16[528,256]{1,0:T(8,128)(2,1)S(1)}, s16[528,256]{1,0:T(8,128)(2,1)S(1)}, u32[]{:S(2)}, u32[]{:S(2)}) collective-permute-start(s16[528,256]{1,0:T(8,128)(2,1)S(1)} %shard_map.119), channel_id=1, source_target_pairs={{0,24},{4,28},{8,16},{12,20},{16,8},{20,12},{24,0},{28,4},{1,25},{... | collective-permute-start | bytes 811016 | tf_op jit(solution)/shard_map/ppermute | solution.py:36
  83.7 13.0 %collective-permute-start.35 = (s16[528,256]{1,0:T(8,128)(2,1)S(1)}, s16[528,256]{1,0:T(8,128)(2,1)S(1)}, u32[]{:S(2)}, u32[]{:S(2)}) collective-permute-start(s16[528,256]{1,0:T(8,128)(2,1)S(1)} %shard_map.120), channel_id=1, source_target_pairs={{0,3},{1,0},{2,1},{3,2},{4,7},{5,4},{6,5},{7,6},{8,11},{9,8},{10,9... | collective-permute-start | bytes 811016 | tf_op jit(solution)/shard_map/ppermute | solution.py:31
  (15 other events, 53.3 us)

commit v9 on v7

--- a/solution.py
+++ b/solution.py
@@ -17,6 +17,7 @@
 FETCH_LIMIT = 38 * 2**20
 SCALE_STEPS = 128.0
 SCALARS = 16
+PARTS = 4
 LONG = pl.CostEstimate(flops=4 * 10**9, bytes_accessed=2**12, transcendentals=0)
 BRIEF = pl.CostEstimate(flops=10**8, bytes_accessed=2**12, transcendentals=0)
 
@@ -34,6 +35,12 @@
 def swapped(x, axis, mask):
     peers = lax.axis_size(axis)
     return lax.ppermute(x, axis, [(i, i ^ mask) for i in range(peers)])
+
+
+def routed(x, mask, by):
+    across, along = lax.axis_size("user"), lax.axis_size("item")
+    pairs = [(u * along + i, (u ^ mask) * along + (i + by) % along) for u in range(across) for i in range(along)]
+    return lax.ppermute(x, ("user", "item"), pairs)
 
 
 def widths(slots, user_tiles, item_tiles):
@@ -271,7 +278,7 @@
 
 
 def users_head_kernel(bits, runs, words, *refs):
-    *pieces, grad, items = refs[runs:]
+    *pieces, _, grad, items = refs[runs:]
     grad[...] = jnp.zeros_like(grad)
     add_user_grads(bits, 0, words, pieces, refs[:runs], items, grad)
 
@@ -297,16 +304,16 @@
     return sum(piece.shape[0] for piece in pieces), *pieces[0].shape[1:]
 
 
-def users_head(bits, words, misfits, pieces, shape):
+def users_head(bits, words, misfits, pieces, shape, after):
     return pl.pallas_call(
         functools.partial(users_head_kernel, bits, len(misfits)),
         out_shape=jax.ShapeDtypeStruct(shape, jnp.float32),
-        in_specs=[IN_SMEM] + [IN_VMEM] * (len(misfits) + len(pieces)),
+        in_specs=[IN_SMEM] + [IN_VMEM] * (len(misfits) + len(pieces)) + [ANY],
         out_specs=IN_VMEM,
         scratch_shapes=[pltpu.VMEM(tiles_of(pieces), jnp.bfloat16)],
         compiler_params=pltpu.CompilerParams(vmem_limit_bytes=SMALL_LIMIT),
         cost_estimate=BRIEF,
-    )(words, *misfits, *pieces)
+    )(words, *misfits, *pieces, after)
 
 
 def users_tail(power, bits, first_run, words, misfits, pieces, factors, noise, partial):
@@ -379,20 +386,26 @@
         new_bf[t] = after.astype(jnp.bfloat16).T
 
 
-def delta_kernel(power, mine, other, *refs):
-    *coded, noise, _, out = refs
+def delta_kernel(power, parts, count, mine, noise, *refs):
+    per, tile, _ = mine.shape
+    others = [ref[t] for ref in refs[:parts] for t in range(ref.shape[0])]
     steps = []
-    for t in range(mine.shape[0]):
-        steps.append(HALF_STEP * power * owner_sum(mine, other, coded, t) + ROOT_STEP * noise[t].astype(jnp.float32))
-    encode(steps, out)
-
-
-def arrive_kernel(coded, factors, new, *new_bf):
+    for t in range(per):
+        grad = mine[t] + others[t]
+        for coded in refs[parts : parts + count]:
+            grad = grad + decoded(coded, t, tile, per)
+        steps.append(HALF_STEP * power * grad + ROOT_STEP * noise[t].astype(jnp.float32))
+    encode(steps, refs[-1])
+
+
+def arrive_kernel(power, count, factors, delta, *refs):
     per, tile, _ = factors.shape
     for t in range(per):
-        after = factors[t] - HALF_STEP * PRIOR * factors[t] + decoded(coded, t, tile, per)
-        new[t] = after
-        for out in new_bf:
+        grad = sum(decoded(ref, t, tile, per) for ref in refs[:count])
+        after = factors[t] - HALF_STEP * PRIOR * factors[t] + decoded(delta, t, tile, per)
+        after = after + HALF_STEP * power * grad
+        refs[count][t] = after
+        for out in refs[count + 1 :]:
             out[t] = after.astype(jnp.bfloat16).T
 
 
@@ -467,20 +480,32 @@
         order += [(item_grads, runs - 1), (item_grads, 0), (join, runs - 1)]
         for call, run in order:
             if call is item_grads:
+                parts = 1 if not run else 2
+                if section and not run:
+                    parts = min(PARTS, per)
                 mine[run], odd_grads, misfits[run] = item_grads(
-                    section, run, per, bits, words, rated, users_bf, chunks[run], after, 2 if run else 1
+                    section, run, per, bits, words, rated, users_bf, chunks[run], after, parts
                 )
                 other[run] = [swapped(grad, "user", 1) for grad in odd_grads]
                 after = [mine[run]]
             else:
-                if run == runs - 1:
+                if run == runs - 1 and not section:
                     after += list(sums.values())
                 after = [join(mine[run], other[run], after)]
-                sums[run] = swapped(after[0], "user", 2 * run)
+                if section and run == runs - 1:
+                    sums[run] = routed(after[0], 2 * run, -section)
+                else:
+                    sums[run] = swapped(after[0], "user", 2 * run)
+        if section:
+            near = [sums[run] for run in range(1, runs - 1)]
+            share = functools.partial(delta_kernel, power, len(other[0]), len(near))
+            share = in_vmem(
+                share, coded_shape(*items.shape), mine[0], v_noise[section], *other[0], *near, after=after
+            )
         sums = [sums[run] for run in range(1, runs)]
         misfits = [misfits[run] for run in range(runs)]
         head = [piece for chunk in chunks[:-1] for piece in chunk]
-        partial = users_head(bits, words, misfits[:-1], head, users.shape)
+        partial = users_head(bits, words, misfits[:-1], head, users.shape, after[0])
         if section == 0:
             items, items_bf = in_vmem(
                 functools.partial(update_kernel, power),
@@ -493,17 +518,9 @@
                 after=(partial,),
             )
         else:
-            delta = in_vmem(
-                functools.partial(delta_kernel, power),
-                coded_shape(*items.shape),
-                mine[0],
-                other[0][0],
-                *sums,
-                v_noise[section],
-                after=(partial,),
-            )
             wanted = pair if section + 1 < sections else pair[:1]
-            items, *turned = in_vmem(arrive_kernel, wanted, shifted(delta, "item", -section), items)
+            arrive = functools.partial(arrive_kernel, power, 1)
+            items, *turned = in_vmem(arrive, wanted, items, routed(share, 0, -section), sums[-1])
             items_bf = turned[0] if turned else None
         users, users_bf = users_tail(
             power, bits, runs - 1, words, misfits[-1], chunks[-1], users, u_noise[section], partial

time: 96.1 us -> 96.1 us (level)
  waiting for transfers between devices: 31.7 us -> 21.8 us
  Pallas kernels: 29.9 us -> 39.3 us
    ppermute x34 -> x36, waiting for transfers between devices: 24.6 us -> 12.6 us  [swapped(): return lax.ppermute(x, axis, [(i, i ^ mask) for i in range(peers)])]
    ppermute x0 -> x2, waiting for transfers between devices: none -> 4.9 us  [routed(): return lax.ppermute(x, ('user', 'item'), pairs)]
    pallas_call x8, Pallas kernels: 12.1 us -> 16.6 us  [item_grads(): pl.pallas_call(functools.partial(items_kernel, section, run, len(pieces),...]
    ppermute x0 -> x2, starting transfers between devices: none -> 3.93 us  [routed(): return lax.ppermute(x, ('user', 'item'), pairs)]
    ppermute x2 -> x1, starting transfers between devices: 4.05 us -> 0.66 us  [shifted(): return lax.ppermute(x, axis, [(i, (i + by) % peers) for i in range(peers)])]
    pallas_call x2, Pallas kernels: 4.84 us -> 7.76 us  [users_head(): pl.pallas_call(functools.partial(users_head_kernel, bits, len(misfits)),...]
    ppermute x2 -> x1, waiting for transfers between devices: 7.17 us -> 4.37 us  [shifted(): return lax.ppermute(x, axis, [(i, (i + by) % peers) for i in range(peers)])]
    pallas_call x2, Pallas kernels: 5.76 us -> 6.75 us  [users_tail(): pl.pallas_call(functools.partial(users_tail_kernel, power, bits, first_ru...]
  transfers between devices with their start and end apart: 36 -> 39, of which waited for: 11 -> 11; matrix products, arithmetic and copies ran while one was open for 2% -> 2% of each run, Pallas kernels for 30% -> 40%
where the time goes in v9:
time: 96.1 us; the launch traced here: 94.4 us
  Pallas kernels  39.3 us (41%)
  starting transfers between devices  28.7 us (30%)
  waiting for transfers between devices  21.8 us (23%)
  local copies, waits for them, and re-layouts  1.9 us (2%)
  other arithmetic  1.71 us (2%)
    ppermute x36, starting transfers between devices, swapped(): return lax.ppermute(x, axis, [(i, i ^ mask) for i in range(peers)])  24.2 us
    pallas_call x8, Pallas kernels, item_grads(): pl.pallas_call(functools.partial(items_kernel, section, run, len(pieces),...  16.6 us
    ppermute x36, waiting for transfers between devices, swapped(): return lax.ppermute(x, axis, [(i, i ^ mask) for i in range(peers)])  12.6 us
    pallas_call x2, Pallas kernels, users_head(): pl.pallas_call(functools.partial(users_head_kernel, bits, len(misfits)),...  7.76 us
    pallas_call x2, Pallas kernels, users_tail(): pl.pallas_call(functools.partial(users_tail_kernel, power, bits, first_ru...  6.75 us
    ppermute x2, waiting for transfers between devices, routed(): return lax.ppermute(x, ('user', 'item'), pairs)  4.9 us
    ppermute x1, waiting for transfers between devices, shifted(): return lax.ppermute(x, axis, [(i, (i + by) % peers) for i in range(peers)])  4.37 us
    ppermute x2, starting transfers between devices, routed(): return lax.ppermute(x, ('user', 'item'), pairs)  3.93 us
  transfers between devices with their start and end apart: 39, of which 11 were waited for; matrix products, arithmetic and copies ran while one was open for 2% of the time, Pallas kernels for 40%

profile of v9, /device:TPU:0, one launch (start us, length us, event | category | flops | bytes accessed | tf_op | source)
XLA Modules:
  0.0 94.4 jit_solution(16654324974196413038)
XLA Ops:
  1.8 3.0 %collective-permute-start.3 = (bf16[4,256,128]{2,1,0:T(8,128)(2,1)S(1)}, bf16[4,256,128]{2,1,0:T(8,128)(2,1)S(1)}, u32[]{:S(2)}, u32[]{:S(2)}) collective-permute-start(bf16[4,256,128]{2,1,0:T(8,128)(2,1)S(1)} %shard_map.98.refs_0_.refs_3_), channel_id=1, source_target_pairs={{0,16},{4,20},{8,24},{12,28},{16,0},{20,4},{24,8},{28,12},{1,17},{... | collective-permute-start | bytes 786440 | tf_op jit(solution)/shard_map/ppermute | solution.py:37
  4.8 1.5 %collective-permute-start = (bf16[4,256,128]{2,1,0:T(8,128)(2,1)S(1)}, bf16[4,256,128]{2,1,0:T(8,128)(2,1)S(1)}, u32[]{:S(2)}, u32[]{:S(2)}) collective-permute-start(bf16[4,256,128]{2,1,0:T(8,128)(2,1)S(1)} %shard_map.98.refs_0_.refs_3_), channel_id=1, source_target_pairs={{0,8},{4,12},{8,0},{12,4},{16,24},{20,28},{24,16},{28,20},{1,9},{5... | collective-permute-start | bytes 786440 | tf_op jit(solution)/shard_map/ppermute | solution.py:37
  6.3 1.7 %convert_element_type.3.users = bf16[16,128,256]{2,1,0:T(8,128)(2,1)S(1)} convert(f32[16,128,256]{2,1,0:T(8,128)} %bitcast.11) | non-fusion elementwise | flops 524288 | bytes 3145728 | tf_op jit(solution)/shard_map/convert_element_type | solution.py:467
  8.7 3.3 %shard_map.96.ratings = bf16[2,224,128,128]{3,2,1,0:T(8,128)(2,1)S(1)} custom-call(s32[2]{0:T(128)S(1)} %bitcast.19, bf16[2,224,128,128]{3,2,1,0:T(8,128)(2,1)} %bitcast.22), custom_call_target="tpu_custom_call" | custom-call | flops 4000000000 | bytes 4096 | tf_op jit(solution)/shard_map/pallas_call | solution.py:154
  14.3 2.3 %shard_map.99 = (f32[4,128,256]{2,1,0:T(8,128)S(1)}, f32[2,128,256]{2,1,0:T(8,128)S(1)}, f32[2,128,256]{2,1,0:T(8,128)S(1)}, bf16[64,256,128]{2,1,0:T(8,128)(2,1)S(1)}) custom-call(s32[1,256]{1,0:T(1,128)S(1)} %shard_map.97.listed.words, bf16[2,224,128,128]{3,2,1,0:T(8,128)(2,1)S(1)} %shard_map.96.ratings, ...), custom_call_target="tpu_custom_call" | custom-call | flops 4000000000 | bytes 4096 | tf_op jit(solution)/shard_map/pallas_call | solution.py:240
  17.5 2.7 %shard_map.100 = (f32[4,128,256]{2,1,0:T(8,128)S(1)}, f32[2,128,256]{2,1,0:T(8,128)S(1)}, f32[2,128,256]{2,1,0:T(8,128)S(1)}, bf16[64,256,128]{2,1,0:T(8,128)(2,1)S(1)}) custom-call(s32[1,256]{1,0:T(1,128)S(1)} %shard_map.97.listed.words, bf16[2,224,128,128]{3,2,1,0:T(8,128)(2,1)S(1)} %shard_map.96.ratings, ...), custom_call_target="tpu_custom_call" | custom-call | flops 4000000000 | bytes 4096 | tf_op jit(solution)/shard_map/pallas_call | solution.py:240
  20.8 1.7 %collective-permute-done.1.refs_0_ = bf16[4,256,128]{2,1,0:T(8,128)(2,1)S(1)} collective-permute-done((bf16[4,256,128]{2,1,0:T(8,128)(2,1)S(1)}, bf16[4,256,128]{2,1,0:T(8,128)(2,1)S(1)}, u32[]{:S(2)}, u32[]{:S(2)}) %collective-permute-start.1) | collective-permute-done | bytes 262176 | tf_op jit(solution)/shard_map/ppermute | solution.py:37
  23.1 1.6 %collective-permute-start.13 = (s16[528,256]{1,0:T(8,128)(2,1)S(1)}, s16[528,256]{1,0:T(8,128)(2,1)S(1)}, u32[]{:S(2)}, u32[]{:S(2)}) collective-permute-start(s16[528,256]{1,0:T(8,128)(2,1)S(1)} %shard_map.101.refs_2_), channel_id=1, source_target_pairs={{0,8},{4,12},{8,0},{12,4},{16,24},{20,28},{24,16},{28,20},{1,9},{5... | collective-permute-start | bytes 811016 | tf_op jit(solution)/shard_map/ppermute | solution.py:37
  24.8 1.6 %collective-permute-start.14 = (s16[528,256]{1,0:T(8,128)(2,1)S(1)}, s16[528,256]{1,0:T(8,128)(2,1)S(1)}, u32[]{:S(2)}, u32[]{:S(2)}) collective-permute-start(s16[528,256]{1,0:T(8,128)(2,1)S(1)} %shard_map.102.refs_2_), channel_id=1, source_target_pairs={{0,16},{4,20},{8,24},{12,28},{16,0},{20,4},{24,8},{28,12},{1,17},{... | collective-permute-start | bytes 811016 | tf_op jit(solution)/shard_map/ppermute | solution.py:37
  26.4 2.3 %shard_map.103 = (f32[4,128,256]{2,1,0:T(8,128)S(1)}, f32[2,128,256]{2,1,0:T(8,128)S(1)}, f32[2,128,256]{2,1,0:T(8,128)S(1)}, bf16[64,256,128]{2,1,0:T(8,128)(2,1)S(1)}) custom-call(s32[1,256]{1,0:T(1,128)S(1)} %shard_map.97.listed.words, bf16[2,224,128,128]{3,2,1,0:T(8,128)(2,1)S(1)} %shard_map.96.ratings, ...), custom_call_target="tpu_custom_call" | custom-call | flops 4000000000 | bytes 4096 | tf_op jit(solution)/shard_map/pallas_call | solution.py:240
  29.5 2.3 %shard_map.104 = (f32[4,128,256]{2,1,0:T(8,128)S(1)}, f32[4,128,256]{2,1,0:T(8,128)S(1)}, bf16[64,256,128]{2,1,0:T(8,128)(2,1)S(1)}) custom-call(s32[1,256]{1,0:T(1,128)S(1)} %shard_map.97.listed.words, bf16[2,224,128,128]{3,2,1,0:T(8,128)(2,1)S(1)} %shard_map.96.ratings, bf16[16,128,256]{2,1,0:T(8,128)(2,1)S(1)} %convert_element_type.3.users, ...), custom_call_target="tpu_custom_call" | custom-call | flops 4000000000 | bytes 4096 | tf_op jit(solution)/shard_map/pallas_call | solution.py:240
  33.4 2.1 %collective-permute-start.16 = (s16[528,256]{1,0:T(8,128)(2,1)S(1)}, s16[528,256]{1,0:T(8,128)(2,1)S(1)}, u32[]{:S(2)}, u32[]{:S(2)}) collective-permute-start(s16[528,256]{1,0:T(8,128)(2,1)S(1)} %shard_map.105.refs_9_), channel_id=1, source_target_pairs={{0,24},{4,28},{8,16},{12,20},{16,8},{20,12},{24,0},{28,4},{1,25},{... | collective-permute-start | bytes 811016 | tf_op jit(solution)/shard_map/ppermute | solution.py:37
  35.7 5.0 %shard_map.106.refs_4_.refs_5_ = f32[16,128,256]{2,1,0:T(8,128)S(1)} custom-call(s32[1,256]{1,0:T(1,128)S(1)} %shard_map.97.listed.words, bf16[64,256,128]{2,1,0:T(8,128)(2,1)S(1)} %get-tuple-element.48.refs_0_, bf16[64,256,128]{2,1,0:T(8,128)(2,1)S(1)} %get-tuple-element.49.refs_1_, bf16[64,256,128]{2,1,0:T(8,128)(2,1)S(1)} %get-tuple-element.50.refs_2_, ...), custom_call_target="tpu_custom_call" | custom-call | flops 100000000 | bytes 4096 | tf_op jit(solution)/shard_map/pallas_call | solution.py:308
  40.8 1.6 %collective-permute-done.16.refs_2_ = s16[528,256]{1,0:T(8,128)(2,1)S(1)} collective-permute-done((s16[528,256]{1,0:T(8,128)(2,1)S(1)}, s16[528,256]{1,0:T(8,128)(2,1)S(1)}, u32[]{:S(2)}, u32[]{:S(2)}) %collective-permute-start.16) | collective-permute-done | bytes 270368 | tf_op jit(solution)/shard_map/ppermute | solution.py:37
  44.5 2.7 %shard_map.107 = (f32[16,128,256]{2,1,0:T(8,128)S(1)}, bf16[16,128,256]{2,1,0:T(8,128)(2,1)S(1)}) custom-call(s32[1,256]{1,0:T(1,128)S(1)} %shard_map.97.listed.words, bf16[64,256,128]{2,1,0:T(8,128)(2,1)S(1)} %get-tuple-element.46.held, bf16[4,256,128]{2,1,0:T(8,128)(2,1)S(1)} %collective-permute-done.1.refs_0_, ...), custom_call_target="tpu_custom_call" | custom-call | flops 100000000 | bytes 4096 | tf_op jit(solution)/shard_map/pallas_call | solution.py:321
  47.2 4.4 %collective-permute-done.17.given = bf16[4,256,128]{2,1,0:T(8,128)(2,1)S(1)} collective-permute-done((bf16[4,256,128]{2,1,0:T(8,128)(2,1)S(1)}, bf16[4,256,128]{2,1,0:T(8,128)(2,1)S(1)}, u32[]{:S(2)}, u32[]{:S(2)}) %collective-permute-start.17) | collective-permute-done | bytes 262176 | tf_op jit(solution)/shard_map/ppermute | solution.py:32
  52.4 2.1 %collective-permute-start.21 = (bf16[4,256,128]{2,1,0:T(8,128)(2,1)S(1)}, bf16[4,256,128]{2,1,0:T(8,128)(2,1)S(1)}, u32[]{:S(2)}, u32[]{:S(2)}) collective-permute-start(bf16[4,256,128]{2,1,0:T(8,128)(2,1)S(1)} %shard_map.109.refs_0_.refs_3_), channel_id=1, source_target_pairs={{0,16},{4,20},{8,24},{12,28},{16,0},{20,4},{24,8},{28,12},{1,17},{... | collective-permute-start | bytes 786440 | tf_op jit(solution)/shard_map/ppermute | solution.py:37
  54.4 3.6 %collective-permute-done.18.refs_0_.refs_5_ = bf16[4,256,128]{2,1,0:T(8,128)(2,1)S(1)} collective-permute-done((bf16[4,256,128]{2,1,0:T(8,128)(2,1)S(1)}, bf16[4,256,128]{2,1,0:T(8,128)(2,1)S(1)}, u32[]{:S(2)}, u32[]{:S(2)}) %collective-permute-start.18) | collective-permute-done | bytes 262176 | tf_op jit(solution)/shard_map/ppermute | solution.py:37
  58.0 1.2 %collective-permute-start.19 = (bf16[4,256,128]{2,1,0:T(8,128)(2,1)S(1)}, bf16[4,256,128]{2,1,0:T(8,128)(2,1)S(1)}, u32[]{:S(2)}, u32[]{:S(2)}) collective-permute-start(bf16[4,256,128]{2,1,0:T(8,128)(2,1)S(1)} %collective-permute-done.18.refs_0_.refs_5_), channel_id=1, source_target_pairs={{0,16},{4,20},{8,24},{12,28},{16,0},{20,4},{24,8},{28,12},{1,17},{... | collective-permute-start | bytes 786440 | tf_op jit(solution)/shard_map/ppermute | solution.py:37
  59.6 1.6 %shard_map.110 = (f32[4,128,256]{2,1,0:T(8,128)S(1)}, f32[2,128,256]{2,1,0:T(8,128)S(1)}, f32[2,128,256]{2,1,0:T(8,128)S(1)}, bf16[64,256,128]{2,1,0:T(8,128)(2,1)S(1)}) custom-call(s32[1,256]{1,0:T(1,128)S(1)} %shard_map.95.refs_1_.listed.words, bf16[2,224,128,128]{3,2,1,0:T(8,128)(2,1)S(1)} %shard_map.96.ratings, ...), custom_call_target="tpu_custom_call" | custom-call | flops 4000000000 | bytes 4096 | tf_op jit(solution)/shard_map/pallas_call | solution.py:240
  61.8 1.8 %shard_map.111 = (f32[4,128,256]{2,1,0:T(8,128)S(1)}, f32[2,128,256]{2,1,0:T(8,128)S(1)}, f32[2,128,256]{2,1,0:T(8,128)S(1)}, bf16[64,256,128]{2,1,0:T(8,128)(2,1)S(1)}) custom-call(s32[1,256]{1,0:T(1,128)S(1)} %shard_map.95.refs_1_.listed.words, bf16[2,224,128,128]{3,2,1,0:T(8,128)(2,1)S(1)} %shard_map.96.ratings, ...), custom_call_target="tpu_custom_call" | custom-call | flops 4000000000 | bytes 4096 | tf_op jit(solution)/shard_map/pallas_call | solution.py:240
  64.1 2.7 %collective-permute-done.19.refs_0_ = bf16[4,256,128]{2,1,0:T(8,128)(2,1)S(1)} collective-permute-done((bf16[4,256,128]{2,1,0:T(8,128)(2,1)S(1)}, bf16[4,256,128]{2,1,0:T(8,128)(2,1)S(1)}, u32[]{:S(2)}, u32[]{:S(2)}) %collective-permute-start.19) | collective-permute-done | bytes 262176 | tf_op jit(solution)/shard_map/ppermute | solution.py:37
  67.4 1.1 %collective-permute-start.35 = (s16[528,256]{1,0:T(8,128)(2,1)S(1)}, s16[528,256]{1,0:T(8,128)(2,1)S(1)}, u32[]{:S(2)}, u32[]{:S(2)}) collective-permute-start(s16[528,256]{1,0:T(8,128)(2,1)S(1)} %shard_map.112.refs_2_), channel_id=1, source_target_pairs={{0,8},{4,12},{8,0},{12,4},{16,24},{20,28},{24,16},{28,20},{1,9},{5... | collective-permute-start | bytes 811016 | tf_op jit(solution)/shard_map/ppermute | solution.py:37
  68.7 1.8 %collective-permute-start.36 = (s16[528,256]{1,0:T(8,128)(2,1)S(1)}, s16[528,256]{1,0:T(8,128)(2,1)S(1)}, u32[]{:S(2)}, u32[]{:S(2)}) collective-permute-start(s16[528,256]{1,0:T(8,128)(2,1)S(1)} %shard_map.113.refs_2_), channel_id=1, source_target_pairs={{0,16},{4,20},{8,24},{12,28},{16,0},{20,4},{24,8},{28,12},{1,17},{... | collective-permute-start | bytes 811016 | tf_op jit(solution)/shard_map/ppermute | solution.py:37
  70.5 2.0 %shard_map.114 = (f32[4,128,256]{2,1,0:T(8,128)S(1)}, f32[2,128,256]{2,1,0:T(8,128)S(1)}, f32[2,128,256]{2,1,0:T(8,128)S(1)}, bf16[64,256,128]{2,1,0:T(8,128)(2,1)S(1)}) custom-call(s32[1,256]{1,0:T(1,128)S(1)} %shard_map.95.refs_1_.listed.words, bf16[2,224,128,128]{3,2,1,0:T(8,128)(2,1)S(1)} %shard_map.96.ratings, ...), custom_call_target="tpu_custom_call" | custom-call | flops 4000000000 | bytes 4096 | tf_op jit(solution)/shard_map/pallas_call | solution.py:240
  73.0 1.6 %shard_map.115 = (f32[4,128,256]{2,1,0:T(8,128)S(1)}, f32[1,128,256]{2,1,0:T(8,128)S(1)}, f32[1,128,256]{2,1,0:T(8,128)S(1)}, f32[1,128,256]{2,1,0:T(8,128)S(1)}...) custom-call(s32[1,256]{1,0:T(1,128)S(1)} %shard_map.95.refs_1_.listed.words, ...), custom_call_target="tpu_custom_call" | custom-call | flops 4000000000 | bytes 4096 | tf_op jit(solution)/shard_map/pallas_call | solution.py:240
  74.8 1.3 %collective-permute-done.31.refs_0_ = f32[1,128,256]{2,1,0:T(8,128)S(1)} collective-permute-done((f32[1,128,256]{2,1,0:T(8,128)S(1)}, f32[1,128,256]{2,1,0:T(8,128)S(1)}, u32[]{:S(2)}, u32[]{:S(2)}) %collective-permute-start.31) | collective-permute-done | bytes 131104 | tf_op jit(solution)/shard_map/ppermute | solution.py:37
  77.4 2.7 %collective-permute-start.38 = (s16[528,256]{1,0:T(8,128)(2,1)S(1)}, s16[528,256]{1,0:T(8,128)(2,1)S(1)}, u32[]{:S(2)}, u32[]{:S(2)}) collective-permute-start(s16[528,256]{1,0:T(8,128)(2,1)S(1)} %shard_map.116.refs_9_.refs_6_), channel_id=1, source_target_pairs={{0,27},{1,24},{2,25},{3,26},{4,31},{5,28},{6,29},{7,30},{8,19},{9,... | collective-permute-start | bytes 811016 | tf_op jit(solution)/shard_map/ppermute | solution.py:43
  80.4 1.3 %collective-permute-start.37 = (s16[528,256]{1,0:T(8,128)(2,1)S(1)}, s16[528,256]{1,0:T(8,128)(2,1)S(1)}, u32[]{:S(2)}, u32[]{:S(2)}) collective-permute-start(s16[528,256]{1,0:T(8,128)(2,1)S(1)} %shard_map.119), channel_id=1, source_target_pairs={{0,3},{1,0},{2,1},{3,2},{4,7},{5,4},{6,5},{7,6},{8,11},{9,8},{10,9... | collective-permute-start | bytes 811016 | tf_op jit(solution)/shard_map/ppermute | solution.py:43
  81.7 2.7 %shard_map.117.refs_4_ = f32[16,128,256]{2,1,0:T(8,128)S(1)} custom-call(s32[1,256]{1,0:T(1,128)S(1)} %shard_map.95.refs_1_.listed.words, bf16[64,256,128]{2,1,0:T(8,128)(2,1)S(1)} %get-tuple-element.66.refs_0_, bf16[64,256,128]{2,1,0:T(8,128)(2,1)S(1)} %get-tuple-element.67.refs_1_, bf16[64,256,128]{2,1,0:T(8,128)(2,1)S(1)} %get-tuple-element.68.refs_2_, ...), custom_call_target="tpu_custom_call" | custom-call | flops 100000000 | bytes 4096 | tf_op jit(solution)/shard_map/pallas_call | solution.py:308
  84.5 4.1 %shard_map.118 = (f32[16,128,256]{2,1,0:T(8,128)}, bf16[16,128,256]{2,1,0:T(8,128)(2,1)}) custom-call(s32[1,256]{1,0:T(1,128)S(1)} %shard_map.95.refs_1_.listed.words, bf16[64,256,128]{2,1,0:T(8,128)(2,1)S(1)} %get-tuple-element.63.held, bf16[4,256,128]{2,1,0:T(8,128)(2,1)S(1)} %collective-permute-done.19.refs_0_, ...), custom_call_target="tpu_custom_call" | custom-call | flops 100000000 | bytes 4096 | tf_op jit(solution)/shard_map/pallas_call | solution.py:321
  88.5 4.9 %collective-permute-done.37.delta = s16[528,256]{1,0:T(8,128)(2,1)S(1)} collective-permute-done((s16[528,256]{1,0:T(8,128)(2,1)S(1)}, s16[528,256]{1,0:T(8,128)(2,1)S(1)}, u32[]{:S(2)}, u32[]{:S(2)}) %collective-permute-start.37) | collective-permute-done | bytes 270368 | tf_op jit(solution)/shard_map/ppermute | solution.py:43
  (93 shorter events, 17.4 us)
Async XLA Ops:
  1.8 12.3 %collective-permute-start.3 = (bf16[4,256,128]{2,1,0:T(8,128)(2,1)S(1)}, bf16[4,256,128]{2,1,0:T(8,128)(2,1)S(1)}, u32[]{:S(2)}, u32[]{:S(2)}) collective-permute-start(bf16[4,256,128]{2,1,0:T(8,128)(2,1)S(1)} %shard_map.98.refs_0_.refs_3_), channel_id=1, source_target_pairs={{0,16},{4,20},{8,24},{12,28},{16,0},{20,4},{24,8},{28,12},{1,17},{... | collective-permute-start | bytes 786440 | tf_op jit(solution)/shard_map/ppermute | solution.py:37
  4.8 7.8 %collective-permute-start = (bf16[4,256,128]{2,1,0:T(8,128)(2,1)S(1)}, bf16[4,256,128]{2,1,0:T(8,128)(2,1)S(1)}, u32[]{:S(2)}, u32[]{:S(2)}) collective-permute-start(bf16[4,256,128]{2,1,0:T(8,128)(2,1)S(1)} %shard_map.98.refs_0_.refs_3_), channel_id=1, source_target_pairs={{0,8},{4,12},{8,0},{12,4},{16,24},{20,28},{24,16},{28,20},{1,9},{5... | collective-permute-start | bytes 786440 | tf_op jit(solution)/shard_map/ppermute | solution.py:37
  13.6 8.8 %collective-permute-start.1 = (bf16[4,256,128]{2,1,0:T(8,128)(2,1)S(1)}, bf16[4,256,128]{2,1,0:T(8,128)(2,1)S(1)}, u32[]{:S(2)}, u32[]{:S(2)}) collective-permute-start(bf16[4,256,128]{2,1,0:T(8,128)(2,1)S(1)} %collective-permute-done.refs_0_.refs_5_), channel_id=1, source_target_pairs={{0,16},{4,20},{8,24},{12,28},{16,0},{20,4},{24,8},{28,12},{1,17},{... | collective-permute-start | bytes 786440 | tf_op jit(solution)/shard_map/ppermute | solution.py:37
  16.7 5.8 %collective-permute-start.8 = (f32[2,128,256]{2,1,0:T(8,128)S(1)}, f32[2,128,256]{2,1,0:T(8,128)S(1)}, u32[]{:S(2)}, u32[]{:S(2)}) collective-permute-start(f32[2,128,256]{2,1,0:T(8,128)S(1)} %get-tuple-element.44), channel_id=1, source_target_pairs={{0,4},{4,0},{8,12},{12,8},{16,20},{20,16},{24,28},{28,24},{1,5},{5... | collective-permute-start | bytes 786440 | tf_op jit(solution)/shard_map/ppermute | solution.py:37
  17.4 5.6 %collective-permute-start.9 = (f32[2,128,256]{2,1,0:T(8,128)S(1)}, f32[2,128,256]{2,1,0:T(8,128)S(1)}, u32[]{:S(2)}, u32[]{:S(2)}) collective-permute-start(f32[2,128,256]{2,1,0:T(8,128)S(1)} %get-tuple-element.45), channel_id=1, source_target_pairs={{0,4},{4,0},{8,12},{12,8},{16,20},{20,16},{24,28},{28,24},{1,5},{5... | collective-permute-start | bytes 786440 | tf_op jit(solution)/shard_map/ppermute | solution.py:37
  20.2 4.5 %collective-permute-start.6 = (f32[2,128,256]{2,1,0:T(8,128)S(1)}, f32[2,128,256]{2,1,0:T(8,128)S(1)}, u32[]{:S(2)}, u32[]{:S(2)}) collective-permute-start(f32[2,128,256]{2,1,0:T(8,128)S(1)} %get-tuple-element.42), channel_id=1, source_target_pairs={{0,4},{4,0},{8,12},{12,8},{16,20},{20,16},{24,28},{28,24},{1,5},{5... | collective-permute-start | bytes 786440 | tf_op jit(solution)/shard_map/ppermute | solution.py:37
  20.7 4.0 %collective-permute-start.7 = (f32[2,128,256]{2,1,0:T(8,128)S(1)}, f32[2,128,256]{2,1,0:T(8,128)S(1)}, u32[]{:S(2)}, u32[]{:S(2)}) collective-permute-start(f32[2,128,256]{2,1,0:T(8,128)S(1)} %get-tuple-element.43), channel_id=1, source_target_pairs={{0,4},{4,0},{8,12},{12,8},{16,20},{20,16},{24,28},{28,24},{1,5},{5... | collective-permute-start | bytes 786440 | tf_op jit(solution)/shard_map/ppermute | solution.py:37
  22.4 4.0 %collective-permute-start.2 = (bf16[4,256,128]{2,1,0:T(8,128)(2,1)S(1)}, bf16[4,256,128]{2,1,0:T(8,128)(2,1)S(1)}, u32[]{:S(2)}, u32[]{:S(2)}) collective-permute-start(bf16[4,256,128]{2,1,0:T(8,128)(2,1)S(1)} %collective-permute-done.1.refs_0_), channel_id=1, source_target_pairs={{0,4},{4,0},{8,12},{12,8},{16,20},{20,16},{24,28},{28,24},{1,5},{5... | collective-permute-start | bytes 786440 | tf_op jit(solution)/shard_map/ppermute | solution.py:37
  22.4 7.1 %collective-permute-start.10 = (bf16[4,256,128]{2,1,0:T(8,128)(2,1)S(1)}, bf16[4,256,128]{2,1,0:T(8,128)(2,1)S(1)}, u32[]{:S(2)}, u32[]{:S(2)}) collective-permute-start(bf16[4,256,128]{2,1,0:T(8,128)(2,1)S(1)} %shard_map.98.refs_0_.refs_3_), channel_id=1, source_target_pairs={{0,4},{4,0},{8,12},{12,8},{16,20},{20,16},{24,28},{28,24},{1,5},{5... | collective-permute-start | bytes 786440 | tf_op jit(solution)/shard_map/ppermute | solution.py:37
  23.1 10.1 %collective-permute-start.13 = (s16[528,256]{1,0:T(8,128)(2,1)S(1)}, s16[528,256]{1,0:T(8,128)(2,1)S(1)}, u32[]{:S(2)}, u32[]{:S(2)}) collective-permute-start(s16[528,256]{1,0:T(8,128)(2,1)S(1)} %shard_map.101.refs_2_), channel_id=1, source_target_pairs={{0,8},{4,12},{8,0},{12,4},{16,24},{20,28},{24,16},{28,20},{1,9},{5... | collective-permute-start | bytes 811016 | tf_op jit(solution)/shard_map/ppermute | solution.py:37
  24.8 8.4 %collective-permute-start.14 = (s16[528,256]{1,0:T(8,128)(2,1)S(1)}, s16[528,256]{1,0:T(8,128)(2,1)S(1)}, u32[]{:S(2)}, u32[]{:S(2)}) collective-permute-start(s16[528,256]{1,0:T(8,128)(2,1)S(1)} %shard_map.102.refs_2_), channel_id=1, source_target_pairs={{0,16},{4,20},{8,24},{12,28},{16,0},{20,4},{24,8},{28,12},{1,17},{... | collective-permute-start | bytes 811016 | tf_op jit(solution)/shard_map/ppermute | solution.py:37
  28.8 4.0 %collective-permute-start.11 = (f32[2,128,256]{2,1,0:T(8,128)S(1)}, f32[2,128,256]{2,1,0:T(8,128)S(1)}, u32[]{:S(2)}, u32[]{:S(2)}) collective-permute-start(f32[2,128,256]{2,1,0:T(8,128)S(1)} %get-tuple-element.51), channel_id=1, source_target_pairs={{0,4},{4,0},{8,12},{12,8},{16,20},{20,16},{24,28},{28,24},{1,5},{5... | collective-permute-start | bytes 786440 | tf_op jit(solution)/shard_map/ppermute | solution.py:37
  31.9 8.9 %collective-permute-start.15 = (f32[4,128,256]{2,1,0:T(8,128)S(1)}, f32[4,128,256]{2,1,0:T(8,128)S(1)}, u32[]{:S(2)}, u32[]{:S(2)}) collective-permute-start(f32[4,128,256]{2,1,0:T(8,128)S(1)} %get-tuple-element.55), channel_id=1, source_target_pairs={{0,4},{4,0},{8,12},{12,8},{16,20},{20,16},{24,28},{28,24},{1,5},{5... | collective-permute-start | bytes 1572872 | tf_op jit(solution)/shard_map/ppermute | solution.py:37
  33.4 9.0 %collective-permute-start.16 = (s16[528,256]{1,0:T(8,128)(2,1)S(1)}, s16[528,256]{1,0:T(8,128)(2,1)S(1)}, u32[]{:S(2)}, u32[]{:S(2)}) collective-permute-start(s16[528,256]{1,0:T(8,128)(2,1)S(1)} %shard_map.105.refs_9_), channel_id=1, source_target_pairs={{0,24},{4,28},{8,16},{12,20},{16,8},{20,12},{24,0},{28,4},{1,25},{... | collective-permute-start | bytes 811016 | tf_op jit(solution)/shard_map/ppermute | solution.py:37
  42.8 8.8 %collective-permute-start.17 = (bf16[4,256,128]{2,1,0:T(8,128)(2,1)S(1)}, bf16[4,256,128]{2,1,0:T(8,128)(2,1)S(1)}, u32[]{:S(2)}, u32[]{:S(2)}) collective-permute-start(bf16[4,256,128]{2,1,0:T(8,128)(2,1)S(1)} %get-tuple-element.56), channel_id=1, source_target_pairs={{0,1},{1,2},{2,3},{3,0},{4,5},{5,6},{6,7},{7,4},{8,9},{9,10},{10,1... | collective-permute-start | bytes 786440 | tf_op jit(solution)/shard_map/ppermute | solution.py:32
  51.6 6.4 %collective-permute-start.18 = (bf16[4,256,128]{2,1,0:T(8,128)(2,1)S(1)}, bf16[4,256,128]{2,1,0:T(8,128)(2,1)S(1)}, u32[]{:S(2)}, u32[]{:S(2)}) collective-permute-start(bf16[4,256,128]{2,1,0:T(8,128)(2,1)S(1)} %shard_map.109.refs_0_.refs_3_), channel_id=1, source_target_pairs={{0,8},{4,12},{8,0},{12,4},{16,24},{20,28},{24,16},{28,20},{1,9},{5... | collective-permute-start | bytes 786440 | tf_op jit(solution)/shard_map/ppermute | solution.py:37
  52.4 6.9 %collective-permute-start.21 = (bf16[4,256,128]{2,1,0:T(8,128)(2,1)S(1)}, bf16[4,256,128]{2,1,0:T(8,128)(2,1)S(1)}, u32[]{:S(2)}, u32[]{:S(2)}) collective-permute-start(bf16[4,256,128]{2,1,0:T(8,128)(2,1)S(1)} %shard_map.109.refs_0_.refs_3_), channel_id=1, source_target_pairs={{0,16},{4,20},{8,24},{12,28},{16,0},{20,4},{24,8},{28,12},{1,17},{... | collective-permute-start | bytes 786440 | tf_op jit(solution)/shard_map/ppermute | solution.py:37
  58.0 8.7 %collective-permute-start.19 = (bf16[4,256,128]{2,1,0:T(8,128)(2,1)S(1)}, bf16[4,256,128]{2,1,0:T(8,128)(2,1)S(1)}, u32[]{:S(2)}, u32[]{:S(2)}) collective-permute-start(bf16[4,256,128]{2,1,0:T(8,128)(2,1)S(1)} %collective-permute-done.18.refs_0_.refs_5_), channel_id=1, source_target_pairs={{0,16},{4,20},{8,24},{12,28},{16,0},{20,4},{24,8},{28,12},{1,17},{... | collective-permute-start | bytes 786440 | tf_op jit(solution)/shard_map/ppermute | solution.py:37
  61.2 5.6 %collective-permute-start.26 = (f32[2,128,256]{2,1,0:T(8,128)S(1)}, f32[2,128,256]{2,1,0:T(8,128)S(1)}, u32[]{:S(2)}, u32[]{:S(2)}) collective-permute-start(f32[2,128,256]{2,1,0:T(8,128)S(1)} %get-tuple-element.61), channel_id=1, source_target_pairs={{0,4},{4,0},{8,12},{12,8},{16,20},{20,16},{24,28},{28,24},{1,5},{5... | collective-permute-start | bytes 786440 | tf_op jit(solution)/shard_map/ppermute | solution.py:37
  61.4 5.9 %collective-permute-start.27 = (f32[2,128,256]{2,1,0:T(8,128)S(1)}, f32[2,128,256]{2,1,0:T(8,128)S(1)}, u32[]{:S(2)}, u32[]{:S(2)}) collective-permute-start(f32[2,128,256]{2,1,0:T(8,128)S(1)} %get-tuple-element.62), channel_id=1, source_target_pairs={{0,4},{4,0},{8,12},{12,8},{16,20},{20,16},{24,28},{28,24},{1,5},{5... | collective-permute-start | bytes 786440 | tf_op jit(solution)/shard_map/ppermute | solution.py:37
  63.5 5.0 %collective-permute-start.24 = (f32[2,128,256]{2,1,0:T(8,128)S(1)}, f32[2,128,256]{2,1,0:T(8,128)S(1)}, u32[]{:S(2)}, u32[]{:S(2)}) collective-permute-start(f32[2,128,256]{2,1,0:T(8,128)S(1)} %get-tuple-element.59), channel_id=1, source_target_pairs={{0,4},{4,0},{8,12},{12,8},{16,20},{20,16},{24,28},{28,24},{1,5},{5... | collective-permute-start | bytes 786440 | tf_op jit(solution)/shard_map/ppermute | solution.py:37
  63.6 4.9 %collective-permute-start.25 = (f32[2,128,256]{2,1,0:T(8,128)S(1)}, f32[2,128,256]{2,1,0:T(8,128)S(1)}, u32[]{:S(2)}, u32[]{:S(2)}) collective-permute-start(f32[2,128,256]{2,1,0:T(8,128)S(1)} %get-tuple-element.60), channel_id=1, source_target_pairs={{0,4},{4,0},{8,12},{12,8},{16,20},{20,16},{24,28},{28,24},{1,5},{5... | collective-permute-start | bytes 786440 | tf_op jit(solution)/shard_map/ppermute | solution.py:37
  66.8 3.7 %collective-permute-start.20 = (bf16[4,256,128]{2,1,0:T(8,128)(2,1)S(1)}, bf16[4,256,128]{2,1,0:T(8,128)(2,1)S(1)}, u32[]{:S(2)}, u32[]{:S(2)}) collective-permute-start(bf16[4,256,128]{2,1,0:T(8,128)(2,1)S(1)} %collective-permute-done.19.refs_0_), channel_id=1, source_target_pairs={{0,4},{4,0},{8,12},{12,8},{16,20},{20,16},{24,28},{28,24},{1,5},{5... | collective-permute-start | bytes 786440 | tf_op jit(solution)/shard_map/ppermute | solution.py:37
  66.8 6.3 %collective-permute-start.28 = (bf16[4,256,128]{2,1,0:T(8,128)(2,1)S(1)}, bf16[4,256,128]{2,1,0:T(8,128)(2,1)S(1)}, u32[]{:S(2)}, u32[]{:S(2)}) collective-permute-start(bf16[4,256,128]{2,1,0:T(8,128)(2,1)S(1)} %shard_map.109.refs_0_.refs_3_), channel_id=1, source_target_pairs={{0,4},{4,0},{8,12},{12,8},{16,20},{20,16},{24,28},{28,24},{1,5},{5... | collective-permute-start | bytes 786440 | tf_op jit(solution)/shard_map/ppermute | solution.py:37
  67.4 12.6 %collective-permute-start.35 = (s16[528,256]{1,0:T(8,128)(2,1)S(1)}, s16[528,256]{1,0:T(8,128)(2,1)S(1)}, u32[]{:S(2)}, u32[]{:S(2)}) collective-permute-start(s16[528,256]{1,0:T(8,128)(2,1)S(1)} %shard_map.112.refs_2_), channel_id=1, source_target_pairs={{0,8},{4,12},{8,0},{12,4},{16,24},{20,28},{24,16},{28,20},{1,9},{5... | collective-permute-start | bytes 811016 | tf_op jit(solution)/shard_map/ppermute | solution.py:37
  68.7 11.4 %collective-permute-start.36 = (s16[528,256]{1,0:T(8,128)(2,1)S(1)}, s16[528,256]{1,0:T(8,128)(2,1)S(1)}, u32[]{:S(2)}, u32[]{:S(2)}) collective-permute-start(s16[528,256]{1,0:T(8,128)(2,1)S(1)} %shard_map.113.refs_2_), channel_id=1, source_target_pairs={{0,16},{4,20},{8,24},{12,28},{16,0},{20,4},{24,8},{28,12},{1,17},{... | collective-permute-start | bytes 811016 | tf_op jit(solution)/shard_map/ppermute | solution.py:37
  72.5 3.7 %collective-permute-start.29 = (f32[2,128,256]{2,1,0:T(8,128)S(1)}, f32[2,128,256]{2,1,0:T(8,128)S(1)}, u32[]{:S(2)}, u32[]{:S(2)}) collective-permute-start(f32[2,128,256]{2,1,0:T(8,128)S(1)} %get-tuple-element.69), channel_id=1, source_target_pairs={{0,4},{4,0},{8,12},{12,8},{16,20},{20,16},{24,28},{28,24},{1,5},{5... | collective-permute-start | bytes 786440 | tf_op jit(solution)/shard_map/ppermute | solution.py:37
  72.5 4.0 %collective-permute-start.30 = (f32[2,128,256]{2,1,0:T(8,128)S(1)}, f32[2,128,256]{2,1,0:T(8,128)S(1)}, u32[]{:S(2)}, u32[]{:S(2)}) collective-permute-start(f32[2,128,256]{2,1,0:T(8,128)S(1)} %get-tuple-element.70), channel_id=1, source_target_pairs={{0,4},{4,0},{8,12},{12,8},{16,20},{20,16},{24,28},{28,24},{1,5},{5... | collective-permute-start | bytes 786440 | tf_op jit(solution)/shard_map/ppermute | solution.py:37
  76.2 3.9 %collective-permute-start.33 = (f32[1,128,256]{2,1,0:T(8,128)S(1)}, f32[1,128,256]{2,1,0:T(8,128)S(1)}, u32[]{:S(2)}, u32[]{:S(2)}) collective-permute-start(f32[1,128,256]{2,1,0:T(8,128)S(1)} %get-tuple-element.76), channel_id=1, source_target_pairs={{0,4},{4,0},{8,12},{12,8},{16,20},{20,16},{24,28},{28,24},{1,5},{5... | collective-permute-start | bytes 393224 | tf_op jit(solution)/shard_map/ppermute | solution.py:37
  76.6 3.5 %collective-permute-start.34 = (f32[1,128,256]{2,1,0:T(8,128)S(1)}, f32[1,128,256]{2,1,0:T(8,128)S(1)}, u32[]{:S(2)}, u32[]{:S(2)}) collective-permute-start(f32[1,128,256]{2,1,0:T(8,128)S(1)} %get-tuple-element.77), channel_id=1, source_target_pairs={{0,4},{4,0},{8,12},{12,8},{16,20},{20,16},{24,28},{28,24},{1,5},{5... | collective-permute-start | bytes 393224 | tf_op jit(solution)/shard_map/ppermute | solution.py:37
  77.4 11.1 %collective-permute-start.38 = (s16[528,256]{1,0:T(8,128)(2,1)S(1)}, s16[528,256]{1,0:T(8,128)(2,1)S(1)}, u32[]{:S(2)}, u32[]{:S(2)}) collective-permute-start(s16[528,256]{1,0:T(8,128)(2,1)S(1)} %shard_map.116.refs_9_.refs_6_), channel_id=1, source_target_pairs={{0,27},{1,24},{2,25},{3,26},{4,31},{5,28},{6,29},{7,30},{8,19},{9,... | collective-permute-start | bytes 811016 | tf_op jit(solution)/shard_map/ppermute | solution.py:43
  80.4 13.0 %collective-permute-start.37 = (s16[528,256]{1,0:T(8,128)(2,1)S(1)}, s16[528,256]{1,0:T(8,128)(2,1)S(1)}, u32[]{:S(2)}, u32[]{:S(2)}) collective-permute-start(s16[528,256]{1,0:T(8,128)(2,1)S(1)} %shard_map.119), channel_id=1, source_target_pairs={{0,3},{1,0},{2,1},{3,2},{4,7},{5,4},{6,5},{7,6},{8,11},{9,8},{10,9... | collective-permute-start | bytes 811016 | tf_op jit(solution)/shard_map/ppermute | solution.py:43
  (16 other events, 45.6 us)
